TPU v7x, 32 devices: a whole 2x2x4 slice. The times are simulated.
32 devices in a mesh: expert: 8 (over z, y), tensor: 4 (over x, core).
Axes of the slice: x: 2, y: 2, z: 4, core: 2. Of those that a mesh axis runs over, the one named last changes fastest.
Arguments:
- hidden_in: bfloat16 [3072, 2048], P('expert'), may hold values from -6 to 6
- cotangent: bfloat16 [3072, 2048], P('expert'), may hold values from -6 to 6
- segments: int32 [3072], P('expert'), may hold values from 0 to 7, as said below
- positions: int32 [3072], P('expert'), may hold values from 0 to 1535, as said below
- routes: int32 [3072, 8], P('expert'), may hold values from 0 to 15, as said below
- attn_gain: float32 [2048], replicated, may hold values from 0.5 to 1.5
- w_query: bfloat16 [2048, 4096], P(None, 'tensor')
- w_key: bfloat16 [2048, 512], P(None, 'tensor')
- value_weight: bfloat16 [2048, 512], P(None, 'tensor'), may hold values from -0.125 to 0.125
- q_gain: float32 [128], replicated
- k_gain: float32 [128], replicated
- w_out: bfloat16 [4096, 2048], P('tensor'), may hold values from -0.5 to 0.5
- ffn_gain: float32 [2048], replicated, may hold values from 0.5 to 1.5
- router: bfloat16 [2048, 16], replicated
- w_gate: bfloat16 [16, 2048, 768], P('expert', None, 'tensor'), may hold values from -0.125 to 0.125
- w_up: bfloat16 [16, 2048, 768], P('expert', None, 'tensor'), may hold values from -0.125 to 0.125
- w_down: bfloat16 [16, 768, 2048], P('expert', 'tensor'), may hold values from -0.4375 to 0.4375
Outputs:
- layer_out: bfloat16 [3072, 2048], P('expert')
- input_grad: float32 [3072, 2048], P('expert')
- attn_gain_grad: float32 [2048], P('expert')
- w_query_grad: float32 [2048, 4096], P('expert', 'tensor')
- w_key_grad: float32 [2048, 512], P('expert', 'tensor')
- w_value_grad: float32 [2048, 512], P('expert', 'tensor')
- q_gain_grad: float32 [128], P('expert')
- k_gain_grad: float32 [128], P('expert')
- w_out_grad: float32 [4096, 2048], P('tensor', 'expert')
- ffn_gain_grad: float32 [2048], P('expert')
- router_grad: float32 [2048, 16], P('expert')
- w_gate_grad: float32 [16, 2048, 768], P('expert', None, 'tensor')
- w_up_grad: float32 [16, 2048, 768], P('expert', None, 'tensor')
- w_down_grad: float32 [16, 768, 2048], P('expert', 'tensor')
Inputs may be any that keep to these rules, and one draw needn't show every extreme that they name: `routes`: each row names 8 different experts. The rows of one block of 384 consecutive tokens name each expert at least 96 and at most 288 times; one expert, the same for every block, is named exactly 288 times in every block. `segments`: each block of 384 consecutive tokens holds exactly 8 documents, numbered 0 to 7 in order; the numbers never fall and rise by at most one from token to token. Within a document positions rise by one from token to token; the first token of each block of 384 tokens has position 0 and the last has position 1535.
All inputs are finite; a program needn't handle non-finite values.
Results may differ from a plain program's by a relative error of at most 0.02.
Values may be sent and summed in bfloat16 or wider, within the bound.
No kernel may reach another device: no remote copies, remote signals or barrier semaphores. Data moves between devices by JAX's collectives and lax.ppermute only.
A program may use at most 320 MiB of HBM per device.

v0:
```python
import jax
import jax.numpy as jnp
from jax import lax
from jax.sharding import PartitionSpec as P

epsilon = 1e-06
rope_base = 1000000.0
far_below = -1e30


def rope_tables(positions, head_size):
    half_size = head_size // 2
    frequency = rope_base ** (-(jnp.arange(half_size, dtype=jnp.float32) * 2.0) / head_size)
    angles = positions.astype(jnp.float32)[:, None] * frequency[None, :]
    cosine = jnp.cos(angles)
    sine_table = jnp.sin(angles)
    return (jnp.concatenate([cosine, cosine], -1), jnp.concatenate([sine_table, sine_table], -1))


def rotate(value_rows, cosine, sine_table):
    half_size = value_rows.shape[-1] // 2
    turned = jnp.concatenate([-value_rows[..., half_size:], value_rows[..., :half_size]], -1)
    return value_rows * cosine[:, None, :] + turned * sine_table[:, None, :]


def rotate_back(gradient, cosine, sine_table):
    half_size = gradient.shape[-1] // 2
    scaled = gradient * sine_table[:, None, :]
    return gradient * cosine[:, None, :] + jnp.concatenate(
        [scaled[..., half_size:], -scaled[..., :half_size]], -1
    )


def norm_back(grad_scaled, value_rows, scales):
    return scales * (
        grad_scaled
        - value_rows * scales * scales * jnp.mean(grad_scaled * value_rows, -1, keepdims=True)
    )


def send_rows(buffer):
    return lax.all_to_all(buffer, "expert", split_axis=0, concat_axis=0, tiled=True)


def return_rows(partial_value):
    summed_part = lax.psum_scatter(partial_value, "tensor", scatter_dimension=1, tiled=True).astype(
        jnp.bfloat16
    )
    complete = lax.all_gather(summed_part, "tensor", axis=1, tiled=True)
    return lax.all_to_all(complete, "expert", split_axis=0, concat_axis=0, tiled=True)


def body(
    hidden_in,
    cotangent,
    segments,
    positions,
    routes,
    attn_gain,
    w_query,
    w_key,
    value_weight,
    q_gain,
    k_gain,
    w_out,
    ffn_gain,
    router,
    w_gate,
    w_up,
    w_down,
):
    tok_count, model_width = hidden_in.shape
    head_size = q_gain.shape[0]
    q_heads = w_query.shape[1] // head_size
    kv_heads = w_key.shape[1] // head_size
    query_group_count = q_heads // kv_heads
    experts = router.shape[1]
    top_count = routes.shape[1]
    local_experts = w_gate.shape[0]
    expert_ranks = lax.axis_size("expert")
    base_load = tok_count * top_count // experts
    capacity = base_load + base_load // 2
    score_scale = head_size ** (-0.5)
    inputs = hidden_in.astype(jnp.float32)
    inv_first = lax.rsqrt(jnp.mean(inputs * inputs, -1, keepdims=True) + epsilon)
    normalized_input = (inputs * inv_first * attn_gain).astype(jnp.bfloat16)
    query_raw = jnp.dot(normalized_input, w_query, preferred_element_type=jnp.float32).reshape(
        tok_count, q_heads, head_size
    )
    key_unrotated = jnp.dot(normalized_input, w_key, preferred_element_type=jnp.float32).reshape(
        tok_count, kv_heads, head_size
    )
    value_rows = (
        jnp.dot(normalized_input, value_weight, preferred_element_type=jnp.float32)
        .astype(jnp.bfloat16)
        .reshape(tok_count, kv_heads, head_size)
    )
    cosine, sine_table = rope_tables(positions, head_size)
    query_inv = lax.rsqrt(jnp.mean(query_raw * query_raw, -1, keepdims=True) + epsilon)
    key_inv = lax.rsqrt(jnp.mean(key_unrotated * key_unrotated, -1, keepdims=True) + epsilon)
    query_hat = query_raw * query_inv
    key_hat = key_unrotated * key_inv
    query_rows = (
        rotate(query_hat * q_gain, cosine, sine_table)
        .astype(jnp.bfloat16)
        .reshape(tok_count, kv_heads, query_group_count, head_size)
    )
    keys_rotated = rotate(key_hat * k_gain, cosine, sine_table).astype(jnp.bfloat16)
    token_index = jnp.arange(tok_count, dtype=jnp.int32)
    allowed = (segments[:, None] == segments[None, :]) & (
        token_index[:, None] >= token_index[None, :]
    )

    def scores_of():
        raw_scores = (
            jnp.einsum(
                "tkgd,skd->kgts", query_rows, keys_rotated, preferred_element_type=jnp.float32
            )
            * score_scale
        )
        return jnp.where(allowed, raw_scores, far_below)

    scores = scores_of()
    top_score = jnp.max(scores, -1, keepdims=True)
    log_total = top_score + jnp.log(jnp.sum(jnp.exp(scores - top_score), -1, keepdims=True))
    prob_low = jnp.exp(scores - log_total).astype(jnp.bfloat16)
    attended_rows = (
        jnp.einsum("kgts,skd->tkgd", prob_low, value_rows, preferred_element_type=jnp.float32)
        .astype(jnp.bfloat16)
        .reshape(tok_count, q_heads * head_size)
    )
    attn_part = jnp.dot(attended_rows, w_out, preferred_element_type=jnp.float32)
    residual = inputs + lax.psum(attn_part, "tensor")
    inv_second = lax.rsqrt(jnp.mean(residual * residual, -1, keepdims=True) + epsilon)
    normed_ffn = (residual * inv_second * ffn_gain).astype(jnp.bfloat16)
    logits = jnp.dot(normed_ffn, router, preferred_element_type=jnp.float32)
    chosen = jnp.take_along_axis(logits, routes, 1)
    gate_weights = jax.nn.softmax(chosen, -1)
    gate_mats, up_mats, down_mats = (w_gate, w_up, w_down)
    flat_routes = routes.reshape(-1)
    expert_ids = jnp.arange(experts, dtype=jnp.int32)
    picked = (flat_routes[:, None] == expert_ids[None, :]).astype(jnp.int32)
    places = jnp.sum(picked * (jnp.cumsum(picked, 0) - 1), 1)
    slot_index = flat_routes * capacity + places
    owners = jnp.arange(tok_count * top_count, dtype=jnp.int32) // top_count
    dispatch = (
        jnp.zeros((experts * capacity, model_width), jnp.bfloat16)
        .at[slot_index]
        .set(normed_ffn[owners])
        .reshape(experts, capacity, model_width)
    )
    received = send_rows(dispatch)
    received = received.reshape(expert_ranks, local_experts, received.shape[1], model_width)
    gate_pre = jnp.einsum("secd,edf->secf", received, gate_mats, preferred_element_type=jnp.float32)
    up_pre = jnp.einsum("secd,edf->secf", received, up_mats, preferred_element_type=jnp.float32)
    activated = jax.nn.silu(gate_pre)
    middle = (activated * up_pre).astype(jnp.bfloat16)
    expert_out = jnp.einsum(
        "secf,efd->secd", middle, down_mats, preferred_element_type=jnp.float32
    ).reshape(experts, -1, model_width)
    returned = return_rows(expert_out).reshape(experts * capacity, model_width)
    routed = returned[slot_index].reshape(tok_count, top_count, model_width)
    layer_out = (
        residual + jnp.sum(gate_weights[:, :, None] * routed.astype(jnp.float32), 1)
    ).astype(jnp.bfloat16)
    grad_out = cotangent.astype(jnp.float32)
    gate_grad = jnp.sum(routed.astype(jnp.float32) * grad_out[:, None, :], -1)
    grad_routed = (
        (gate_weights[:, :, None] * grad_out[:, None, :])
        .astype(jnp.bfloat16)
        .reshape(tok_count * top_count, model_width)
    )
    grad_dispatch = (
        jnp.zeros((experts * capacity, model_width), jnp.bfloat16)
        .at[slot_index]
        .set(grad_routed)
        .reshape(experts, capacity, model_width)
    )
    grad_received = send_rows(grad_dispatch)
    grad_received = grad_received.reshape(
        expert_ranks, local_experts, grad_received.shape[1], model_width
    )
    grad_middle = jnp.einsum(
        "secd,efd->secf", grad_received, down_mats, preferred_element_type=jnp.float32
    )
    w_down_grad = jnp.einsum(
        "secf,secd->efd", middle, grad_received, preferred_element_type=jnp.float32
    )
    sigmoid_gate = jax.nn.sigmoid(gate_pre)
    grad_gate_pre = (
        grad_middle * up_pre * sigmoid_gate * (1.0 + gate_pre * (1.0 - sigmoid_gate))
    ).astype(jnp.bfloat16)
    grad_up_pre = (grad_middle * activated).astype(jnp.bfloat16)
    w_gate_grad = jnp.einsum(
        "secd,secf->edf", received, grad_gate_pre, preferred_element_type=jnp.float32
    )
    w_up_grad = jnp.einsum(
        "secd,secf->edf", received, grad_up_pre, preferred_element_type=jnp.float32
    )
    grad_rows = jnp.einsum(
        "secf,edf->secd", grad_gate_pre, gate_mats, preferred_element_type=jnp.float32
    ) + jnp.einsum("secf,edf->secd", grad_up_pre, up_mats, preferred_element_type=jnp.float32)
    grad_back = return_rows(grad_rows.reshape(experts, -1, model_width)).reshape(
        experts * capacity, model_width
    )
    grad_normed_ffn = jnp.sum(
        grad_back[slot_index].reshape(tok_count, top_count, model_width).astype(jnp.float32), 1
    )
    grad_chosen = gate_weights * (gate_grad - jnp.sum(gate_weights * gate_grad, -1, keepdims=True))
    grad_logits = jnp.sum(
        (routes[:, :, None] == expert_ids[None, None, :]).astype(jnp.float32)
        * grad_chosen[:, :, None],
        1,
    ).astype(jnp.bfloat16)
    router_grad = jnp.einsum(
        "td,te->de", normed_ffn, grad_logits, preferred_element_type=jnp.float32
    )
    grad_normed_ffn = grad_normed_ffn + jnp.einsum(
        "te,de->td", grad_logits, router, preferred_element_type=jnp.float32
    )
    ffn_gain_grad = jnp.sum(grad_normed_ffn * residual * inv_second, 0)
    grad_residual = grad_out + norm_back(grad_normed_ffn * ffn_gain, residual, inv_second)
    grad_attn = grad_residual.astype(jnp.bfloat16)
    w_out_grad = jnp.einsum(
        "tc,td->cd", attended_rows, grad_attn, preferred_element_type=jnp.float32
    )
    grad_attended = (
        jnp.einsum("td,cd->tc", grad_attn, w_out, preferred_element_type=jnp.float32)
        .astype(jnp.bfloat16)
        .reshape(tok_count, kv_heads, query_group_count, head_size)
    )
    probability = jnp.exp(scores_of() - log_total)
    prob_again = probability.astype(jnp.bfloat16)
    grad_prob = jnp.einsum(
        "tkgd,skd->kgts", grad_attended, value_rows, preferred_element_type=jnp.float32
    )
    grad_scores = (
        probability * (grad_prob - jnp.sum(probability * grad_prob, -1, keepdims=True))
    ).astype(jnp.bfloat16)
    grad_queries = (
        jnp.einsum("kgts,skd->tkgd", grad_scores, keys_rotated, preferred_element_type=jnp.float32)
        * score_scale
    ).reshape(tok_count, q_heads, head_size)
    grad_keys = (
        jnp.einsum("kgts,tkgd->skd", grad_scores, query_rows, preferred_element_type=jnp.float32)
        * score_scale
    )
    grad_values = (
        jnp.einsum("kgts,tkgd->skd", prob_again, grad_attended, preferred_element_type=jnp.float32)
        .astype(jnp.bfloat16)
        .reshape(tok_count, kv_heads * head_size)
    )
    grad_query_rot = rotate_back(grad_queries, cosine, sine_table)
    grad_key_rot = rotate_back(grad_keys, cosine, sine_table)
    q_gain_part = jnp.sum((grad_query_rot * query_hat).reshape(-1, head_size), 0)
    k_gain_part = jnp.sum((grad_key_rot * key_hat).reshape(-1, head_size), 0)
    grad_query_raw = (
        norm_back(grad_query_rot * q_gain, query_raw, query_inv)
        .astype(jnp.bfloat16)
        .reshape(tok_count, q_heads * head_size)
    )
    grad_key_raw = (
        norm_back(grad_key_rot * k_gain, key_unrotated, key_inv)
        .astype(jnp.bfloat16)
        .reshape(tok_count, kv_heads * head_size)
    )
    w_query_grad = jnp.einsum(
        "td,tc->dc", normalized_input, grad_query_raw, preferred_element_type=jnp.float32
    )
    w_key_grad = jnp.einsum(
        "td,tc->dc", normalized_input, grad_key_raw, preferred_element_type=jnp.float32
    )
    w_value_grad = jnp.einsum(
        "td,tc->dc", normalized_input, grad_values, preferred_element_type=jnp.float32
    )
    grad_normed_part = jnp.einsum(
        "tc,dc->td", grad_query_raw, w_query, preferred_element_type=jnp.float32
    )
    grad_normed_part = grad_normed_part + jnp.einsum(
        "tc,dc->td", grad_key_raw, w_key, preferred_element_type=jnp.float32
    )
    grad_normed_part = grad_normed_part + jnp.einsum(
        "tc,dc->td", grad_values, value_weight, preferred_element_type=jnp.float32
    )
    grad_normed, q_gain_grad, k_gain_grad = (
        lax.psum(grad_normed_part.astype(jnp.bfloat16), "tensor").astype(jnp.float32),
        lax.psum(q_gain_part.astype(jnp.bfloat16), "tensor").astype(jnp.float32),
        lax.psum(k_gain_part.astype(jnp.bfloat16), "tensor").astype(jnp.float32),
    )
    attn_gain_grad = jnp.sum(grad_normed * inputs * inv_first, 0)
    input_grad = grad_residual + norm_back(grad_normed * attn_gain, inputs, inv_first)
    summed = (
        lax.psum_scatter(
            w_query_grad.astype(jnp.bfloat16), "expert", scatter_dimension=0, tiled=True
        ).astype(jnp.float32),
        lax.psum_scatter(
            w_key_grad.astype(jnp.bfloat16), "expert", scatter_dimension=0, tiled=True
        ).astype(jnp.float32),
        lax.psum_scatter(
            w_value_grad.astype(jnp.bfloat16), "expert", scatter_dimension=0, tiled=True
        ).astype(jnp.float32),
        lax.psum_scatter(
            w_out_grad.astype(jnp.bfloat16), "expert", scatter_dimension=1, tiled=True
        ).astype(jnp.float32),
        lax.psum_scatter(
            router_grad.astype(jnp.bfloat16), "expert", scatter_dimension=0, tiled=True
        ).astype(jnp.float32),
        lax.psum_scatter(
            attn_gain_grad.astype(jnp.bfloat16), "expert", scatter_dimension=0, tiled=True
        ).astype(jnp.float32),
        lax.psum_scatter(
            ffn_gain_grad.astype(jnp.bfloat16), "expert", scatter_dimension=0, tiled=True
        ).astype(jnp.float32),
        lax.psum_scatter(
            q_gain_grad.astype(jnp.bfloat16), "expert", scatter_dimension=0, tiled=True
        ).astype(jnp.float32),
        lax.psum_scatter(
            k_gain_grad.astype(jnp.bfloat16), "expert", scatter_dimension=0, tiled=True
        ).astype(jnp.float32),
    )
    return (
        layer_out,
        input_grad,
        summed[5],
        summed[0],
        summed[1],
        summed[2],
        summed[7],
        summed[8],
        summed[3],
        summed[6],
        summed[4],
        w_gate_grad,
        w_up_grad,
        w_down_grad,
    )


def solution(mesh):
    placed = (
        P("expert", None),
        P("expert", None),
        P("expert"),
        P("expert"),
        P("expert", None),
        P(),
        P(None, "tensor"),
        P(None, "tensor"),
        P(None, "tensor"),
        P(),
        P(),
        P("tensor", None),
        P(),
        P(),
        P("expert", None, "tensor"),
        P("expert", None, "tensor"),
        P("expert", "tensor", None),
    )
    return jax.shard_map(
        body,
        mesh=mesh,
        in_specs=placed,
        out_specs=(
            P("expert", None),
            P("expert", None),
            P("expert"),
            P("expert", "tensor"),
            P("expert", "tensor"),
            P("expert", "tensor"),
            P("expert"),
            P("expert"),
            P("tensor", "expert"),
            P("expert"),
            P("expert", None),
            P("expert", None, "tensor"),
            P("expert", None, "tensor"),
            P("expert", "tensor", None),
        ),
        check_vma=False,
    )
```

profile of v0, /device:TPU:0, one launch (start us, length us, event | category | flops | bytes accessed | tf_op | source)
XLA Modules:
  0.0 2823.3 jit_solution(18348251637545116201)
XLA Ops:
  9.2 4.5 fusion.101
  17.5 3.1 copy.242
  25.7 2.8 multiply_multiply_fusion
  29.8 3.0 copy.289
  37.1 3.1 copy.290
  43.0 3.1 copy.291
  46.0 4.1 fusion.43
  55.1 3.9 fusion.107
  62.9 4.6 reduce-window.6
  69.8 60.5 %all-reduce.9.cloned.1.call-done = f32[384,2048]{1,0:T(8,128)} async-done(((f32[384,2048]{1,0:T(8,128)}), f32[384,2048]{1,0:T(8,128)}) %all-reduce.9.cloned.1.call-update) | async-done | bytes 3145744 | tf_op jit(solution)/shard_map/psum | solution.py:133
  130.3 2.4 multiply_reduce_fusion.2
  134.7 15.9 gather_fusion
  150.6 29.0 %scatter_custom_fusion = bf16[4608,2048]{1,0:T(8,128)(2,1)} fusion(s32[3072]{0:T(1024)S(1)} %bitcast.340, bf16[3072,2048]{1,0:T(8,128)(2,1)} %gather_fusion, bf16[]{:T(256)} %constant.79.clone.1), kind=kCustom, calls=%fused_computation.25 | custom fusion | bytes 18874880 | tf_op jit(solution)/shard_map/scatter | solution.py:149
  179.5 6.2 all-to-all-start
  186.5 24.9 gather_fusion.3
  212.1 10.0 mul.562
  222.1 8.9 mul.563
  231.0 33.1 %scatter_custom_fusion.1 = bf16[4608,2048]{1,0:T(8,128)(2,1)} fusion(s32[3072]{0:T(1024)S(1)} %bitcast.341, f32[3072,2048]{1,0:T(8,128)} %mul.562, f32[384,8,2048]{2,1,0:T(8,128)} %mul.563, bf16[]{:T(256)} %constant.79.clone.1), kind=kCustom, calls=%fused_computation.23 | custom fusion | flops 12582912 | bytes 69206016 | tf_op jit(solution)/shard_map/scatter | solution.py:176
  264.1 329.5 %all-to-all-done = bf16[16,288,2048]{2,1,0:T(8,128)(2,1)} async-done(((bf16[16,288,2048]{2,1,0:T(8,128)(2,1)}), bf16[16,288,2048]{2,1,0:T(8,128)(2,1)}, u32[]{:S(2)}, u32[]{:S(2)}) %all-to-all-start) | async-done | bytes 18874400 | tf_op jit(solution)/shard_map/all_to_all | solution.py:42
  593.6 6.2 all-to-all-start.2
  599.9 10.6 fusion.7
  610.5 10.5 fusion.9
  621.0 385.9 %all-to-all-done.2 = bf16[16,288,2048]{2,1,0:T(8,128)(2,1)} async-done(((bf16[16,288,2048]{2,1,0:T(8,128)(2,1)}), bf16[16,288,2048]{2,1,0:T(8,128)(2,1)}, u32[]{:S(2)}, u32[]{:S(2)}) %all-to-all-start.2) | async-done | bytes 18874400 | tf_op jit(solution)/shard_map/all_to_all | solution.py:42
  1007.0 14.2 fusion.22
  1021.2 16.9 fusion.59
  1038.0 28.8 %add_bitcast_fusion = f32[8,2,288,2048]{3,2,0,1:T(8,128)} fusion(f32[2,8,288,2048]{3,2,1,0:T(8,128)} %fusion.59, bf16[8,2,288,192]{3,2,0,1:T(8,128)(2,1)} %get-tuple-element.31, bf16[2,2048,192]{1,2,0:T(8,128)(2,1)} %param.32), kind=kOutput, calls=%fused_computation.6 | convolution fusion | flops 3633315840 | bytes 78839808 | tf_op jit(solution)/shard_map/secf,edf->secd/dot_general | solution.py:202
  1066.9 27.6 copy.259
  1094.6 260.3 %reduce-scatter.10.cloned.1.call-done = f32[16,72,2048]{2,1,0:T(8,128)} async-done(((f32[16,288,2048]{2,1,0:T(8,128)}), f32[16,72,2048]{2,1,0:T(8,128)}) %reduce-scatter.10.cloned.1.call-update) | async-done | bytes 9437200 | tf_op jit(solution)/shard_map/reduce_scatter | solution.py:46
  1354.9 6.5 convert_element_type.205
  1361.5 22.5 convolution_bitcast_fusion
  1383.9 27.7 copy.256
  1411.6 69.9 %all-gather.5.cloned.1.call-done = bf16[16,288,2048]{2,1,0:T(8,128)(2,1)} async-done(((bf16[16,72,2048]{2,1,0:T(8,128)(2,1)}), bf16[16,288,2048]{2,1,0:T(8,128)(2,1)}) %all-gather.5.cloned.1.call-update) | async-done | bytes 18874384 | tf_op jit(solution)/shard_map/all_gather | solution.py:49
  1481.5 5.9 all-to-all-start.3
  1487.4 258.3 %reduce-scatter.8.cloned.1.call-done = f32[16,72,2048]{2,1,0:T(8,128)} async-done(((f32[16,288,2048]{2,1,0:T(8,128)}), f32[16,72,2048]{2,1,0:T(8,128)}) %reduce-scatter.8.cloned.1.call-update) | async-done | bytes 9437200 | tf_op jit(solution)/shard_map/reduce_scatter | solution.py:46
  1745.7 6.6 convert_element_type.197
  1752.3 120.1 %all-gather.3.cloned.1.call-done = bf16[16,288,2048]{2,1,0:T(8,128)(2,1)} async-done(((bf16[16,72,2048]{2,1,0:T(8,128)(2,1)}), bf16[16,288,2048]{2,1,0:T(8,128)(2,1)}) %all-gather.3.cloned.1.call-update) | async-done | bytes 18874384 | tf_op jit(solution)/shard_map/all_gather | solution.py:49
  1872.4 23.5 all-to-all-done.3
  1895.9 5.9 all-to-all-start.1
  1905.6 4.6 copy.269
  1910.2 32.6 %gather_fusion.2 = bf16[3072,2048]{1,0:T(8,128)(2,1)} fusion(bf16[4608,2048]{1,0:T(8,128)(2,1)} %bitcast.43, s32[3072]{0:T(1024)S(1)} %broadcast_clamp_fusion), kind=kCustom, calls=%fused_computation.2 | custom fusion | bytes 25178112 | tf_op jit(solution)/shard_map/gather | solution.py:207
  1942.8 12.0 convert_reduce_fusion
  1954.8 354.6 %all-to-all-done.1 = bf16[16,288,2048]{2,1,0:T(8,128)(2,1)} async-done(((bf16[16,288,2048]{2,1,0:T(8,128)(2,1)}), bf16[16,288,2048]{2,1,0:T(8,128)(2,1)}, u32[]{:S(2)}, u32[]{:S(2)}) %all-to-all-start.1) | async-done | bytes 18874400 | tf_op jit(solution)/shard_map/all_to_all | solution.py:50
  2309.5 32.7 %gather_fusion.1 = bf16[3072,2048]{1,0:T(8,128)(2,1)} fusion(bf16[4608,2048]{1,0:T(8,128)(2,1)} %bitcast.32, s32[3072]{0:T(1024)S(1)} %broadcast_clamp_fusion), kind=kCustom, calls=%fused_computation.1 | custom fusion | bytes 25178112 | tf_op jit(solution)/shard_map/gather | solution.py:162
  2342.1 13.6 fusion.1
  2357.3 4.7 multiply_reduce_fusion
  2362.0 4.6 multiply_add_fusion
  2381.8 3.1 copy.293
  2384.8 3.9 fusion.52
  2388.7 3.0 copy.292
  2395.5 3.3 fusion.50
  2408.4 6.2 convolution_convert_fusion
  2415.8 4.4 convolution_convert_fusion.1
  2422.8 10.6 convolution_bitcast_fusion.1
  2433.3 10.6 convolution_bitcast_fusion.2
  2443.9 12.0 fusion.40
  2455.9 2.4 fusion.39
  2458.4 20.2 all-reduce.4
  2478.7 23.6 reduce-scatter.20.cloned.1.call-done
  2503.6 5.6 all-reduce.5
  2510.9 5.2 fusion.35
  2516.2 50.5 %reduce-scatter.16.cloned.1.call-done = bf16[256,128]{1,0:T(8,128)(2,1)} async-done(((bf16[2048,128]{1,0:T(8,128)(2,1)}), bf16[256,128]{1,0:T(8,128)(2,1)}) %reduce-scatter.16.cloned.1.call-update) | async-done | bytes 65552 | tf_op jit(solution)/shard_map/reduce_scatter | solution.py:299
  2568.1 63.8 %reduce-scatter.14.cloned.1.call-done = bf16[256,128]{1,0:T(8,128)(2,1)} async-done(((bf16[2048,128]{1,0:T(8,128)(2,1)}), bf16[256,128]{1,0:T(8,128)(2,1)}) %reduce-scatter.14.cloned.1.call-update) | async-done | bytes 65552 | tf_op jit(solution)/shard_map/reduce_scatter | solution.py:296
  2633.4 89.3 %reduce-scatter.18.cloned.1.call-done = bf16[1024,256]{1,0:T(8,128)(2,1)} async-done(((bf16[1024,2048]{1,0:T(8,128)(2,1)}), bf16[1024,256]{1,0:T(8,128)(2,1)}) %reduce-scatter.18.cloned.1.call-update) | async-done | bytes 524304 | tf_op jit(solution)/shard_map/reduce_scatter | solution.py:302
  2724.8 89.7 %reduce-scatter.12.cloned.1.call-done = bf16[256,1024]{1,0:T(8,128)(2,1)} async-done(((bf16[2048,1024]{1,0:T(8,128)(2,1)}), bf16[256,1024]{1,0:T(8,128)(2,1)}) %reduce-scatter.12.cloned.1.call-update) | async-done | bytes 524304 | tf_op jit(solution)/shard_map/reduce_scatter | solution.py:293
  (308 shorter events, 79.8 us)
Async XLA Ops:
  7.2 999.8 %copy-start = (bf16[2,192,2048]{2,1,0:T(8,128)(2,1)S(1)}, bf16[2,192,2048]{2,1,0:T(8,128)(2,1)}, u32[]{:S(2)}) copy-start(bf16[2,192,2048]{2,1,0:T(8,128)(2,1)} %param.33) | copy-start | bytes 4718596
  7.2 123.1 %all-reduce.9.cloned.1.call-start = ((), (), s32[]{:S(2)}) async-start(), calls=%async_computation.11 | async-start | bytes 6291456 | tf_op jit(solution)/shard_map/psum | solution.py:133
  9.2 13.9 copy-start.80
  15.2 5.4 copy-start.90
  15.2 5.4 copy-start.86
  15.2 5.4 copy-start.7
  15.2 5.4 copy-start.76
  17.5 5.5 copy-start.85
  20.6 25.4 copy-start.74
  20.6 3.3 copy-start.83
  23.1 28.0 copy-start.25
  23.9 9.4 copy-start.33
  23.9 9.4 copy-start.69
  33.3 3.8 copy-start.44
  33.3 3.8 copy-start.46
  37.1 4.6 copy-start.38
  51.1 4.0 copy-start.22
  69.8 161.2 %copy-start.71 = (s32[3072,1]{0,1:T(1,128)}, s32[3072,1]{0,1:T(1,128)S(1)}, u32[]{:S(2)}) copy-start(s32[3072,1]{0,1:T(1,128)S(1)} %compare_select_fusion.1) | copy-start | bytes 36868
  69.8 64.6 %copy-start.67 = (f32[2048]{0:T(1024)S(1)}, f32[2048]{0:T(1024)}, u32[]{:S(2)}) copy-start(f32[2048]{0:T(1024)} %param.29) | copy-start | bytes 24580
  132.7 17.9 copy-start.78
  134.7 51.3 %copy-start.2 = (bf16[384,2048]{1,0:T(8,128)(2,1)}, bf16[384,2048]{1,0:T(8,128)(2,1)S(1)}, u32[]{:S(2)}) copy-start(bf16[384,2048]{1,0:T(8,128)(2,1)S(1)} %multiply_convert_fusion) | copy-start | bytes 4718596
  179.5 6.5 copy-start.59
  179.5 414.1 %all-to-all-start = ((bf16[16,288,2048]{2,1,0:T(8,128)(2,1)}), bf16[16,288,2048]{2,1,0:T(8,128)(2,1)}, u32[]{:S(2)}, u32[]{:S(2)}) async-start(bf16[16,288,2048]{2,1,0:T(8,128)(2,1)} %bitcast.322), calls=%async_computation | async-start | bytes 37748736 | tf_op jit(solution)/shard_map/all_to_all | solution.py:42
  211.8 10.3 copy-start.60
  211.9 10.1 copy-start.36
  212.1 10.0 copy-start.18
  593.6 6.3 copy-start.40
  593.6 413.3 %all-to-all-start.2 = ((bf16[16,288,2048]{2,1,0:T(8,128)(2,1)}), bf16[16,288,2048]{2,1,0:T(8,128)(2,1)}, u32[]{:S(2)}, u32[]{:S(2)}) async-start(bf16[16,288,2048]{2,1,0:T(8,128)(2,1)} %bitcast.321), calls=%async_computation.3 | async-start | bytes 37748736 | tf_op jit(solution)/shard_map/all_to_all | solution.py:42
  599.9 755.0 %reduce-scatter.10.cloned.1.call-start = ((), (), s32[]{:S(2)}) async-start(), calls=%async_computation.14 | async-start | bytes 47185920 | tf_op jit(solution)/shard_map/reduce_scatter | solution.py:46
  599.9 10.6 copy-start.41
  1021.1 16.9 copy-start.28
  1094.5 387.0 %all-gather.5.cloned.1.call-start = ((), (), s32[]{:S(2)}) async-start(), calls=%async_computation.15 | async-start | bytes 23592960 | tf_op jit(solution)/shard_map/all_gather | solution.py:49
  1361.4 384.3 %reduce-scatter.8.cloned.1.call-start = ((), (), s32[]{:S(2)}) async-start(), calls=%async_computation.12 | async-start | bytes 47185920 | tf_op jit(solution)/shard_map/reduce_scatter | solution.py:46
  1481.5 414.4 %all-to-all-start.3 = ((bf16[16,288,2048]{2,1,0:T(8,128)(2,1)}), bf16[16,288,2048]{2,1,0:T(8,128)(2,1)}, u32[]{:S(2)}, u32[]{:S(2)}) async-start(bf16[16,288,2048]{2,1,0:T(8,128)(2,1)} %all-gather.5.cloned.1.call-done), calls=%async_computation.5 | async-start | bytes 37748736 | tf_op jit(solution)/shard_map/all_to_all | solution.py:50
  1487.4 385.0 %all-gather.3.cloned.1.call-start = ((), (), s32[]{:S(2)}) async-start(), calls=%async_computation.13 | async-start | bytes 23592960 | tf_op jit(solution)/shard_map/all_gather | solution.py:49
  1752.3 149.6 %copy-start.10 = (f32[384,1024]{1,0:T(8,128)S(1)}, f32[384,1024]{1,0:T(8,128)}, u32[]{:S(2)}) copy-start(f32[384,1024]{1,0:T(8,128)} %copy-done.9) | copy-start | bytes 4718596
  1895.9 413.6 %all-to-all-start.1 = ((bf16[16,288,2048]{2,1,0:T(8,128)(2,1)}), bf16[16,288,2048]{2,1,0:T(8,128)(2,1)}, u32[]{:S(2)}, u32[]{:S(2)}) async-start(bf16[16,288,2048]{2,1,0:T(8,128)(2,1)} %all-gather.3.cloned.1.call-done), calls=%async_computation.2 | async-start | bytes 37748736 | tf_op jit(solution)/shard_map/all_to_all | solution.py:50
  1901.8 554.1 %all-reduce.11.cloned.1.call-start = ((), (), s32[]{:S(2)}) async-start(), calls=%async_computation.16 | async-start | bytes 3145728 | tf_op jit(solution)/shard_map/psum | solution.py:286
  1905.6 4.6 copy-start.72
  2309.5 32.7 %copy-start.37 = (f32[384,8]{1,0:T(8,128)S(1)}, f32[384,8]{1,0:T(8,128)}, u32[]{:S(2)}) copy-start(f32[384,8]{1,0:T(8,128)} %copy-done.36) | copy-start | bytes 36868
  2342.1 15.1 copy-start.52
  2342.1 15.1 copy-start.79
  2357.3 4.7 copy-start.65
  2357.3 4.7 copy-start.6
  2357.3 4.7 copy-start.68
  2357.3 12.8 slice-start
  2362.0 6.3 copy-start.23
  2362.0 8.1 slice-start.1
  2376.4 3.2 copy-start.15
  2376.4 3.2 copy-start.87
  2381.8 3.1 copy-start.62
  2391.7 3.7 copy-start.14
  2391.8 3.6 copy-start.16
  2391.9 3.6 copy-start.24
  2391.9 3.6 copy-start.75
  2395.4 3.4 copy-start.91
  2403.8 98.6 %reduce-scatter.20.cloned.1.call-start = ((), (), s32[]{:S(2)}) async-start(), calls=%async_computation.21 | async-start | bytes 73728 | tf_op jit(solution)/shard_map/reduce_scatter | solution.py:305
  2404.8 3.6 copy-start.30
  2404.8 161.8 %reduce-scatter.16.cloned.1.call-start = ((), (), s32[]{:S(2)}) async-start(), calls=%async_computation.19 | async-start | bytes 589824 | tf_op jit(solution)/shard_map/reduce_scatter | solution.py:299
  2406.7 225.2 %reduce-scatter.14.cloned.1.call-start = ((), (), s32[]{:S(2)}) async-start(), calls=%async_computation.18 | async-start | bytes 589824 | tf_op jit(solution)/shard_map/reduce_scatter | solution.py:296
  2408.4 314.3 %reduce-scatter.18.cloned.1.call-start = ((), (), s32[]{:S(2)}) async-start(), calls=%async_computation.20 | async-start | bytes 4718592 | tf_op jit(solution)/shard_map/reduce_scatter | solution.py:302
  2414.7 399.8 %reduce-scatter.12.cloned.1.call-start = ((), (), s32[]{:S(2)}) async-start(), calls=%async_computation.17 | async-start | bytes 4718592 | tf_op jit(solution)/shard_map/reduce_scatter | solution.py:293
  2433.3 10.6 copy-start.27
  2510.9 305.6 %copy-start.1 = (bf16[2,192,2048]{2,1,0:T(8,128)(2,1)S(1)}, bf16[2,192,2048]{2,1,0:T(8,128)(2,1)}, u32[]{:S(2)}) copy-start(bf16[2,192,2048]{2,1,0:T(8,128)(2,1)} %param.33) | copy-start | bytes 4718596
  (46 other events, 81.1 us)
Sparse Core Ops, SparseCore 0:
  59.1 71.1 all-reduce.8
  1094.6 260.1 reduce-scatter.9
  1361.5 119.9 all-gather.4
  1484.1 261.5 reduce-scatter.7
  1752.4 119.9 all-gather.2
  2403.9 40.9 all-reduce.10
  2448.6 53.7 reduce-scatter.19
  2505.7 60.9 reduce-scatter.15
  2570.9 60.9 reduce-scatter.13
  2635.4 87.2 reduce-scatter.17
  2726.8 87.6 reduce-scatter.11
where the time goes:
time: 2840 us; the launch traced here: 2820 us
  waiting for transfers between devices  2180 us (77%)
  local copies, waits for them, and re-layouts  256 us (9%)
  matrix products  184 us (6%)
  other arithmetic  137 us (5%)
    all_to_all x2, waiting for transfers between devices, send_rows(): lax.all_to_all(buffer, 'expert', split_axis=0, concat_axis=0, tiled=True)  715 us
    reduce_scatter x2, waiting for transfers between devices, return_rows(): lax.psum_scatter(partial_value, 'tensor', scatter_dimension=1, tiled=True)  519 us
    all_to_all x2, waiting for transfers between devices, return_rows(): lax.all_to_all(complete, 'expert', split_axis=0, concat_axis=0, tiled=True)  378 us
    all_gather x2, waiting for transfers between devices, return_rows(): complete = lax.all_gather(summed_part, 'tensor', axis=1, tiled=True)  190 us
    reduce_scatter x1, waiting for transfers between devices, body(): lax.psum_scatter(w_query_grad.astype(jnp.bfloat16), 'expert', scatter_dim...  89.7 us
    reduce_scatter x1, waiting for transfers between devices, body(): lax.psum_scatter(w_out_grad.astype(jnp.bfloat16), 'expert', scatter_dimen...  89.3 us
    reduce_scatter x1, waiting for transfers between devices, body(): lax.psum_scatter(w_key_grad.astype(jnp.bfloat16), 'expert', scatter_dimen...  63.8 us
    psum x1, waiting for transfers between devices, body(): residual = inputs + lax.psum(attn_part, 'tensor')  60.5 us
  transfers between devices with their start and end apart: 15, of which 14 were waited for; matrix products, arithmetic and copies ran while one was open for 10% of the time, Pallas kernels for 0%

commit v1 on v0

v1 whole, which is shorter than its diff:
```python
import jax
import jax.numpy as jnp
from jax import lax
from jax.sharding import PartitionSpec as P

epsilon = 1e-06
rope_base = 1000000.0
far_below = -1e30


def rope_tables(positions, head_size):
    half_size = head_size // 2
    frequency = rope_base ** (-(jnp.arange(half_size, dtype=jnp.float32) * 2.0) / head_size)
    angles = positions.astype(jnp.float32)[:, None] * frequency[None, :]
    cosine = jnp.cos(angles)
    sine_table = jnp.sin(angles)
    return (jnp.concatenate([cosine, cosine], -1), jnp.concatenate([sine_table, sine_table], -1))


def rotate(value_rows, cosine, sine_table):
    half_size = value_rows.shape[-1] // 2
    turned = jnp.concatenate([-value_rows[..., half_size:], value_rows[..., :half_size]], -1)
    return value_rows * cosine[:, None, :] + turned * sine_table[:, None, :]


def rotate_back(gradient, cosine, sine_table):
    half_size = gradient.shape[-1] // 2
    scaled = gradient * sine_table[:, None, :]
    return gradient * cosine[:, None, :] + jnp.concatenate(
        [scaled[..., half_size:], -scaled[..., :half_size]], -1
    )


def norm_back(grad_scaled, value_rows, scales):
    return scales * (
        grad_scaled
        - value_rows * scales * scales * jnp.mean(grad_scaled * value_rows, -1, keepdims=True)
    )


def bf(value):
    return value.astype(jnp.bfloat16)


def mm(left, right, contract=(1, 0)):
    return lax.dot_general(
        left, right, (((contract[0],), (contract[1],)), ((), ())), preferred_element_type=jnp.float32
    )


def swap(value, step):
    size = lax.axis_size("tensor")
    return lax.ppermute(value, "tensor", [(i, i ^ step) for i in range(size)])


class Tokens:
    def __init__(self):
        self.size = lax.axis_size("expert")
        self.line = self.size == 8
        self.me = lax.axis_index("expert")

    def across(self, value, ranks=range(4)):
        pairs = [(z * 2 + y, z * 2 + 1 - y) for z in ranks for y in range(2)]
        return lax.ppermute(value, "expert", pairs)

    def along(self, value, step, ranks):
        pairs = [(z * 2 + y, (z + step) * 2 + y) for z in ranks for y in range(2)]
        return lax.ppermute(value, "expert", pairs)

    def gather(self, own):
        if not self.line:
            return lax.all_gather(own, "expert", axis=0, tiled=False)
        up = [self.along(own, 1, (0, 1, 2))]
        down = [self.along(own, -1, (1, 2, 3))]
        other = self.across(own)
        up.append(self.along(up[0], 1, (1, 2)))
        down.append(self.along(down[0], -1, (1, 2)))
        up_other = [self.across(up[0], (1, 2, 3))]
        down_other = [self.across(down[0], (0, 1, 2))]
        up.append(self.along(up[1], 1, (2,)))
        down.append(self.along(down[1], -1, (1,)))
        up_other.append(self.across(up[1], (2, 3)))
        down_other.append(self.across(down[1], (0, 1)))
        up_other.append(self.across(up[2], (3,)))
        down_other.append(self.across(down[2], (0,)))
        z = self.me // 2
        same = [own] + [jnp.where(z >= 3 - i, up[2 - i], down[i]) for i in range(3)]
        rest = [other] + [jnp.where(z >= 3 - i, up_other[2 - i], down_other[i]) for i in range(3)]
        return jnp.stack(same + rest)

    def scatter(self, parts):
        if not self.line:
            return lax.psum_scatter(parts, "expert", scatter_dimension=0, tiled=False).astype(
                jnp.float32
            )
        sums = [None] * 4
        for i in (3, 1, 2, 0):
            sums[i] = parts[i].astype(jnp.float32) + self.across(parts[4 + i]).astype(jnp.float32)
        up = self.along(bf(sums[3]), 1, (0,)).astype(jnp.float32)
        down = self.along(bf(sums[1]), -1, (3,)).astype(jnp.float32)
        up = self.along(bf(sums[2] + up), 1, (0, 1)).astype(jnp.float32)
        down = self.along(bf(sums[2] + down), -1, (2, 3)).astype(jnp.float32)
        up = self.along(bf(sums[1] + up), 1, (0, 1, 2)).astype(jnp.float32)
        down = self.along(bf(sums[3] + down), -1, (1, 2, 3)).astype(jnp.float32)
        return sums[0] + up + down

    def places(self):
        p = jnp.arange(self.size, dtype=jnp.int32)
        if not self.line:
            return p
        z, y = self.me // 2, self.me % 2
        return (z + p % 4) % 4 * 2 + (y ^ (p // 4))

    def slots(self):
        a = jnp.arange(self.size, dtype=jnp.int32)
        if not self.line:
            return a
        z, y = self.me // 2, self.me % 2
        return (a // 2 - z) % 4 + 4 * ((a % 2) ^ y)


def pick_blocks(blocks, index):
    return jnp.stack([lax.dynamic_index_in_dim(blocks, index[i], 0, False) for i in range(blocks.shape[0])])


def body(
    hidden_in,
    cotangent,
    segments,
    positions,
    routes,
    attn_gain,
    w_query,
    w_key,
    value_weight,
    q_gain,
    k_gain,
    w_out,
    ffn_gain,
    router,
    w_gate,
    w_up,
    w_down,
):
    tok_count, model_width = hidden_in.shape
    head_size = q_gain.shape[0]
    q_heads = w_query.shape[1] // head_size
    kv_heads = w_key.shape[1] // head_size
    query_group_count = q_heads // kv_heads
    experts = router.shape[1]
    local_experts, _, hidden = w_gate.shape
    score_scale = head_size ** (-0.5)
    tensor_size = lax.axis_size("tensor")
    tensor_rank = lax.axis_index("tensor")
    expert_rank = lax.axis_index("expert")
    shard_rows = tok_count // tensor_size
    order = Tokens()
    group = order.size
    places, slots = order.places(), order.slots()

    def own_rows(value):
        return lax.dynamic_slice_in_dim(value, tensor_rank * shard_rows, shard_rows)

    cot_own = own_rows(cotangent)
    grad_all = lax.all_gather(cot_own, "expert", axis=0, tiled=False)
    grad_all = pick_blocks(grad_all, places).reshape(group * shard_rows, model_width)
    expert_ids = jnp.arange(experts, dtype=jnp.int32)
    routes_own = own_rows(routes)
    routes_all = lax.all_gather(routes_own, "expert", axis=0, tiled=False)
    routes_all = pick_blocks(routes_all, places).reshape(group * shard_rows, -1)

    def mask_of(route_rows):
        return jnp.any(route_rows[:, :, None] == expert_ids[None, None, :], 1)

    mask_own, mask_all = mask_of(routes_own), mask_of(routes_all)
    in_own = jnp.concatenate(
        [w_gate[i] for i in range(local_experts)] + [w_up[i] for i in range(local_experts)], 1
    )
    down_own = w_down.reshape(local_experts * hidden, model_width)
    in_far, down_far = swap(in_own, 2), swap(down_own, 2)
    in_mats = [in_own, swap(in_own, 1), in_far, swap(in_far, 1)]
    down_mats = [down_own, swap(down_own, 1), down_far, swap(down_far, 1)]

    inputs = hidden_in.astype(jnp.float32)
    inv_first = lax.rsqrt(jnp.mean(inputs * inputs, -1, keepdims=True) + epsilon)
    normalized_input = (inputs * inv_first * attn_gain).astype(jnp.bfloat16)
    query_raw = jnp.dot(normalized_input, w_query, preferred_element_type=jnp.float32).reshape(
        tok_count, q_heads, head_size
    )
    key_unrotated = jnp.dot(normalized_input, w_key, preferred_element_type=jnp.float32).reshape(
        tok_count, kv_heads, head_size
    )
    value_rows = (
        jnp.dot(normalized_input, value_weight, preferred_element_type=jnp.float32)
        .astype(jnp.bfloat16)
        .reshape(tok_count, kv_heads, head_size)
    )
    cosine, sine_table = rope_tables(positions, head_size)
    query_inv = lax.rsqrt(jnp.mean(query_raw * query_raw, -1, keepdims=True) + epsilon)
    key_inv = lax.rsqrt(jnp.mean(key_unrotated * key_unrotated, -1, keepdims=True) + epsilon)
    query_hat = query_raw * query_inv
    key_hat = key_unrotated * key_inv
    query_rows = (
        rotate(query_hat * q_gain, cosine, sine_table)
        .astype(jnp.bfloat16)
        .reshape(tok_count, kv_heads, query_group_count, head_size)
    )
    keys_rotated = rotate(key_hat * k_gain, cosine, sine_table).astype(jnp.bfloat16)
    token_index = jnp.arange(tok_count, dtype=jnp.int32)
    allowed = (segments[:, None] == segments[None, :]) & (
        token_index[:, None] >= token_index[None, :]
    )

    def scores_of():
        raw_scores = (
            jnp.einsum(
                "tkgd,skd->kgts", query_rows, keys_rotated, preferred_element_type=jnp.float32
            )
            * score_scale
        )
        return jnp.where(allowed, raw_scores, far_below)

    scores = scores_of()
    top_score = jnp.max(scores, -1, keepdims=True)
    log_total = top_score + jnp.log(jnp.sum(jnp.exp(scores - top_score), -1, keepdims=True))
    prob_low = jnp.exp(scores - log_total).astype(jnp.bfloat16)
    attended_rows = (
        jnp.einsum("kgts,skd->tkgd", prob_low, value_rows, preferred_element_type=jnp.float32)
        .astype(jnp.bfloat16)
        .reshape(tok_count, q_heads * head_size)
    )

    pair_count = tensor_size // 2

    def reduce_rows(part):
        part = part.reshape(pair_count, 2, shard_rows, model_width)
        low = tensor_rank % 2
        keep = lax.dynamic_index_in_dim(part, low, 1, False)
        give = lax.dynamic_index_in_dim(part, 1 - low, 1, False)
        half = keep.astype(jnp.float32) + swap(bf(give), 1).astype(jnp.float32)
        high = tensor_rank // 2
        keep = lax.dynamic_index_in_dim(half, high, 0, False)
        give = lax.dynamic_index_in_dim(half, 1 - high, 0, False)
        return keep + swap(bf(give), 2).astype(jnp.float32)

    def gather_rows(own):
        far = swap(own, 2)
        high, low = tensor_rank // 2, tensor_rank % 2
        mine = jnp.where(high == 0, jnp.stack([own, far]), jnp.stack([far, own]))
        theirs = swap(mine, 1)
        both = jnp.where(low == 0, jnp.stack([mine, theirs], 1), jnp.stack([theirs, mine], 1))
        return both.reshape(tok_count, model_width)

    attn_sum = reduce_rows(jnp.dot(attended_rows, w_out, preferred_element_type=jnp.float32))
    residual = own_rows(hidden_in).astype(jnp.float32) + attn_sum
    inv_second = lax.rsqrt(jnp.mean(residual * residual, -1, keepdims=True) + epsilon)
    normed_ffn = (residual * inv_second * ffn_gain).astype(jnp.bfloat16)

    def gates_of(rows, mask):
        logits = jnp.where(mask, mm(rows, router), far_below)
        return jax.nn.softmax(logits, -1)

    gates_own = gates_of(normed_ffn, mask_own)
    normed_all = order.gather(normed_ffn).reshape(group * shard_rows, model_width)
    gates_all = gates_of(normed_all, mask_all)
    local_gates = lax.dynamic_slice_in_dim(
        gates_all, expert_rank * local_experts, local_experts, 1
    )
    gate_wide = jnp.repeat(local_gates, hidden, axis=1)
    width = local_experts * hidden

    out_part = jnp.zeros((group * shard_rows, model_width), jnp.float32)
    back_part = jnp.zeros((group * shard_rows, model_width), jnp.float32)
    gate_grad_all = jnp.zeros((group * shard_rows, local_experts), jnp.float32)
    pre_grads, gated_middles = [], []
    for in_mat, down_mat in zip(in_mats, down_mats):
        pre = mm(normed_all, in_mat)
        gate_pre, up_pre = pre[:, :width], pre[:, width:]
        sigmoid_gate = jax.nn.sigmoid(gate_pre)
        activated = gate_pre * sigmoid_gate
        middle = activated * up_pre
        gated = bf(middle * gate_wide)
        grad_middle = mm(grad_all, down_mat, (1, 1))
        gate_grad_all = gate_grad_all + jnp.sum(
            (middle * grad_middle).reshape(-1, local_experts, hidden), -1
        )
        grad_middle = grad_middle * gate_wide
        grad_gate_pre = bf(
            grad_middle * up_pre * sigmoid_gate * (1.0 + gate_pre * (1.0 - sigmoid_gate))
        )
        grad_up_pre = bf(grad_middle * activated)
        pre_grad = jnp.concatenate([grad_gate_pre, grad_up_pre], 1)
        back_part = back_part + mm(pre_grad, in_mat, (1, 1))
        out_part = out_part + mm(gated, down_mat)
        pre_grads.append(pre_grad)
        gated_middles.append(gated)

    gate_grad_send = pick_blocks(
        gate_grad_all.T.reshape(local_experts, group, shard_rows).transpose(1, 0, 2), slots
    )
    gate_grad_own = (
        lax.all_to_all(gate_grad_send, "expert", split_axis=0, concat_axis=0, tiled=True)
        .reshape(experts, shard_rows)
        .T
    )
    back_sum = order.scatter(bf(back_part).reshape(group, shard_rows, model_width))
    out_blocks = pick_blocks(bf(out_part).reshape(group, shard_rows, model_width), slots)
    out_sum = lax.psum_scatter(out_blocks, "expert", scatter_dimension=0, tiled=False)
    layer_out = gather_rows(bf(residual + out_sum.astype(jnp.float32)))

    def weight_grads(step):
        return (
            mm(normed_all, pre_grads[step], (0, 0)),
            mm(gated_middles[step], grad_all, (0, 0)),
        )

    def give(parts, step):
        return [swap(bf(part), step).astype(jnp.float32) for part in parts]

    near = give(weight_grads(1), 1)
    far = give(weight_grads(3), 1)
    far = give([a + b for a, b in zip(weight_grads(2), far)], 2)
    in_grad, down_grad = [a + b + c for a, b, c in zip(weight_grads(0), near, far)]
    w_gate_grad = jnp.stack([in_grad[:, i * hidden : (i + 1) * hidden] for i in range(local_experts)])
    w_up_grad = jnp.stack(
        [in_grad[:, width + i * hidden : width + (i + 1) * hidden] for i in range(local_experts)]
    )
    w_down_grad = down_grad.reshape(local_experts, hidden, model_width)

    grad_out = cot_own.astype(jnp.float32)
    grad_chosen = gates_own * (
        gate_grad_own - jnp.sum(gates_own * gate_grad_own, -1, keepdims=True)
    )
    grad_logits = bf(jnp.where(mask_own, grad_chosen, 0.0))
    router_part = mm(normed_ffn, grad_logits, (0, 0))
    grad_normed_ffn = back_sum + mm(grad_logits, router, (1, 1))
    ffn_gain_part = jnp.sum(grad_normed_ffn * residual * inv_second, 0)
    grad_residual = grad_out + norm_back(grad_normed_ffn * ffn_gain, residual, inv_second)
    grad_attn = gather_rows(bf(grad_residual))
    w_out_part = bf(mm(attended_rows, grad_attn, (0, 0)))
    w_out_grad = lax.psum_scatter(w_out_part, "expert", scatter_dimension=1, tiled=True).astype(
        jnp.float32
    )
    grad_attended = bf(mm(grad_attn, w_out, (1, 1))).reshape(
        tok_count, kv_heads, query_group_count, head_size
    )
    probability = jnp.exp(scores_of() - log_total)
    prob_again = probability.astype(jnp.bfloat16)
    grad_prob = jnp.einsum(
        "tkgd,skd->kgts", grad_attended, value_rows, preferred_element_type=jnp.float32
    )
    grad_scores = (
        probability * (grad_prob - jnp.sum(probability * grad_prob, -1, keepdims=True))
    ).astype(jnp.bfloat16)
    grad_queries = (
        jnp.einsum("kgts,skd->tkgd", grad_scores, keys_rotated, preferred_element_type=jnp.float32)
        * score_scale
    ).reshape(tok_count, q_heads, head_size)
    grad_keys = (
        jnp.einsum("kgts,tkgd->skd", grad_scores, query_rows, preferred_element_type=jnp.float32)
        * score_scale
    )
    grad_values = (
        jnp.einsum("kgts,tkgd->skd", prob_again, grad_attended, preferred_element_type=jnp.float32)
        .astype(jnp.bfloat16)
        .reshape(tok_count, kv_heads * head_size)
    )
    grad_query_rot = rotate_back(grad_queries, cosine, sine_table)
    grad_key_rot = rotate_back(grad_keys, cosine, sine_table)
    q_gain_part = jnp.sum((grad_query_rot * query_hat).reshape(-1, head_size), 0)
    k_gain_part = jnp.sum((grad_key_rot * key_hat).reshape(-1, head_size), 0)
    grad_query_raw = (
        norm_back(grad_query_rot * q_gain, query_raw, query_inv)
        .astype(jnp.bfloat16)
        .reshape(tok_count, q_heads * head_size)
    )
    grad_key_raw = (
        norm_back(grad_key_rot * k_gain, key_unrotated, key_inv)
        .astype(jnp.bfloat16)
        .reshape(tok_count, kv_heads * head_size)
    )
    grad_heads = jnp.concatenate([grad_query_raw, grad_key_raw, grad_values], 1)
    grad_normed_part = (
        mm(grad_query_raw, w_query, (1, 1))
        + mm(grad_key_raw, w_key, (1, 1))
        + mm(grad_values, value_weight, (1, 1))
    )
    attn_gain_part = jnp.sum(grad_normed_part * inputs * inv_first, 0)
    grad_normed = reduce_rows(grad_normed_part)
    inputs_own, inv_own = own_rows(inputs), own_rows(inv_first)
    input_grad = gather_rows(
        bf(grad_residual + norm_back(grad_normed * attn_gain, inputs_own, inv_own))
    ).astype(jnp.float32)

    heads_part = mm(normalized_input, grad_heads, (0, 0))
    small_width = 128
    gain_rows = jnp.stack([q_gain_part, k_gain_part], 1).reshape(group, -1, 2)
    gain_cols = jnp.pad(
        gain_rows, ((0, 0), (0, model_width // group - gain_rows.shape[1]), (0, 0))
    ).reshape(model_width, 2)
    small = jnp.concatenate([attn_gain_part[:, None], ffn_gain_part[:, None], gain_cols, router_part], 1)
    small = jnp.pad(small, ((0, 0), (0, small_width - small.shape[1])))
    packed = lax.psum_scatter(
        bf(jnp.concatenate([heads_part, small], 1)), "expert", scatter_dimension=0, tiled=True
    )
    query_width, key_width = w_query.shape[1], w_key.shape[1]
    w_query_grad = packed[:, :query_width].astype(jnp.float32)
    w_key_grad = packed[:, query_width : query_width + key_width].astype(jnp.float32)
    w_value_grad = packed[:, query_width + key_width : query_width + 2 * key_width].astype(jnp.float32)
    small = packed[:, query_width + 2 * key_width :]
    small = small.astype(jnp.float32) + swap(small, 1).astype(jnp.float32)
    small = small + swap(bf(small), 2).astype(jnp.float32)
    gain_count = head_size // group
    return (
        layer_out,
        input_grad,
        small[:, 0],
        w_query_grad,
        w_key_grad,
        w_value_grad,
        small[:gain_count, 2],
        small[:gain_count, 3],
        w_out_grad,
        small[:, 1],
        small[:, 4 : 4 + experts],
        w_gate_grad,
        w_up_grad,
        w_down_grad,
    )


def solution(mesh):
    placed = (
        P("expert", None),
        P("expert", None),
        P("expert"),
        P("expert"),
        P("expert", None),
        P(),
        P(None, "tensor"),
        P(None, "tensor"),
        P(None, "tensor"),
        P(),
        P(),
        P("tensor", None),
        P(),
        P(),
        P("expert", None, "tensor"),
        P("expert", None, "tensor"),
        P("expert", "tensor", None),
    )
    return jax.shard_map(
        body,
        mesh=mesh,
        in_specs=placed,
        out_specs=(
            P("expert", None),
            P("expert", None),
            P("expert"),
            P("expert", "tensor"),
            P("expert", "tensor"),
            P("expert", "tensor"),
            P("expert"),
            P("expert"),
            P("tensor", "expert"),
            P("expert"),
            P("expert", None),
            P("expert", None, "tensor"),
            P("expert", None, "tensor"),
            P("expert", "tensor", None),
        ),
        check_vma=False,
    )
```

time: 2840 us -> 771 us (0.27)
  waiting for transfers between devices: 2180 us -> 268 us
  local copies, waits for them, and re-layouts: 256 us -> 91.7 us
  other arithmetic: 137 us -> 85.7 us
  starting transfers between devices: 24.7 us -> 61.5 us
  between operations: 16.5 us -> 46.5 us
    all_to_all x4 -> x1, waiting for transfers between devices: 1090 us -> 0.01 us  [body(): lax.all_to_all(gate_grad_send, 'expert', split_axis=0, concat_axis=0, til...]
    reduce_scatter x7 -> x3, waiting for transfers between devices: 835 us -> 52.3 us  [the longest x1 52.3 us: body(): lax.psum_scatter(w_out_part, 'expert', scatter_dimension=1, tiled=True)]
    ppermute x0 -> x47, waiting for transfers between devices: none -> 216 us  [the longest x24 163 us: swap(): return lax.ppermute(value, 'tensor', [(i, i ^ step) for i in range(size)])]
    all_gather x2 -> x1, waiting for transfers between devices: 190 us -> 0.01 us  [body(): grad_all = lax.all_gather(cot_own, 'expert', axis=0, tiled=False)]
    gather x8 -> x0, local copies, waits for them, and re-layouts: 107 us -> none  [the longest x1 32.7 us: body(): routed = returned[slot_index].reshape(tok_count, top_count, model_width)]
    psum x2 -> x0, waiting for transfers between devices: 60.5 us -> none  [the longest x1 60.5 us: body(): residual = inputs + lax.psum(attn_part, 'tensor')]
    ppermute x0 -> x47, starting transfers between devices: none -> 57 us  [the longest x12 25.3 us: along(): return lax.ppermute(value, 'expert', pairs)]
    scatter x1 -> x0, other arithmetic: 33.1 us -> none  [body(): grad_dispatch = jnp.zeros((experts * capacity, model_width), jnp.bfloat16...]
  transfers between devices with their start and end apart: 15 -> 52, of which waited for: 14 -> 15; matrix products, arithmetic and copies ran while one was open for 10% -> 33% of each run, Pallas kernels for 0% -> 0%
where the time goes in v1:
time: 771 us; the launch traced here: 759 us
  waiting for transfers between devices  268 us (35%)
  matrix products  174 us (23%)
  local copies, waits for them, and re-layouts  91.7 us (12%)
  other arithmetic  85.7 us (11%)
  starting transfers between devices  61.5 us (8%)
  between operations  46.5 us (6%)
  blocking collectives  31.4 us (4%)
    ppermute x24, waiting for transfers between devices, swap(): return lax.ppermute(value, 'tensor', [(i, i ^ step) for i in range(size)])  163 us
    dot_general x34, matrix products, mm(): lax.dot_general(left, right, (((contract[0],), (contract[1],)), ((), ()))...  146 us
    reduce_scatter x1, waiting for transfers between devices, body(): lax.psum_scatter(w_out_part, 'expert', scatter_dimension=1, tiled=True)  52.3 us
    unnamed x262, local copies, waits for them, and re-layouts  37.3 us
    ppermute x12, waiting for transfers between devices, along(): return lax.ppermute(value, 'expert', pairs)  34.4 us
    all_gather x1, blocking collectives, body(): routes_all = lax.all_gather(routes_own, 'expert', axis=0, tiled=False)  31.4 us
    ppermute x12, starting transfers between devices, along(): return lax.ppermute(value, 'expert', pairs)  25.3 us
    ppermute x11, waiting for transfers between devices, across(): return lax.ppermute(value, 'expert', pairs)  17.8 us
  transfers between devices with their start and end apart: 52, of which 15 were waited for; matrix products, arithmetic and copies ran while one was open for 33% of the time, Pallas kernels for 0%

profile of v1, /device:TPU:0, one launch (start us, length us, event | category | flops | bytes accessed | tf_op | source)
XLA Modules:
  0.0 758.8 jit_solution(5481233314252481372)
XLA Ops:
  9.6 4.5 fusion.110
  15.6 3.0 copy.209
  20.6 2.8 fusion.30
  31.2 3.0 copy.254
  35.5 3.0 copy.253
  39.7 3.0 copy.252
  42.8 3.6 fusion.6
  55.3 6.1 fusion.3
  67.1 2.7 collective-permute-start.17
  94.3 31.4 %all-gather.2 = s32[8,96,8]{1,2,0:T(8,128)S(1)} all-gather(s32[1,96,8]{1,2,0:T(8,128)S(1)} %fusion.205), channel_id=2, replica_groups=mesh['expert'=8,'tensor'=4] {'expert'}, dimensions={0}, use_global_device_ids=true | all-gather | bytes 27648 | tf_op jit(solution)/shard_map/all_gather | solution.py:169
  125.7 55.0 %collective-permute-done.1 = bf16[96,2048]{1,0:T(8,128)(2,1)S(1)} collective-permute-done((bf16[96,2048]{1,0:T(8,128)(2,1)S(1)}, bf16[96,2048]{1,0:T(8,128)(2,1)S(1)}, u32[]{:S(2)}, u32[]{:S(2)}) %collective-permute-start.1) | collective-permute-done | bytes 393248 | tf_op jit(solution)/shard_map/ppermute | solution.py:53
  183.1 4.5 collective-permute-start.2
  188.9 6.0 collective-permute-done.2
  215.7 4.5 copy.228
  235.1 9.8 %collective-permute-done.7 = bf16[96,2048]{1,0:T(8,128)(2,1)S(1)} collective-permute-done((bf16[96,2048]{1,0:T(8,128)(2,1)}, bf16[96,2048]{1,0:T(8,128)(2,1)S(1)}, u32[]{:S(2)}, u32[]{:S(2)}) %collective-permute-start.7) | collective-permute-done | bytes 393248 | tf_op jit(solution)/shard_map/ppermute | solution.py:68
  249.8 5.7 collective-permute-done.10
  260.1 6.0 collective-permute-done.12
  269.9 5.9 collective-permute-done.14
  276.6 3.0 fusion.119
  280.3 6.0 fusion.121
  286.3 5.9 fusion.125
  292.2 6.0 fusion.123
  302.8 4.0 fusion.128
  306.8 6.4 multiply_convert_fusion.6
  317.0 6.2 fusion.122
  323.2 2.9 fusion.129
  326.2 6.5 fusion.57
  332.6 6.0 fusion.124
  338.7 6.6 fusion.56
  345.3 4.7 fusion.127
  350.1 6.0 multiply_convert_fusion.2
  364.3 5.0 fusion.55
  369.3 7.5 add_convert_fusion.1
  384.1 4.2 all-to-all-start
  393.6 3.4 collective-permute-start.27
  397.0 3.5 fusion.126
  400.6 3.5 collective-permute-done.27
  405.3 4.4 collective-permute-start.28
  409.7 7.2 add_convert_fusion.2
  427.1 3.0 collective-permute-start.29
  436.2 13.6 %collective-permute-done.32 = bf16[96,2048]{1,0:T(8,128)(2,1)S(1)} collective-permute-done((bf16[96,2048]{1,0:T(8,128)(2,1)S(1)}, bf16[96,2048]{1,0:T(8,128)(2,1)S(1)}, u32[]{:S(2)}, u32[]{:S(2)}) %collective-permute-start.32) | collective-permute-done | bytes 393248 | tf_op jit(solution)/shard_map/ppermute | solution.py:68
  456.4 4.9 collective-permute-done.33
  482.7 3.1 copy.256
  485.7 3.9 fusion.14
  489.7 3.1 copy.255
  492.8 3.5 bitcast_multiply_fusion.16
  497.6 3.1 fusion.31
  507.7 2.6 multiply_reduce_fusion
  510.5 3.4 convolution_convert_fusion
  513.9 3.0 pad_maximum_fusion
  517.0 6.7 convolution_convert_fusion.2
  524.2 2.5 convolution_convert_fusion.4
  526.8 4.7 convolution_convert_fusion.3
  532.0 2.6 convolution_convert_fusion.5
  534.5 4.4 convolution_convert_fusion.1
  540.0 4.2 add_convert_fusion.3
  545.6 6.0 add_convert_fusion
  558.6 22.9 %collective-permute-done.46 = bf16[384,2048]{1,0:T(8,128)(2,1)S(1)} collective-permute-done((bf16[384,2048]{1,0:T(8,128)(2,1)S(1)}, bf16[384,2048]{1,0:T(8,128)(2,1)S(1)}, u32[]{:S(2)}, u32[]{:S(2)}) %collective-permute-start.46) | collective-permute-done | bytes 1572896 | tf_op jit(solution)/shard_map/ppermute | solution.py:53
  581.4 3.7 convert_add_fusion.1
  585.2 71.7 %collective-permute-done.36 = bf16[96,2048]{1,0:T(8,128)(2,1)S(1)} collective-permute-done((bf16[96,2048]{1,0:T(8,128)(2,1)S(1)}, bf16[96,2048]{1,0:T(8,128)(2,1)S(1)}, u32[]{:S(2)}, u32[]{:S(2)}) %collective-permute-start.36) | collective-permute-done | bytes 393248 | tf_op jit(solution)/shard_map/ppermute | solution.py:53
  657.7 2.4 add_convert_fusion.7
  662.2 5.8 convert_add_fusion
  670.5 8.8 %collective-permute-done.37 = bf16[96,2048]{1,0:T(8,128)(2,1)S(1)} collective-permute-done((bf16[96,2048]{1,0:T(8,128)(2,1)S(1)}, bf16[96,2048]{1,0:T(8,128)(2,1)S(1)}, u32[]{:S(2)}, u32[]{:S(2)}) %collective-permute-start.37) | collective-permute-done | bytes 393248 | tf_op jit(solution)/shard_map/ppermute | solution.py:53
  691.4 52.3 %reduce-scatter.8.cloned.1.call-done = bf16[1024,256]{1,0:T(8,128)(2,1)} async-done(((bf16[1024,2048]{1,0:T(8,128)(2,1)}), bf16[1024,256]{1,0:T(8,128)(2,1)}) %reduce-scatter.8.cloned.1.call-update) | async-done | bytes 524304 | tf_op jit(solution)/shard_map/reduce_scatter | solution.py:341
  (484 shorter events, 196.9 us)
Async XLA Ops:
  7.2 291.1 %all-gather.5.cloned.1.call-start = ((), (), s32[]{:S(2)}) async-start(), calls=%async_computation.7 | async-start | bytes 3538944 | tf_op jit(solution)/shard_map/all_gather | solution.py:165
  9.6 14.6 %copy-start.95 = (f32[384]{0:T(512)}, f32[384]{0:T(512)S(1)}, u32[]{:S(2)}) copy-start(f32[384]{0:T(512)S(1)} %add_rsqrt_fusion.2) | copy-start | bytes 4612
  25.2 17.6 %copy-start.86 = (f32[1024]{0:T(1024)}, f32[1024]{0:T(1024)S(1)}, u32[]{:S(2)}) copy-start(f32[1024]{0:T(1024)S(1)} %broadcast_bitcast_fusion) | copy-start | bytes 12292
  63.1 10.1 %collective-permute-start = (bf16[2,96,2048]{2,1,0:T(8,128)(2,1)S(1)}, bf16[2,96,2048]{2,1,0:T(8,128)(2,1)}, u32[]{:S(2)}, u32[]{:S(2)}) collective-permute-start(bf16[2,96,2048]{2,1,0:T(8,128)(2,1)S(1)} %fusion.42), channel_id=1, source_target_pairs={{0,1},{1,0},{2,3},{3,2},{4,5},{5,4},{6,7},{7,6},{8,9},{9,8},{10,11... | collective-permute-start | bytes 2359304 | tf_op jit(solution)/shard_map/ppermute | solution.py:53
  67.1 219.2 %collective-permute-start.17 = (bf16[2048,768]{0,1:T(8,128)(2,1)}, bf16[2048,768]{0,1:T(8,128)(2,1)}, u32[]{:S(2)}, u32[]{:S(2)}) collective-permute-start(bf16[2048,768]{0,1:T(8,128)(2,1)} %pad_maximum_fusion.1), channel_id=1, source_target_pairs={{0,2},{1,3},{2,0},{3,1},{4,6},{5,7},{6,4},{7,5},{8,10},{9,11},{10,... | collective-permute-start | bytes 9437192 | tf_op jit(solution)/shard_map/ppermute | solution.py:53
  69.8 222.5 %collective-permute-start.15 = (bf16[2048,768]{0,1:T(8,128)(2,1)}, bf16[2048,768]{0,1:T(8,128)(2,1)}, u32[]{:S(2)}, u32[]{:S(2)}) collective-permute-start(bf16[2048,768]{0,1:T(8,128)(2,1)} %pad_maximum_fusion.1), channel_id=1, source_target_pairs={{0,1},{1,0},{2,3},{3,2},{4,5},{5,4},{6,7},{7,6},{8,9},{9,8},{10,11... | collective-permute-start | bytes 9437192 | tf_op jit(solution)/shard_map/ppermute | solution.py:53
  71.6 197.8 %collective-permute-start.18 = (bf16[384,2048]{1,0:T(8,128)(2,1)}, bf16[384,2048]{1,0:T(8,128)(2,1)}, u32[]{:S(2)}, u32[]{:S(2)}) collective-permute-start(bf16[384,2048]{1,0:T(8,128)(2,1)} %bitcast.43), channel_id=1, source_target_pairs={{0,2},{1,3},{2,0},{3,1},{4,6},{5,7},{6,4},{7,5},{8,10},{9,11},{10,... | collective-permute-start | bytes 4718600 | tf_op jit(solution)/shard_map/ppermute | solution.py:53
  76.2 106.1 %copy-start.78 = (f32[2048]{0:T(1024)S(1)}, f32[2048]{0:T(1024)}, u32[]{:S(2)}) copy-start(f32[2048]{0:T(1024)} %param.29) | copy-start | bytes 24580
  76.2 104.5 %collective-permute-start.1 = (bf16[96,2048]{1,0:T(8,128)(2,1)S(1)}, bf16[96,2048]{1,0:T(8,128)(2,1)S(1)}, u32[]{:S(2)}, u32[]{:S(2)}) collective-permute-start(bf16[96,2048]{1,0:T(8,128)(2,1)S(1)} %fusion.68), channel_id=1, source_target_pairs={{0,2},{1,3},{2,0},{3,1},{4,6},{5,7},{6,4},{7,5},{8,10},{9,11},{10,... | collective-permute-start | bytes 1179656 | tf_op jit(solution)/shard_map/ppermute | solution.py:53
  182.2 14.1 %copy-start.100 = (f32[96]{0:T(128)}, f32[96]{0:T(128)S(1)}, u32[]{:S(2)}) copy-start(f32[96]{0:T(128)S(1)} %add_rsqrt_fusion.3) | copy-start | bytes 1156
  183.1 11.8 %collective-permute-start.2 = (bf16[96,2048]{1,0:T(8,128)(2,1)S(1)}, bf16[96,2048]{1,0:T(8,128)(2,1)}, u32[]{:S(2)}, u32[]{:S(2)}) collective-permute-start(bf16[96,2048]{1,0:T(8,128)(2,1)S(1)} %get-tuple-element.107), channel_id=1, source_target_pairs={{0,8},{4,12},{8,16},{12,20},{16,24},{20,28},{1,9},{5,13},{9,17},{1... | collective-permute-start | bytes 1179656 | tf_op jit(solution)/shard_map/ppermute | solution.py:68
  187.6 13.6 %collective-permute-start.5 = (bf16[96,2048]{1,0:T(8,128)(2,1)S(1)}, bf16[96,2048]{1,0:T(8,128)(2,1)}, u32[]{:S(2)}, u32[]{:S(2)}) collective-permute-start(bf16[96,2048]{1,0:T(8,128)(2,1)S(1)} %get-tuple-element.107), channel_id=1, source_target_pairs={{8,0},{12,4},{16,8},{20,12},{24,16},{28,20},{9,1},{13,5},{17,9},{2... | collective-permute-start | bytes 1179656 | tf_op jit(solution)/shard_map/ppermute | solution.py:68
  194.9 7.6 collective-permute-start.3
  201.2 27.4 %collective-permute-start.6 = (bf16[96,2048]{1,0:T(8,128)(2,1)}, bf16[96,2048]{1,0:T(8,128)(2,1)}, u32[]{:S(2)}, u32[]{:S(2)}) collective-permute-start(bf16[96,2048]{1,0:T(8,128)(2,1)} %collective-permute-done.5), channel_id=1, source_target_pairs={{8,0},{12,4},{16,8},{20,12},{9,1},{13,5},{17,9},{21,13},{10,2},{14... | collective-permute-start | bytes 1179656 | tf_op jit(solution)/shard_map/ppermute | solution.py:68
  202.5 27.6 %collective-permute-start.4 = (bf16[96,2048]{1,0:T(8,128)(2,1)}, bf16[96,2048]{1,0:T(8,128)(2,1)}, u32[]{:S(2)}, u32[]{:S(2)}) collective-permute-start(bf16[96,2048]{1,0:T(8,128)(2,1)} %collective-permute-done.3), channel_id=1, source_target_pairs={{16,24},{20,28},{17,25},{21,29},{18,26},{22,30},{19,27},{23,31}} | collective-permute-start | bytes 1179656 | tf_op jit(solution)/shard_map/ppermute | solution.py:68
  228.5 19.7 %collective-permute-start.8 = (bf16[96,2048]{1,0:T(8,128)(2,1)S(1)}, bf16[96,2048]{1,0:T(8,128)(2,1)S(1)}, u32[]{:S(2)}, u32[]{:S(2)}) collective-permute-start(bf16[96,2048]{1,0:T(8,128)(2,1)S(1)} %get-tuple-element.107), channel_id=1, source_target_pairs={{0,4},{4,0},{8,12},{12,8},{16,20},{20,16},{24,28},{28,24},{1,5},{5... | collective-permute-start | bytes 1179656 | tf_op jit(solution)/shard_map/ppermute | solution.py:64
  230.1 14.8 %collective-permute-start.7 = (bf16[96,2048]{1,0:T(8,128)(2,1)}, bf16[96,2048]{1,0:T(8,128)(2,1)S(1)}, u32[]{:S(2)}, u32[]{:S(2)}) collective-permute-start(bf16[96,2048]{1,0:T(8,128)(2,1)} %collective-permute-done.6), channel_id=1, source_target_pairs={{8,0},{12,4},{9,1},{13,5},{10,2},{14,6},{11,3},{15,7}} | collective-permute-start | bytes 1179656 | tf_op jit(solution)/shard_map/ppermute | solution.py:68
  244.9 10.5 %collective-permute-start.10 = (bf16[96,2048]{1,0:T(8,128)(2,1)}, bf16[96,2048]{1,0:T(8,128)(2,1)S(1)}, u32[]{:S(2)}, u32[]{:S(2)}) collective-permute-start(bf16[96,2048]{1,0:T(8,128)(2,1)} %collective-permute-done.5), channel_id=1, source_target_pairs={{0,4},{4,0},{8,12},{12,8},{16,20},{20,16},{1,5},{5,1},{9,13},{13,9... | collective-permute-start | bytes 1179656 | tf_op jit(solution)/shard_map/ppermute | solution.py:64
  248.2 28.5 %copy-start.72 = (bf16[2048,16]{0,1:T(8,128)(2,1)S(1)}, bf16[2048,16]{0,1:T(8,128)(2,1)}, u32[]{:S(2)}) copy-start(bf16[2048,16]{0,1:T(8,128)(2,1)} %param.30) | copy-start | bytes 196612
  248.2 28.5 %copy-start.81 = (pred[768,16]{0,1:T(8,128)(4,1)S(1)}, pred[768,16]{0,1:T(8,128)(4,1)}, u32[]{:S(2)}) copy-start(pred[768,16]{0,1:T(8,128)(4,1)} %fusion.70) | copy-start | bytes 36868
  248.2 8.0 %collective-permute-start.9 = (bf16[96,2048]{1,0:T(8,128)(2,1)}, bf16[96,2048]{1,0:T(8,128)(2,1)S(1)}, u32[]{:S(2)}, u32[]{:S(2)}) collective-permute-start(bf16[96,2048]{1,0:T(8,128)(2,1)} %collective-permute-done.4), channel_id=1, source_target_pairs={{24,28},{28,24},{25,29},{29,25},{26,30},{30,26},{27,31},{31,27}} | collective-permute-start | bytes 1179656 | tf_op jit(solution)/shard_map/ppermute | solution.py:64
  255.5 4.0 collective-permute-start.11
  256.1 10.0 %collective-permute-start.12 = (bf16[96,2048]{1,0:T(8,128)(2,1)}, bf16[96,2048]{1,0:T(8,128)(2,1)S(1)}, u32[]{:S(2)}, u32[]{:S(2)}) collective-permute-start(bf16[96,2048]{1,0:T(8,128)(2,1)} %collective-permute-done.6), channel_id=1, source_target_pairs={{0,4},{4,0},{8,12},{12,8},{1,5},{5,1},{9,13},{13,9},{2,6},{6,2},{1... | collective-permute-start | bytes 1179656 | tf_op jit(solution)/shard_map/ppermute | solution.py:64
  259.4 10.0 %collective-permute-start.13 = (bf16[96,2048]{1,0:T(8,128)(2,1)}, bf16[96,2048]{1,0:T(8,128)(2,1)S(1)}, u32[]{:S(2)}, u32[]{:S(2)}) collective-permute-start(bf16[96,2048]{1,0:T(8,128)(2,1)} %collective-permute-done.2), channel_id=1, source_target_pairs={{8,12},{12,8},{16,20},{20,16},{24,28},{28,24},{9,13},{13,9},{17,21... | collective-permute-start | bytes 1179656 | tf_op jit(solution)/shard_map/ppermute | solution.py:64
  266.1 9.7 %collective-permute-start.14 = (bf16[96,2048]{1,0:T(8,128)(2,1)S(1)}, bf16[96,2048]{1,0:T(8,128)(2,1)S(1)}, u32[]{:S(2)}, u32[]{:S(2)}) collective-permute-start(bf16[96,2048]{1,0:T(8,128)(2,1)S(1)} %collective-permute-done.7), channel_id=1, source_target_pairs={{0,4},{4,0},{1,5},{5,1},{2,6},{6,2},{3,7},{7,3}} | collective-permute-start | bytes 1179656 | tf_op jit(solution)/shard_map/ppermute | solution.py:64
  269.4 37.4 %collective-permute-start.16 = (bf16[384,2048]{1,0:T(8,128)(2,1)}, bf16[384,2048]{1,0:T(8,128)(2,1)}, u32[]{:S(2)}, u32[]{:S(2)}) collective-permute-start(bf16[384,2048]{1,0:T(8,128)(2,1)} %bitcast.43), channel_id=1, source_target_pairs={{0,1},{1,0},{2,3},{3,2},{4,5},{5,4},{6,7},{7,6},{8,9},{9,8},{10,11... | collective-permute-start | bytes 4718600 | tf_op jit(solution)/shard_map/ppermute | solution.py:53
  269.4 80.7 %collective-permute-start.20 = (bf16[384,2048]{1,0:T(8,128)(2,1)}, bf16[384,2048]{1,0:T(8,128)(2,1)}, u32[]{:S(2)}, u32[]{:S(2)}) collective-permute-start(bf16[384,2048]{1,0:T(8,128)(2,1)} %collective-permute-done.18), channel_id=1, source_target_pairs={{0,1},{1,0},{2,3},{3,2},{4,5},{5,4},{6,7},{7,6},{8,9},{9,8},{10,11... | collective-permute-start | bytes 4718600 | tf_op jit(solution)/shard_map/ppermute | solution.py:53
  286.3 59.1 %collective-permute-start.19 = (bf16[2048,768]{0,1:T(8,128)(2,1)}, bf16[2048,768]{0,1:T(8,128)(2,1)}, u32[]{:S(2)}, u32[]{:S(2)}) collective-permute-start(bf16[2048,768]{0,1:T(8,128)(2,1)} %collective-permute-done.17), channel_id=1, source_target_pairs={{0,1},{1,0},{2,3},{3,2},{4,5},{5,4},{6,7},{7,6},{8,9},{9,8},{10,11... | collective-permute-start | bytes 9437192 | tf_op jit(solution)/shard_map/ppermute | solution.py:53
  379.6 12.7 %collective-permute-start.26 = (bf16[96,2048]{1,0:T(8,128)(2,1)}, bf16[96,2048]{1,0:T(8,128)(2,1)}, u32[]{:S(2)}, u32[]{:S(2)}) collective-permute-start(bf16[96,2048]{1,0:T(8,128)(2,1)} %get-tuple-element.129), channel_id=1, source_target_pairs={{0,4},{4,0},{8,12},{12,8},{16,20},{20,16},{24,28},{28,24},{1,5},{5... | collective-permute-start | bytes 1179656 | tf_op jit(solution)/shard_map/ppermute | solution.py:64
  384.1 42.3 %all-to-all-start = ((f32[8,2,96]{2,1,0:T(2,128)}), f32[8,2,96]{2,1,0:T(2,128)}, u32[]{:S(2)}, u32[]{:S(2)}) async-start(f32[8,2,96]{2,1,0:T(2,128)} %constant_dynamic-update-slice_fusion.8), calls=%async_computation.1 | async-start | bytes 16384 | tf_op jit(solution)/shard_map/all_to_all | solution.py:302
  388.3 269.3 %reduce-scatter.4.cloned.1.call-start = ((), (), s32[]{:S(2)}) async-start(), calls=%async_computation.4 | async-start | bytes 3538944 | tf_op jit(solution)/shard_map/reduce_scatter | solution.py:308
  388.3 12.3 %collective-permute-start.25 = (bf16[96,2048]{1,0:T(8,128)(2,1)}, bf16[96,2048]{1,0:T(8,128)(2,1)S(1)}, u32[]{:S(2)}, u32[]{:S(2)}) collective-permute-start(bf16[96,2048]{1,0:T(8,128)(2,1)} %get-tuple-element.130), channel_id=1, source_target_pairs={{0,4},{4,0},{8,12},{12,8},{16,20},{20,16},{24,28},{28,24},{1,5},{5... | collective-permute-start | bytes 1179656 | tf_op jit(solution)/shard_map/ppermute | solution.py:64
  390.3 26.7 %collective-permute-start.24 = (bf16[96,2048]{1,0:T(8,128)(2,1)}, bf16[96,2048]{1,0:T(8,128)(2,1)S(1)}, u32[]{:S(2)}, u32[]{:S(2)}) collective-permute-start(bf16[96,2048]{1,0:T(8,128)(2,1)} %get-tuple-element.131), channel_id=1, source_target_pairs={{0,4},{4,0},{8,12},{12,8},{16,20},{20,16},{24,28},{28,24},{1,5},{5... | collective-permute-start | bytes 1179656 | tf_op jit(solution)/shard_map/ppermute | solution.py:64
  390.4 44.3 %collective-permute-start.23 = (bf16[96,2048]{1,0:T(8,128)(2,1)}, bf16[96,2048]{1,0:T(8,128)(2,1)}, u32[]{:S(2)}, u32[]{:S(2)}) collective-permute-start(bf16[96,2048]{1,0:T(8,128)(2,1)} %get-tuple-element.128), channel_id=1, source_target_pairs={{0,4},{4,0},{8,12},{12,8},{16,20},{20,16},{24,28},{28,24},{1,5},{5... | collective-permute-start | bytes 1179656 | tf_op jit(solution)/shard_map/ppermute | solution.py:64
  393.6 10.6 %collective-permute-start.27 = (bf16[96,2048]{1,0:T(8,128)(2,1)S(1)}, bf16[96,2048]{1,0:T(8,128)(2,1)S(1)}, u32[]{:S(2)}, u32[]{:S(2)}) collective-permute-start(bf16[96,2048]{1,0:T(8,128)(2,1)S(1)} %fusion.59), channel_id=1, source_target_pairs={{0,8},{4,12},{1,9},{5,13},{2,10},{6,14},{3,11},{7,15}} | collective-permute-start | bytes 1179656 | tf_op jit(solution)/shard_map/ppermute | solution.py:68
  405.3 11.7 %collective-permute-start.28 = (bf16[96,2048]{1,0:T(8,128)(2,1)S(1)}, bf16[96,2048]{1,0:T(8,128)(2,1)S(1)}, u32[]{:S(2)}, u32[]{:S(2)}) collective-permute-start(bf16[96,2048]{1,0:T(8,128)(2,1)S(1)} %add_convert_fusion.11), channel_id=1, source_target_pairs={{0,8},{4,12},{8,16},{12,20},{1,9},{5,13},{9,17},{13,21},{2,10},{6,... | collective-permute-start | bytes 1179656 | tf_op jit(solution)/shard_map/ppermute | solution.py:68
  419.3 2.2 collective-permute-start.30
  423.4 6.7 collective-permute-start.31
  426.4 23.4 %copy-start.101 = (f32[96]{0:T(128)S(1)}, f32[96]{0:T(128)}, u32[]{:S(2)}) copy-start(f32[96]{0:T(128)} %copy-done.100) | copy-start | bytes 1156
  427.1 9.0 %collective-permute-start.29 = (bf16[96,2048]{1,0:T(8,128)(2,1)}, bf16[96,2048]{1,0:T(8,128)(2,1)S(1)}, u32[]{:S(2)}, u32[]{:S(2)}) collective-permute-start(bf16[96,2048]{1,0:T(8,128)(2,1)} %get-tuple-element.122), channel_id=1, source_target_pairs={{0,8},{4,12},{8,16},{12,20},{16,24},{20,28},{1,9},{5,13},{9,17},{1... | collective-permute-start | bytes 1179656 | tf_op jit(solution)/shard_map/ppermute | solution.py:68
  431.5 18.2 %collective-permute-start.32 = (bf16[96,2048]{1,0:T(8,128)(2,1)S(1)}, bf16[96,2048]{1,0:T(8,128)(2,1)S(1)}, u32[]{:S(2)}, u32[]{:S(2)}) collective-permute-start(bf16[96,2048]{1,0:T(8,128)(2,1)S(1)} %add_convert_fusion.8), channel_id=1, source_target_pairs={{8,0},{12,4},{16,8},{20,12},{24,16},{28,20},{9,1},{13,5},{17,9},{2... | collective-permute-start | bytes 1179656 | tf_op jit(solution)/shard_map/ppermute | solution.py:68
  434.7 20.2 %copy-start.18 = (bf16[768,2048]{1,0:T(8,128)(2,1)S(1)}, bf16[768,2048]{1,0:T(8,128)(2,1)}, u32[]{:S(2)}) copy-start(bf16[768,2048]{1,0:T(8,128)(2,1)} %copy-done.17) | copy-start | bytes 9437188
  453.5 7.8 %collective-permute-start.33 = (bf16[96,2048]{1,0:T(8,128)(2,1)S(1)}, bf16[96,2048]{1,0:T(8,128)(2,1)S(1)}, u32[]{:S(2)}, u32[]{:S(2)}) collective-permute-start(bf16[96,2048]{1,0:T(8,128)(2,1)S(1)} %fusion.109), channel_id=1, source_target_pairs={{0,2},{1,3},{2,0},{3,1},{4,6},{5,7},{6,4},{7,5},{8,10},{9,11},{10,... | collective-permute-start | bytes 1179656 | tf_op jit(solution)/shard_map/ppermute | solution.py:53
  462.4 6.3 collective-permute-start.34
  464.0 220.5 %reduce-scatter.6.cloned.1.call-start = ((), (), s32[]{:S(2)}) async-start(), calls=%async_computation.5 | async-start | bytes 6488064 | tf_op jit(solution)/shard_map/reduce_scatter | solution.py:403
  516.9 226.8 %reduce-scatter.8.cloned.1.call-start = ((), (), s32[]{:S(2)}) async-start(), calls=%async_computation.6 | async-start | bytes 4718592 | tf_op jit(solution)/shard_map/reduce_scatter | solution.py:341
  523.7 21.9 %collective-permute-start.42 = (bf16[2048,768]{0,1:T(8,128)(2,1)}, bf16[2048,768]{0,1:T(8,128)(2,1)}, u32[]{:S(2)}, u32[]{:S(2)}) collective-permute-start(bf16[2048,768]{0,1:T(8,128)(2,1)} %convolution_convert_fusion.2), channel_id=1, source_target_pairs={{0,1},{1,0},{2,3},{3,2},{4,5},{5,4},{6,7},{7,6},{8,9},{9,8},{10,11... | collective-permute-start | bytes 9437192 | tf_op jit(solution)/shard_map/ppermute | solution.py:53
  526.7 12.3 %collective-permute-start.45 = (bf16[384,2048]{1,0:T(8,128)(2,1)}, bf16[384,2048]{1,0:T(8,128)(2,1)}, u32[]{:S(2)}, u32[]{:S(2)}) collective-permute-start(bf16[384,2048]{1,0:T(8,128)(2,1)} %convolution_convert_fusion.4), channel_id=1, source_target_pairs={{0,1},{1,0},{2,3},{3,2},{4,5},{5,4},{6,7},{7,6},{8,9},{9,8},{10,11... | collective-permute-start | bytes 4718600 | tf_op jit(solution)/shard_map/ppermute | solution.py:53
  531.5 130.7 %collective-permute-start.41 = (bf16[2048,768]{0,1:T(8,128)(2,1)}, bf16[2048,768]{0,1:T(8,128)(2,1)}, u32[]{:S(2)}, u32[]{:S(2)}) collective-permute-start(bf16[2048,768]{0,1:T(8,128)(2,1)} %convolution_convert_fusion.3), channel_id=1, source_target_pairs={{0,1},{1,0},{2,3},{3,2},{4,5},{5,4},{6,7},{7,6},{8,9},{9,8},{10,11... | collective-permute-start | bytes 9437192 | tf_op jit(solution)/shard_map/ppermute | solution.py:53
  534.5 24.1 %collective-permute-start.44 = (bf16[384,2048]{1,0:T(8,128)(2,1)}, bf16[384,2048]{1,0:T(8,128)(2,1)}, u32[]{:S(2)}, u32[]{:S(2)}) collective-permute-start(bf16[384,2048]{1,0:T(8,128)(2,1)} %convolution_convert_fusion.5), channel_id=1, source_target_pairs={{0,1},{1,0},{2,3},{3,2},{4,5},{5,4},{6,7},{7,6},{8,9},{9,8},{10,11... | collective-permute-start | bytes 4718600 | tf_op jit(solution)/shard_map/ppermute | solution.py:53
  544.2 37.3 %collective-permute-start.46 = (bf16[384,2048]{1,0:T(8,128)(2,1)S(1)}, bf16[384,2048]{1,0:T(8,128)(2,1)S(1)}, u32[]{:S(2)}, u32[]{:S(2)}) collective-permute-start(bf16[384,2048]{1,0:T(8,128)(2,1)S(1)} %add_convert_fusion.3), channel_id=1, source_target_pairs={{0,2},{1,3},{2,0},{3,1},{4,6},{5,7},{6,4},{7,5},{8,10},{9,11},{10,... | collective-permute-start | bytes 4718600 | tf_op jit(solution)/shard_map/ppermute | solution.py:53
  551.5 110.7 %collective-permute-start.43 = (bf16[2048,768]{0,1:T(8,128)(2,1)}, bf16[2048,768]{0,1:T(8,128)(2,1)}, u32[]{:S(2)}, u32[]{:S(2)}) collective-permute-start(bf16[2048,768]{0,1:T(8,128)(2,1)} %add_convert_fusion), channel_id=1, source_target_pairs={{0,2},{1,3},{2,0},{3,1},{4,6},{5,7},{6,4},{7,5},{8,10},{9,11},{10,... | collective-permute-start | bytes 9437192 | tf_op jit(solution)/shard_map/ppermute | solution.py:53
  552.5 4.5 collective-permute-start.35
  553.0 103.8 %copy-start.25 = (f32[384,2048]{1,0:T(8,128)}, f32[384,2048]{1,0:T(8,128)S(1)}, u32[]{:S(2)}) copy-start(f32[384,2048]{1,0:T(8,128)S(1)} %convert_element_type.302) | copy-start | bytes 9437188
  557.3 100.3 %copy-start.102 = (f32[96]{0:T(128)S(1)}, f32[96]{0:T(128)}, u32[]{:S(2)}) copy-start(f32[96]{0:T(128)} %copy-done.100) | copy-start | bytes 1156
  557.3 100.3 %copy-start.107 = (f32[96]{0:T(128)S(1)}, f32[96]{0:T(128)}, u32[]{:S(2)}) copy-start(f32[96]{0:T(128)} %copy-done.106) | copy-start | bytes 1156
  557.3 99.5 %collective-permute-start.36 = (bf16[96,2048]{1,0:T(8,128)(2,1)S(1)}, bf16[96,2048]{1,0:T(8,128)(2,1)S(1)}, u32[]{:S(2)}, u32[]{:S(2)}) collective-permute-start(bf16[96,2048]{1,0:T(8,128)(2,1)S(1)} %fusion.69), channel_id=1, source_target_pairs={{0,2},{1,3},{2,0},{3,1},{4,6},{5,7},{6,4},{7,5},{8,10},{9,11},{10,... | collective-permute-start | bytes 1179656 | tf_op jit(solution)/shard_map/ppermute | solution.py:53
  660.1 21.4 %collective-permute-start.21 = (bf16[96,2048]{1,0:T(8,128)(2,1)S(1)}, bf16[96,2048]{1,0:T(8,128)(2,1)S(1)}, u32[]{:S(2)}, u32[]{:S(2)}) collective-permute-start(bf16[96,2048]{1,0:T(8,128)(2,1)S(1)} %get-tuple-element.151), channel_id=1, source_target_pairs={{0,2},{1,3},{2,0},{3,1},{4,6},{5,7},{6,4},{7,5},{8,10},{9,11},{10,... | collective-permute-start | bytes 1179656 | tf_op jit(solution)/shard_map/ppermute | solution.py:53
  661.5 17.9 %collective-permute-start.37 = (bf16[96,2048]{1,0:T(8,128)(2,1)S(1)}, bf16[96,2048]{1,0:T(8,128)(2,1)S(1)}, u32[]{:S(2)}, u32[]{:S(2)}) collective-permute-start(bf16[96,2048]{1,0:T(8,128)(2,1)S(1)} %get-tuple-element.150), channel_id=1, source_target_pairs={{0,2},{1,3},{2,0},{3,1},{4,6},{5,7},{6,4},{7,5},{8,10},{9,11},{10,... | collective-permute-start | bytes 1179656 | tf_op jit(solution)/shard_map/ppermute | solution.py:53
  679.4 3.0 collective-permute-start.38
  681.6 3.9 collective-permute-start.22
  685.4 60.5 %collective-permute-start.39 = (bf16[256,128]{0,1:T(8,128)(2,1)S(1)}, bf16[256,128]{0,1:T(8,128)(2,1)S(1)}, u32[]{:S(2)}, u32[]{:S(2)}) collective-permute-start(bf16[256,128]{0,1:T(8,128)(2,1)S(1)} %get-tuple-element.154), channel_id=1, source_target_pairs={{0,1},{1,0},{2,3},{3,2},{4,5},{5,4},{6,7},{7,6},{8,9},{9,8},{10,11... | collective-permute-start | bytes 196616 | tf_op jit(solution)/shard_map/ppermute | solution.py:53
  689.5 56.3 %copy-start.65 = (bf16[256,1408]{0,1:T(8,128)(2,1)S(1)}, bf16[256,1408]{0,1:T(8,128)(2,1)}, u32[]{:S(2)}) copy-start(bf16[256,1408]{0,1:T(8,128)(2,1)} %reduce-scatter.6.cloned.1.call-done) | copy-start | bytes 2162692
  745.8 4.4 collective-permute-start.40
  (101 other events, 394.4 us)
Sparse Core Ops, SparseCore 0:
  71.7 61.2 all-gather.4
  464.1 74.6 reduce-scatter.3
  542.5 109.4 reduce-scatter.5
  655.4 88.2 reduce-scatter.7

commit v2 on v1

v2 whole, which is shorter than its diff:
```python
import functools

import jax
import jax.numpy as jnp
from jax import lax
from jax.experimental import pallas as pl
from jax.experimental.pallas import tpu as pltpu
from jax.sharding import PartitionSpec as P

epsilon = 1e-06
rope_base = 1000000.0
far_below = -1e30


def rope_tables(positions, head_size):
    half_size = head_size // 2
    frequency = rope_base ** (-(jnp.arange(half_size, dtype=jnp.float32) * 2.0) / head_size)
    angles = positions.astype(jnp.float32)[:, None] * frequency[None, :]
    cosine = jnp.cos(angles)
    sine_table = jnp.sin(angles)
    return (jnp.concatenate([cosine, cosine], -1), jnp.concatenate([sine_table, sine_table], -1))


def norm_back(grad_scaled, value_rows, scales):
    return scales * (
        grad_scaled
        - value_rows * scales * scales * jnp.mean(grad_scaled * value_rows, -1, keepdims=True)
    )


def bf(value):
    return value.astype(jnp.bfloat16)


def mm(left, right, contract=(1, 0)):
    return lax.dot_general(
        left, right, (((contract[0],), (contract[1],)), ((), ())), preferred_element_type=jnp.float32
    )


def after(values, first):
    if first is None:
        return values
    return lax.optimization_barrier((*values, first))[: len(values)]


def swap(value, step):
    size = lax.axis_size("tensor")
    return lax.ppermute(value, "tensor", [(i, i ^ step) for i in range(size)])


vmem_bytes = 58 * 2**20
small_cost = pl.CostEstimate(flops=2**20, bytes_accessed=2**16, transcendentals=0)


def whole(shape):
    return pl.BlockSpec(shape, lambda *_: (0,) * len(shape))


def turn(rows):
    return pltpu.roll(rows, rows.shape[-1] // 2, 1)


def inverse_rms(rows):
    return lax.rsqrt(jnp.mean(rows * rows, -1, keepdims=True) + epsilon)


def split_rows(rank_ref, total, keep, give):
    rows = keep.shape[1]
    low = rank_ref[0] % 2
    for high in range(keep.shape[0]):
        start = pl.multiple_of((2 * high + low) * rows, rows)
        keep[high] = total[pl.ds(start, rows), :]
        start = pl.multiple_of((2 * high + 1 - low) * rows, rows)
        give[high] = bf(total[pl.ds(start, rows), :])


def attend_kernel(
    rank_ref, x, gain, w_query, w_key, w_value, q_gain, k_gain, cosine, sine, seg_col, seg_row, w_out,
    xn, qp, kp, q, k, v, prob, o, keep, give, total,
):
    step, steps = pl.program_id(0), pl.num_programs(0)
    tokens, head = kp.shape
    cut = keep.shape[1]

    @pl.when(step == 0)
    def _():
        @pl.loop(0, tokens // cut)
        def _(i):
            rows = pl.ds(pl.multiple_of(i * cut, cut), cut)
            value = x[rows, :].astype(jnp.float32)
            xn[rows, :] = bf(value * inverse_rms(value) * gain[...])

        raw = mm(xn[...], w_key[...])
        kp[...] = raw
        scaled = raw * inverse_rms(raw) * k_gain[...]
        k[...] = bf(scaled * cosine[...] + turn(scaled) * sine[...])
        v[...] = bf(mm(xn[...], w_value[...]))
        total[...] = jnp.zeros_like(total)

    raw_pair = mm(xn[...], w_query[...])
    qp[...] = raw_pair
    visible = (seg_col[...] == seg_row[...]) & (
        lax.broadcasted_iota(jnp.int32, (tokens, tokens), 0)
        >= lax.broadcasted_iota(jnp.int32, (tokens, tokens), 1)
    )
    for i in range(prob.shape[0]):
        cols = slice(i * head, (i + 1) * head)
        raw = raw_pair[:, cols]
        scaled = raw * inverse_rms(raw) * q_gain[...]
        rows = bf(scaled * cosine[...] + turn(scaled) * sine[...])
        q[:, cols] = rows
        scores = jnp.where(visible, mm(rows, k[...], (1, 1)) * head**-0.5, far_below)
        weight = jnp.exp(scores - jnp.max(scores, -1, keepdims=True))
        low = bf(weight * (1.0 / jnp.sum(weight, -1, keepdims=True)))
        prob[i] = low
        o[:, cols] = bf(mm(low, v[...]))
    wide = 512

    @pl.loop(0, total.shape[1] // wide)
    def _(n):
        at = pl.ds(pl.multiple_of(n * wide, wide), wide)
        total[:, at] += mm(o[...], w_out[:, at])

    @pl.when(step == steps - 1)
    def _():
        split_rows(rank_ref, total, keep, give)


def attend(rank, x, gain, w_query, w_key, w_value, q_gain, k_gain, cosine, sine, segments, w_out, cut):
    tokens, width = x.shape
    head = q_gain.shape[0]
    query = w_query.shape[1]
    pair = 2
    steps = query // (pair * head)
    heads = pl.BlockSpec((tokens, pair * head), lambda j, _: (0, j))
    halves = tokens // cut // 2
    return pl.pallas_call(
        attend_kernel,
        grid_spec=pltpu.PrefetchScalarGridSpec(
            num_scalar_prefetch=1,
            grid=(steps,),
            in_specs=[
                whole((tokens, width)),
                whole((1, width)),
                pl.BlockSpec((width, pair * head), lambda j, _: (0, j)),
                whole((width, head)),
                whole((width, head)),
                whole((1, head)),
                whole((1, head)),
                whole((tokens, head)),
                whole((tokens, head)),
                whole((tokens, 1)),
                whole((1, tokens)),
                pl.BlockSpec((pair * head, width), lambda j, _: (j, 0)),
            ],
            out_specs=[
                whole((tokens, width)),
                heads,
                whole((tokens, head)),
                heads,
                whole((tokens, head)),
                whole((tokens, head)),
                pl.BlockSpec((pair, tokens, tokens), lambda j, _: (j, 0, 0)),
                heads,
                whole((halves, cut, width)),
                whole((halves, cut, width)),
            ],
            scratch_shapes=[pltpu.VMEM((tokens, width), jnp.float32)],
        ),
        out_shape=[
            jax.ShapeDtypeStruct((tokens, width), jnp.bfloat16),
            jax.ShapeDtypeStruct((tokens, query), jnp.float32),
            jax.ShapeDtypeStruct((tokens, head), jnp.float32),
            jax.ShapeDtypeStruct((tokens, query), jnp.bfloat16),
            jax.ShapeDtypeStruct((tokens, head), jnp.bfloat16),
            jax.ShapeDtypeStruct((tokens, head), jnp.bfloat16),
            jax.ShapeDtypeStruct((query // head, tokens, tokens), jnp.bfloat16),
            jax.ShapeDtypeStruct((tokens, query), jnp.bfloat16),
            jax.ShapeDtypeStruct((halves, cut, width), jnp.float32),
            jax.ShapeDtypeStruct((halves, cut, width), jnp.bfloat16),
        ],
        compiler_params=pltpu.CompilerParams(vmem_limit_bytes=vmem_bytes),
        cost_estimate=small_cost,
        name="attend",
    )(
        rank, x, gain[None], w_query, w_key, w_value, q_gain[None], k_gain[None], cosine, sine,
        segments[:, None], segments[None, :], w_out,
    )


def attend_back_kernel(
    rank_ref, x, xn, dattn, w_query, w_key, w_value, q_gain, k_gain, cosine, sine, w_out, qp, kp, q, k, v, prob,
    packed, gains, attn_gain, keep, give, total, dk, dv, low,
):
    step, steps = pl.program_id(0), pl.num_programs(0)
    tokens, head = kp.shape
    cut = keep.shape[1]
    scale = head**-0.5
    width = x.shape[1]
    wide = 512
    blocks = packed.shape[0]
    block_rows = width // blocks

    def unrotate(grad):
        return grad * cosine[...] - turn(grad) * sine[...]

    def unnorm(grad, raw, inverse, gain):
        scaled = grad * gain
        return inverse * (scaled - raw * inverse * inverse * jnp.mean(scaled * raw, -1, keepdims=True))

    def add_total(left, right, at):
        total[:, at] += mm(left, right[at, :], (1, 1))

    def put_packed(n):
        at = pl.ds(pl.multiple_of(n * wide, wide), wide)
        grad = bf(mm(xn[:, at], low[...], (0, 0)))
        many = wide // block_rows
        first = n * many
        packed[pl.ds(first, many), pl.ds(0, block_rows), :] = grad.reshape(many, block_rows, -1)

    @pl.when(step == 0)
    def _():
        total[...] = jnp.zeros_like(total)
        dk[...] = jnp.zeros_like(dk)
        dv[...] = jnp.zeros_like(dv)
        gains[...] = jnp.zeros_like(gains)

    @pl.when(step < steps - 1)
    def _():
        dout_pair = bf(mm(dattn[...], w_out[...], (1, 1)))
        for i in range(prob.shape[0]):
            cols = slice(i * head, (i + 1) * head)
            dout = dout_pair[:, cols]
            weight = prob[i]
            dp = mm(dout, v[...], (1, 1))
            wide_weight = weight.astype(jnp.float32)
            ds = bf(wide_weight * (dp - jnp.sum(wide_weight * dp, -1, keepdims=True)))
            dv[...] += mm(weight, dout, (0, 0))
            dk[...] += mm(ds, q[:, cols], (0, 0))
            dqu = unrotate(mm(ds, k[...]) * scale)
            raw = qp[:, cols]
            inverse = inverse_rms(raw)
            gains[0:1, :] += jnp.sum(dqu * raw * inverse, 0, keepdims=True)
            low[:, cols] = bf(unnorm(dqu, raw, inverse, q_gain[...]))

        @pl.loop(0, width // wide)
        def _(n):
            put_packed(n)
            add_total(low[...], w_query, pl.ds(pl.multiple_of(n * wide, wide), wide))

    @pl.when(step == steps - 1)
    def _():
        dku = unrotate(dk[...] * scale)
        raw = kp[...]
        inverse = inverse_rms(raw)
        gains[1:2, :] = jnp.sum(dku * raw * inverse, 0, keepdims=True)
        low[:, :head] = bf(unnorm(dku, raw, inverse, k_gain[...]))
        low[:, head:] = bf(dv[...])

        @pl.loop(0, width // wide)
        def _(n):
            put_packed(n)
            at = pl.ds(pl.multiple_of(n * wide, wide), wide)
            add_total(low[:, :head], w_key, at)
            add_total(low[:, head:], w_value, at)

        attn_gain[...] = jnp.zeros_like(attn_gain)

        @pl.loop(0, tokens // cut)
        def _(i):
            rows = pl.ds(pl.multiple_of(i * cut, cut), cut)
            value = x[rows, :].astype(jnp.float32)
            attn_gain[...] += jnp.sum(total[rows, :] * value * inverse_rms(value), 0, keepdims=True)

        split_rows(rank_ref, total, keep, give)


def attend_back(
    rank, x, xn, dattn, w_query, w_key, w_value, q_gain, k_gain, cosine, sine, w_out, qp, kp, q, k, v, prob,
    cut, blocks, spare,
):
    tokens, width = x.shape
    head = q_gain.shape[0]
    query = w_query.shape[1]
    pair = 2
    steps = query // (pair * head)
    last = steps - 1
    heads = pl.BlockSpec((tokens, pair * head), lambda j, _: (0, jnp.minimum(j, last)))
    halves = tokens // cut // 2
    block_rows = width // blocks + spare
    return pl.pallas_call(
        attend_back_kernel,
        grid_spec=pltpu.PrefetchScalarGridSpec(
            num_scalar_prefetch=1,
            grid=(steps + 1,),
            in_specs=[
                whole((tokens, width)),
                whole((tokens, width)),
                whole((tokens, width)),
                pl.BlockSpec((width, pair * head), lambda j, _: (0, jnp.minimum(j, last))),
                whole((width, head)),
                whole((width, head)),
                whole((1, head)),
                whole((1, head)),
                whole((tokens, head)),
                whole((tokens, head)),
                pl.BlockSpec((pair * head, width), lambda j, _: (jnp.minimum(j, last), 0)),
                heads,
                whole((tokens, head)),
                heads,
                whole((tokens, head)),
                whole((tokens, head)),
                pl.BlockSpec((pair, tokens, tokens), lambda j, _: (jnp.minimum(j, last), 0, 0)),
            ],
            out_specs=[
                pl.BlockSpec((blocks, block_rows, pair * head), lambda j, _: (0, 0, j)),
                whole((8, head)),
                whole((1, width)),
                whole((halves, cut, width)),
                whole((halves, cut, width)),
            ],
            scratch_shapes=[
                pltpu.VMEM((tokens, width), jnp.float32),
                pltpu.VMEM((tokens, head), jnp.float32),
                pltpu.VMEM((tokens, head), jnp.float32),
                pltpu.VMEM((tokens, pair * head), jnp.bfloat16),
            ],
        ),
        out_shape=[
            jax.ShapeDtypeStruct((blocks, block_rows, query + 2 * head), jnp.bfloat16),
            jax.ShapeDtypeStruct((8, head), jnp.float32),
            jax.ShapeDtypeStruct((1, width), jnp.float32),
            jax.ShapeDtypeStruct((halves, cut, width), jnp.float32),
            jax.ShapeDtypeStruct((halves, cut, width), jnp.bfloat16),
        ],
        compiler_params=pltpu.CompilerParams(vmem_limit_bytes=vmem_bytes),
        cost_estimate=small_cost,
        name="attend_back",
    )(
        rank, x, xn, dattn, w_query, w_key, w_value, q_gain[None], k_gain[None], cosine, sine, w_out,
        qp, kp, q, k, v, prob,
    )


class Loads:
    def __init__(self, sources, target, sems, shards):
        height = sources[0].shape[0]
        self.each = len(sources) // shards
        self.copies = [
            pltpu.make_async_copy(source, target.at[pl.ds(i * height, height), :], sems.at[i])
            for i, source in enumerate(sources)
        ]

    def start(self):
        for copy in self.copies:
            copy.start()

    def wait(self, shard):
        for copy in self.copies[shard * self.each : (shard + 1) * self.each]:
            copy.wait()


def forward_kernel(rank_ref, hn, routes, router, *rest, shards, local, hidden, top_count):
    in_hbm, down_hbm = rest[: 2 * shards], rest[2 * shards : 3 * shards]
    out, pre_out, gated, gates, gates_wide, in_all, down_all, in_sems, down_sems = rest[3 * shards :]
    chunk, shard = pl.program_id(0), pl.program_id(1)
    width = local * hidden
    rows = hn.shape[0]
    in_loads = Loads(in_hbm, in_all, in_sems, shards)
    down_loads = Loads(down_hbm, down_all, down_sems, shards)

    @pl.when((chunk == 0) & (shard == 0))
    def _():
        in_loads.start()
        down_loads.start()

    @pl.when(shard == 0)
    def _():
        names = lax.broadcasted_iota(jnp.int32, (rows, router.shape[0]), 1).astype(jnp.float32)
        chosen = routes[...].astype(jnp.float32)
        mask = jnp.zeros(names.shape, jnp.bool_)
        for j in range(top_count):
            mask = mask | (chosen[:, j : j + 1] == names)
        logits = jnp.where(mask, mm(hn[...], router[...], (1, 1)), far_below)
        weight = jnp.exp(logits - jnp.max(logits, -1, keepdims=True))
        weight = weight * (1.0 / jnp.sum(weight, -1, keepdims=True))
        lanes = lax.broadcasted_iota(jnp.int32, gates.shape, 1)
        packed = jnp.zeros(gates.shape, jnp.float32)
        for i in range(local):
            here = names == (rank_ref[1] * local + i).astype(jnp.float32)
            value = jnp.sum(jnp.where(here, weight, 0.0), -1, keepdims=True)
            gates_wide[:, i * hidden : (i + 1) * hidden] = jnp.broadcast_to(value, (rows, hidden))
            packed = packed + jnp.where(lanes == i, value, 0.0)
        gates[...] = packed

    for i in range(shards):
        @pl.when((chunk == 0) & (shard == i))
        def _(i=i):
            in_loads.wait(i)

    at = pl.multiple_of(shard * 2 * width, 2 * width)
    pre = mm(hn[...], in_all[pl.ds(at, 2 * width), :], (1, 1))
    pre_out[...] = pre
    middle = jax.nn.silu(pre[:, :width]) * pre[:, width:]
    gated[:, pl.ds(pl.multiple_of(shard * width, width), width)] = bf(middle * gates_wide[...])

    @pl.when(shard == shards - 1)
    def _():
        @pl.when(chunk == 0)
        def _():
            for i in range(shards):
                down_loads.wait(i)

        wide = 512

        @pl.loop(0, out.shape[1] // wide)
        def _(n):
            cols = pl.ds(pl.multiple_of(n * wide, wide), wide)
            out[:, cols] = bf(mm(gated[...], down_all[:, cols]))


def backward_kernel(rank_ref, g, gates, pre_in, *rest, shards, local, hidden):
    in_hbm, down_hbm = rest[: 2 * shards], rest[2 * shards : 3 * shards]
    back, pre_grad, in_all, down_all, totals, in_sems, down_sems = rest[3 * shards :]
    chunk, shard = pl.program_id(0), pl.program_id(1)
    width = local * hidden
    rows, model = g.shape
    in_loads = Loads(in_hbm, in_all, in_sems, shards)
    down_loads = Loads(down_hbm, down_all, down_sems, shards)

    @pl.when((chunk == 0) & (shard == 0))
    def _():
        down_loads.start()
        in_loads.start()

    for i in range(shards):
        @pl.when((chunk == 0) & (shard == i))
        def _(i=i):
            down_loads.wait(i)

    @pl.when(shard == 0)
    def _():
        totals[...] = jnp.zeros_like(totals)

    at = pl.multiple_of(shard * width, width)
    grad_middle_all = mm(g[...], down_all[pl.ds(at, width), :], (1, 1))
    lanes = lax.broadcasted_iota(jnp.int32, totals.shape, 1)
    experts_at = lax.broadcasted_iota(jnp.int32, (rows, width), 1)
    gate_wide = jnp.zeros((rows, width), jnp.float32)
    for e in range(local):
        gate_wide = jnp.where(experts_at // hidden == e, gates[:, e : e + 1], gate_wide)
    gate_pre, up_pre = pre_in[:, :width], pre_in[:, width:]
    sigmoid_gate = jax.nn.sigmoid(gate_pre)
    activated = gate_pre * sigmoid_gate
    product = activated * up_pre * grad_middle_all
    added = jnp.zeros(totals.shape, jnp.float32)
    for e in range(local):
        part = jnp.sum(product[:, e * hidden : (e + 1) * hidden], -1, keepdims=True)
        added = added + jnp.where(lanes == e, part, 0.0)
    totals[...] += added
    grad_middle = grad_middle_all * gate_wide
    at = pl.multiple_of(shard * 2 * width, 2 * width)
    pre_grad[:, pl.ds(at, width)] = bf(
        grad_middle * up_pre * sigmoid_gate * (1.0 + gate_pre * (1.0 - sigmoid_gate))
    )
    pre_grad[:, pl.ds(pl.multiple_of(at + width, width), width)] = bf(grad_middle * activated)

    @pl.when(shard == shards - 1)
    def _():
        @pl.when(chunk == 0)
        def _():
            for i in range(shards):
                in_loads.wait(i)

        wide = 512

        @pl.loop(0, model // wide)
        def _(n):
            cols = pl.ds(pl.multiple_of(n * wide, wide), wide)
            back[:, cols] = bf(mm(pre_grad[...], in_all[:, cols]))

        spare = back.shape[1] - model
        places = lax.broadcasted_iota(jnp.int32, (rows, spare), 1)
        tail = jnp.zeros((rows, spare), jnp.float32)
        for e in range(local):
            value = totals[:, e : e + 1]
            high = bf(value).astype(jnp.float32)
            here = rank_ref[1] * local + e
            tail = tail + jnp.where(places == here, high, 0.0)
            tail = tail + jnp.where(places == spare // 2 + here, value - high, 0.0)
        back[:, model:] = bf(tail)


def expert_specs(tokens, model, shards, width):
    rows = tokens
    while rows > 768:
        rows //= 2

    def block(cols, step=None):
        if step is None:
            return pl.BlockSpec((rows, cols), lambda c, s, _: (c, 0))
        return pl.BlockSpec((rows, cols), lambda c, s, _: (c, s if step < 0 else step))

    scratch = [
        pltpu.VMEM((shards * 2 * width, model), jnp.bfloat16),
        pltpu.VMEM((shards * width, model), jnp.bfloat16),
        pltpu.SemaphoreType.DMA((2 * shards,)),
        pltpu.SemaphoreType.DMA((shards,)),
    ]
    return rows, block, [pl.BlockSpec(memory_space=pl.ANY)] * (3 * shards), scratch


def experts_forward(ranks, hn, sent, router, in_mats, down_mats, local, top_count):
    tokens, model = hn.shape
    shards, width = len(down_mats), down_mats[0].shape[0]
    rows, block, hbm, scratch = expert_specs(tokens, model, shards, width)
    return pl.pallas_call(
        functools.partial(
            forward_kernel, shards=shards, local=local, hidden=width // local, top_count=top_count
        ),
        grid_spec=pltpu.PrefetchScalarGridSpec(
            num_scalar_prefetch=1,
            grid=(tokens // rows, shards),
            in_specs=[block(model), block(128, model // 128), whole(router.shape)] + hbm,
            out_specs=[block(model), block(2 * width, -1), block(shards * width), block(128)],
            scratch_shapes=[pltpu.VMEM((rows, width), jnp.float32)] + scratch,
        ),
        out_shape=[
            jax.ShapeDtypeStruct((tokens, model), jnp.bfloat16),
            jax.ShapeDtypeStruct((tokens, shards * 2 * width), jnp.float32),
            jax.ShapeDtypeStruct((tokens, shards * width), jnp.bfloat16),
            jax.ShapeDtypeStruct((tokens, 128), jnp.float32),
        ],
        compiler_params=pltpu.CompilerParams(vmem_limit_bytes=vmem_bytes),
        cost_estimate=small_cost,
        name="experts_forward",
    )(ranks, hn, sent, router, *in_mats, *down_mats)


def experts_backward(ranks, sent, gates, pre, in_mats, down_mats, local, spare):
    tokens, model = sent.shape[0], down_mats[0].shape[1]
    shards, width = len(down_mats), down_mats[0].shape[0]
    rows, block, hbm, scratch = expert_specs(tokens, model, shards, width)
    return pl.pallas_call(
        functools.partial(backward_kernel, shards=shards, local=local, hidden=width // local),
        grid_spec=pltpu.PrefetchScalarGridSpec(
            num_scalar_prefetch=1,
            grid=(tokens // rows, shards),
            in_specs=[block(model), block(128), block(2 * width, -1)] + hbm,
            out_specs=[block(model + spare), block(shards * 2 * width)],
            scratch_shapes=scratch[:2] + [pltpu.VMEM((rows, 128), jnp.float32)] + scratch[2:],
        ),
        out_shape=[
            jax.ShapeDtypeStruct((tokens, model + spare), jnp.bfloat16),
            jax.ShapeDtypeStruct((tokens, shards * 2 * width), jnp.bfloat16),
        ],
        compiler_params=pltpu.CompilerParams(vmem_limit_bytes=vmem_bytes),
        cost_estimate=small_cost,
        name="experts_backward",
    )(ranks, sent, gates, pre, *in_mats, *down_mats)


def out_grad_kernel(dattn, o, packed):
    packed[...] = bf(mm(dattn[...], o[...], (0, 0))).reshape(packed.shape)


def out_grad(dattn, o, blocks):
    tokens, width = dattn.shape
    cols = o.shape[1]
    rows = width // blocks
    many = max(1, 256 // rows)
    return pl.pallas_call(
        out_grad_kernel,
        grid=(blocks // many,),
        in_specs=[pl.BlockSpec((tokens, many * rows), lambda i: (0, i)), whole(o.shape)],
        out_specs=pl.BlockSpec((many, rows, cols), lambda i: (i, 0, 0)),
        out_shape=jax.ShapeDtypeStruct((blocks, rows, cols), jnp.bfloat16),
        compiler_params=pltpu.CompilerParams(vmem_limit_bytes=vmem_bytes),
        cost_estimate=small_cost,
        name="out_grad",
    )(dattn, o)


class Tokens:
    def __init__(self):
        self.size = lax.axis_size("expert")
        self.line = self.size == 8
        self.me = lax.axis_index("expert")
        self.z, self.y = self.me // 2, self.me % 2

    def across(self, value):
        return lax.ppermute(value, "expert", [(i, i ^ 1) for i in range(8)])

    def along(self, value, step):
        return lax.ppermute(value, "expert", [(i, i ^ (2 * step)) for i in range(8)])

    def place(self, step, other):
        return (self.z ^ step) * 2 + (1 - self.y if other else self.y)

    def gather(self, own, early=None, late=None):
        if not self.line:
            return lax.all_gather(own, "expert", axis=0, tiled=False)
        blocks = [own] + [self.along(own, step) for step in (1, 2, 3)]
        others = [self.across(own)]
        (blocks[1],) = after((blocks[1],), early)
        blocks[2], blocks[3] = after((blocks[2], blocks[3]), late)
        others += [self.across(value) for value in blocks[1:]]
        rows = jnp.zeros((self.size, *own.shape), own.dtype)
        for step in range(4):
            for value, other in ((blocks[step], False), (others[step], True)):
                rows = lax.dynamic_update_index_in_dim(rows, value, self.place(step, other), 0)
        return rows

    def scatter(self, parts, first=None, second=None, last=None):
        if not self.line:
            return lax.psum_scatter(parts, "expert", scatter_dimension=0, tiled=False).astype(
                jnp.float32
            )

        def part(step, other):
            return lax.dynamic_index_in_dim(parts, self.place(step, other), 0, False)

        sums = {}
        for step in (3, 2, 1, 0):
            sums[step] = part(step, False).astype(jnp.float32)
            sums[step] = sums[step] + self.across(part(step, True)).astype(jnp.float32)
        given = {step: bf(sums[step]) for step in (3, 2, 1)}
        (given[2],) = after((given[2],), first)
        (given[1],) = after((given[1],), second)
        arrived = after(tuple(self.along(given[step], step) for step in (3, 2, 1)), last)
        return sums[0] + sum(value.astype(jnp.float32) for value in arrived)


def body(
    hidden_in,
    cotangent,
    segments,
    positions,
    routes,
    attn_gain,
    w_query,
    w_key,
    value_weight,
    q_gain,
    k_gain,
    w_out,
    ffn_gain,
    router,
    w_gate,
    w_up,
    w_down,
):
    tok_count, model_width = hidden_in.shape
    head_size = q_gain.shape[0]
    experts = router.shape[1]
    local_experts, _, hidden = w_gate.shape
    tensor_size = lax.axis_size("tensor")
    tensor_rank = lax.axis_index("tensor")
    expert_rank = lax.axis_index("expert")
    shard_rows = tok_count // tensor_size
    order = Tokens()
    group = order.size

    def own_rows(value):
        return lax.dynamic_slice_in_dim(value, tensor_rank * shard_rows, shard_rows)

    cot_own = own_rows(cotangent)
    routes_own = own_rows(routes)
    spare_cols = 128
    routes_wide = jnp.pad(bf(routes_own), ((0, 0), (0, spare_cols - routes.shape[1])))
    sent_own = jnp.concatenate([cot_own, routes_wide], 1)
    (hidden_in,) = after((hidden_in,), sent_own)
    sent = lax.all_gather(sent_own, "expert", axis=0, tiled=True)
    grad_all = sent[:, :model_width]
    expert_ids = jnp.arange(experts, dtype=jnp.int32)

    def mask_of(route_rows):
        return jnp.any(route_rows[:, :, None] == expert_ids[None, None, :], 1)

    mask_own = mask_of(routes_own)
    own_mats = [value.reshape(local_experts * hidden, model_width) for value in (w_gate.transpose(0, 2, 1), w_up.transpose(0, 2, 1), w_down)]

    cosine, sine_table = rope_tables(positions, head_size)
    half = jnp.arange(head_size, dtype=jnp.int32) < head_size // 2
    sine_table = jnp.where(half, -sine_table, sine_table)
    ranks = jnp.stack([tensor_rank, expert_rank]).astype(jnp.int32)
    normalized_input, qp, kp, q, k, v, prob, attended_rows, keep, give_part = attend(
        ranks, hidden_in, attn_gain, w_query, w_key, value_weight, q_gain, k_gain, cosine, sine_table,
        segments, w_out, shard_rows,
    )

    def reduce_rows(keep, give, first=None):
        half = keep + swap(give, 1).astype(jnp.float32)
        high = tensor_rank // 2
        keep = lax.dynamic_index_in_dim(half, high, 0, False)
        give = bf(lax.dynamic_index_in_dim(half, 1 - high, 0, False))
        (give,) = after((give,), first)
        return keep + swap(give, 2).astype(jnp.float32)

    def gather_rows(own):
        far = swap(own, 2)
        high, low = tensor_rank // 2, tensor_rank % 2
        mine = jnp.where(high == 0, jnp.stack([own, far]), jnp.stack([far, own]))
        theirs = swap(mine, 1)
        both = jnp.where(low == 0, jnp.stack([mine, theirs], 1), jnp.stack([theirs, mine], 1))
        return both.reshape(tok_count, model_width)

    far_gate = swap(own_mats[0], 2)
    attn_sum = reduce_rows(keep, give_part, far_gate)
    residual = own_rows(hidden_in).astype(jnp.float32) + attn_sum
    inv_second = lax.rsqrt(jnp.mean(residual * residual, -1, keepdims=True) + epsilon)
    normed_ffn = (residual * inv_second * ffn_gain).astype(jnp.bfloat16)

    def gates_of(rows, mask):
        logits = jnp.where(mask, mm(rows, router), far_below)
        return jax.nn.softmax(logits, -1)

    gates_own = gates_of(normed_ffn, mask_own)
    far_up = swap(own_mats[1], 2)
    far_mats = [far_gate, far_up, swap(own_mats[2], 2)]
    normed_all = order.gather(normed_ffn, sent, far_up).reshape(group * shard_rows, model_width)
    near_mats = [swap(value, 1) for value in own_mats]
    last_mats = [swap(value, 1) for value in far_mats]
    shards = (own_mats, near_mats, far_mats, last_mats)
    in_mats = [value for shard in shards for value in shard[:2]]
    down_mats = [shard[2] for shard in shards]
    width = local_experts * hidden
    out_part, pre, gated_middles, gates_packed = experts_forward(
        ranks, normed_all, sent, router.T, in_mats, down_mats, local_experts, routes.shape[1]
    )
    out_sum = lax.psum_scatter(
        out_part.reshape(group, shard_rows, model_width), "expert", scatter_dimension=0, tiled=False
    )
    spare_cols = 128 * (-(-2 * experts // 128))
    back_part, pre_grads = experts_backward(
        ranks, sent, gates_packed, pre, in_mats, down_mats, local_experts, spare_cols
    )
    back_sum = order.scatter(back_part.reshape(group, shard_rows, -1), second=out_sum)
    gate_grad_own = (
        back_sum[:, model_width : model_width + experts]
        + back_sum[:, model_width + spare_cols // 2 :][:, :experts]
    )
    back_sum = back_sum[:, :model_width]
    def weight_grads(step):
        cols = slice(step * 2 * width, (step + 1) * 2 * width)
        mids = slice(step * width, (step + 1) * width)
        return mm(pre_grads[:, cols], normed_all, (0, 0)), mm(gated_middles[:, mids], grad_all, (0, 0))

    def give(parts, step):
        return [swap(bf(part), step).astype(jnp.float32) for part in parts]

    far = give(weight_grads(3), 1)
    near = give(weight_grads(1), 1)
    far_part = [bf(a + b) for a, b in zip(weight_grads(2), far)]
    near_part = [a + b for a, b in zip(weight_grads(0), near)]
    far_part = [far_part[0][:width], far_part[0][width:], far_part[1]]
    arrived = give(far_part, 2)
    grad_out = cot_own.astype(jnp.float32)
    grad_chosen = gates_own * (
        gate_grad_own - jnp.sum(gates_own * gate_grad_own, -1, keepdims=True)
    )
    grad_logits = bf(jnp.where(mask_own, grad_chosen, 0.0))
    router_part = mm(normed_ffn, grad_logits, (0, 0))
    grad_normed_ffn = back_sum + mm(grad_logits, router, (1, 1))
    ffn_gain_part = jnp.sum(grad_normed_ffn * residual * inv_second, 0)
    grad_residual = grad_out + norm_back(grad_normed_ffn * ffn_gain, residual, inv_second)
    grad_attn = gather_rows(bf(grad_residual))
    out_blocks = out_grad(grad_attn, attended_rows, group)
    (grad_attn,) = after((grad_attn,), out_blocks)
    w_out_grad = (
        lax.psum_scatter(
            out_blocks, "expert", scatter_dimension=0, tiled=False
        )
        .astype(jnp.float32)
        .T
    )
    slice_rows = model_width // group
    spare = 16
    packed, gain_parts, attn_gain_part, keep, give_part = attend_back(
        ranks, hidden_in, normalized_input, grad_attn, w_query, w_key, value_weight, q_gain, k_gain, cosine,
        sine_table, w_out, qp, kp, q, k, v, prob, shard_rows, group, spare,
    )
    (give_part,) = after((give_part,), arrived[0])
    grad_normed = reduce_rows(keep, give_part)
    layer_out = gather_rows(bf(residual + out_sum.astype(jnp.float32)))
    inputs_own = own_rows(hidden_in).astype(jnp.float32)
    inv_own = lax.rsqrt(jnp.mean(inputs_own * inputs_own, -1, keepdims=True) + epsilon)
    input_grad = gather_rows(
        bf(grad_residual + norm_back(grad_normed * attn_gain, inputs_own, inv_own))
    ).astype(jnp.float32)

    small = jnp.concatenate(
        [
            router_part.reshape(group, -1),
            attn_gain_part.reshape(group, -1),
            ffn_gain_part.reshape(group, -1),
            jnp.broadcast_to(gain_parts[:2].reshape(1, -1), (group, 2 * head_size)),
        ],
        1,
    )
    small = jnp.pad(small, ((0, 0), (0, spare * packed.shape[2] - small.shape[1])))
    packed = lax.dynamic_update_slice(
        packed, bf(small).reshape(group, spare, packed.shape[2]), (0, slice_rows, 0)
    )
    packed = order.scatter(packed, first=arrived[1], second=arrived[2], last=w_out_grad)
    query_width, key_width = w_query.shape[1], w_key.shape[1]
    w_query_grad = packed[:slice_rows, :query_width]
    w_key_grad = packed[:slice_rows, query_width : query_width + key_width]
    w_value_grad = packed[:slice_rows, query_width + key_width :]
    small = packed[slice_rows:]
    small = small + swap(bf(small), 1).astype(jnp.float32)
    small = (small + swap(bf(small), 2).astype(jnp.float32)).reshape(-1)
    cuts = [slice_rows * experts, slice_rows, slice_rows, head_size, head_size]
    router_grad, attn_gain_grad, ffn_gain_grad, q_gain_all, k_gain_all = [
        small[sum(cuts[:i]) : sum(cuts[: i + 1])] for i in range(len(cuts))
    ]
    parts = [near_part[0][:width], near_part[0][width:], near_part[1]]
    gate_t, up_t, w_down_grad = [
        (a + b).reshape(local_experts, hidden, model_width) for a, b in zip(parts, arrived)
    ]
    w_gate_grad, w_up_grad = gate_t.transpose(0, 2, 1), up_t.transpose(0, 2, 1)
    gain_count = head_size // group
    gain_at = expert_rank * gain_count
    return (
        layer_out,
        input_grad,
        attn_gain_grad,
        w_query_grad,
        w_key_grad,
        w_value_grad,
        lax.dynamic_slice_in_dim(q_gain_all, gain_at, gain_count),
        lax.dynamic_slice_in_dim(k_gain_all, gain_at, gain_count),
        w_out_grad,
        ffn_gain_grad,
        router_grad.reshape(slice_rows, experts),
        w_gate_grad,
        w_up_grad,
        w_down_grad,
    )


def solution(mesh):
    placed = (
        P("expert", None),
        P("expert", None),
        P("expert"),
        P("expert"),
        P("expert", None),
        P(),
        P(None, "tensor"),
        P(None, "tensor"),
        P(None, "tensor"),
        P(),
        P(),
        P("tensor", None),
        P(),
        P(),
        P("expert", None, "tensor"),
        P("expert", None, "tensor"),
        P("expert", "tensor", None),
    )
    return jax.shard_map(
        body,
        mesh=mesh,
        in_specs=placed,
        out_specs=(
            P("expert", None),
            P("expert", None),
            P("expert"),
            P("expert", "tensor"),
            P("expert", "tensor"),
            P("expert", "tensor"),
            P("expert"),
            P("expert"),
            P("tensor", "expert"),
            P("expert"),
            P("expert", None),
            P("expert", None, "tensor"),
            P("expert", None, "tensor"),
            P("expert", "tensor", None),
        ),
        check_vma=False,
    )
```

time: 771 us -> 583 us (0.76)
  matrix products: 174 us -> 39.4 us
  Pallas kernels: 0 us -> 119 us
  local copies, waits for them, and re-layouts: 91.7 us -> 35.2 us
  other arithmetic: 85.7 us -> 29.3 us
  between operations: 46.5 us -> 15 us
  blocking collectives: 31.4 us -> 0 us
  waiting for transfers between devices: 268 us -> 281 us
    pallas_call x0 -> x5, Pallas kernels: none -> 119 us  [the longest x1 36.1 us: experts_backward(): pl.pallas_call(functools.partial(backward_kernel, shards=shards, local=lo...]
    ppermute x23 -> x21, waiting for transfers between devices: 52.3 us -> 166 us  [the longest x9 86.2 us: along(): return lax.ppermute(value, 'expert', [(i, i ^ 2 * step) for i in range(8)])]
    dot_general x34 -> x11, matrix products: 146 us -> 39.4 us  [mm(): lax.dot_general(left, right, (((contract[0],), (contract[1],)), ((), ()))...]
    reduce_scatter x2 -> x1, waiting for transfers between devices: 52.3 us -> 0.02 us  [body(): lax.psum_scatter(out_part.reshape(group, shard_rows, model_width), 'exper...]
    ppermute x24 -> x28, waiting for transfers between devices: 163 us -> 115 us  [swap(): return lax.ppermute(value, 'tensor', [(i, i ^ step) for i in range(size)])]
    all_gather x1 -> x0, blocking collectives: 31.4 us -> none  [body(): routes_all = lax.all_gather(routes_own, 'expert', axis=0, tiled=False)]
    unnamed x262 -> x61, local copies, waits for them, and re-layouts: 37.3 us -> 7.86 us
    dot_general x10 -> x0, matrix products: 28 us -> none  [the longest x1 6.09 us: body(): jnp.dot(attended_rows, w_out, preferred_element_type=jnp.float32)]
  transfers between devices with their start and end apart: 52 -> 52, of which waited for: 15 -> 25; matrix products, arithmetic and copies ran while one was open for 33% -> 16% of each run, Pallas kernels for 0% -> 17%
where the time goes in v2:
time: 583 us; the launch traced here: 574 us
  waiting for transfers between devices  281 us (48%)
  Pallas kernels  119 us (20%)
  starting transfers between devices  55.2 us (9%)
  matrix products  39.4 us (7%)
  local copies, waits for them, and re-layouts  35.2 us (6%)
  other arithmetic  29.3 us (5%)
  between operations  15 us (3%)
    ppermute x28, waiting for transfers between devices, swap(): return lax.ppermute(value, 'tensor', [(i, i ^ step) for i in range(size)])  115 us
    ppermute x9, waiting for transfers between devices, along(): return lax.ppermute(value, 'expert', [(i, i ^ 2 * step) for i in range(8)])  86.2 us
    ppermute x12, waiting for transfers between devices, across(): return lax.ppermute(value, 'expert', [(i, i ^ 1) for i in range(8)])  79.5 us
    dot_general x11, matrix products, mm(): lax.dot_general(left, right, (((contract[0],), (contract[1],)), ((), ()))...  39.4 us
    pallas_call x1, Pallas kernels, experts_backward(): pl.pallas_call(functools.partial(backward_kernel, shards=shards, local=lo...  36.1 us
    pallas_call x1, Pallas kernels, attend_back(): pl.pallas_call(attend_back_kernel, grid_spec=pltpu.PrefetchScalarGridSpec...  28.9 us
    ppermute x9, starting transfers between devices, along(): return lax.ppermute(value, 'expert', [(i, i ^ 2 * step) for i in range(8)])  26.9 us
    pallas_call x1, Pallas kernels, experts_forward(): pl.pallas_call(functools.partial(forward_kernel, shards=shards, local=loc...  24.4 us
  transfers between devices with their start and end apart: 52, of which 25 were waited for; matrix products, arithmetic and copies ran while one was open for 16% of the time, Pallas kernels for 17%

profile of v2, /device:TPU:0, one launch (start us, length us, event | category | flops | bytes accessed | tf_op | source)
XLA Modules:
  0.0 574.3 jit_solution(10463534248431834323)
XLA Ops:
  10.0 3.0 collective-permute-start.1
  17.3 21.7 %attend.1 = (bf16[384,2048]{1,0:T(8,128)(2,1)}, f32[384,1024]{1,0:T(8,128)}, f32[384,128]{1,0:T(8,128)}, bf16[384,1024]{1,0:T(8,128)(2,1)}, bf16[384,128]{1,0:T(...) custom-call(s32[2]{0:T(128)} %pad_add_fusion.rank_ref, ...), custom_call_target="tpu_custom_call" | custom-call | flops 1048576 | bytes 65536 | tf_op jit(solution)/shard_map/attend/pallas_call | solution.py:138
  39.1 2.5 collective-permute-done
  42.4 2.0 convert_add_fusion.2
  45.2 2.4 collective-permute-done.1.rest_4_
  47.6 1.7 collective-permute-start.2
  49.6 10.2 %collective-permute-done.2 = bf16[96,2048]{1,0:T(8,128)(2,1)S(1)} collective-permute-done((bf16[96,2048]{1,0:T(8,128)(2,1)}, bf16[96,2048]{1,0:T(8,128)(2,1)S(1)}, u32[]{:S(2)}, u32[]{:S(2)}) %collective-permute-start.2) | collective-permute-done | bytes 393248 | tf_op jit(solution)/shard_map/ppermute | solution.py:49
  62.2 2.9 collective-permute-start.6
  66.5 1.5 collective-permute-start.3
  68.0 24.0 %collective-permute-done.8.rest_5_ = bf16[384,2048]{1,0:T(8,128)(2,1)} collective-permute-done((bf16[384,2048]{1,0:T(8,128)(2,1)}, bf16[384,2048]{1,0:T(8,128)(2,1)}, u32[]{:S(2)}, u32[]{:S(2)}) %collective-permute-start.8) | collective-permute-done | bytes 1572896 | tf_op jit(solution)/shard_map/ppermute | solution.py:49
  92.0 1.4 collective-permute-start.16
  93.4 6.4 %collective-permute-done.6 = bf16[96,2048]{1,0:T(8,128)(2,1)} collective-permute-done((bf16[96,2048]{1,0:T(8,128)(2,1)S(1)}, bf16[96,2048]{1,0:T(8,128)(2,1)}, u32[]{:S(2)}, u32[]{:S(2)}) %collective-permute-start.6) | collective-permute-done | bytes 393248 | tf_op jit(solution)/shard_map/ppermute | solution.py:596
  99.9 8.4 %collective-permute-start.4 = (bf16[96,2048]{1,0:T(8,128)(2,1)S(1)}, bf16[96,2048]{1,0:T(8,128)(2,1)}, u32[]{:S(2)}, u32[]{:S(2)}) collective-permute-start(bf16[96,2048]{1,0:T(8,128)(2,1)S(1)} %get-tuple-element.131), channel_id=1, source_target_pairs={{0,8},{4,12},{8,0},{12,4},{16,24},{20,28},{24,16},{28,20},{1,9},{5... | collective-permute-start | bytes 1179656 | tf_op jit(solution)/shard_map/ppermute | solution.py:596
  110.4 6.8 %collective-permute-done.4 = bf16[96,2048]{1,0:T(8,128)(2,1)} collective-permute-done((bf16[96,2048]{1,0:T(8,128)(2,1)S(1)}, bf16[96,2048]{1,0:T(8,128)(2,1)}, u32[]{:S(2)}, u32[]{:S(2)}) %collective-permute-start.4) | collective-permute-done | bytes 393248 | tf_op jit(solution)/shard_map/ppermute | solution.py:596
  119.2 8.1 %collective-permute-done.5 = bf16[96,2048]{1,0:T(8,128)(2,1)S(1)} collective-permute-done((bf16[96,2048]{1,0:T(8,128)(2,1)}, bf16[96,2048]{1,0:T(8,128)(2,1)S(1)}, u32[]{:S(2)}, u32[]{:S(2)}) %collective-permute-start.5) | collective-permute-done | bytes 393248 | tf_op jit(solution)/shard_map/ppermute | solution.py:593
  128.9 7.8 %collective-permute-done.10 = bf16[96,2048]{1,0:T(8,128)(2,1)S(1)} collective-permute-done((bf16[96,2048]{1,0:T(8,128)(2,1)}, bf16[96,2048]{1,0:T(8,128)(2,1)S(1)}, u32[]{:S(2)}, u32[]{:S(2)}) %collective-permute-start.10) | collective-permute-done | bytes 393248 | tf_op jit(solution)/shard_map/ppermute | solution.py:593
  142.0 24.4 %experts_forward.1 = (bf16[768,2048]{1,0:T(8,128)(2,1)}, f32[768,3072]{1,0:T(8,128)}, bf16[768,1536]{1,0:T(8,128)(2,1)}, f32[768,128]{1,0:T(8,128)}) custom-call(s32[2]{0:T(128)} %pad_add_fusion.rank_ref, bf16[768,2048]{1,0:T(8,128)(2,1)} %bitcast.146, bf16[768,2176]{1,0:T(8,128)(2,1)} %all-gather.2.cloned.1.call-done.routes.g, bf16[16,2048]{1,0:T(8,128)(2,1)} %bitcast.175, ...), custom_call_target="tpu_custom_call" | custom-call | flops 1048576 | bytes 65536 | tf_op jit(solution)/shard_map/experts_forward/pallas_call | solution.py:518
  167.8 36.1 %experts_backward.1 = (bf16[768,2176]{1,0:T(8,128)(2,1)}, bf16[768,3072]{1,0:T(8,128)(2,1)}) custom-call(s32[2]{0:T(128)} %pad_add_fusion.rank_ref, bf16[768,2176]{1,0:T(8,128)(2,1)} %all-gather.2.cloned.1.call-done.routes.g, f32[768,128]{1,0:T(8,128)} %get-tuple-element.56.gates, f32[768,3072]{1,0:T(8,128)} %get-tuple-element.57.pre_in, ...), custom_call_target="tpu_custom_call" | custom-call | flops 1048576 | bytes 65536 | tf_op jit(solution)/shard_map/experts_backward/pallas_call | solution.py:545
  203.9 1.7 dynamic-slice_bitcast_fusion.7
  206.0 1.6 collective-permute-start.25
  208.0 1.6 collective-permute-start.20
  209.7 5.3 convolution_convert_fusion.1
  215.0 5.6 convolution_convert_fusion
  220.6 1.7 collective-permute-done.21
  222.3 9.0 %collective-permute-done.25 = bf16[96,2176]{1,0:T(8,128)(2,1)S(1)} collective-permute-done((bf16[96,2176]{1,0:T(8,128)(2,1)S(1)}, bf16[96,2176]{1,0:T(8,128)(2,1)S(1)}, u32[]{:S(2)}, u32[]{:S(2)}) %collective-permute-start.25) | collective-permute-done | bytes 417824 | tf_op jit(solution)/shard_map/ppermute | solution.py:593
  231.2 13.2 %collective-permute-done.23 = bf16[96,2176]{1,0:T(8,128)(2,1)S(1)} collective-permute-done((bf16[96,2176]{1,0:T(8,128)(2,1)S(1)}, bf16[96,2176]{1,0:T(8,128)(2,1)S(1)}, u32[]{:S(2)}, u32[]{:S(2)}) %collective-permute-start.23) | collective-permute-done | bytes 417824 | tf_op jit(solution)/shard_map/ppermute | solution.py:593
  245.7 1.7 collective-permute-start.24
  247.4 1.8 collective-permute-start.22
  249.2 2.6 convolution_convert_fusion.2
  251.8 2.6 convolution_convert_fusion.3
  254.4 11.1 %collective-permute-done.26 = bf16[96,2176]{1,0:T(8,128)(2,1)S(1)} collective-permute-done((bf16[96,2176]{1,0:T(8,128)(2,1)S(1)}, bf16[96,2176]{1,0:T(8,128)(2,1)S(1)}, u32[]{:S(2)}, u32[]{:S(2)}) %collective-permute-start.26) | collective-permute-done | bytes 417824 | tf_op jit(solution)/shard_map/ppermute | solution.py:596
  265.5 11.6 %collective-permute-done.24 = bf16[96,2176]{1,0:T(8,128)(2,1)S(1)} collective-permute-done((bf16[96,2176]{1,0:T(8,128)(2,1)S(1)}, bf16[96,2176]{1,0:T(8,128)(2,1)S(1)}, u32[]{:S(2)}, u32[]{:S(2)}) %collective-permute-start.24) | collective-permute-done | bytes 417824 | tf_op jit(solution)/shard_map/ppermute | solution.py:596
  279.1 3.2 fusion.40
  283.2 4.3 add_convert_fusion.1
  288.6 5.7 collective-permute-done.27
  294.5 5.8 %add_convert_fusion = bf16[768,2048]{1,0:T(8,128)(2,1)} fusion(bf16[768,2048]{1,0:T(8,128)(2,1)} %collective-permute-done.29, bf16[768,2048]{1,0:T(8,128)(2,1)S(1)} %bitcast.149, bf16[768,3072]{1,0:T(8,128)(2,1)} %get-tuple-element.71), kind=kOutput, calls=%fused_computation.1 | convolution fusion | flops 2420637696 | bytes 10616832 | tf_op jit(solution)/shard_map/dot_general | solution.py:36
  301.9 8.1 %out_grad.1 = bf16[8,256,1024]{2,1,0:T(8,128)(2,1)} custom-call(bf16[384,2048]{1,0:T(8,128)(2,1)} %bitcast.144, bf16[384,1024]{1,0:T(8,128)(2,1)} %get-tuple-element.61.o), custom_call_target="tpu_custom_call" | custom-call | flops 1048576 | bytes 65536 | tf_op jit(solution)/shard_map/out_grad/pallas_call | solution.py:573
  310.1 4.0 fusion.41
  318.4 1.8 reshape.336
  320.2 7.9 %collective-permute-done.43 = bf16[384,2048]{1,0:T(8,128)(2,1)} collective-permute-done((bf16[384,2048]{1,0:T(8,128)(2,1)}, bf16[384,2048]{1,0:T(8,128)(2,1)}, u32[]{:S(2)}, u32[]{:S(2)}) %collective-permute-start.43) | collective-permute-done | bytes 1572896 | tf_op jit(solution)/shard_map/ppermute | solution.py:49
  328.1 5.3 add_add_fusion
  333.4 5.1 convert_add_fusion
  339.5 22.3 %collective-permute-done.39 = bf16[384,2048]{1,0:T(8,128)(2,1)} collective-permute-done((bf16[384,2048]{1,0:T(8,128)(2,1)}, bf16[384,2048]{1,0:T(8,128)(2,1)}, u32[]{:S(2)}, u32[]{:S(2)}) %collective-permute-start.39) | collective-permute-done | bytes 1572896 | tf_op jit(solution)/shard_map/ppermute | solution.py:49
  361.8 33.7 %collective-permute-done.30 = bf16[384,2048]{1,0:T(8,128)(2,1)} collective-permute-done((bf16[384,2048]{1,0:T(8,128)(2,1)}, bf16[384,2048]{1,0:T(8,128)(2,1)}, u32[]{:S(2)}, u32[]{:S(2)}) %collective-permute-start.30) | collective-permute-done | bytes 1572896 | tf_op jit(solution)/shard_map/ppermute | solution.py:49
  395.5 5.6 slice_add_fusion
  401.1 2.3 collective-permute-done.18
  403.8 28.9 %attend_back.1 = (bf16[8,272,1280]{2,1,0:T(8,128)(2,1)}, f32[8,128]{1,0:T(8,128)}, f32[1,2048]{1,0:T(1,128)}, f32[2,96,2048]{2,1,0:T(8,128)}, bf16[2,96,2048]{2,1,0:T(8,128)(2,1)}) custom-call(s32[2]{0:T(128)} %pad_add_fusion.rank_ref, bf16[384,2048]{1,0:T(8,128)(2,1)} %x.5, bf16[384,2048]{1,0:T(8,128)(2,1)} %get-tuple-element.60.xn, ...), custom_call_target="tpu_custom_call" | custom-call | flops 1048576 | bytes 65536 | tf_op jit(solution)/shard_map/attend_back/pallas_call | solution.py:292
  435.5 1.6 convert_add_fusion.1
  439.1 1.6 copy-done.13
  440.9 1.8 collective-permute-start.41
  443.0 1.7 collective-permute-start.36
  445.0 3.5 collective-permute-done.32
  449.5 9.9 %collective-permute-done.41 = bf16[272,1280]{1,0:T(8,128)(2,1)S(1)} collective-permute-done((bf16[272,1280]{1,0:T(8,128)(2,1)S(1)}, bf16[272,1280]{1,0:T(8,128)(2,1)S(1)}, u32[]{:S(2)}, u32[]{:S(2)}) %collective-permute-start.41) | collective-permute-done | bytes 696352 | tf_op jit(solution)/shard_map/ppermute | solution.py:593
  459.5 14.9 %collective-permute-done.38 = bf16[272,1280]{1,0:T(8,128)(2,1)S(1)} collective-permute-done((bf16[272,1280]{1,0:T(8,128)(2,1)S(1)}, bf16[272,1280]{1,0:T(8,128)(2,1)S(1)}, u32[]{:S(2)}, u32[]{:S(2)}) %collective-permute-start.38) | collective-permute-done | bytes 696352 | tf_op jit(solution)/shard_map/ppermute | solution.py:593
  474.4 14.9 %collective-permute-done.36 = bf16[272,1280]{1,0:T(8,128)(2,1)S(1)} collective-permute-done((bf16[272,1280]{1,0:T(8,128)(2,1)S(1)}, bf16[272,1280]{1,0:T(8,128)(2,1)S(1)}, u32[]{:S(2)}, u32[]{:S(2)}) %collective-permute-start.36) | collective-permute-done | bytes 696352 | tf_op jit(solution)/shard_map/ppermute | solution.py:593
  489.3 1.7 fusion.5
  491.0 3.4 collective-permute-start.37
  494.4 6.3 %collective-permute-start.40 = (bf16[272,1280]{1,0:T(8,128)(2,1)}, bf16[272,1280]{1,0:T(8,128)(2,1)}, u32[]{:S(2)}, u32[]{:S(2)}) collective-permute-start(bf16[272,1280]{1,0:T(8,128)(2,1)} %get-tuple-element.76), channel_id=1, source_target_pairs={{0,16},{4,20},{8,24},{12,28},{16,0},{20,4},{24,8},{28,12},{1,17},{... | collective-permute-start | bytes 2088968 | tf_op jit(solution)/shard_map/ppermute | solution.py:596
  503.1 8.6 %collective-permute-done.37 = bf16[272,1280]{1,0:T(8,128)(2,1)S(1)} collective-permute-done((bf16[272,1280]{1,0:T(8,128)(2,1)}, bf16[272,1280]{1,0:T(8,128)(2,1)S(1)}, u32[]{:S(2)}, u32[]{:S(2)}) %collective-permute-start.37) | collective-permute-done | bytes 696352 | tf_op jit(solution)/shard_map/ppermute | solution.py:596
  511.7 41.7 %collective-permute-done.40 = bf16[272,1280]{1,0:T(8,128)(2,1)} collective-permute-done((bf16[272,1280]{1,0:T(8,128)(2,1)}, bf16[272,1280]{1,0:T(8,128)(2,1)}, u32[]{:S(2)}, u32[]{:S(2)}) %collective-permute-start.40) | collective-permute-done | bytes 696352 | tf_op jit(solution)/shard_map/ppermute | solution.py:596
  553.4 2.4 fusion.8
  555.9 1.8 fusion.4
  557.7 1.9 copy.59
  559.6 1.8 collective-permute-start.46
  (201 shorter events, 53.3 us)
Async XLA Ops:
  7.2 110.0 %all-gather.2.cloned.1.call-start = ((), (), s32[]{:S(2)}) async-start(), calls=%async_computation.2 | async-start | bytes 3760128 | tf_op jit(solution)/shard_map/all_gather | solution.py:674
  9.9 269.2 %reduce-scatter.3.cloned.1.call-start = ((), (), s32[]{:S(2)}) async-start(), calls=%async_computation.3 | async-start | bytes 3538944 | tf_op jit(solution)/shard_map/reduce_scatter | solution.py:732
  10.0 37.6 %collective-permute-start.1 = (bf16[384,2048]{1,0:T(8,128)(2,1)}, bf16[384,2048]{1,0:T(8,128)(2,1)S(1)}, u32[]{:S(2)}, u32[]{:S(2)}) collective-permute-start(bf16[384,2048]{1,0:T(8,128)(2,1)} %bitcast.8.rest_0_), channel_id=1, source_target_pairs={{0,2},{1,3},{2,0},{3,1},{4,6},{5,7},{6,4},{7,5},{8,10},{9,11},{10,... | collective-permute-start | bytes 4718600 | tf_op jit(solution)/shard_map/ppermute | solution.py:49
  39.0 2.6 collective-permute-start
  44.4 17.7 %copy-start.23 = (f32[2048]{0:T(1024)S(1)}, f32[2048]{0:T(1024)}, u32[]{:S(2)}) copy-start(f32[2048]{0:T(1024)} %param.29) | copy-start | bytes 24580
  47.6 13.6 %copy-start.11 = (bf16[384,2048]{1,0:T(8,128)(2,1)}, bf16[384,2048]{1,0:T(8,128)(2,1)S(1)}, u32[]{:S(2)}) copy-start(bf16[384,2048]{1,0:T(8,128)(2,1)S(1)} %collective-permute-done.1.rest_4_) | copy-start | bytes 4718596
  47.6 12.3 %collective-permute-start.2 = (bf16[96,2048]{1,0:T(8,128)(2,1)}, bf16[96,2048]{1,0:T(8,128)(2,1)S(1)}, u32[]{:S(2)}, u32[]{:S(2)}) collective-permute-start(bf16[96,2048]{1,0:T(8,128)(2,1)} %fusion.33), channel_id=1, source_target_pairs={{0,2},{1,3},{2,0},{3,1},{4,6},{5,7},{6,4},{7,5},{8,10},{9,11},{10,... | collective-permute-start | bytes 1179656 | tf_op jit(solution)/shard_map/ppermute | solution.py:49
  49.3 42.7 %collective-permute-start.8 = (bf16[384,2048]{1,0:T(8,128)(2,1)}, bf16[384,2048]{1,0:T(8,128)(2,1)}, u32[]{:S(2)}, u32[]{:S(2)}) collective-permute-start(bf16[384,2048]{1,0:T(8,128)(2,1)} %bitcast.14.rest_1_), channel_id=1, source_target_pairs={{0,2},{1,3},{2,0},{3,1},{4,6},{5,7},{6,4},{7,5},{8,10},{9,11},{10,... | collective-permute-start | bytes 4718600 | tf_op jit(solution)/shard_map/ppermute | solution.py:49
  61.2 58.1 %copy-start.27 = (f32[96]{0:T(128)}, f32[96]{0:T(128)S(1)}, u32[]{:S(2)}) copy-start(f32[96]{0:T(128)S(1)} %add_rsqrt_fusion.1) | copy-start | bytes 1156
  62.2 104.6 %copy-start.14 = (bf16[96,2048]{1,0:T(8,128)(2,1)}, bf16[96,2048]{1,0:T(8,128)(2,1)S(1)}, u32[]{:S(2)}) copy-start(bf16[96,2048]{1,0:T(8,128)(2,1)S(1)} %get-tuple-element.131) | copy-start | bytes 1179652
  62.2 37.6 %collective-permute-start.6 = (bf16[96,2048]{1,0:T(8,128)(2,1)S(1)}, bf16[96,2048]{1,0:T(8,128)(2,1)}, u32[]{:S(2)}, u32[]{:S(2)}) collective-permute-start(bf16[96,2048]{1,0:T(8,128)(2,1)S(1)} %get-tuple-element.131), channel_id=1, source_target_pairs={{0,16},{4,20},{8,24},{12,28},{16,0},{20,4},{24,8},{28,12},{1,17},{... | collective-permute-start | bytes 1179656 | tf_op jit(solution)/shard_map/ppermute | solution.py:596
  65.1 34.7 %collective-permute-start.7 = (bf16[96,2048]{1,0:T(8,128)(2,1)S(1)}, bf16[96,2048]{1,0:T(8,128)(2,1)}, u32[]{:S(2)}, u32[]{:S(2)}) collective-permute-start(bf16[96,2048]{1,0:T(8,128)(2,1)S(1)} %get-tuple-element.131), channel_id=1, source_target_pairs={{0,24},{4,28},{8,16},{12,20},{16,8},{20,12},{24,0},{28,4},{1,25},{... | collective-permute-start | bytes 1179656 | tf_op jit(solution)/shard_map/ppermute | solution.py:596
  66.5 41.8 %collective-permute-start.3 = (bf16[96,2048]{1,0:T(8,128)(2,1)S(1)}, bf16[96,2048]{1,0:T(8,128)(2,1)}, u32[]{:S(2)}, u32[]{:S(2)}) collective-permute-start(bf16[96,2048]{1,0:T(8,128)(2,1)S(1)} %get-tuple-element.131), channel_id=1, source_target_pairs={{0,4},{4,0},{8,12},{12,8},{16,20},{20,16},{24,28},{28,24},{1,5},{5... | collective-permute-start | bytes 1179656 | tf_op jit(solution)/shard_map/ppermute | solution.py:593
  68.0 60.2 %collective-permute-start.11 = (bf16[384,2048]{1,0:T(8,128)(2,1)}, bf16[384,2048]{1,0:T(8,128)(2,1)}, u32[]{:S(2)}, u32[]{:S(2)}) collective-permute-start(bf16[384,2048]{1,0:T(8,128)(2,1)} %bitcast.8.rest_0_), channel_id=1, source_target_pairs={{0,1},{1,0},{2,3},{3,2},{4,5},{5,4},{6,7},{7,6},{8,9},{9,8},{10,11... | collective-permute-start | bytes 4718600 | tf_op jit(solution)/shard_map/ppermute | solution.py:49
  92.0 36.3 %collective-permute-start.16 = (bf16[384,2048]{1,0:T(8,128)(2,1)}, bf16[384,2048]{1,0:T(8,128)(2,1)}, u32[]{:S(2)}, u32[]{:S(2)}) collective-permute-start(bf16[384,2048]{1,0:T(8,128)(2,1)} %bitcast.23.rest_8_), channel_id=1, source_target_pairs={{0,2},{1,3},{2,0},{3,1},{4,6},{5,7},{6,4},{7,5},{8,10},{9,11},{10,... | collective-permute-start | bytes 4718600 | tf_op jit(solution)/shard_map/ppermute | solution.py:49
  99.8 40.0 %collective-permute-start.12 = (bf16[384,2048]{1,0:T(8,128)(2,1)}, bf16[384,2048]{1,0:T(8,128)(2,1)}, u32[]{:S(2)}, u32[]{:S(2)}) collective-permute-start(bf16[384,2048]{1,0:T(8,128)(2,1)} %bitcast.14.rest_1_), channel_id=1, source_target_pairs={{0,1},{1,0},{2,3},{3,2},{4,5},{5,4},{6,7},{7,6},{8,9},{9,8},{10,11... | collective-permute-start | bytes 4718600 | tf_op jit(solution)/shard_map/ppermute | solution.py:49
  99.9 17.3 %collective-permute-start.4 = (bf16[96,2048]{1,0:T(8,128)(2,1)S(1)}, bf16[96,2048]{1,0:T(8,128)(2,1)}, u32[]{:S(2)}, u32[]{:S(2)}) collective-permute-start(bf16[96,2048]{1,0:T(8,128)(2,1)S(1)} %get-tuple-element.131), channel_id=1, source_target_pairs={{0,8},{4,12},{8,0},{12,4},{16,24},{20,28},{24,16},{28,20},{1,9},{5... | collective-permute-start | bytes 1179656 | tf_op jit(solution)/shard_map/ppermute | solution.py:596
  108.3 20.5 %collective-permute-start.9 = (bf16[96,2048]{1,0:T(8,128)(2,1)}, bf16[96,2048]{1,0:T(8,128)(2,1)}, u32[]{:S(2)}, u32[]{:S(2)}) collective-permute-start(bf16[96,2048]{1,0:T(8,128)(2,1)} %collective-permute-done.6), channel_id=1, source_target_pairs={{0,4},{4,0},{8,12},{12,8},{16,20},{20,16},{24,28},{28,24},{1,5},{5... | collective-permute-start | bytes 1179656 | tf_op jit(solution)/shard_map/ppermute | solution.py:593
  117.2 10.2 %collective-permute-start.5 = (bf16[96,2048]{1,0:T(8,128)(2,1)}, bf16[96,2048]{1,0:T(8,128)(2,1)S(1)}, u32[]{:S(2)}, u32[]{:S(2)}) collective-permute-start(bf16[96,2048]{1,0:T(8,128)(2,1)} %collective-permute-done.4), channel_id=1, source_target_pairs={{0,4},{4,0},{8,12},{12,8},{16,20},{20,16},{24,28},{28,24},{1,5},{5... | collective-permute-start | bytes 1179656 | tf_op jit(solution)/shard_map/ppermute | solution.py:593
  127.3 9.3 %collective-permute-start.10 = (bf16[96,2048]{1,0:T(8,128)(2,1)}, bf16[96,2048]{1,0:T(8,128)(2,1)S(1)}, u32[]{:S(2)}, u32[]{:S(2)}) collective-permute-start(bf16[96,2048]{1,0:T(8,128)(2,1)} %collective-permute-done.7), channel_id=1, source_target_pairs={{0,4},{4,0},{8,12},{12,8},{16,20},{20,16},{24,28},{28,24},{1,5},{5... | collective-permute-start | bytes 1179656 | tf_op jit(solution)/shard_map/ppermute | solution.py:593
  128.2 11.7 %collective-permute-start.15 = (bf16[384,2048]{1,0:T(8,128)(2,1)}, bf16[384,2048]{1,0:T(8,128)(2,1)S(1)}, u32[]{:S(2)}, u32[]{:S(2)}) collective-permute-start(bf16[384,2048]{1,0:T(8,128)(2,1)} %bitcast.23.rest_8_), channel_id=1, source_target_pairs={{0,1},{1,0},{2,3},{3,2},{4,5},{5,4},{6,7},{7,6},{8,9},{9,8},{10,11... | collective-permute-start | bytes 4718600 | tf_op jit(solution)/shard_map/ppermute | solution.py:49
  128.3 11.6 %collective-permute-start.13 = (bf16[384,2048]{1,0:T(8,128)(2,1)}, bf16[384,2048]{1,0:T(8,128)(2,1)}, u32[]{:S(2)}, u32[]{:S(2)}) collective-permute-start(bf16[384,2048]{1,0:T(8,128)(2,1)} %copy-done.11), channel_id=1, source_target_pairs={{0,1},{1,0},{2,3},{3,2},{4,5},{5,4},{6,7},{7,6},{8,9},{9,8},{10,11... | collective-permute-start | bytes 4718600 | tf_op jit(solution)/shard_map/ppermute | solution.py:49
  128.8 11.1 %collective-permute-start.14 = (bf16[384,2048]{1,0:T(8,128)(2,1)}, bf16[384,2048]{1,0:T(8,128)(2,1)}, u32[]{:S(2)}, u32[]{:S(2)}) collective-permute-start(bf16[384,2048]{1,0:T(8,128)(2,1)} %collective-permute-done.8.rest_5_), channel_id=1, source_target_pairs={{0,1},{1,0},{2,3},{3,2},{4,5},{5,4},{6,7},{7,6},{8,9},{9,8},{10,11... | collective-permute-start | bytes 4718600 | tf_op jit(solution)/shard_map/ppermute | solution.py:49
  136.7 3.8 collective-permute-start.17
  166.5 335.5 %reduce-scatter.5.cloned.1.call-start = ((), (), s32[]{:S(2)}) async-start(), calls=%async_computation.4 | async-start | bytes 4718592 | tf_op jit(solution)/shard_map/reduce_scatter | solution.py:772
  205.6 16.7 %collective-permute-start.21 = (bf16[96,2176]{1,0:T(8,128)(2,1)S(1)}, bf16[96,2176]{1,0:T(8,128)(2,1)S(1)}, u32[]{:S(2)}, u32[]{:S(2)}) collective-permute-start(bf16[96,2176]{1,0:T(8,128)(2,1)S(1)} %get-tuple-element.146), channel_id=1, source_target_pairs={{0,4},{4,0},{8,12},{12,8},{16,20},{20,16},{24,28},{28,24},{1,5},{5... | collective-permute-start | bytes 1253384 | tf_op jit(solution)/shard_map/ppermute | solution.py:593
  206.0 25.2 %collective-permute-start.25 = (bf16[96,2176]{1,0:T(8,128)(2,1)S(1)}, bf16[96,2176]{1,0:T(8,128)(2,1)S(1)}, u32[]{:S(2)}, u32[]{:S(2)}) collective-permute-start(bf16[96,2176]{1,0:T(8,128)(2,1)S(1)} %get-tuple-element.144), channel_id=1, source_target_pairs={{0,4},{4,0},{8,12},{12,8},{16,20},{20,16},{24,28},{28,24},{1,5},{5... | collective-permute-start | bytes 1253384 | tf_op jit(solution)/shard_map/ppermute | solution.py:593
  207.7 36.8 %collective-permute-start.23 = (bf16[96,2176]{1,0:T(8,128)(2,1)S(1)}, bf16[96,2176]{1,0:T(8,128)(2,1)S(1)}, u32[]{:S(2)}, u32[]{:S(2)}) collective-permute-start(bf16[96,2176]{1,0:T(8,128)(2,1)S(1)} %get-tuple-element.145), channel_id=1, source_target_pairs={{0,4},{4,0},{8,12},{12,8},{16,20},{20,16},{24,28},{28,24},{1,5},{5... | collective-permute-start | bytes 1253384 | tf_op jit(solution)/shard_map/ppermute | solution.py:593
  208.0 46.4 %collective-permute-start.20 = (bf16[96,2176]{1,0:T(8,128)(2,1)S(1)}, bf16[96,2176]{1,0:T(8,128)(2,1)S(1)}, u32[]{:S(2)}, u32[]{:S(2)}) collective-permute-start(bf16[96,2176]{1,0:T(8,128)(2,1)S(1)} %get-tuple-element.143), channel_id=1, source_target_pairs={{0,4},{4,0},{8,12},{12,8},{16,20},{20,16},{24,28},{28,24},{1,5},{5... | collective-permute-start | bytes 1253384 | tf_op jit(solution)/shard_map/ppermute | solution.py:593
  215.0 29.4 %copy-start.16 = (bf16[768,2176]{1,0:T(8,128)(2,1)S(1)}, bf16[768,2176]{1,0:T(8,128)(2,1)}, u32[]{:S(2)}) copy-start(bf16[768,2176]{1,0:T(8,128)(2,1)} %get-tuple-element.58) | copy-start | bytes 10027012
  215.0 79.5 %collective-permute-start.29 = (bf16[768,2048]{1,0:T(8,128)(2,1)}, bf16[768,2048]{1,0:T(8,128)(2,1)}, u32[]{:S(2)}, u32[]{:S(2)}) collective-permute-start(bf16[768,2048]{1,0:T(8,128)(2,1)} %convolution_convert_fusion.1), channel_id=1, source_target_pairs={{0,1},{1,0},{2,3},{3,2},{4,5},{5,4},{6,7},{7,6},{8,9},{9,8},{10,11... | collective-permute-start | bytes 9437192 | tf_op jit(solution)/shard_map/ppermute | solution.py:49
  215.0 34.2 %copy-start.22 = (bf16[768,1536]{1,0:T(8,128)(2,1)S(1)}, bf16[768,1536]{1,0:T(8,128)(2,1)}, u32[]{:S(2)}) copy-start(bf16[768,1536]{1,0:T(8,128)(2,1)} %get-tuple-element.77) | copy-start | bytes 7077892
  220.6 28.6 %copy-start.2 = (bf16[768,2176]{1,0:T(8,128)(2,1)S(1)}, bf16[768,2176]{1,0:T(8,128)(2,1)}, u32[]{:S(2)}) copy-start(bf16[768,2176]{1,0:T(8,128)(2,1)} %all-gather.2.cloned.1.call-done.routes.g) | copy-start | bytes 10027012
  244.7 20.8 %collective-permute-start.26 = (bf16[96,2176]{1,0:T(8,128)(2,1)S(1)}, bf16[96,2176]{1,0:T(8,128)(2,1)S(1)}, u32[]{:S(2)}, u32[]{:S(2)}) collective-permute-start(bf16[96,2176]{1,0:T(8,128)(2,1)S(1)} %get-tuple-element.59), channel_id=1, source_target_pairs={{0,8},{4,12},{8,0},{12,4},{16,24},{20,28},{24,16},{28,20},{1,9},{5... | collective-permute-start | bytes 1253384 | tf_op jit(solution)/shard_map/ppermute | solution.py:596
  245.7 31.4 %collective-permute-start.24 = (bf16[96,2176]{1,0:T(8,128)(2,1)S(1)}, bf16[96,2176]{1,0:T(8,128)(2,1)S(1)}, u32[]{:S(2)}, u32[]{:S(2)}) collective-permute-start(bf16[96,2176]{1,0:T(8,128)(2,1)S(1)} %get-tuple-element.149), channel_id=1, source_target_pairs={{0,16},{4,20},{8,24},{12,28},{16,0},{20,4},{24,8},{28,12},{1,17},{... | collective-permute-start | bytes 1253384 | tf_op jit(solution)/shard_map/ppermute | solution.py:596
  247.4 29.7 %collective-permute-start.22 = (bf16[96,2176]{1,0:T(8,128)(2,1)S(1)}, bf16[96,2176]{1,0:T(8,128)(2,1)S(1)}, u32[]{:S(2)}, u32[]{:S(2)}) collective-permute-start(bf16[96,2176]{1,0:T(8,128)(2,1)S(1)} %get-tuple-element.147), channel_id=1, source_target_pairs={{0,24},{4,28},{8,16},{12,20},{16,8},{20,12},{24,0},{28,4},{1,25},{... | collective-permute-start | bytes 1253384 | tf_op jit(solution)/shard_map/ppermute | solution.py:596
  251.8 26.0 %copy-start.4 = (f32[96,2048]{1,0:T(8,128)S(1)}, f32[96,2048]{1,0:T(8,128)}, u32[]{:S(2)}) copy-start(f32[96,2048]{1,0:T(8,128)} %copy-done.3) | copy-start | bytes 2359300
  251.8 26.0 %copy-start.21 = (bf16[2048,16]{0,1:T(8,128)(2,1)S(1)}, bf16[2048,16]{0,1:T(8,128)(2,1)}, u32[]{:S(2)}) copy-start(bf16[2048,16]{0,1:T(8,128)(2,1)} %param.30) | copy-start | bytes 196612
  251.8 26.0 %copy-start.24 = (f32[2048]{0:T(1024)S(1)}, f32[2048]{0:T(1024)}, u32[]{:S(2)}) copy-start(f32[2048]{0:T(1024)} %param.29) | copy-start | bytes 24580
  251.8 26.0 %copy-start.28 = (f32[96]{0:T(128)S(1)}, f32[96]{0:T(128)}, u32[]{:S(2)}) copy-start(f32[96]{0:T(128)} %copy-done.27) | copy-start | bytes 1156
  254.4 79.0 %collective-permute-start.47 = (bf16[768,2048]{1,0:T(8,128)(2,1)}, bf16[768,2048]{1,0:T(8,128)(2,1)}, u32[]{:S(2)}, u32[]{:S(2)}) collective-permute-start(bf16[768,2048]{1,0:T(8,128)(2,1)} %convolution_convert_fusion), channel_id=1, source_target_pairs={{0,1},{1,0},{2,3},{3,2},{4,5},{5,4},{6,7},{7,6},{8,9},{9,8},{10,11... | collective-permute-start | bytes 9437192 | tf_op jit(solution)/shard_map/ppermute | solution.py:49
  265.5 54.6 %collective-permute-start.48 = (bf16[384,2048]{1,0:T(8,128)(2,1)}, bf16[384,2048]{1,0:T(8,128)(2,1)}, u32[]{:S(2)}, u32[]{:S(2)}) collective-permute-start(bf16[384,2048]{1,0:T(8,128)(2,1)} %convolution_convert_fusion.2), channel_id=1, source_target_pairs={{0,1},{1,0},{2,3},{3,2},{4,5},{5,4},{6,7},{7,6},{8,9},{9,8},{10,11... | collective-permute-start | bytes 4718600 | tf_op jit(solution)/shard_map/ppermute | solution.py:49
  277.1 6.1 %collective-permute-start.42 = (bf16[384,2048]{1,0:T(8,128)(2,1)}, bf16[384,2048]{1,0:T(8,128)(2,1)}, u32[]{:S(2)}, u32[]{:S(2)}) collective-permute-start(bf16[384,2048]{1,0:T(8,128)(2,1)} %convolution_convert_fusion.3), channel_id=1, source_target_pairs={{0,1},{1,0},{2,3},{3,2},{4,5},{5,4},{6,7},{7,6},{8,9},{9,8},{10,11... | collective-permute-start | bytes 4718600 | tf_op jit(solution)/shard_map/ppermute | solution.py:49
  282.4 11.9 %collective-permute-start.27 = (bf16[96,2048]{1,0:T(8,128)(2,1)S(1)}, bf16[96,2048]{1,0:T(8,128)(2,1)S(1)}, u32[]{:S(2)}, u32[]{:S(2)}) collective-permute-start(bf16[96,2048]{1,0:T(8,128)(2,1)S(1)} %get-tuple-element.128), channel_id=1, source_target_pairs={{0,2},{1,3},{2,0},{3,1},{4,6},{5,7},{6,4},{7,5},{8,10},{9,11},{10,... | collective-permute-start | bytes 1179656 | tf_op jit(solution)/shard_map/ppermute | solution.py:49
  287.5 40.6 %collective-permute-start.43 = (bf16[384,2048]{1,0:T(8,128)(2,1)}, bf16[384,2048]{1,0:T(8,128)(2,1)}, u32[]{:S(2)}, u32[]{:S(2)}) collective-permute-start(bf16[384,2048]{1,0:T(8,128)(2,1)} %add_convert_fusion.1), channel_id=1, source_target_pairs={{0,2},{1,3},{2,0},{3,1},{4,6},{5,7},{6,4},{7,5},{8,10},{9,11},{10,... | collective-permute-start | bytes 4718600 | tf_op jit(solution)/shard_map/ppermute | solution.py:49
  294.4 6.0 %collective-permute-start.28 = (bf16[2,96,2048]{2,1,0:T(8,128)(2,1)S(1)}, bf16[2,96,2048]{2,1,0:T(8,128)(2,1)S(1)}, u32[]{:S(2)}, u32[]{:S(2)}) collective-permute-start(bf16[2,96,2048]{2,1,0:T(8,128)(2,1)S(1)} %maximum_select_fusion.5), channel_id=1, source_target_pairs={{0,1},{1,0},{2,3},{3,2},{4,5},{5,4},{6,7},{7,6},{8,9},{9,8},{10,11... | collective-permute-start | bytes 2359304 | tf_op jit(solution)/shard_map/ppermute | solution.py:49
  314.1 47.7 %collective-permute-start.39 = (bf16[384,2048]{1,0:T(8,128)(2,1)}, bf16[384,2048]{1,0:T(8,128)(2,1)}, u32[]{:S(2)}, u32[]{:S(2)}) collective-permute-start(bf16[384,2048]{1,0:T(8,128)(2,1)} %get-tuple-element.150), channel_id=1, source_target_pairs={{0,2},{1,3},{2,0},{3,1},{4,6},{5,7},{6,4},{7,5},{8,10},{9,11},{10,... | collective-permute-start | bytes 4718600 | tf_op jit(solution)/shard_map/ppermute | solution.py:49
  315.0 80.5 %collective-permute-start.30 = (bf16[384,2048]{1,0:T(8,128)(2,1)}, bf16[384,2048]{1,0:T(8,128)(2,1)}, u32[]{:S(2)}, u32[]{:S(2)}) collective-permute-start(bf16[384,2048]{1,0:T(8,128)(2,1)} %get-tuple-element.151), channel_id=1, source_target_pairs={{0,2},{1,3},{2,0},{3,1},{4,6},{5,7},{6,4},{7,5},{8,10},{9,11},{10,... | collective-permute-start | bytes 4718600 | tf_op jit(solution)/shard_map/ppermute | solution.py:49
  338.5 64.9 %collective-permute-start.18 = (bf16[96,2048]{1,0:T(8,128)(2,1)S(1)}, bf16[96,2048]{1,0:T(8,128)(2,1)S(1)}, u32[]{:S(2)}, u32[]{:S(2)}) collective-permute-start(bf16[96,2048]{1,0:T(8,128)(2,1)S(1)} %copy-done.15), channel_id=1, source_target_pairs={{0,2},{1,3},{2,0},{3,1},{4,6},{5,7},{6,4},{7,5},{8,10},{9,11},{10,... | collective-permute-start | bytes 1179656 | tf_op jit(solution)/shard_map/ppermute | solution.py:49
  403.6 34.0 %collective-permute-start.19 = (bf16[2,96,2048]{2,1,0:T(8,128)(2,1)S(1)}, bf16[2,96,2048]{2,1,0:T(8,128)(2,1)S(1)}, u32[]{:S(2)}, u32[]{:S(2)}) collective-permute-start(bf16[2,96,2048]{2,1,0:T(8,128)(2,1)S(1)} %maximum_select_fusion.4), channel_id=1, source_target_pairs={{0,1},{1,0},{2,3},{3,2},{4,5},{5,4},{6,7},{7,6},{8,9},{9,8},{10,11... | collective-permute-start | bytes 2359304 | tf_op jit(solution)/shard_map/ppermute | solution.py:49
  432.7 2.8 collective-permute-start.31
  437.2 11.3 %collective-permute-start.32 = (bf16[96,2048]{1,0:T(8,128)(2,1)S(1)}, bf16[96,2048]{1,0:T(8,128)(2,1)S(1)}, u32[]{:S(2)}, u32[]{:S(2)}) collective-permute-start(bf16[96,2048]{1,0:T(8,128)(2,1)S(1)} %fusion.34), channel_id=1, source_target_pairs={{0,2},{1,3},{2,0},{3,1},{4,6},{5,7},{6,4},{7,5},{8,10},{9,11},{10,... | collective-permute-start | bytes 1179656 | tf_op jit(solution)/shard_map/ppermute | solution.py:49
  440.9 18.6 %collective-permute-start.41 = (bf16[272,1280]{1,0:T(8,128)(2,1)S(1)}, bf16[272,1280]{1,0:T(8,128)(2,1)S(1)}, u32[]{:S(2)}, u32[]{:S(2)}) collective-permute-start(bf16[272,1280]{1,0:T(8,128)(2,1)S(1)} %get-tuple-element.137), channel_id=1, source_target_pairs={{0,4},{4,0},{8,12},{12,8},{16,20},{20,16},{24,28},{28,24},{1,5},{5... | collective-permute-start | bytes 2088968 | tf_op jit(solution)/shard_map/ppermute | solution.py:593
  442.7 31.7 %collective-permute-start.38 = (bf16[272,1280]{1,0:T(8,128)(2,1)S(1)}, bf16[272,1280]{1,0:T(8,128)(2,1)S(1)}, u32[]{:S(2)}, u32[]{:S(2)}) collective-permute-start(bf16[272,1280]{1,0:T(8,128)(2,1)S(1)} %get-tuple-element.138), channel_id=1, source_target_pairs={{0,4},{4,0},{8,12},{12,8},{16,20},{20,16},{24,28},{28,24},{1,5},{5... | collective-permute-start | bytes 2088968 | tf_op jit(solution)/shard_map/ppermute | solution.py:593
  443.0 46.3 %collective-permute-start.36 = (bf16[272,1280]{1,0:T(8,128)(2,1)S(1)}, bf16[272,1280]{1,0:T(8,128)(2,1)S(1)}, u32[]{:S(2)}, u32[]{:S(2)}) collective-permute-start(bf16[272,1280]{1,0:T(8,128)(2,1)S(1)} %get-tuple-element.139), channel_id=1, source_target_pairs={{0,4},{4,0},{8,12},{12,8},{16,20},{20,16},{24,28},{28,24},{1,5},{5... | collective-permute-start | bytes 2088968 | tf_op jit(solution)/shard_map/ppermute | solution.py:593
  444.8 108.7 %collective-permute-start.35 = (bf16[272,1280]{1,0:T(8,128)(2,1)S(1)}, bf16[272,1280]{1,0:T(8,128)(2,1)}, u32[]{:S(2)}, u32[]{:S(2)}) collective-permute-start(bf16[272,1280]{1,0:T(8,128)(2,1)S(1)} %get-tuple-element.136), channel_id=1, source_target_pairs={{0,4},{4,0},{8,12},{12,8},{16,20},{20,16},{24,28},{28,24},{1,5},{5... | collective-permute-start | bytes 2088968 | tf_op jit(solution)/shard_map/ppermute | solution.py:593
  449.2 51.6 %collective-permute-start.33 = (bf16[96,2048]{1,0:T(8,128)(2,1)S(1)}, bf16[96,2048]{1,0:T(8,128)(2,1)S(1)}, u32[]{:S(2)}, u32[]{:S(2)}) collective-permute-start(bf16[96,2048]{1,0:T(8,128)(2,1)S(1)} %fusion.24), channel_id=1, source_target_pairs={{0,2},{1,3},{2,0},{3,1},{4,6},{5,7},{6,4},{7,5},{8,10},{9,11},{10,... | collective-permute-start | bytes 1179656 | tf_op jit(solution)/shard_map/ppermute | solution.py:49
  491.0 20.7 %collective-permute-start.37 = (bf16[272,1280]{1,0:T(8,128)(2,1)}, bf16[272,1280]{1,0:T(8,128)(2,1)S(1)}, u32[]{:S(2)}, u32[]{:S(2)}) collective-permute-start(bf16[272,1280]{1,0:T(8,128)(2,1)} %get-tuple-element.142), channel_id=1, source_target_pairs={{0,24},{4,28},{8,16},{12,20},{16,8},{20,12},{24,0},{28,4},{1,25},{... | collective-permute-start | bytes 2088968 | tf_op jit(solution)/shard_map/ppermute | solution.py:596
  494.4 59.0 %collective-permute-start.40 = (bf16[272,1280]{1,0:T(8,128)(2,1)}, bf16[272,1280]{1,0:T(8,128)(2,1)}, u32[]{:S(2)}, u32[]{:S(2)}) collective-permute-start(bf16[272,1280]{1,0:T(8,128)(2,1)} %get-tuple-element.76), channel_id=1, source_target_pairs={{0,16},{4,20},{8,24},{12,28},{16,0},{20,4},{24,8},{28,12},{1,17},{... | collective-permute-start | bytes 2088968 | tf_op jit(solution)/shard_map/ppermute | solution.py:596
  500.8 52.7 %collective-permute-start.44 = (bf16[272,1280]{1,0:T(8,128)(2,1)}, bf16[272,1280]{1,0:T(8,128)(2,1)}, u32[]{:S(2)}, u32[]{:S(2)}) collective-permute-start(bf16[272,1280]{1,0:T(8,128)(2,1)} %get-tuple-element.78), channel_id=1, source_target_pairs={{0,8},{4,12},{8,0},{12,4},{16,24},{20,28},{24,16},{28,20},{1,9},{5... | collective-permute-start | bytes 2088968 | tf_op jit(solution)/shard_map/ppermute | solution.py:596
  501.8 54.1 %collective-permute-start.34 = (bf16[2,96,2048]{2,1,0:T(8,128)(2,1)}, bf16[2,96,2048]{2,1,0:T(8,128)(2,1)}, u32[]{:S(2)}, u32[]{:S(2)}) collective-permute-start(bf16[2,96,2048]{2,1,0:T(8,128)(2,1)} %maximum_select_fusion.7), channel_id=1, source_target_pairs={{0,1},{1,0},{2,3},{3,2},{4,5},{5,4},{6,7},{7,6},{8,9},{9,8},{10,11... | collective-permute-start | bytes 2359304 | tf_op jit(solution)/shard_map/ppermute | solution.py:49
  511.7 41.7 %copy-start.19 = (bf16[272,1280]{1,0:T(8,128)(2,1)}, bf16[272,1280]{1,0:T(8,128)(2,1)S(1)}, u32[]{:S(2)}) copy-start(bf16[272,1280]{1,0:T(8,128)(2,1)S(1)} %collective-permute-done.37) | copy-start | bytes 2088964
  555.8 3.8 collective-permute-start.45
  559.6 4.9 collective-permute-start.46
  (17 other events, 88.4 us)
Sparse Core Ops, SparseCore 0:
  10.8 85.9 all-gather.1
  166.6 83.4 reduce-scatter.2
  310.2 94.2 reduce-scatter.4

commit v3 on v2

--- a/solution.py
+++ b/solution.py
@@ -38,10 +38,8 @@
     )
 
 
-def after(values, first):
-    if first is None:
-        return values
-    return lax.optimization_barrier((*values, first))[: len(values)]
+def tie(*values):
+    return lax.optimization_barrier(values)
 
 
 def swap(value, step):
@@ -335,7 +333,7 @@
             jax.ShapeDtypeStruct((halves, cut, width), jnp.bfloat16),
         ],
         compiler_params=pltpu.CompilerParams(vmem_limit_bytes=vmem_bytes),
-        cost_estimate=small_cost,
+        cost_estimate=pl.CostEstimate(flops=3 * 10**10, bytes_accessed=2**20, transcendentals=0),
         name="attend_back",
     )(
         rank, x, xn, dattn, w_query, w_key, w_value, q_gain[None], k_gain[None], cosine, sine, w_out,
@@ -352,8 +350,8 @@
             for i, source in enumerate(sources)
         ]
 
-    def start(self):
-        for copy in self.copies:
+    def start(self, shard):
+        for copy in self.copies[shard * self.each : (shard + 1) * self.each]:
             copy.start()
 
     def wait(self, shard):
@@ -361,225 +359,209 @@
             copy.wait()
 
 
-def forward_kernel(rank_ref, hn, routes, router, *rest, shards, local, hidden, top_count):
-    in_hbm, down_hbm = rest[: 2 * shards], rest[2 * shards : 3 * shards]
-    out, pre_out, gated, gates, gates_wide, in_all, down_all, in_sems, down_sems = rest[3 * shards :]
+def experts_kernel(rank_ref, hn, g, *rest, shards, before, local, hidden, top_count):
+    last = before > 0
+    every = before + shards
+    in_count = every if last else shards
+    if last:
+        gates, totals_in, pre_before, gated_before = rest[:4]
+        rest = rest[4:]
+    else:
+        sent, router = rest[:2]
+        rest = rest[2:]
+    in_hbm, down_hbm, rest = rest[: 2 * in_count], rest[2 * in_count : 3 * in_count], rest[3 * in_count :]
+    if last:
+        out, back, pre_grad, gated = rest[:4]
+        rest = rest[4:]
+        totals = rest[-1]
+    else:
+        pre_grad, gated, gates, totals = rest[:4]
+        rest = rest[4:]
+    in_all, down_all, gates_wide, in_sems, down_sems = rest[:5]
     chunk, shard = pl.program_id(0), pl.program_id(1)
     width = local * hidden
-    rows = hn.shape[0]
-    in_loads = Loads(in_hbm, in_all, in_sems, shards)
-    down_loads = Loads(down_hbm, down_all, down_sems, shards)
+    rows, model = hn.shape
+    first = before if last else 0
+    in_loads = Loads(in_hbm, in_all, in_sems, in_count)
+    down_loads = Loads(down_hbm, down_all, down_sems, in_count)
+    owner = lax.broadcasted_iota(jnp.int32, (rows, width), 1) // hidden
 
     @pl.when((chunk == 0) & (shard == 0))
     def _():
-        in_loads.start()
-        down_loads.start()
+        order = list(range(first, in_count)) + list(range(first))
+        for i in order:
+            in_loads.start(i)
+            down_loads.start(i)
 
     @pl.when(shard == 0)
     def _():
-        names = lax.broadcasted_iota(jnp.int32, (rows, router.shape[0]), 1).astype(jnp.float32)
-        chosen = routes[...].astype(jnp.float32)
-        mask = jnp.zeros(names.shape, jnp.bool_)
-        for j in range(top_count):
-            mask = mask | (chosen[:, j : j + 1] == names)
-        logits = jnp.where(mask, mm(hn[...], router[...], (1, 1)), far_below)
-        weight = jnp.exp(logits - jnp.max(logits, -1, keepdims=True))
-        weight = weight * (1.0 / jnp.sum(weight, -1, keepdims=True))
-        lanes = lax.broadcasted_iota(jnp.int32, gates.shape, 1)
-        packed = jnp.zeros(gates.shape, jnp.float32)
-        for i in range(local):
-            here = names == (rank_ref[1] * local + i).astype(jnp.float32)
-            value = jnp.sum(jnp.where(here, weight, 0.0), -1, keepdims=True)
-            gates_wide[:, i * hidden : (i + 1) * hidden] = jnp.broadcast_to(value, (rows, hidden))
-            packed = packed + jnp.where(lanes == i, value, 0.0)
-        gates[...] = packed
+        if last:
+            totals[...] = totals_in[...]
+        else:
+            names = lax.broadcasted_iota(jnp.int32, (rows, router.shape[0]), 1).astype(jnp.float32)
+            chosen = sent[...].astype(jnp.float32)
+            mask = jnp.zeros(names.shape, jnp.bool_)
+            for j in range(top_count):
+                mask = mask | (chosen[:, j : j + 1] == names)
+            logits = jnp.where(mask, mm(hn[...], router[...], (1, 1)), far_below)
+            weight = jnp.exp(logits - jnp.max(logits, -1, keepdims=True))
+            weight = weight * (1.0 / jnp.sum(weight, -1, keepdims=True))
+            lanes = lax.broadcasted_iota(jnp.int32, gates.shape, 1)
+            packed = jnp.zeros(gates.shape, jnp.float32)
+            for e in range(local):
+                here = names == (rank_ref[1] * local + e).astype(jnp.float32)
+                value = jnp.sum(jnp.where(here, weight, 0.0), -1, keepdims=True)
+                packed = packed + jnp.where(lanes == e, value, 0.0)
+            gates[...] = packed
+            totals[...] = jnp.zeros_like(totals)
+        wide = jnp.zeros((rows, width), jnp.float32)
+        for e in range(local):
+            wide = jnp.where(owner == e, gates[:, e : e + 1], wide)
+        gates_wide[...] = wide
 
     for i in range(shards):
         @pl.when((chunk == 0) & (shard == i))
         def _(i=i):
-            in_loads.wait(i)
-
-    at = pl.multiple_of(shard * 2 * width, 2 * width)
-    pre = mm(hn[...], in_all[pl.ds(at, 2 * width), :], (1, 1))
-    pre_out[...] = pre
-    middle = jax.nn.silu(pre[:, :width]) * pre[:, width:]
-    gated[:, pl.ds(pl.multiple_of(shard * width, width), width)] = bf(middle * gates_wide[...])
-
-    @pl.when(shard == shards - 1)
-    def _():
-        @pl.when(chunk == 0)
-        def _():
-            for i in range(shards):
-                down_loads.wait(i)
-
-        wide = 512
-
-        @pl.loop(0, out.shape[1] // wide)
-        def _(n):
-            cols = pl.ds(pl.multiple_of(n * wide, wide), wide)
-            out[:, cols] = bf(mm(gated[...], down_all[:, cols]))
-
-
-def backward_kernel(rank_ref, g, gates, pre_in, *rest, shards, local, hidden):
-    in_hbm, down_hbm = rest[: 2 * shards], rest[2 * shards : 3 * shards]
-    back, pre_grad, in_all, down_all, totals, in_sems, down_sems = rest[3 * shards :]
-    chunk, shard = pl.program_id(0), pl.program_id(1)
-    width = local * hidden
-    rows, model = g.shape
-    in_loads = Loads(in_hbm, in_all, in_sems, shards)
-    down_loads = Loads(down_hbm, down_all, down_sems, shards)
-
-    @pl.when((chunk == 0) & (shard == 0))
-    def _():
-        down_loads.start()
-        in_loads.start()
-
-    for i in range(shards):
-        @pl.when((chunk == 0) & (shard == i))
-        def _(i=i):
-            down_loads.wait(i)
-
-    @pl.when(shard == 0)
-    def _():
-        totals[...] = jnp.zeros_like(totals)
-
-    at = pl.multiple_of(shard * width, width)
-    grad_middle_all = mm(g[...], down_all[pl.ds(at, width), :], (1, 1))
-    lanes = lax.broadcasted_iota(jnp.int32, totals.shape, 1)
-    experts_at = lax.broadcasted_iota(jnp.int32, (rows, width), 1)
-    gate_wide = jnp.zeros((rows, width), jnp.float32)
-    for e in range(local):
-        gate_wide = jnp.where(experts_at // hidden == e, gates[:, e : e + 1], gate_wide)
-    gate_pre, up_pre = pre_in[:, :width], pre_in[:, width:]
+            in_loads.wait(first + i)
+            down_loads.wait(first + i)
+
+    in_at = pl.multiple_of((first + shard) * 2 * width, 2 * width)
+    down_at = pl.multiple_of((first + shard) * width, width)
+    pre = mm(hn[...], in_all[pl.ds(in_at, 2 * width), :], (1, 1))
+    grad_middle = mm(g[...], down_all[pl.ds(down_at, width), :], (1, 1))
+    gate_pre, up_pre = pre[:, :width], pre[:, width:]
     sigmoid_gate = jax.nn.sigmoid(gate_pre)
     activated = gate_pre * sigmoid_gate
-    product = activated * up_pre * grad_middle_all
-    added = jnp.zeros(totals.shape, jnp.float32)
+    middle = activated * up_pre
+    mid_at = pl.multiple_of(shard * width, width)
+    gated[:, pl.ds(mid_at, width)] = bf(middle * gates_wide[...])
+    product = middle * grad_middle
+    lanes = lax.broadcasted_iota(jnp.int32, totals.shape, 1)
+    added = totals[...]
     for e in range(local):
-        part = jnp.sum(product[:, e * hidden : (e + 1) * hidden], -1, keepdims=True)
-        added = added + jnp.where(lanes == e, part, 0.0)
-    totals[...] += added
-    grad_middle = grad_middle_all * gate_wide
-    at = pl.multiple_of(shard * 2 * width, 2 * width)
-    pre_grad[:, pl.ds(at, width)] = bf(
-        grad_middle * up_pre * sigmoid_gate * (1.0 + gate_pre * (1.0 - sigmoid_gate))
-    )
-    pre_grad[:, pl.ds(pl.multiple_of(at + width, width), width)] = bf(grad_middle * activated)
-
-    @pl.when(shard == shards - 1)
-    def _():
-        @pl.when(chunk == 0)
+        value = jnp.sum(jnp.where(owner == e, product, 0.0), -1, keepdims=True)
+        added = added + jnp.where(lanes == e, value, 0.0)
+    totals[...] = added
+    grad_middle = grad_middle * gates_wide[...]
+    gate_at = pl.multiple_of(shard * 2 * width, 2 * width)
+    pre_grad[:, pl.ds(gate_at, width)] = bf(
+        grad_middle * up_pre * (sigmoid_gate + activated * (1.0 - sigmoid_gate))
+    )
+    pre_grad[:, pl.ds(pl.multiple_of(gate_at + width, width), width)] = bf(grad_middle * activated)
+
+    if last:
+
+        @pl.when(shard == shards - 1)
         def _():
-            for i in range(shards):
-                in_loads.wait(i)
-
-        wide = 512
-
-        @pl.loop(0, model // wide)
-        def _(n):
-            cols = pl.ds(pl.multiple_of(n * wide, wide), wide)
-            back[:, cols] = bf(mm(pre_grad[...], in_all[:, cols]))
-
-        spare = back.shape[1] - model
-        places = lax.broadcasted_iota(jnp.int32, (rows, spare), 1)
-        tail = jnp.zeros((rows, spare), jnp.float32)
-        for e in range(local):
-            value = totals[:, e : e + 1]
-            high = bf(value).astype(jnp.float32)
-            here = rank_ref[1] * local + e
-            tail = tail + jnp.where(places == here, high, 0.0)
-            tail = tail + jnp.where(places == spare // 2 + here, value - high, 0.0)
-        back[:, model:] = bf(tail)
-
-
-def expert_specs(tokens, model, shards, width):
+            @pl.when(chunk == 0)
+            def _():
+                for i in range(before):
+                    in_loads.wait(i)
+                    down_loads.wait(i)
+
+            wide = 512
+
+            @pl.loop(0, model // wide)
+            def _(n):
+                cols = pl.ds(pl.multiple_of(n * wide, wide), wide)
+                cut = before * width
+                back[:, cols] = bf(
+                    mm(pre_before[...], in_all[: 2 * cut, cols]) + mm(pre_grad[...], in_all[2 * cut :, cols])
+                )
+                out[:, cols] = bf(
+                    mm(gated_before[...], down_all[:cut, cols]) + mm(gated[...], down_all[cut:, cols])
+                )
+
+            spare = back.shape[1] - model
+            places = lax.broadcasted_iota(jnp.int32, (rows, spare), 1)
+            tail = jnp.zeros((rows, spare), jnp.float32)
+            for e in range(local):
+                value = totals[:, e : e + 1]
+                high = bf(value).astype(jnp.float32)
+                here = rank_ref[1] * local + e
+                tail = tail + jnp.where(places == here, high, 0.0)
+                tail = tail + jnp.where(places == spare // 2 + here, value - high, 0.0)
+            back[:, model:] = bf(tail)
+
+
+def run_experts(ranks, hn, sent, in_mats, down_mats, local, top_count, router=None, before=None, spare=0):
+    tokens, model = hn.shape
+    width = down_mats[0].shape[0]
+    every = len(down_mats)
+    earlier = 0 if before is None else before[2].shape[1] // (2 * width)
+    shards = every - earlier
     rows = tokens
     while rows > 768:
         rows //= 2
 
-    def block(cols, step=None):
-        if step is None:
-            return pl.BlockSpec((rows, cols), lambda c, s, _: (c, 0))
-        return pl.BlockSpec((rows, cols), lambda c, s, _: (c, s if step < 0 else step))
-
+    def block(cols, step=0):
+        return pl.BlockSpec((rows, cols), lambda c, s, _: (c, step), pipeline_mode=pl.Buffered(1))
+
+    hbm = [pl.BlockSpec(memory_space=pl.ANY)] * (3 * every)
     scratch = [
-        pltpu.VMEM((shards * 2 * width, model), jnp.bfloat16),
-        pltpu.VMEM((shards * width, model), jnp.bfloat16),
-        pltpu.SemaphoreType.DMA((2 * shards,)),
-        pltpu.SemaphoreType.DMA((shards,)),
+        pltpu.VMEM((every * 2 * width, model), jnp.bfloat16),
+        pltpu.VMEM((every * width, model), jnp.bfloat16),
+        pltpu.VMEM((rows, width), jnp.float32),
+        pltpu.SemaphoreType.DMA((2 * every,)),
+        pltpu.SemaphoreType.DMA((every,)),
     ]
-    return rows, block, [pl.BlockSpec(memory_space=pl.ANY)] * (3 * shards), scratch
-
-
-def experts_forward(ranks, hn, sent, router, in_mats, down_mats, local, top_count):
-    tokens, model = hn.shape
-    shards, width = len(down_mats), down_mats[0].shape[0]
-    rows, block, hbm, scratch = expert_specs(tokens, model, shards, width)
+    own = [(shards * 2 * width, jnp.bfloat16), (shards * width, jnp.bfloat16)]
+    if before is None:
+        extra, specs = (sent, router), [block(128, model // 128), whole(router.shape)]
+        outs = own + [(128, jnp.float32)] * 2
+    else:
+        extra = before
+        specs = [block(value.shape[1]) for value in before]
+        outs = [(model, jnp.bfloat16), (model + spare, jnp.bfloat16)] + own
+        scratch.append(pltpu.VMEM((rows, 128), jnp.float32))
     return pl.pallas_call(
         functools.partial(
-            forward_kernel, shards=shards, local=local, hidden=width // local, top_count=top_count
+            experts_kernel, shards=shards, before=earlier, local=local, hidden=width // local, top_count=top_count
         ),
         grid_spec=pltpu.PrefetchScalarGridSpec(
             num_scalar_prefetch=1,
             grid=(tokens // rows, shards),
-            in_specs=[block(model), block(128, model // 128), whole(router.shape)] + hbm,
-            out_specs=[block(model), block(2 * width, -1), block(shards * width), block(128)],
-            scratch_shapes=[pltpu.VMEM((rows, width), jnp.float32)] + scratch,
+            in_specs=[block(model), block(model)] + specs + hbm,
+            out_specs=[block(cols) for cols, _ in outs],
+            scratch_shapes=scratch,
         ),
-        out_shape=[
-            jax.ShapeDtypeStruct((tokens, model), jnp.bfloat16),
-            jax.ShapeDtypeStruct((tokens, shards * 2 * width), jnp.float32),
-            jax.ShapeDtypeStruct((tokens, shards * width), jnp.bfloat16),
-            jax.ShapeDtypeStruct((tokens, 128), jnp.float32),
-        ],
+        out_shape=[jax.ShapeDtypeStruct((tokens, cols), kind) for cols, kind in outs],
         compiler_params=pltpu.CompilerParams(vmem_limit_bytes=vmem_bytes),
         cost_estimate=small_cost,
-        name="experts_forward",
-    )(ranks, hn, sent, router, *in_mats, *down_mats)
-
-
-def experts_backward(ranks, sent, gates, pre, in_mats, down_mats, local, spare):
-    tokens, model = sent.shape[0], down_mats[0].shape[1]
-    shards, width = len(down_mats), down_mats[0].shape[0]
-    rows, block, hbm, scratch = expert_specs(tokens, model, shards, width)
-    return pl.pallas_call(
-        functools.partial(backward_kernel, shards=shards, local=local, hidden=width // local),
-        grid_spec=pltpu.PrefetchScalarGridSpec(
-            num_scalar_prefetch=1,
-            grid=(tokens // rows, shards),
-            in_specs=[block(model), block(128), block(2 * width, -1)] + hbm,
-            out_specs=[block(model + spare), block(shards * 2 * width)],
-            scratch_shapes=scratch[:2] + [pltpu.VMEM((rows, 128), jnp.float32)] + scratch[2:],
-        ),
-        out_shape=[
-            jax.ShapeDtypeStruct((tokens, model + spare), jnp.bfloat16),
-            jax.ShapeDtypeStruct((tokens, shards * 2 * width), jnp.bfloat16),
-        ],
-        compiler_params=pltpu.CompilerParams(vmem_limit_bytes=vmem_bytes),
-        cost_estimate=small_cost,
-        name="experts_backward",
-    )(ranks, sent, gates, pre, *in_mats, *down_mats)
-
-
-def out_grad_kernel(dattn, o, packed):
-    packed[...] = bf(mm(dattn[...], o[...], (0, 0))).reshape(packed.shape)
-
-
-def out_grad(dattn, o, blocks):
+        name="experts_near" if before is None else "experts_far",
+    )(ranks, hn, sent, *extra, *in_mats, *down_mats)
+
+
+def out_grad_kernel(dattn, o, y, packed):
+    many, height, width = y.shape
+    cols = o.shape[1]
+    rows = dattn.shape[1] // many
+    packed[:, :rows, :] = bf(mm(dattn[...], o[...], (0, 0))).reshape(many, rows, cols)
+    for i in range(width // cols):
+        packed[:, rows + i * height : rows + (i + 1) * height, :] = y[:, :, i * cols : (i + 1) * cols]
+
+
+def out_grad(dattn, o, y):
     tokens, width = dattn.shape
+    blocks, height, _ = y.shape
     cols = o.shape[1]
     rows = width // blocks
     many = max(1, 256 // rows)
+    full = rows + height * (width // cols)
     return pl.pallas_call(
         out_grad_kernel,
         grid=(blocks // many,),
-        in_specs=[pl.BlockSpec((tokens, many * rows), lambda i: (0, i)), whole(o.shape)],
-        out_specs=pl.BlockSpec((many, rows, cols), lambda i: (i, 0, 0)),
-        out_shape=jax.ShapeDtypeStruct((blocks, rows, cols), jnp.bfloat16),
+        in_specs=[
+            pl.BlockSpec((tokens, many * rows), lambda i: (0, i)),
+            whole(o.shape),
+            pl.BlockSpec((many, height, width), lambda i: (i, 0, 0)),
+        ],
+        out_specs=pl.BlockSpec((many, full, cols), lambda i: (i, 0, 0)),
+        out_shape=jax.ShapeDtypeStruct((blocks, full, cols), jnp.bfloat16),
         compiler_params=pltpu.CompilerParams(vmem_limit_bytes=vmem_bytes),
         cost_estimate=small_cost,
         name="out_grad",
-    )(dattn, o)
+    )(dattn, o, y)
 
 
 class Tokens:
@@ -598,38 +580,38 @@
     def place(self, step, other):
         return (self.z ^ step) * 2 + (1 - self.y if other else self.y)
 
-    def gather(self, own, early=None, late=None):
+    def gather(self, own, early):
         if not self.line:
-            return lax.all_gather(own, "expert", axis=0, tiled=False)
+            return lax.all_gather(own, "expert", axis=0, tiled=False), early
         blocks = [own] + [self.along(own, step) for step in (1, 2, 3)]
         others = [self.across(own)]
-        (blocks[1],) = after((blocks[1],), early)
-        blocks[2], blocks[3] = after((blocks[2], blocks[3]), late)
+        blocks[1], early = tie(blocks[1], early)
         others += [self.across(value) for value in blocks[1:]]
         rows = jnp.zeros((self.size, *own.shape), own.dtype)
         for step in range(4):
             for value, other in ((blocks[step], False), (others[step], True)):
                 rows = lax.dynamic_update_index_in_dim(rows, value, self.place(step, other), 0)
-        return rows
-
-    def scatter(self, parts, first=None, second=None, last=None):
+        return rows, early
+
+    def scatter(self, parts, begun, late, last):
         if not self.line:
-            return lax.psum_scatter(parts, "expert", scatter_dimension=0, tiled=False).astype(
-                jnp.float32
-            )
+            total = lax.psum_scatter(parts, "expert", scatter_dimension=0, tiled=False)
+            return total.astype(jnp.float32), begun, late, last
 
         def part(step, other):
             return lax.dynamic_index_in_dim(parts, self.place(step, other), 0, False)
 
-        sums = {}
-        for step in (3, 2, 1, 0):
-            sums[step] = part(step, False).astype(jnp.float32)
-            sums[step] = sums[step] + self.across(part(step, True)).astype(jnp.float32)
-        given = {step: bf(sums[step]) for step in (3, 2, 1)}
-        (given[2],) = after((given[2],), first)
-        (given[1],) = after((given[1],), second)
-        arrived = after(tuple(self.along(given[step], step) for step in (3, 2, 1)), last)
-        return sums[0] + sum(value.astype(jnp.float32) for value in arrived)
+        def pair_sum(step):
+            return part(step, False).astype(jnp.float32) + across[step].astype(jnp.float32)
+
+        across = {step: self.across(part(step, True)) for step in (3, 2, 1, 0)}
+        across[3], begun = tie(across[3], begun)
+        moved = {step: self.along(bf(pair_sum(step)), step) for step in (3, 2)}
+        across[1], moved[3] = tie(across[1], moved[3])
+        moved[1] = self.along(bf(pair_sum(1)), 1)
+        across[0], moved[2], late = tie(across[0], moved[2], late)
+        moved[1], last = tie(moved[1], last)
+        return pair_sum(0) + sum(value.astype(jnp.float32) for value in moved.values()), begun, late, last
 
 
 def body(
@@ -670,9 +652,8 @@
     spare_cols = 128
     routes_wide = jnp.pad(bf(routes_own), ((0, 0), (0, spare_cols - routes.shape[1])))
     sent_own = jnp.concatenate([cot_own, routes_wide], 1)
-    (hidden_in,) = after((hidden_in,), sent_own)
+    hidden_in, sent_own = tie(hidden_in, sent_own)
     sent = lax.all_gather(sent_own, "expert", axis=0, tiled=True)
-    grad_all = sent[:, :model_width]
     expert_ids = jnp.arange(experts, dtype=jnp.int32)
 
     def mask_of(route_rows):
@@ -690,24 +671,24 @@
         segments, w_out, shard_rows,
     )
 
-    def reduce_rows(keep, give, first=None):
+    def reduce_rows(keep, give, first=()):
         half = keep + swap(give, 1).astype(jnp.float32)
         high = tensor_rank // 2
         keep = lax.dynamic_index_in_dim(half, high, 0, False)
-        give = bf(lax.dynamic_index_in_dim(half, 1 - high, 0, False))
-        (give,) = after((give,), first)
-        return keep + swap(give, 2).astype(jnp.float32)
+        give, first = tie(bf(lax.dynamic_index_in_dim(half, 1 - high, 0, False)), first)
+        return keep + swap(give, 2).astype(jnp.float32), first
 
     def gather_rows(own):
         far = swap(own, 2)
-        high, low = tensor_rank // 2, tensor_rank % 2
-        mine = jnp.where(high == 0, jnp.stack([own, far]), jnp.stack([far, own]))
-        theirs = swap(mine, 1)
-        both = jnp.where(low == 0, jnp.stack([mine, theirs], 1), jnp.stack([theirs, mine], 1))
-        return both.reshape(tok_count, model_width)
+        both = jnp.stack([own, far])
+        near = swap(both, 1)
+        rows = jnp.zeros((tensor_size, shard_rows, model_width), own.dtype)
+        for value, step in ((own, 0), (far, 2), (near[0], 1), (near[1], 3)):
+            rows = lax.dynamic_update_index_in_dim(rows, value, tensor_rank ^ step, 0)
+        return rows.reshape(tok_count, model_width)
 
     far_gate = swap(own_mats[0], 2)
-    attn_sum = reduce_rows(keep, give_part, far_gate)
+    attn_sum, far_gate = reduce_rows(keep, give_part, far_gate)
     residual = own_rows(hidden_in).astype(jnp.float32) + attn_sum
     inv_second = lax.rsqrt(jnp.mean(residual * residual, -1, keepdims=True) + epsilon)
     normed_ffn = (residual * inv_second * ffn_gain).astype(jnp.bfloat16)
@@ -719,33 +700,30 @@
     gates_own = gates_of(normed_ffn, mask_own)
     far_up = swap(own_mats[1], 2)
     far_mats = [far_gate, far_up, swap(own_mats[2], 2)]
-    normed_all = order.gather(normed_ffn, sent, far_up).reshape(group * shard_rows, model_width)
+    normed_all, sent = order.gather(normed_ffn, sent)
+    normed_all = normed_all.reshape(group * shard_rows, model_width)
+    grad_all = sent[:, :model_width]
     near_mats = [swap(value, 1) for value in own_mats]
     last_mats = [swap(value, 1) for value in far_mats]
     shards = (own_mats, near_mats, far_mats, last_mats)
     in_mats = [value for shard in shards for value in shard[:2]]
     down_mats = [shard[2] for shard in shards]
     width = local_experts * hidden
-    out_part, pre, gated_middles, gates_packed = experts_forward(
-        ranks, normed_all, sent, router.T, in_mats, down_mats, local_experts, routes.shape[1]
-    )
-    out_sum = lax.psum_scatter(
-        out_part.reshape(group, shard_rows, model_width), "expert", scatter_dimension=0, tiled=False
+    given = (ranks, normed_all, sent)
+    near_count = len(shards) // 2
+    pre_near, gated_near, gates_packed, marks = run_experts(
+        *given, in_mats[: 2 * near_count], down_mats[:near_count], local_experts, routes.shape[1], router.T
     )
     spare_cols = 128 * (-(-2 * experts // 128))
-    back_part, pre_grads = experts_backward(
-        ranks, sent, gates_packed, pre, in_mats, down_mats, local_experts, spare_cols
-    )
-    back_sum = order.scatter(back_part.reshape(group, shard_rows, -1), second=out_sum)
-    gate_grad_own = (
-        back_sum[:, model_width : model_width + experts]
-        + back_sum[:, model_width + spare_cols // 2 :][:, :experts]
-    )
-    back_sum = back_sum[:, :model_width]
+    out_part, back_part, pre_last, gated_last = run_experts(
+        *given, in_mats, down_mats, local_experts, routes.shape[1],
+        before=(gates_packed, marks, pre_near, gated_near), spare=spare_cols,
+    )
     def weight_grads(step):
-        cols = slice(step * 2 * width, (step + 1) * 2 * width)
-        mids = slice(step * width, (step + 1) * width)
-        return mm(pre_grads[:, cols], normed_all, (0, 0)), mm(gated_middles[:, mids], grad_all, (0, 0))
+        pre, gated = ((pre_near, gated_near), (pre_last, gated_last))[step // near_count]
+        at = step % near_count
+        pre, gated = pre[:, at * 2 * width : (at + 1) * 2 * width], gated[:, at * width : (at + 1) * width]
+        return mm(pre, normed_all, (0, 0)), mm(gated, grad_all, (0, 0))
 
     def give(parts, step):
         return [swap(bf(part), step).astype(jnp.float32) for part in parts]
@@ -755,7 +733,17 @@
     far_part = [bf(a + b) for a, b in zip(weight_grads(2), far)]
     near_part = [a + b for a, b in zip(weight_grads(0), near)]
     far_part = [far_part[0][:width], far_part[0][width:], far_part[1]]
-    arrived = give(far_part, 2)
+
+    far_part = tuple(far_part)
+    arrived = [swap(far_part[0], 2)]
+    back_sum, far_part, _, arrived[0] = order.scatter(
+        back_part.reshape(group, shard_rows, -1), far_part, (), arrived[0]
+    )
+    gate_grad_own = (
+        back_sum[:, model_width : model_width + experts]
+        + back_sum[:, model_width + spare_cols // 2 :][:, :experts]
+    )
+    back_sum = back_sum[:, :model_width]
     grad_out = cot_own.astype(jnp.float32)
     grad_chosen = gates_own * (
         gate_grad_own - jnp.sum(gates_own * gate_grad_own, -1, keepdims=True)
@@ -766,24 +754,18 @@
     ffn_gain_part = jnp.sum(grad_normed_ffn * residual * inv_second, 0)
     grad_residual = grad_out + norm_back(grad_normed_ffn * ffn_gain, residual, inv_second)
     grad_attn = gather_rows(bf(grad_residual))
-    out_blocks = out_grad(grad_attn, attended_rows, group)
-    (grad_attn,) = after((grad_attn,), out_blocks)
-    w_out_grad = (
-        lax.psum_scatter(
-            out_blocks, "expert", scatter_dimension=0, tiled=False
-        )
-        .astype(jnp.float32)
-        .T
-    )
+    grad_attn, *left = tie(grad_attn, *far_part[1:])
+    arrived += [swap(piece, 2) for piece in left]
+    out_blocks = out_grad(grad_attn, attended_rows, out_part.reshape(group, shard_rows, model_width))
+    grad_attn, out_blocks = tie(grad_attn, out_blocks)
+    out_blocks = lax.psum_scatter(out_blocks, "expert", scatter_dimension=0, tiled=False)
     slice_rows = model_width // group
     spare = 16
     packed, gain_parts, attn_gain_part, keep, give_part = attend_back(
         ranks, hidden_in, normalized_input, grad_attn, w_query, w_key, value_weight, q_gain, k_gain, cosine,
         sine_table, w_out, qp, kp, q, k, v, prob, shard_rows, group, spare,
     )
-    (give_part,) = after((give_part,), arrived[0])
-    grad_normed = reduce_rows(keep, give_part)
-    layer_out = gather_rows(bf(residual + out_sum.astype(jnp.float32)))
+    grad_normed, _ = reduce_rows(keep, give_part)
     inputs_own = own_rows(hidden_in).astype(jnp.float32)
     inv_own = lax.rsqrt(jnp.mean(inputs_own * inputs_own, -1, keepdims=True) + epsilon)
     input_grad = gather_rows(
@@ -803,7 +785,11 @@
     packed = lax.dynamic_update_slice(
         packed, bf(small).reshape(group, spare, packed.shape[2]), (0, slice_rows, 0)
     )
-    packed = order.scatter(packed, first=arrived[1], second=arrived[2], last=w_out_grad)
+    packed, _, out_blocks, _ = order.scatter(packed, (), out_blocks, ())
+    out_blocks = out_blocks.astype(jnp.float32)
+    w_out_grad = out_blocks[:slice_rows].T
+    out_sum = out_blocks[slice_rows:].reshape(-1, shard_rows, out_blocks.shape[1]).transpose(1, 0, 2)
+    layer_out = gather_rows(bf(residual + out_sum.reshape(shard_rows, model_width)))
     query_width, key_width = w_query.shape[1], w_key.shape[1]
     w_query_grad = packed[:slice_rows, :query_width]
     w_key_grad = packed[:slice_rows, query_width : query_width + key_width]
@@ -817,7 +803,8 @@
     ]
     parts = [near_part[0][:width], near_part[0][width:], near_part[1]]
     gate_t, up_t, w_down_grad = [
-        (a + b).reshape(local_experts, hidden, model_width) for a, b in zip(parts, arrived)
+        (a + b.astype(jnp.float32)).reshape(local_experts, hidden, model_width)
+        for a, b in zip(parts, arrived)
     ]
     w_gate_grad, w_up_grad = gate_t.transpose(0, 2, 1), up_t.transpose(0, 2, 1)
     gain_count = head_size // group

time: 583 us -> 525 us (0.901)
  the two profiles are of different devices: /device:TPU:0 before, /device:TPU:25 now
where the time goes in v3:
time: 525 us; the launch traced here: 515 us
  waiting for transfers between devices  217 us (41%)
  Pallas kernels  115 us (22%)
  starting transfers between devices  62.8 us (12%)
  local copies, waits for them, and re-layouts  42.4 us (8%)
  matrix products  31.8 us (6%)
  other arithmetic  29.8 us (6%)
  between operations  15.2 us (3%)
    ppermute x28, waiting for transfers between devices, swap(): return lax.ppermute(value, 'tensor', [(i, i ^ step) for i in range(size)])  117 us
    ppermute x9, waiting for transfers between devices, along(): return lax.ppermute(value, 'expert', [(i, i ^ 2 * step) for i in range(8)])  75.6 us
    pallas_call x2, Pallas kernels, run_experts(): pl.pallas_call(functools.partial(experts_kernel, shards=shards, before=ea...  55.5 us
    ppermute x28, starting transfers between devices, swap(): return lax.ppermute(value, 'tensor', [(i, i ^ step) for i in range(size)])  35.6 us
    dot_general x11, matrix products, mm(): lax.dot_general(left, right, (((contract[0],), (contract[1],)), ((), ()))...  31.8 us
    pallas_call x1, Pallas kernels, attend_back(): pl.pallas_call(attend_back_kernel, grid_spec=pltpu.PrefetchScalarGridSpec...  28.9 us
    ppermute x12, waiting for transfers between devices, across(): return lax.ppermute(value, 'expert', [(i, i ^ 1) for i in range(8)])  24.3 us
    pallas_call x1, Pallas kernels, attend(): pl.pallas_call(attend_kernel, grid_spec=pltpu.PrefetchScalarGridSpec(num_...  21.6 us
  transfers between devices with their start and end apart: 51, of which 23 were waited for; matrix products, arithmetic and copies ran while one was open for 14% of the time, Pallas kernels for 13%

profile of v3, /device:TPU:25, one launch (start us, length us, event | category | flops | bytes accessed | tf_op | source)
XLA Modules:
  0.0 514.8 jit_solution(7977113829774204225)
XLA Ops:
  10.0 1.3 collective-permute-start.1
  14.9 21.6 %attend.1 = (bf16[384,2048]{1,0:T(8,128)(2,1)}, f32[384,1024]{1,0:T(8,128)}, f32[384,128]{1,0:T(8,128)}, bf16[384,1024]{1,0:T(8,128)(2,1)}, bf16[384,128]{1,0:T(...) custom-call(s32[2]{0:T(128)} %pad_add_fusion.rank_ref, ...), custom_call_target="tpu_custom_call" | custom-call | flops 1048576 | bytes 65536 | tf_op jit(solution)/shard_map/attend/pallas_call | solution.py:136
  37.5 2.1 collective-permute-done
  39.7 1.6 convert_add_fusion.3
  41.3 4.3 collective-permute-done.1.rest_8_
  46.8 8.0 %collective-permute-done.2 = bf16[96,2048]{1,0:T(8,128)(2,1)S(1)} collective-permute-done((bf16[96,2048]{1,0:T(8,128)(2,1)S(1)}, bf16[96,2048]{1,0:T(8,128)(2,1)S(1)}, u32[]{:S(2)}, u32[]{:S(2)}) %collective-permute-start.2) | collective-permute-done | bytes 393248 | tf_op jit(solution)/shard_map/ppermute | solution.py:47
  57.1 1.3 collective-permute-start.3
  58.4 2.6 collective-permute-start.10
  62.7 7.1 %collective-permute-done.3 = bf16[96,2048]{1,0:T(8,128)(2,1)} collective-permute-done((bf16[96,2048]{1,0:T(8,128)(2,1)S(1)}, bf16[96,2048]{1,0:T(8,128)(2,1)}, u32[]{:S(2)}, u32[]{:S(2)}) %collective-permute-start.3) | collective-permute-done | bytes 393248 | tf_op jit(solution)/shard_map/ppermute | solution.py:575
  71.1 18.1 %collective-permute-done.4 = bf16[96,2048]{1,0:T(8,128)(2,1)S(1)} collective-permute-done((bf16[96,2048]{1,0:T(8,128)(2,1)S(1)}, bf16[96,2048]{1,0:T(8,128)(2,1)S(1)}, u32[]{:S(2)}, u32[]{:S(2)}) %collective-permute-start.4) | collective-permute-done | bytes 393248 | tf_op jit(solution)/shard_map/ppermute | solution.py:578
  92.7 9.4 %collective-permute-done.8 = bf16[96,2048]{1,0:T(8,128)(2,1)} collective-permute-done((bf16[96,2048]{1,0:T(8,128)(2,1)S(1)}, bf16[96,2048]{1,0:T(8,128)(2,1)}, u32[]{:S(2)}, u32[]{:S(2)}) %collective-permute-start.8) | collective-permute-done | bytes 393248 | tf_op jit(solution)/shard_map/ppermute | solution.py:578
  103.6 2.0 collective-permute-start.11
  105.7 25.4 %collective-permute-done.16.rest_14_ = bf16[384,2048]{1,0:T(8,128)(2,1)} collective-permute-done((bf16[384,2048]{1,0:T(8,128)(2,1)}, bf16[384,2048]{1,0:T(8,128)(2,1)}, u32[]{:S(2)}, u32[]{:S(2)}) %collective-permute-start.16) | collective-permute-done | bytes 1572896 | tf_op jit(solution)/shard_map/ppermute | solution.py:47
  134.6 1.6 copy-done.7
  136.8 17.7 %experts_near.1 = (bf16[768,1536]{1,0:T(8,128)(2,1)}, bf16[768,768]{1,0:T(8,128)(2,1)}, f32[768,128]{1,0:T(8,128)}, f32[768,128]{1,0:T(8,128)}) custom-call(s32[2]{0:T(128)} %pad_add_fusion.rank_ref, bf16[768,2048]{1,0:T(8,128)(2,1)} %bitcast.136, bf16[768,2176]{1,0:T(8,128)(2,1)} %all-gather.2.cloned.1.call-done.g.rest_0_, ...), custom_call_target="tpu_custom_call" | custom-call | flops 1048576 | bytes 65536 | tf_op jit(solution)/shard_map/experts_near/pallas_call | solution.py:517
  154.6 37.7 %experts_far.1 = (bf16[768,2048]{1,0:T(8,128)(2,1)}, bf16[768,2176]{1,0:T(8,128)(2,1)}, bf16[768,1536]{1,0:T(8,128)(2,1)}, bf16[768,768]{1,0:T(8,128)(2,1)}) custom-call(s32[2]{0:T(128)} %pad_add_fusion.rank_ref, bf16[768,2048]{1,0:T(8,128)(2,1)} %bitcast.137, bf16[768,2176]{1,0:T(8,128)(2,1)} %all-gather.2.cloned.1.call-done.g.rest_0_, ...), custom_call_target="tpu_custom_call" | custom-call | flops 1048576 | bytes 65536 | tf_op jit(solution)/shard_map/experts_far/pallas_call | solution.py:517
  192.4 5.0 convolution_convert_fusion.1
  197.6 1.4 convolution_convert_fusion.3
  201.9 3.5 collective-permute-done.24
  205.4 2.6 add_convert_fusion.1
  208.0 3.4 add_convert_fusion
  211.5 2.1 fusion.41
  216.5 3.7 collective-permute-done.21
  220.2 6.5 %collective-permute-done.25 = bf16[96,2176]{1,0:T(8,128)(2,1)S(1)} collective-permute-done((bf16[96,2176]{1,0:T(8,128)(2,1)S(1)}, bf16[96,2176]{1,0:T(8,128)(2,1)S(1)}, u32[]{:S(2)}, u32[]{:S(2)}) %collective-permute-start.25) | collective-permute-done | bytes 417824 | tf_op jit(solution)/shard_map/ppermute | solution.py:578
  226.7 2.5 collective-permute-done.19
  230.3 4.8 collective-permute-start.20
  235.4 1.4 fusion.45
  238.1 15.4 %collective-permute-done.20 = bf16[96,2176]{1,0:T(8,128)(2,1)} collective-permute-done((bf16[96,2176]{1,0:T(8,128)(2,1)}, bf16[96,2176]{1,0:T(8,128)(2,1)}, u32[]{:S(2)}, u32[]{:S(2)}) %collective-permute-start.20) | collective-permute-done | bytes 417824 | tf_op jit(solution)/shard_map/ppermute | solution.py:578
  253.6 1.8 fusion.15
  256.3 1.4 constant_dynamic-update-slice_fusion.5
  260.2 8.0 %collective-permute-done.28 = bf16[96,2048]{1,0:T(8,128)(2,1)S(1)} collective-permute-done((bf16[96,2048]{1,0:T(8,128)(2,1)S(1)}, bf16[96,2048]{1,0:T(8,128)(2,1)S(1)}, u32[]{:S(2)}, u32[]{:S(2)}) %collective-permute-start.28) | collective-permute-done | bytes 393248 | tf_op jit(solution)/shard_map/ppermute | solution.py:47
  269.2 2.3 collective-permute-start.29
  271.5 1.8 constant_dynamic-update-slice_fusion.4
  273.8 1.8 slice_dynamic-update-slice_fusion.5
  275.5 1.8 slice_dynamic-update-slice_fusion.4
  277.3 9.5 %out_grad.1 = bf16[8,448,1024]{2,1,0:T(8,128)(2,1)} custom-call(bf16[384,2048]{1,0:T(8,128)(2,1)} %bitcast.142, bf16[384,1024]{1,0:T(8,128)(2,1)} %get-tuple-element.87.o, bf16[8,96,2048]{2,1,0:T(8,128)(2,1)} %bitcast.154), custom_call_target="tpu_custom_call" | custom-call | flops 1048576 | bytes 65536 | tf_op jit(solution)/shard_map/out_grad/pallas_call | solution.py:551
  286.8 3.9 convolution_convert_fusion.2
  291.1 4.0 convolution_convert_fusion
  296.5 1.8 reshape.156
  298.3 28.9 %attend_back.1 = (bf16[8,272,1280]{2,1,0:T(8,128)(2,1)}, f32[8,128]{1,0:T(8,128)}, f32[1,2048]{1,0:T(1,128)}, f32[2,96,2048]{2,1,0:T(8,128)}, bf16[2,96,2048]{2,1,0:T(8,128)(2,1)}) custom-call(s32[2]{0:T(128)} %pad_add_fusion.rank_ref, bf16[384,2048]{1,0:T(8,128)(2,1)} %x.5, bf16[384,2048]{1,0:T(8,128)(2,1)} %get-tuple-element.66.xn, ...), custom_call_target="tpu_custom_call" | custom-call | flops 30000001024 | bytes 1048576 | tf_op jit(solution)/shard_map/attend_back/pallas_call | solution.py:290
  329.9 2.1 dynamic-slice_bitcast_fusion
  333.4 4.7 convert_add_fusion
  339.6 9.8 %collective-permute-done.40 = bf16[272,1280]{1,0:T(8,128)(2,1)S(1)} collective-permute-done((bf16[272,1280]{1,0:T(8,128)(2,1)S(1)}, bf16[272,1280]{1,0:T(8,128)(2,1)S(1)}, u32[]{:S(2)}, u32[]{:S(2)}) %collective-permute-start.40) | collective-permute-done | bytes 696352 | tf_op jit(solution)/shard_map/ppermute | solution.py:575
  349.8 1.3 collective-permute-start.36
  351.1 1.3 fusion.5
  352.4 30.2 %collective-permute-done.36 = bf16[96,2048]{1,0:T(8,128)(2,1)S(1)} collective-permute-done((bf16[96,2048]{1,0:T(8,128)(2,1)S(1)}, bf16[96,2048]{1,0:T(8,128)(2,1)S(1)}, u32[]{:S(2)}, u32[]{:S(2)}) %collective-permute-start.36) | collective-permute-done | bytes 393248 | tf_op jit(solution)/shard_map/ppermute | solution.py:47
  382.7 2.1 collective-permute-start.41
  385.3 1.7 constant_dynamic-update-slice_fusion.1
  387.0 1.3 collective-permute-start.46
  388.3 12.6 %collective-permute-done.41 = bf16[272,1280]{1,0:T(8,128)(2,1)S(1)} collective-permute-done((bf16[272,1280]{1,0:T(8,128)(2,1)S(1)}, bf16[272,1280]{1,0:T(8,128)(2,1)S(1)}, u32[]{:S(2)}, u32[]{:S(2)}) %collective-permute-start.41) | collective-permute-done | bytes 696352 | tf_op jit(solution)/shard_map/ppermute | solution.py:578
  402.0 1.7 fusion.4
  403.7 26.7 %collective-permute-done.37 = bf16[96,2048]{1,0:T(8,128)(2,1)S(1)} collective-permute-done((bf16[96,2048]{1,0:T(8,128)(2,1)S(1)}, bf16[96,2048]{1,0:T(8,128)(2,1)S(1)}, u32[]{:S(2)}, u32[]{:S(2)}) %collective-permute-start.37) | collective-permute-done | bytes 393248 | tf_op jit(solution)/shard_map/ppermute | solution.py:47
  430.4 12.3 %collective-permute-start.32 = (bf16[272,1280]{1,0:T(8,128)(2,1)S(1)}, bf16[272,1280]{1,0:T(8,128)(2,1)}, u32[]{:S(2)}, u32[]{:S(2)}) collective-permute-start(bf16[272,1280]{1,0:T(8,128)(2,1)S(1)} %get-tuple-element.169), channel_id=1, source_target_pairs={{0,16},{4,20},{8,24},{12,28},{16,0},{20,4},{24,8},{28,12},{1,17},{... | collective-permute-start | bytes 2088968 | tf_op jit(solution)/shard_map/ppermute | solution.py:578
  442.8 6.6 %collective-permute-start.38 = (bf16[2,96,2048]{2,1,0:T(8,128)(2,1)S(1)}, bf16[2,96,2048]{2,1,0:T(8,128)(2,1)S(1)}, u32[]{:S(2)}, u32[]{:S(2)}) collective-permute-start(bf16[2,96,2048]{2,1,0:T(8,128)(2,1)S(1)} %pad_maximum_fusion.2), channel_id=1, source_target_pairs={{0,1},{1,0},{2,3},{3,2},{4,5},{5,4},{6,7},{7,6},{8,9},{9,8},{10,11... | collective-permute-start | bytes 2359304 | tf_op jit(solution)/shard_map/ppermute | solution.py:47
  449.5 4.7 convert_add_fusion.1
  454.2 5.1 slice_add_fusion
  459.4 6.9 %collective-permute-done.42 = bf16[272,1280]{1,0:T(8,128)(2,1)S(1)} collective-permute-done((bf16[272,1280]{1,0:T(8,128)(2,1)S(1)}, bf16[272,1280]{1,0:T(8,128)(2,1)S(1)}, u32[]{:S(2)}, u32[]{:S(2)}) %collective-permute-start.42) | collective-permute-done | bytes 696352 | tf_op jit(solution)/shard_map/ppermute | solution.py:578
  466.4 2.1 bitcast_convert_fusion
  469.4 5.9 %collective-permute-done.32 = bf16[272,1280]{1,0:T(8,128)(2,1)} collective-permute-done((bf16[272,1280]{1,0:T(8,128)(2,1)S(1)}, bf16[272,1280]{1,0:T(8,128)(2,1)}, u32[]{:S(2)}, u32[]{:S(2)}) %collective-permute-start.32) | collective-permute-done | bytes 696352 | tf_op jit(solution)/shard_map/ppermute | solution.py:578
  475.3 2.2 fusion.6
  477.5 4.3 collective-permute-start.43
  488.0 1.3 copy.51
  489.3 8.7 %collective-permute-done.44 = bf16[16,1280]{1,0:T(8,128)(2,1)S(1)} collective-permute-done((bf16[16,1280]{1,0:T(8,128)(2,1)S(1)}, bf16[16,1280]{1,0:T(8,128)(2,1)S(1)}, u32[]{:S(2)}, u32[]{:S(2)}) %collective-permute-start.44) | collective-permute-done | bytes 40992 | tf_op jit(solution)/shard_map/ppermute | solution.py:47
  498.1 2.0 pad_maximum_fusion.1
  (241 shorter events, 60.8 us)
Async XLA Ops:
  7.2 83.2 %all-gather.2.cloned.1.call-start = ((), (), s32[]{:S(2)}) async-start(), calls=%async_computation.1 | async-start | bytes 3760128 | tf_op jit(solution)/shard_map/all_gather | solution.py:656
  9.9 465.3 %reduce-scatter.2.cloned.1.call-start = ((), (), s32[]{:S(2)}) async-start(), calls=%async_computation.2 | async-start | bytes 8257536 | tf_op jit(solution)/shard_map/reduce_scatter | solution.py:761
  10.0 35.6 %collective-permute-start.1 = (bf16[384,2048]{1,0:T(8,128)(2,1)}, bf16[384,2048]{1,0:T(8,128)(2,1)}, u32[]{:S(2)}, u32[]{:S(2)}) collective-permute-start(bf16[384,2048]{1,0:T(8,128)(2,1)} %bitcast.8.rest_2_.rest_4_), channel_id=1, source_target_pairs={{0,2},{1,3},{2,0},{3,1},{4,6},{5,7},{6,4},{7,5},{8,10},{9,11},{10,... | collective-permute-start | bytes 4718600 | tf_op jit(solution)/shard_map/ppermute | solution.py:47
  36.5 3.1 collective-permute-start
  45.6 9.2 %collective-permute-start.2 = (bf16[96,2048]{1,0:T(8,128)(2,1)S(1)}, bf16[96,2048]{1,0:T(8,128)(2,1)S(1)}, u32[]{:S(2)}, u32[]{:S(2)}) collective-permute-start(bf16[96,2048]{1,0:T(8,128)(2,1)S(1)} %fusion.31), channel_id=1, source_target_pairs={{0,2},{1,3},{2,0},{3,1},{4,6},{5,7},{6,4},{7,5},{8,10},{9,11},{10,... | collective-permute-start | bytes 1179656 | tf_op jit(solution)/shard_map/ppermute | solution.py:47
  57.1 76.3 %copy-start.16 = (bf16[96,2048]{1,0:T(8,128)(2,1)}, bf16[96,2048]{1,0:T(8,128)(2,1)S(1)}, u32[]{:S(2)}) copy-start(bf16[96,2048]{1,0:T(8,128)(2,1)S(1)} %get-tuple-element.163) | copy-start | bytes 1179652
  57.1 12.7 %collective-permute-start.3 = (bf16[96,2048]{1,0:T(8,128)(2,1)S(1)}, bf16[96,2048]{1,0:T(8,128)(2,1)}, u32[]{:S(2)}, u32[]{:S(2)}) collective-permute-start(bf16[96,2048]{1,0:T(8,128)(2,1)S(1)} %get-tuple-element.163), channel_id=1, source_target_pairs={{0,4},{4,0},{8,12},{12,8},{16,20},{20,16},{24,28},{28,24},{1,5},{5... | collective-permute-start | bytes 1179656 | tf_op jit(solution)/shard_map/ppermute | solution.py:575
  58.4 45.1 %collective-permute-start.10 = (bf16[384,2048]{1,0:T(8,128)(2,1)}, bf16[384,2048]{1,0:T(8,128)(2,1)}, u32[]{:S(2)}, u32[]{:S(2)}) collective-permute-start(bf16[384,2048]{1,0:T(8,128)(2,1)} %bitcast.8.rest_2_.rest_4_), channel_id=1, source_target_pairs={{0,1},{1,0},{2,3},{3,2},{4,5},{5,4},{6,7},{7,6},{8,9},{9,8},{10,11... | collective-permute-start | bytes 4718600 | tf_op jit(solution)/shard_map/ppermute | solution.py:47
  61.1 44.5 %collective-permute-start.13 = (bf16[384,2048]{1,0:T(8,128)(2,1)}, bf16[384,2048]{1,0:T(8,128)(2,1)}, u32[]{:S(2)}, u32[]{:S(2)}) collective-permute-start(bf16[384,2048]{1,0:T(8,128)(2,1)} %bitcast.21.rest_3_.rest_5_), channel_id=1, source_target_pairs={{0,2},{1,3},{2,0},{3,1},{4,6},{5,7},{6,4},{7,5},{8,10},{9,11},{10,... | collective-permute-start | bytes 4718600 | tf_op jit(solution)/shard_map/ppermute | solution.py:47
  62.3 68.8 %collective-permute-start.16 = (bf16[384,2048]{1,0:T(8,128)(2,1)}, bf16[384,2048]{1,0:T(8,128)(2,1)}, u32[]{:S(2)}, u32[]{:S(2)}) collective-permute-start(bf16[384,2048]{1,0:T(8,128)(2,1)} %bitcast.23.rest_6_.rest_12_), channel_id=1, source_target_pairs={{0,2},{1,3},{2,0},{3,1},{4,6},{5,7},{6,4},{7,5},{8,10},{9,11},{10,... | collective-permute-start | bytes 4718600 | tf_op jit(solution)/shard_map/ppermute | solution.py:47
  62.6 26.6 %collective-permute-start.4 = (bf16[96,2048]{1,0:T(8,128)(2,1)S(1)}, bf16[96,2048]{1,0:T(8,128)(2,1)S(1)}, u32[]{:S(2)}, u32[]{:S(2)}) collective-permute-start(bf16[96,2048]{1,0:T(8,128)(2,1)S(1)} %get-tuple-element.163), channel_id=1, source_target_pairs={{0,8},{4,12},{8,0},{12,4},{16,24},{20,28},{24,16},{28,20},{1,9},{5... | collective-permute-start | bytes 1179656 | tf_op jit(solution)/shard_map/ppermute | solution.py:578
  69.8 21.4 %collective-permute-start.6 = (bf16[96,2048]{1,0:T(8,128)(2,1)S(1)}, bf16[96,2048]{1,0:T(8,128)(2,1)}, u32[]{:S(2)}, u32[]{:S(2)}) collective-permute-start(bf16[96,2048]{1,0:T(8,128)(2,1)S(1)} %get-tuple-element.163), channel_id=1, source_target_pairs={{0,16},{4,20},{8,24},{12,28},{16,0},{20,4},{24,8},{28,12},{1,17},{... | collective-permute-start | bytes 1179656 | tf_op jit(solution)/shard_map/ppermute | solution.py:578
  89.9 12.1 %collective-permute-start.8 = (bf16[96,2048]{1,0:T(8,128)(2,1)S(1)}, bf16[96,2048]{1,0:T(8,128)(2,1)}, u32[]{:S(2)}, u32[]{:S(2)}) collective-permute-start(bf16[96,2048]{1,0:T(8,128)(2,1)S(1)} %get-tuple-element.163), channel_id=1, source_target_pairs={{0,24},{4,28},{8,16},{12,20},{16,8},{20,12},{24,0},{28,4},{1,25},{... | collective-permute-start | bytes 1179656 | tf_op jit(solution)/shard_map/ppermute | solution.py:578
  91.2 11.2 %collective-permute-start.5 = (bf16[96,2048]{1,0:T(8,128)(2,1)}, bf16[96,2048]{1,0:T(8,128)(2,1)S(1)}, u32[]{:S(2)}, u32[]{:S(2)}) collective-permute-start(bf16[96,2048]{1,0:T(8,128)(2,1)} %copy-done.35), channel_id=1, source_target_pairs={{0,4},{4,0},{8,12},{12,8},{16,20},{20,16},{24,28},{28,24},{1,5},{5... | collective-permute-start | bytes 1179656 | tf_op jit(solution)/shard_map/ppermute | solution.py:575
  102.1 29.9 %collective-permute-start.7 = (bf16[96,2048]{1,0:T(8,128)(2,1)}, bf16[96,2048]{1,0:T(8,128)(2,1)S(1)}, u32[]{:S(2)}, u32[]{:S(2)}) collective-permute-start(bf16[96,2048]{1,0:T(8,128)(2,1)} %collective-permute-done.6), channel_id=1, source_target_pairs={{0,4},{4,0},{8,12},{12,8},{16,20},{20,16},{24,28},{28,24},{1,5},{5... | collective-permute-start | bytes 1179656 | tf_op jit(solution)/shard_map/ppermute | solution.py:575
  102.4 29.5 %collective-permute-start.9 = (bf16[96,2048]{1,0:T(8,128)(2,1)}, bf16[96,2048]{1,0:T(8,128)(2,1)S(1)}, u32[]{:S(2)}, u32[]{:S(2)}) collective-permute-start(bf16[96,2048]{1,0:T(8,128)(2,1)} %collective-permute-done.8), channel_id=1, source_target_pairs={{0,4},{4,0},{8,12},{12,8},{16,20},{20,16},{24,28},{28,24},{1,5},{5... | collective-permute-start | bytes 1179656 | tf_op jit(solution)/shard_map/ppermute | solution.py:575
  103.6 31.0 %collective-permute-start.11 = (bf16[384,2048]{1,0:T(8,128)(2,1)}, bf16[384,2048]{1,0:T(8,128)(2,1)S(1)}, u32[]{:S(2)}, u32[]{:S(2)}) collective-permute-start(bf16[384,2048]{1,0:T(8,128)(2,1)} %bitcast.21.rest_3_.rest_5_), channel_id=1, source_target_pairs={{0,1},{1,0},{2,3},{3,2},{4,5},{5,4},{6,7},{7,6},{8,9},{9,8},{10,11... | collective-permute-start | bytes 4718600 | tf_op jit(solution)/shard_map/ppermute | solution.py:47
  105.6 29.0 %collective-permute-start.12 = (bf16[384,2048]{1,0:T(8,128)(2,1)}, bf16[384,2048]{1,0:T(8,128)(2,1)}, u32[]{:S(2)}, u32[]{:S(2)}) collective-permute-start(bf16[384,2048]{1,0:T(8,128)(2,1)} %bitcast.23.rest_6_.rest_12_), channel_id=1, source_target_pairs={{0,1},{1,0},{2,3},{3,2},{4,5},{5,4},{6,7},{7,6},{8,9},{9,8},{10,11... | collective-permute-start | bytes 4718600 | tf_op jit(solution)/shard_map/ppermute | solution.py:47
  131.1 23.5 %collective-permute-start.14 = (bf16[384,2048]{1,0:T(8,128)(2,1)}, bf16[384,2048]{1,0:T(8,128)(2,1)}, u32[]{:S(2)}, u32[]{:S(2)}) collective-permute-start(bf16[384,2048]{1,0:T(8,128)(2,1)} %collective-permute-done.1.rest_8_), channel_id=1, source_target_pairs={{0,1},{1,0},{2,3},{3,2},{4,5},{5,4},{6,7},{7,6},{8,9},{9,8},{10,11... | collective-permute-start | bytes 4718600 | tf_op jit(solution)/shard_map/ppermute | solution.py:47
  131.9 22.7 %collective-permute-start.15 = (bf16[384,2048]{1,0:T(8,128)(2,1)}, bf16[384,2048]{1,0:T(8,128)(2,1)}, u32[]{:S(2)}, u32[]{:S(2)}) collective-permute-start(bf16[384,2048]{1,0:T(8,128)(2,1)} %collective-permute-done.13.rest_9_), channel_id=1, source_target_pairs={{0,1},{1,0},{2,3},{3,2},{4,5},{5,4},{6,7},{7,6},{8,9},{9,8},{10,11... | collective-permute-start | bytes 4718600 | tf_op jit(solution)/shard_map/ppermute | solution.py:47
  131.9 22.7 %collective-permute-start.17 = (bf16[384,2048]{1,0:T(8,128)(2,1)}, bf16[384,2048]{1,0:T(8,128)(2,1)}, u32[]{:S(2)}, u32[]{:S(2)}) collective-permute-start(bf16[384,2048]{1,0:T(8,128)(2,1)} %collective-permute-done.16.rest_14_), channel_id=1, source_target_pairs={{0,1},{1,0},{2,3},{3,2},{4,5},{5,4},{6,7},{7,6},{8,9},{9,8},{10,11... | collective-permute-start | bytes 4718600 | tf_op jit(solution)/shard_map/ppermute | solution.py:47
  197.4 10.6 %collective-permute-start.23 = (bf16[768,2048]{1,0:T(8,128)(2,1)S(1)}, bf16[768,2048]{1,0:T(8,128)(2,1)S(1)}, u32[]{:S(2)}, u32[]{:S(2)}) collective-permute-start(bf16[768,2048]{1,0:T(8,128)(2,1)S(1)} %convolution_convert_fusion.1), channel_id=1, source_target_pairs={{0,1},{1,0},{2,3},{3,2},{4,5},{5,4},{6,7},{7,6},{8,9},{9,8},{10,11... | collective-permute-start | bytes 9437192 | tf_op jit(solution)/shard_map/ppermute | solution.py:47
  199.0 6.4 %collective-permute-start.24 = (bf16[384,2048]{1,0:T(8,128)(2,1)S(1)}, bf16[384,2048]{1,0:T(8,128)(2,1)S(1)}, u32[]{:S(2)}, u32[]{:S(2)}) collective-permute-start(bf16[384,2048]{1,0:T(8,128)(2,1)S(1)} %convolution_convert_fusion.3), channel_id=1, source_target_pairs={{0,1},{1,0},{2,3},{3,2},{4,5},{5,4},{6,7},{7,6},{8,9},{9,8},{10,11... | collective-permute-start | bytes 4718600 | tf_op jit(solution)/shard_map/ppermute | solution.py:47
  200.4 13.2 %collective-permute-start.22 = (bf16[96,2176]{1,0:T(8,128)(2,1)S(1)}, bf16[96,2176]{1,0:T(8,128)(2,1)S(1)}, u32[]{:S(2)}, u32[]{:S(2)}) collective-permute-start(bf16[96,2176]{1,0:T(8,128)(2,1)S(1)} %get-tuple-element.177), channel_id=1, source_target_pairs={{0,4},{4,0},{8,12},{12,8},{16,20},{20,16},{24,28},{28,24},{1,5},{5... | collective-permute-start | bytes 1253384 | tf_op jit(solution)/shard_map/ppermute | solution.py:575
  200.6 7.4 %copy-start.42 = (bf16[768,1536]{1,0:T(8,128)(2,1)S(1)}, bf16[768,1536]{1,0:T(8,128)(2,1)}, u32[]{:S(2)}) copy-start(bf16[768,1536]{1,0:T(8,128)(2,1)} %get-tuple-element.77) | copy-start | bytes 7077892
  200.6 19.6 %collective-permute-start.21 = (bf16[96,2176]{1,0:T(8,128)(2,1)S(1)}, bf16[96,2176]{1,0:T(8,128)(2,1)S(1)}, u32[]{:S(2)}, u32[]{:S(2)}) collective-permute-start(bf16[96,2176]{1,0:T(8,128)(2,1)S(1)} %get-tuple-element.178), channel_id=1, source_target_pairs={{0,4},{4,0},{8,12},{12,8},{16,20},{20,16},{24,28},{28,24},{1,5},{5... | collective-permute-start | bytes 1253384 | tf_op jit(solution)/shard_map/ppermute | solution.py:575
  213.7 21.7 %copy-start.33 = (bf16[2048,16]{0,1:T(8,128)(2,1)S(1)}, bf16[2048,16]{0,1:T(8,128)(2,1)}, u32[]{:S(2)}) copy-start(bf16[2048,16]{0,1:T(8,128)(2,1)} %param.30) | copy-start | bytes 196612
  213.7 13.0 %collective-permute-start.25 = (bf16[96,2176]{1,0:T(8,128)(2,1)S(1)}, bf16[96,2176]{1,0:T(8,128)(2,1)S(1)}, u32[]{:S(2)}, u32[]{:S(2)}) collective-permute-start(bf16[96,2176]{1,0:T(8,128)(2,1)S(1)} %fusion.13), channel_id=1, source_target_pairs={{0,24},{4,28},{8,16},{12,20},{16,8},{20,12},{24,0},{28,4},{1,25},{... | collective-permute-start | bytes 1253384 | tf_op jit(solution)/shard_map/ppermute | solution.py:578
  213.8 15.4 %collective-permute-start.19 = (bf16[96,2176]{1,0:T(8,128)(2,1)S(1)}, bf16[96,2176]{1,0:T(8,128)(2,1)S(1)}, u32[]{:S(2)}, u32[]{:S(2)}) collective-permute-start(bf16[96,2176]{1,0:T(8,128)(2,1)S(1)} %get-tuple-element.176), channel_id=1, source_target_pairs={{0,4},{4,0},{8,12},{12,8},{16,20},{20,16},{24,28},{28,24},{1,5},{5... | collective-permute-start | bytes 1253384 | tf_op jit(solution)/shard_map/ppermute | solution.py:575
  214.1 39.5 %collective-permute-start.27 = (bf16[384,2048]{1,0:T(8,128)(2,1)}, bf16[384,2048]{1,0:T(8,128)(2,1)}, u32[]{:S(2)}, u32[]{:S(2)}) collective-permute-start(bf16[384,2048]{1,0:T(8,128)(2,1)} %get-tuple-element.181), channel_id=1, source_target_pairs={{0,2},{1,3},{2,0},{3,1},{4,6},{5,7},{6,4},{7,5},{8,10},{9,11},{10,... | collective-permute-start | bytes 4718600 | tf_op jit(solution)/shard_map/ppermute | solution.py:47
  215.3 22.9 %collective-permute-start.18 = (bf16[96,2176]{1,0:T(8,128)(2,1)}, bf16[96,2176]{1,0:T(8,128)(2,1)}, u32[]{:S(2)}, u32[]{:S(2)}) collective-permute-start(bf16[96,2176]{1,0:T(8,128)(2,1)} %get-tuple-element.179), channel_id=1, source_target_pairs={{0,4},{4,0},{8,12},{12,8},{16,20},{20,16},{24,28},{28,24},{1,5},{5... | collective-permute-start | bytes 1253384 | tf_op jit(solution)/shard_map/ppermute | solution.py:575
  230.3 23.2 %collective-permute-start.20 = (bf16[96,2176]{1,0:T(8,128)(2,1)}, bf16[96,2176]{1,0:T(8,128)(2,1)}, u32[]{:S(2)}, u32[]{:S(2)}) collective-permute-start(bf16[96,2176]{1,0:T(8,128)(2,1)} %get-tuple-element.174), channel_id=1, source_target_pairs={{0,16},{4,20},{8,24},{12,28},{16,0},{20,4},{24,8},{28,12},{1,17},{... | collective-permute-start | bytes 1253384 | tf_op jit(solution)/shard_map/ppermute | solution.py:578
  235.1 18.4 %collective-permute-start.26 = (bf16[96,2176]{1,0:T(8,128)(2,1)}, bf16[96,2176]{1,0:T(8,128)(2,1)}, u32[]{:S(2)}, u32[]{:S(2)}) collective-permute-start(bf16[96,2176]{1,0:T(8,128)(2,1)} %get-tuple-element.175), channel_id=1, source_target_pairs={{0,8},{4,12},{8,0},{12,4},{16,24},{20,28},{24,16},{28,20},{1,9},{5... | collective-permute-start | bytes 1253384 | tf_op jit(solution)/shard_map/ppermute | solution.py:578
  236.9 18.7 %copy-start.4 = (f32[96,2048]{1,0:T(8,128)S(1)}, f32[96,2048]{1,0:T(8,128)}, u32[]{:S(2)}) copy-start(f32[96,2048]{1,0:T(8,128)} %copy-done.3) | copy-start | bytes 2359300
  236.9 18.7 %copy-start.39 = (f32[96]{0:T(128)S(1)}, f32[96]{0:T(128)}, u32[]{:S(2)}) copy-start(f32[96]{0:T(128)} %copy-done.38) | copy-start | bytes 1156
  259.0 9.2 %collective-permute-start.28 = (bf16[96,2048]{1,0:T(8,128)(2,1)S(1)}, bf16[96,2048]{1,0:T(8,128)(2,1)S(1)}, u32[]{:S(2)}, u32[]{:S(2)}) collective-permute-start(bf16[96,2048]{1,0:T(8,128)(2,1)S(1)} %get-tuple-element.161), channel_id=1, source_target_pairs={{0,2},{1,3},{2,0},{3,1},{4,6},{5,7},{6,4},{7,5},{8,10},{9,11},{10,... | collective-permute-start | bytes 1179656 | tf_op jit(solution)/shard_map/ppermute | solution.py:47
  269.2 4.6 collective-permute-start.29
  290.7 152.0 %collective-permute-start.47 = (bf16[384,2048]{1,0:T(8,128)(2,1)}, bf16[384,2048]{1,0:T(8,128)(2,1)}, u32[]{:S(2)}, u32[]{:S(2)}) collective-permute-start(bf16[384,2048]{1,0:T(8,128)(2,1)} %convolution_convert_fusion.2), channel_id=1, source_target_pairs={{0,1},{1,0},{2,3},{3,2},{4,5},{5,4},{6,7},{7,6},{8,9},{9,8},{10,11... | collective-permute-start | bytes 4718600 | tf_op jit(solution)/shard_map/ppermute | solution.py:47
  295.2 37.2 %collective-permute-start.45 = (bf16[768,2048]{1,0:T(8,128)(2,1)}, bf16[768,2048]{1,0:T(8,128)(2,1)}, u32[]{:S(2)}, u32[]{:S(2)}) collective-permute-start(bf16[768,2048]{1,0:T(8,128)(2,1)} %convolution_convert_fusion), channel_id=1, source_target_pairs={{0,1},{1,0},{2,3},{3,2},{4,5},{5,4},{6,7},{7,6},{8,9},{9,8},{10,11... | collective-permute-start | bytes 9437192 | tf_op jit(solution)/shard_map/ppermute | solution.py:47
  327.9 21.6 %collective-permute-start.35 = (bf16[2,96,2048]{2,1,0:T(8,128)(2,1)}, bf16[2,96,2048]{2,1,0:T(8,128)(2,1)S(1)}, u32[]{:S(2)}, u32[]{:S(2)}) collective-permute-start(bf16[2,96,2048]{2,1,0:T(8,128)(2,1)} %get-tuple-element.102), channel_id=1, source_target_pairs={{0,1},{1,0},{2,3},{3,2},{4,5},{5,4},{6,7},{7,6},{8,9},{9,8},{10,11... | collective-permute-start | bytes 2359304 | tf_op jit(solution)/shard_map/ppermute | solution.py:47
  332.0 17.5 %copy-start.27 = (f32[2,96,2048]{2,1,0:T(8,128)S(1)}, f32[2,96,2048]{2,1,0:T(8,128)}, u32[]{:S(2)}) copy-start(f32[2,96,2048]{2,1,0:T(8,128)} %get-tuple-element.101) | copy-start | bytes 4718596
  332.0 17.3 %collective-permute-start.40 = (bf16[272,1280]{1,0:T(8,128)(2,1)S(1)}, bf16[272,1280]{1,0:T(8,128)(2,1)S(1)}, u32[]{:S(2)}, u32[]{:S(2)}) collective-permute-start(bf16[272,1280]{1,0:T(8,128)(2,1)S(1)} %get-tuple-element.170), channel_id=1, source_target_pairs={{0,4},{4,0},{8,12},{12,8},{16,20},{20,16},{24,28},{28,24},{1,5},{5... | collective-permute-start | bytes 2088968 | tf_op jit(solution)/shard_map/ppermute | solution.py:575
  338.1 104.7 %collective-permute-start.48 = (bf16[384,2048]{1,0:T(8,128)(2,1)S(1)}, bf16[384,2048]{1,0:T(8,128)(2,1)S(1)}, u32[]{:S(2)}, u32[]{:S(2)}) collective-permute-start(bf16[384,2048]{1,0:T(8,128)(2,1)S(1)} %copy-done.43), channel_id=1, source_target_pairs={{0,2},{1,3},{2,0},{3,1},{4,6},{5,7},{6,4},{7,5},{8,10},{9,11},{10,... | collective-permute-start | bytes 4718600 | tf_op jit(solution)/shard_map/ppermute | solution.py:47
  339.4 47.7 %collective-permute-start.39 = (bf16[272,1280]{1,0:T(8,128)(2,1)S(1)}, bf16[272,1280]{1,0:T(8,128)(2,1)S(1)}, u32[]{:S(2)}, u32[]{:S(2)}) collective-permute-start(bf16[272,1280]{1,0:T(8,128)(2,1)S(1)} %get-tuple-element.171), channel_id=1, source_target_pairs={{0,4},{4,0},{8,12},{12,8},{16,20},{20,16},{24,28},{28,24},{1,5},{5... | collective-permute-start | bytes 2088968 | tf_op jit(solution)/shard_map/ppermute | solution.py:575
  349.4 51.6 %collective-permute-start.31 = (bf16[272,1280]{1,0:T(8,128)(2,1)S(1)}, bf16[272,1280]{1,0:T(8,128)(2,1)S(1)}, u32[]{:S(2)}, u32[]{:S(2)}) collective-permute-start(bf16[272,1280]{1,0:T(8,128)(2,1)S(1)} %get-tuple-element.172), channel_id=1, source_target_pairs={{0,4},{4,0},{8,12},{12,8},{16,20},{20,16},{24,28},{28,24},{1,5},{5... | collective-permute-start | bytes 2088968 | tf_op jit(solution)/shard_map/ppermute | solution.py:575
  349.7 35.1 %copy-start.15 = (bf16[384,2048]{1,0:T(8,128)(2,1)S(1)}, bf16[384,2048]{1,0:T(8,128)(2,1)}, u32[]{:S(2)}) copy-start(bf16[384,2048]{1,0:T(8,128)(2,1)} %x.5) | copy-start | bytes 4718596
  349.7 35.0 %copy-start.37 = (f32[2048]{0:T(1024)S(1)}, f32[2048]{0:T(1024)}, u32[]{:S(2)}) copy-start(f32[2048]{0:T(1024)} %param.22) | copy-start | bytes 24580
  349.8 32.9 %collective-permute-start.36 = (bf16[96,2048]{1,0:T(8,128)(2,1)S(1)}, bf16[96,2048]{1,0:T(8,128)(2,1)S(1)}, u32[]{:S(2)}, u32[]{:S(2)}) collective-permute-start(bf16[96,2048]{1,0:T(8,128)(2,1)S(1)} %fusion.32), channel_id=1, source_target_pairs={{0,2},{1,3},{2,0},{3,1},{4,6},{5,7},{6,4},{7,5},{8,10},{9,11},{10,... | collective-permute-start | bytes 1179656 | tf_op jit(solution)/shard_map/ppermute | solution.py:47
  352.4 32.9 %copy-start.5 = (f32[96,2048]{1,0:T(8,128)S(1)}, f32[96,2048]{1,0:T(8,128)}, u32[]{:S(2)}) copy-start(f32[96,2048]{1,0:T(8,128)} %copy-done.3) | copy-start | bytes 2359300
  352.4 32.9 %copy-start.12 = (f32[96,2048]{1,0:T(8,128)S(1)}, f32[96,2048]{1,0:T(8,128)}, u32[]{:S(2)}) copy-start(f32[96,2048]{1,0:T(8,128)} %copy-done.11) | copy-start | bytes 2359300
  382.7 18.3 %collective-permute-start.41 = (bf16[272,1280]{1,0:T(8,128)(2,1)S(1)}, bf16[272,1280]{1,0:T(8,128)(2,1)S(1)}, u32[]{:S(2)}, u32[]{:S(2)}) collective-permute-start(bf16[272,1280]{1,0:T(8,128)(2,1)S(1)} %fusion.5), channel_id=1, source_target_pairs={{0,24},{4,28},{8,16},{12,20},{16,8},{20,12},{24,0},{28,4},{1,25},{... | collective-permute-start | bytes 2088968 | tf_op jit(solution)/shard_map/ppermute | solution.py:578
  387.0 67.2 %collective-permute-start.46 = (bf16[384,2048]{1,0:T(8,128)(2,1)S(1)}, bf16[384,2048]{1,0:T(8,128)(2,1)S(1)}, u32[]{:S(2)}, u32[]{:S(2)}) collective-permute-start(bf16[384,2048]{1,0:T(8,128)(2,1)S(1)} %copy-done.26), channel_id=1, source_target_pairs={{0,2},{1,3},{2,0},{3,1},{4,6},{5,7},{6,4},{7,5},{8,10},{9,11},{10,... | collective-permute-start | bytes 4718600 | tf_op jit(solution)/shard_map/ppermute | solution.py:47
  401.0 67.6 %collective-permute-start.30 = (bf16[272,1280]{1,0:T(8,128)(2,1)S(1)}, bf16[272,1280]{1,0:T(8,128)(2,1)S(1)}, u32[]{:S(2)}, u32[]{:S(2)}) collective-permute-start(bf16[272,1280]{1,0:T(8,128)(2,1)S(1)} %get-tuple-element.173), channel_id=1, source_target_pairs={{0,4},{4,0},{8,12},{12,8},{16,20},{20,16},{24,28},{28,24},{1,5},{5... | collective-permute-start | bytes 2088968 | tf_op jit(solution)/shard_map/ppermute | solution.py:575
  401.0 29.4 %collective-permute-start.37 = (bf16[96,2048]{1,0:T(8,128)(2,1)S(1)}, bf16[96,2048]{1,0:T(8,128)(2,1)S(1)}, u32[]{:S(2)}, u32[]{:S(2)}) collective-permute-start(bf16[96,2048]{1,0:T(8,128)(2,1)S(1)} %get-tuple-element.157), channel_id=1, source_target_pairs={{0,2},{1,3},{2,0},{3,1},{4,6},{5,7},{6,4},{7,5},{8,10},{9,11},{10,... | collective-permute-start | bytes 1179656 | tf_op jit(solution)/shard_map/ppermute | solution.py:47
  403.7 45.8 %copy-start.20 = (bf16[768,768]{1,0:T(8,128)(2,1)S(1)}, bf16[768,768]{1,0:T(8,128)(2,1)}, u32[]{:S(2)}) copy-start(bf16[768,768]{1,0:T(8,128)(2,1)} %get-tuple-element.73.rest_3_) | copy-start | bytes 3538948
  430.4 44.9 %collective-permute-start.32 = (bf16[272,1280]{1,0:T(8,128)(2,1)S(1)}, bf16[272,1280]{1,0:T(8,128)(2,1)}, u32[]{:S(2)}, u32[]{:S(2)}) collective-permute-start(bf16[272,1280]{1,0:T(8,128)(2,1)S(1)} %get-tuple-element.169), channel_id=1, source_target_pairs={{0,16},{4,20},{8,24},{12,28},{16,0},{20,4},{24,8},{28,12},{1,17},{... | collective-permute-start | bytes 2088968 | tf_op jit(solution)/shard_map/ppermute | solution.py:578
  442.8 23.5 %collective-permute-start.42 = (bf16[272,1280]{1,0:T(8,128)(2,1)S(1)}, bf16[272,1280]{1,0:T(8,128)(2,1)S(1)}, u32[]{:S(2)}, u32[]{:S(2)}) collective-permute-start(bf16[272,1280]{1,0:T(8,128)(2,1)S(1)} %get-tuple-element.168), channel_id=1, source_target_pairs={{0,8},{4,12},{8,0},{12,4},{16,24},{20,28},{24,16},{28,20},{1,9},{5... | collective-permute-start | bytes 2088968 | tf_op jit(solution)/shard_map/ppermute | solution.py:578
  442.8 23.4 %collective-permute-start.38 = (bf16[2,96,2048]{2,1,0:T(8,128)(2,1)S(1)}, bf16[2,96,2048]{2,1,0:T(8,128)(2,1)S(1)}, u32[]{:S(2)}, u32[]{:S(2)}) collective-permute-start(bf16[2,96,2048]{2,1,0:T(8,128)(2,1)S(1)} %pad_maximum_fusion.2), channel_id=1, source_target_pairs={{0,1},{1,0},{2,3},{3,2},{4,5},{5,4},{6,7},{7,6},{8,9},{9,8},{10,11... | collective-permute-start | bytes 2359304 | tf_op jit(solution)/shard_map/ppermute | solution.py:47
  466.4 8.9 %copy-start.30 = (bf16[272,1280]{1,0:T(8,128)(2,1)S(1)}, bf16[272,1280]{1,0:T(8,128)(2,1)}, u32[]{:S(2)}) copy-start(bf16[272,1280]{1,0:T(8,128)(2,1)} %copy-done.29) | copy-start | bytes 2088964
  477.5 9.8 %collective-permute-start.43 = (bf16[16,1280]{1,0:T(8,128)(2,1)S(1)}, bf16[16,1280]{1,0:T(8,128)(2,1)S(1)}, u32[]{:S(2)}, u32[]{:S(2)}) collective-permute-start(bf16[16,1280]{1,0:T(8,128)(2,1)S(1)} %slice.219), channel_id=1, source_target_pairs={{0,1},{1,0},{2,3},{3,2},{4,5},{5,4},{6,7},{7,6},{8,9},{9,8},{10,11... | collective-permute-start | bytes 122888 | tf_op jit(solution)/shard_map/ppermute | solution.py:47
  486.3 11.7 %collective-permute-start.33 = (bf16[96,2048]{1,0:T(8,128)(2,1)S(1)}, bf16[96,2048]{1,0:T(8,128)(2,1)}, u32[]{:S(2)}, u32[]{:S(2)}) collective-permute-start(bf16[96,2048]{1,0:T(8,128)(2,1)S(1)} %get-tuple-element.159), channel_id=1, source_target_pairs={{0,2},{1,3},{2,0},{3,1},{4,6},{5,7},{6,4},{7,5},{8,10},{9,11},{10,... | collective-permute-start | bytes 1179656 | tf_op jit(solution)/shard_map/ppermute | solution.py:47
  487.3 10.7 %collective-permute-start.44 = (bf16[16,1280]{1,0:T(8,128)(2,1)S(1)}, bf16[16,1280]{1,0:T(8,128)(2,1)S(1)}, u32[]{:S(2)}, u32[]{:S(2)}) collective-permute-start(bf16[16,1280]{1,0:T(8,128)(2,1)S(1)} %fusion.34), channel_id=1, source_target_pairs={{0,2},{1,3},{2,0},{3,1},{4,6},{5,7},{6,4},{7,5},{8,10},{9,11},{10,... | collective-permute-start | bytes 122888 | tf_op jit(solution)/shard_map/ppermute | solution.py:47
  489.3 14.2 %copy-start.24 = (bf16[4,96,2048]{2,1,0:T(8,128)(2,1)S(1)}, bf16[4,96,2048]{2,1,0:T(8,128)(2,1)}, u32[]{:S(2)}) copy-start(bf16[4,96,2048]{2,1,0:T(8,128)(2,1)} %copy-done.23) | copy-start | bytes 4718596
  500.0 4.5 collective-permute-start.34
  (32 other events, 94.9 us)
Sparse Core Ops, SparseCore 0:
  10.8 74.5 all-gather.1
  286.9 170.7 reduce-scatter.1

commit v4 on v3

--- a/solution.py
+++ b/solution.py
@@ -532,38 +532,6 @@
     )(ranks, hn, sent, *extra, *in_mats, *down_mats)
 
 
-def out_grad_kernel(dattn, o, y, packed):
-    many, height, width = y.shape
-    cols = o.shape[1]
-    rows = dattn.shape[1] // many
-    packed[:, :rows, :] = bf(mm(dattn[...], o[...], (0, 0))).reshape(many, rows, cols)
-    for i in range(width // cols):
-        packed[:, rows + i * height : rows + (i + 1) * height, :] = y[:, :, i * cols : (i + 1) * cols]
-
-
-def out_grad(dattn, o, y):
-    tokens, width = dattn.shape
-    blocks, height, _ = y.shape
-    cols = o.shape[1]
-    rows = width // blocks
-    many = max(1, 256 // rows)
-    full = rows + height * (width // cols)
-    return pl.pallas_call(
-        out_grad_kernel,
-        grid=(blocks // many,),
-        in_specs=[
-            pl.BlockSpec((tokens, many * rows), lambda i: (0, i)),
-            whole(o.shape),
-            pl.BlockSpec((many, height, width), lambda i: (i, 0, 0)),
-        ],
-        out_specs=pl.BlockSpec((many, full, cols), lambda i: (i, 0, 0)),
-        out_shape=jax.ShapeDtypeStruct((blocks, full, cols), jnp.bfloat16),
-        compiler_params=pltpu.CompilerParams(vmem_limit_bytes=vmem_bytes),
-        cost_estimate=small_cost,
-        name="out_grad",
-    )(dattn, o, y)
-
-
 class Tokens:
     def __init__(self):
         self.size = lax.axis_size("expert")
@@ -593,10 +561,10 @@
                 rows = lax.dynamic_update_index_in_dim(rows, value, self.place(step, other), 0)
         return rows, early
 
-    def scatter(self, parts, begun, late, last):
+    def scatter(self, parts, begun, late, last, middle=()):
         if not self.line:
             total = lax.psum_scatter(parts, "expert", scatter_dimension=0, tiled=False)
-            return total.astype(jnp.float32), begun, late, last
+            return total.astype(jnp.float32), begun, late, last, middle
 
         def part(step, other):
             return lax.dynamic_index_in_dim(parts, self.place(step, other), 0, False)
@@ -607,11 +575,12 @@
         across = {step: self.across(part(step, True)) for step in (3, 2, 1, 0)}
         across[3], begun = tie(across[3], begun)
         moved = {step: self.along(bf(pair_sum(step)), step) for step in (3, 2)}
-        across[1], moved[3] = tie(across[1], moved[3])
+        across[1], moved[3], middle = tie(across[1], moved[3], middle)
         moved[1] = self.along(bf(pair_sum(1)), 1)
         across[0], moved[2], late = tie(across[0], moved[2], late)
         moved[1], last = tie(moved[1], last)
-        return pair_sum(0) + sum(value.astype(jnp.float32) for value in moved.values()), begun, late, last
+        total = pair_sum(0) + sum(value.astype(jnp.float32) for value in moved.values())
+        return total, begun, late, last, middle
 
 
 def body(
@@ -699,8 +668,11 @@
 
     gates_own = gates_of(normed_ffn, mask_own)
     far_up = swap(own_mats[1], 2)
-    far_mats = [far_gate, far_up, swap(own_mats[2], 2)]
-    normed_all, sent = order.gather(normed_ffn, sent)
+    far_down = swap(own_mats[2], 2)
+    normed_all, (sent, far_up) = order.gather(normed_ffn, (sent, far_up))
+    normed_all, attended_rows, far_down = tie(normed_all, attended_rows, far_down)
+    far_mats = [far_gate, far_up, far_down]
+    attended_all = lax.all_gather(attended_rows, "expert", axis=0, tiled=True)
     normed_all = normed_all.reshape(group * shard_rows, model_width)
     grad_all = sent[:, :model_width]
     near_mats = [swap(value, 1) for value in own_mats]
@@ -736,8 +708,8 @@
 
     far_part = tuple(far_part)
     arrived = [swap(far_part[0], 2)]
-    back_sum, far_part, _, arrived[0] = order.scatter(
-        back_part.reshape(group, shard_rows, -1), far_part, (), arrived[0]
+    back_sum, far_part, attended_all, arrived[0], _ = order.scatter(
+        back_part.reshape(group, shard_rows, -1), far_part, attended_all, arrived[0]
     )
     gate_grad_own = (
         back_sum[:, model_width : model_width + experts]
@@ -756,11 +728,20 @@
     grad_attn = gather_rows(bf(grad_residual))
     grad_attn, *left = tie(grad_attn, *far_part[1:])
     arrived += [swap(piece, 2) for piece in left]
-    out_blocks = out_grad(grad_attn, attended_rows, out_part.reshape(group, shard_rows, model_width))
-    grad_attn, out_blocks = tie(grad_attn, out_blocks)
-    out_blocks = lax.psum_scatter(out_blocks, "expert", scatter_dimension=0, tiled=False)
     slice_rows = model_width // group
+    attn_cols = lax.all_to_all(
+        grad_attn.reshape(tok_count, group, slice_rows).transpose(1, 0, 2),
+        "expert",
+        split_axis=0,
+        concat_axis=0,
+        tiled=True,
+    ).reshape(group * tok_count, slice_rows)
+    grad_attn, out_part = tie(grad_attn, out_part)
+    out_sum = lax.psum_scatter(
+        out_part.reshape(group, shard_rows, model_width), "expert", scatter_dimension=0, tiled=False
+    )
     spare = 16
+    grad_attn, attn_cols = tie(grad_attn, attn_cols)
     packed, gain_parts, attn_gain_part, keep, give_part = attend_back(
         ranks, hidden_in, normalized_input, grad_attn, w_query, w_key, value_weight, q_gain, k_gain, cosine,
         sine_table, w_out, qp, kp, q, k, v, prob, shard_rows, group, spare,
@@ -785,11 +766,9 @@
     packed = lax.dynamic_update_slice(
         packed, bf(small).reshape(group, spare, packed.shape[2]), (0, slice_rows, 0)
     )
-    packed, _, out_blocks, _ = order.scatter(packed, (), out_blocks, ())
-    out_blocks = out_blocks.astype(jnp.float32)
-    w_out_grad = out_blocks[:slice_rows].T
-    out_sum = out_blocks[slice_rows:].reshape(-1, shard_rows, out_blocks.shape[1]).transpose(1, 0, 2)
-    layer_out = gather_rows(bf(residual + out_sum.reshape(shard_rows, model_width)))
+    packed, out_sum, _, _, _ = order.scatter(packed, out_sum, (), ())
+    w_out_grad = mm(attended_all, attn_cols, (0, 0))
+    layer_out = gather_rows(bf(residual + out_sum.astype(jnp.float32)))
     query_width, key_width = w_query.shape[1], w_key.shape[1]
     w_query_grad = packed[:slice_rows, :query_width]
     w_key_grad = packed[:slice_rows, query_width : query_width + key_width]

time: 525 us -> 520 us (level)
  the two profiles are of different devices: /device:TPU:25 before, /device:TPU:0 now
where the time goes in v4:
time: 520 us; the launch traced here: 510 us
  waiting for transfers between devices  220 us (42%)
  Pallas kernels  106 us (20%)
  starting transfers between devices  55.6 us (11%)
  matrix products  39.8 us (8%)
  local copies, waits for them, and re-layouts  39.7 us (8%)
  other arithmetic  33.1 us (6%)
  between operations  14.8 us (3%)
    ppermute x9, waiting for transfers between devices, along(): return lax.ppermute(value, 'expert', [(i, i ^ 2 * step) for i in range(8)])  79 us
    ppermute x28, waiting for transfers between devices, swap(): return lax.ppermute(value, 'tensor', [(i, i ^ step) for i in range(size)])  72.4 us
    ppermute x12, waiting for transfers between devices, across(): return lax.ppermute(value, 'expert', [(i, i ^ 1) for i in range(8)])  58.8 us
    pallas_call x2, Pallas kernels, run_experts(): pl.pallas_call(functools.partial(experts_kernel, shards=shards, before=ea...  55.6 us
    dot_general x12, matrix products, mm(): lax.dot_general(left, right, (((contract[0],), (contract[1],)), ((), ()))...  39.8 us
    pallas_call x1, Pallas kernels, attend_back(): pl.pallas_call(attend_back_kernel, grid_spec=pltpu.PrefetchScalarGridSpec...  29.1 us
    pallas_call x1, Pallas kernels, attend(): pl.pallas_call(attend_kernel, grid_spec=pltpu.PrefetchScalarGridSpec(num_...  21.6 us
    ppermute x9, starting transfers between devices, along(): return lax.ppermute(value, 'expert', [(i, i ^ 2 * step) for i in range(8)])  19.3 us
  transfers between devices with their start and end apart: 53, of which 31 were waited for; matrix products, arithmetic and copies ran while one was open for 19% of the time, Pallas kernels for 21%

profile of v4, /device:TPU:0, one launch (start us, length us, event | category | flops | bytes accessed | tf_op | source)
XLA Modules:
  0.0 509.7 jit_solution(13666580600721932581)
XLA Ops:
  10.0 3.0 collective-permute-start.1
  16.6 21.6 %attend.1 = (bf16[384,2048]{1,0:T(8,128)(2,1)}, f32[384,1024]{1,0:T(8,128)}, f32[384,128]{1,0:T(8,128)}, bf16[384,1024]{1,0:T(8,128)(2,1)}, bf16[384,128]{1,0:T(...) custom-call(s32[2]{0:T(128)} %pad_add_fusion.rank_ref, ...), custom_call_target="tpu_custom_call" | custom-call | flops 1048576 | bytes 65536 | tf_op jit(solution)/shard_map/attend/pallas_call | solution.py:136
  38.4 2.5 collective-permute-done
  41.7 1.8 convert_add_fusion.3
  43.5 3.9 collective-permute-done.1.rest_8_
  47.5 1.7 collective-permute-start.2
  49.5 10.0 %collective-permute-done.2 = bf16[96,2048]{1,0:T(8,128)(2,1)S(1)} collective-permute-done((bf16[96,2048]{1,0:T(8,128)(2,1)S(1)}, bf16[96,2048]{1,0:T(8,128)(2,1)S(1)}, u32[]{:S(2)}, u32[]{:S(2)}) %collective-permute-start.2) | collective-permute-done | bytes 393248 | tf_op jit(solution)/shard_map/ppermute | solution.py:47
  61.9 1.8 collective-permute-start.3
  63.7 2.6 collective-permute-start.7
  67.6 1.5 collective-permute-start.11
  69.1 3.1 collective-permute-done.3
  73.7 26.6 %collective-permute-done.7 = bf16[96,2048]{1,0:T(8,128)(2,1)} collective-permute-done((bf16[96,2048]{1,0:T(8,128)(2,1)S(1)}, bf16[96,2048]{1,0:T(8,128)(2,1)}, u32[]{:S(2)}, u32[]{:S(2)}) %collective-permute-start.7) | collective-permute-done | bytes 393248 | tf_op jit(solution)/shard_map/ppermute | solution.py:546
  105.6 20.9 %collective-permute-done.6 = bf16[96,2048]{1,0:T(8,128)(2,1)S(1)} collective-permute-done((bf16[96,2048]{1,0:T(8,128)(2,1)}, bf16[96,2048]{1,0:T(8,128)(2,1)S(1)}, u32[]{:S(2)}, u32[]{:S(2)}) %collective-permute-start.6) | collective-permute-done | bytes 393248 | tf_op jit(solution)/shard_map/ppermute | solution.py:543
  131.9 4.0 collective-permute-done.12.rest_4_.rest_6_
  136.8 2.2 collective-permute-done.14.rest_7_.rest_13_
  139.1 17.8 %experts_near.1 = (bf16[768,1536]{1,0:T(8,128)(2,1)}, bf16[768,768]{1,0:T(8,128)(2,1)}, f32[768,128]{1,0:T(8,128)}, f32[768,128]{1,0:T(8,128)}) custom-call(s32[2]{0:T(128)} %pad_add_fusion.rank_ref, bf16[768,2048]{1,0:T(8,128)(2,1)} %bitcast.140, bf16[768,2176]{1,0:T(8,128)(2,1)} %all-gather.3.cloned.1.call-done.g.rest_0_, ...), custom_call_target="tpu_custom_call" | custom-call | flops 1048576 | bytes 65536 | tf_op jit(solution)/shard_map/experts_near/pallas_call | solution.py:517
  156.9 37.8 %experts_far.1 = (bf16[768,2048]{1,0:T(8,128)(2,1)}, bf16[768,2176]{1,0:T(8,128)(2,1)}, bf16[768,1536]{1,0:T(8,128)(2,1)}, bf16[768,768]{1,0:T(8,128)(2,1)}) custom-call(s32[2]{0:T(128)} %pad_add_fusion.rank_ref, bf16[768,2048]{1,0:T(8,128)(2,1)} %bitcast.141, bf16[768,2176]{1,0:T(8,128)(2,1)} %all-gather.3.cloned.1.call-done.g.rest_0_, ...), custom_call_target="tpu_custom_call" | custom-call | flops 1048576 | bytes 65536 | tf_op jit(solution)/shard_map/experts_far/pallas_call | solution.py:517
  194.8 5.0 convolution_convert_fusion.1
  205.0 2.8 collective-permute-done.24
  207.8 2.6 add_convert_fusion.1
  210.4 3.4 add_convert_fusion
  213.8 2.1 fusion.41
  215.9 1.6 collective-permute-done.22
  217.7 3.4 collective-permute-start.25
  224.5 2.0 collective-permute-done.21
  226.5 14.0 %collective-permute-done.25 = bf16[96,2176]{1,0:T(8,128)(2,1)S(1)} collective-permute-done((bf16[96,2176]{1,0:T(8,128)(2,1)S(1)}, bf16[96,2176]{1,0:T(8,128)(2,1)S(1)}, u32[]{:S(2)}, u32[]{:S(2)}) %collective-permute-start.25) | collective-permute-done | bytes 417824 | tf_op jit(solution)/shard_map/ppermute | solution.py:546
  241.6 8.8 %collective-permute-start.20 = (bf16[96,2176]{1,0:T(8,128)(2,1)}, bf16[96,2176]{1,0:T(8,128)(2,1)}, u32[]{:S(2)}, u32[]{:S(2)}) collective-permute-start(bf16[96,2176]{1,0:T(8,128)(2,1)} %get-tuple-element.176), channel_id=1, source_target_pairs={{0,16},{4,20},{8,24},{12,28},{16,0},{20,4},{24,8},{28,12},{1,17},{... | collective-permute-start | bytes 1253384 | tf_op jit(solution)/shard_map/ppermute | solution.py:546
  252.9 16.0 %collective-permute-done.26 = bf16[96,2176]{1,0:T(8,128)(2,1)} collective-permute-done((bf16[96,2176]{1,0:T(8,128)(2,1)}, bf16[96,2176]{1,0:T(8,128)(2,1)}, u32[]{:S(2)}, u32[]{:S(2)}) %collective-permute-start.26) | collective-permute-done | bytes 417824 | tf_op jit(solution)/shard_map/ppermute | solution.py:546
  269.6 1.8 fusion.15
  272.4 1.9 constant_dynamic-update-slice_fusion.5
  276.9 4.0 convolution_convert_fusion
  280.9 5.1 %collective-permute-done.28 = bf16[96,2048]{1,0:T(8,128)(2,1)S(1)} collective-permute-done((bf16[96,2048]{1,0:T(8,128)(2,1)S(1)}, bf16[96,2048]{1,0:T(8,128)(2,1)S(1)}, u32[]{:S(2)}, u32[]{:S(2)}) %collective-permute-start.28) | collective-permute-done | bytes 393248 | tf_op jit(solution)/shard_map/ppermute | solution.py:47
  287.0 1.8 constant_dynamic-update-slice_fusion.4
  289.7 1.8 slice_dynamic-update-slice_fusion.5
  291.4 1.8 slice_dynamic-update-slice_fusion.4
  293.2 2.7 copy.55
  295.9 4.5 all-to-all-start
  300.5 1.6 collective-permute-start.46
  302.1 3.9 convolution_convert_fusion.2
  306.0 6.3 %convert_add_fusion = f32[768,2048]{1,0:T(8,128)} fusion(bf16[768,2048]{1,0:T(8,128)(2,1)} %collective-permute-done.45, bf16[768,2048]{1,0:T(8,128)(2,1)S(1)} %bitcast.145, bf16[768,1536]{1,0:T(8,128)(2,1)S(1)} %copy-done.21), kind=kOutput, calls=%fused_computation | convolution fusion | flops 2419064832 | bytes 13762560 | tf_op jit(solution)/shard_map/dot_general | solution.py:36
  313.5 1.8 reshape.157
  315.9 22.3 %collective-permute-done.46 = bf16[384,2048]{1,0:T(8,128)(2,1)} collective-permute-done((bf16[384,2048]{1,0:T(8,128)(2,1)}, bf16[384,2048]{1,0:T(8,128)(2,1)}, u32[]{:S(2)}, u32[]{:S(2)}) %collective-permute-start.46) | collective-permute-done | bytes 1572896 | tf_op jit(solution)/shard_map/ppermute | solution.py:47
  338.1 8.0 %slice_add_fusion = (f32[384,2048]{1,0:T(8,128)}, f32[384,2048]{1,0:T(8,128)}) fusion(f32[768,2048]{1,0:T(8,128)} %convert_add_fusion, bf16[384,2048]{1,0:T(8,128)(2,1)} %collective-permute-done.46, bf16[384,2048]{1,0:T(8,128)(2,1)} %collective-permute-done.27), kind=kLoop, calls=%fused_computation.4 | loop fusion | flops 3145728 | bytes 15728640 | tf_op jit(solution)/shard_map/add | solution.py:785
  346.1 10.1 %all-to-all-done = bf16[8,384,256]{2,1,0:T(8,128)(2,1)} async-done(((bf16[8,384,256]{2,1,0:T(8,128)(2,1)}), bf16[8,384,256]{2,1,0:T(8,128)(2,1)}, u32[]{:S(2)}, u32[]{:S(2)}) %all-to-all-start) | async-done | bytes 1572896 | tf_op jit(solution)/shard_map/all_to_all | solution.py:732
  356.2 29.1 %attend_back.1 = (bf16[8,272,1280]{2,1,0:T(8,128)(2,1)}, f32[8,128]{1,0:T(8,128)}, f32[1,2048]{1,0:T(1,128)}, f32[2,96,2048]{2,1,0:T(8,128)}, bf16[2,96,2048]{2,1,0:T(8,128)(2,1)}) custom-call(s32[2]{0:T(128)} %pad_add_fusion.rank_ref, bf16[384,2048]{1,0:T(8,128)(2,1)} %x.5, bf16[384,2048]{1,0:T(8,128)(2,1)} %get-tuple-element.74.xn, ...), custom_call_target="tpu_custom_call" | custom-call | flops 30000001024 | bytes 1048576 | tf_op jit(solution)/shard_map/attend_back/pallas_call | solution.py:290
  385.4 5.1 %convert_add_fusion.1 = f32[384,2048]{1,0:T(8,128)} fusion(bf16[384,2048]{1,0:T(8,128)(2,1)} %collective-permute-done.48, bf16[384,2048]{1,0:T(8,128)(2,1)} %collective-permute-done.47, bf16[768,2176]{1,0:T(8,128)(2,1)S(1)} %copy-done.2, bf16[768,768]{1,0:T(8,128)(2,1)S(1)} %copy-done.19), kind=kOutput, calls=%fused_computation.6 | convolution fusion | flops 1211105280 | bytes 10027008 | tf_op jit(solution)/shard_map/dot_general | solution.py:36
  391.3 1.9 convert_add_fusion.2
  393.3 1.8 collective-permute-start.34
  395.1 9.7 %collective-permute-done.34 = bf16[96,2048]{1,0:T(8,128)(2,1)S(1)} collective-permute-done((bf16[96,2048]{1,0:T(8,128)(2,1)S(1)}, bf16[96,2048]{1,0:T(8,128)(2,1)S(1)}, u32[]{:S(2)}, u32[]{:S(2)}) %collective-permute-start.34) | collective-permute-done | bytes 393248 | tf_op jit(solution)/shard_map/ppermute | solution.py:47
  405.4 1.6 constant_dynamic-update-slice_fusion.1
  407.0 1.8 collective-permute-start.35
  409.5 3.0 dynamic-slice_bitcast_fusion.1
  417.9 6.0 %fusion.46 = f32[1024,256]{1,0:T(8,128)} fusion(bf16[3072,1024]{1,0:T(8,128)(2,1)} %all-gather.5.cloned.1.call-done, bf16[3072,256]{1,0:T(8,128)(2,1)} %bitcast.37), kind=kOutput, calls=%fused_computation.140 | convolution fusion | flops 1610612736 | bytes 8912896 | tf_op jit(solution)/shard_map/dot_general | solution.py:36
  424.1 7.1 %collective-permute-done.30 = bf16[272,1280]{1,0:T(8,128)(2,1)} collective-permute-done((bf16[272,1280]{1,0:T(8,128)(2,1)S(1)}, bf16[272,1280]{1,0:T(8,128)(2,1)}, u32[]{:S(2)}, u32[]{:S(2)}) %collective-permute-start.30) | collective-permute-done | bytes 696352 | tf_op jit(solution)/shard_map/ppermute | solution.py:543
  431.2 1.5 fusion.5
  435.5 2.1 bitcast_convert_fusion
  437.7 5.2 %collective-permute-done.31 = bf16[96,2048]{1,0:T(8,128)(2,1)S(1)} collective-permute-done((bf16[96,2048]{1,0:T(8,128)(2,1)S(1)}, bf16[96,2048]{1,0:T(8,128)(2,1)S(1)}, u32[]{:S(2)}, u32[]{:S(2)}) %collective-permute-start.31) | collective-permute-done | bytes 393248 | tf_op jit(solution)/shard_map/ppermute | solution.py:47
  443.0 3.1 collective-permute-done.40
  446.1 2.9 collective-permute-done.41
  449.0 12.0 %collective-permute-done.38 = bf16[272,1280]{1,0:T(8,128)(2,1)} collective-permute-done((bf16[272,1280]{1,0:T(8,128)(2,1)}, bf16[272,1280]{1,0:T(8,128)(2,1)}, u32[]{:S(2)}, u32[]{:S(2)}) %collective-permute-start.38) | collective-permute-done | bytes 696352 | tf_op jit(solution)/shard_map/ppermute | solution.py:543
  461.0 2.1 fusion.6
  465.4 9.0 %collective-permute-done.37 = bf16[272,1280]{1,0:T(8,128)(2,1)} collective-permute-done((bf16[272,1280]{1,0:T(8,128)(2,1)S(1)}, bf16[272,1280]{1,0:T(8,128)(2,1)}, u32[]{:S(2)}, u32[]{:S(2)}) %collective-permute-start.37) | collective-permute-done | bytes 696352 | tf_op jit(solution)/shard_map/ppermute | solution.py:543
  474.3 17.5 %collective-permute-done.39 = bf16[272,1280]{1,0:T(8,128)(2,1)S(1)} collective-permute-done((bf16[272,1280]{1,0:T(8,128)(2,1)S(1)}, bf16[272,1280]{1,0:T(8,128)(2,1)S(1)}, u32[]{:S(2)}, u32[]{:S(2)}) %collective-permute-start.39) | collective-permute-done | bytes 696352 | tf_op jit(solution)/shard_map/ppermute | solution.py:546
  493.1 1.8 fusion.7
  (223 shorter events, 66.7 us)
Async XLA Ops:
  7.2 96.2 %all-gather.3.cloned.1.call-start = ((), (), s32[]{:S(2)}) async-start(), calls=%async_computation.2 | async-start | bytes 3760128 | tf_op jit(solution)/shard_map/all_gather | solution.py:625
  8.1 7.2 %copy-start.31 = (s32[384]{0:T(512)S(1)}, s32[384]{0:T(512)}, u32[]{:S(2)}) copy-start(s32[384]{0:T(512)} %param.19) | copy-start | bytes 4612
  9.9 259.6 %all-gather.5.cloned.1.call-start = ((), (), s32[]{:S(2)}) async-start(), calls=%async_computation.3 | async-start | bytes 7077888 | tf_op jit(solution)/shard_map/all_gather | solution.py:675
  10.0 37.5 %collective-permute-start.1 = (bf16[384,2048]{1,0:T(8,128)(2,1)S(1)}, bf16[384,2048]{1,0:T(8,128)(2,1)}, u32[]{:S(2)}, u32[]{:S(2)}) collective-permute-start(bf16[384,2048]{1,0:T(8,128)(2,1)S(1)} %bitcast.152), channel_id=1, source_target_pairs={{0,2},{1,3},{2,0},{3,1},{4,6},{5,7},{6,4},{7,5},{8,10},{9,11},{10,... | collective-permute-start | bytes 4718600 | tf_op jit(solution)/shard_map/ppermute | solution.py:47
  38.3 2.6 collective-permute-start
  47.5 12.1 %collective-permute-start.2 = (bf16[96,2048]{1,0:T(8,128)(2,1)S(1)}, bf16[96,2048]{1,0:T(8,128)(2,1)S(1)}, u32[]{:S(2)}, u32[]{:S(2)}) collective-permute-start(bf16[96,2048]{1,0:T(8,128)(2,1)S(1)} %fusion.31), channel_id=1, source_target_pairs={{0,2},{1,3},{2,0},{3,1},{4,6},{5,7},{6,4},{7,5},{8,10},{9,11},{10,... | collective-permute-start | bytes 1179656 | tf_op jit(solution)/shard_map/ppermute | solution.py:47
  49.2 54.1 %collective-permute-start.5 = (bf16[384,2048]{1,0:T(8,128)(2,1)}, bf16[384,2048]{1,0:T(8,128)(2,1)}, u32[]{:S(2)}, u32[]{:S(2)}) collective-permute-start(bf16[384,2048]{1,0:T(8,128)(2,1)} %bitcast.12.rest_3_.rest_5_), channel_id=1, source_target_pairs={{0,2},{1,3},{2,0},{3,1},{4,6},{5,7},{6,4},{7,5},{8,10},{9,11},{10,... | collective-permute-start | bytes 4718600 | tf_op jit(solution)/shard_map/ppermute | solution.py:47
  61.9 65.7 %copy-start.16 = (bf16[96,2048]{1,0:T(8,128)(2,1)}, bf16[96,2048]{1,0:T(8,128)(2,1)S(1)}, u32[]{:S(2)}) copy-start(bf16[96,2048]{1,0:T(8,128)(2,1)S(1)} %get-tuple-element.165) | copy-start | bytes 1179652
  61.9 10.3 %collective-permute-start.3 = (bf16[96,2048]{1,0:T(8,128)(2,1)S(1)}, bf16[96,2048]{1,0:T(8,128)(2,1)}, u32[]{:S(2)}, u32[]{:S(2)}) collective-permute-start(bf16[96,2048]{1,0:T(8,128)(2,1)S(1)} %get-tuple-element.165), channel_id=1, source_target_pairs={{0,4},{4,0},{8,12},{12,8},{16,20},{20,16},{24,28},{28,24},{1,5},{5... | collective-permute-start | bytes 1179656 | tf_op jit(solution)/shard_map/ppermute | solution.py:543
  63.7 36.6 %collective-permute-start.7 = (bf16[96,2048]{1,0:T(8,128)(2,1)S(1)}, bf16[96,2048]{1,0:T(8,128)(2,1)}, u32[]{:S(2)}, u32[]{:S(2)}) collective-permute-start(bf16[96,2048]{1,0:T(8,128)(2,1)S(1)} %get-tuple-element.165), channel_id=1, source_target_pairs={{0,16},{4,20},{8,24},{12,28},{16,0},{20,4},{24,8},{28,12},{1,17},{... | collective-permute-start | bytes 1179656 | tf_op jit(solution)/shard_map/ppermute | solution.py:546
  66.3 35.1 %collective-permute-start.9 = (bf16[96,2048]{1,0:T(8,128)(2,1)S(1)}, bf16[96,2048]{1,0:T(8,128)(2,1)}, u32[]{:S(2)}, u32[]{:S(2)}) collective-permute-start(bf16[96,2048]{1,0:T(8,128)(2,1)S(1)} %get-tuple-element.165), channel_id=1, source_target_pairs={{0,24},{4,28},{8,16},{12,20},{16,8},{20,12},{24,0},{28,4},{1,25},{... | collective-permute-start | bytes 1179656 | tf_op jit(solution)/shard_map/ppermute | solution.py:546
  67.6 63.1 %collective-permute-start.11 = (bf16[384,2048]{1,0:T(8,128)(2,1)}, bf16[384,2048]{1,0:T(8,128)(2,1)}, u32[]{:S(2)}, u32[]{:S(2)}) collective-permute-start(bf16[384,2048]{1,0:T(8,128)(2,1)} %bitcast.19.rest_6_.rest_12_), channel_id=1, source_target_pairs={{0,2},{1,3},{2,0},{3,1},{4,6},{5,7},{6,4},{7,5},{8,10},{9,11},{10,... | collective-permute-start | bytes 4718600 | tf_op jit(solution)/shard_map/ppermute | solution.py:47
  72.2 31.2 %collective-permute-start.4 = (bf16[96,2048]{1,0:T(8,128)(2,1)S(1)}, bf16[96,2048]{1,0:T(8,128)(2,1)}, u32[]{:S(2)}, u32[]{:S(2)}) collective-permute-start(bf16[96,2048]{1,0:T(8,128)(2,1)S(1)} %get-tuple-element.165), channel_id=1, source_target_pairs={{0,8},{4,12},{8,0},{12,4},{16,24},{20,28},{24,16},{28,20},{1,9},{5... | collective-permute-start | bytes 1179656 | tf_op jit(solution)/shard_map/ppermute | solution.py:546
  100.3 27.3 %collective-permute-start.8 = (bf16[96,2048]{1,0:T(8,128)(2,1)}, bf16[96,2048]{1,0:T(8,128)(2,1)}, u32[]{:S(2)}, u32[]{:S(2)}) collective-permute-start(bf16[96,2048]{1,0:T(8,128)(2,1)} %collective-permute-done.7), channel_id=1, source_target_pairs={{0,4},{4,0},{8,12},{12,8},{16,20},{20,16},{24,28},{28,24},{1,5},{5... | collective-permute-start | bytes 1179656 | tf_op jit(solution)/shard_map/ppermute | solution.py:543
  101.4 28.3 %collective-permute-start.10 = (bf16[96,2048]{1,0:T(8,128)(2,1)}, bf16[96,2048]{1,0:T(8,128)(2,1)}, u32[]{:S(2)}, u32[]{:S(2)}) collective-permute-start(bf16[96,2048]{1,0:T(8,128)(2,1)} %collective-permute-done.9), channel_id=1, source_target_pairs={{0,4},{4,0},{8,12},{12,8},{16,20},{20,16},{24,28},{28,24},{1,5},{5... | collective-permute-start | bytes 1179656 | tf_op jit(solution)/shard_map/ppermute | solution.py:543
  103.4 23.1 %collective-permute-start.6 = (bf16[96,2048]{1,0:T(8,128)(2,1)}, bf16[96,2048]{1,0:T(8,128)(2,1)S(1)}, u32[]{:S(2)}, u32[]{:S(2)}) collective-permute-start(bf16[96,2048]{1,0:T(8,128)(2,1)} %collective-permute-done.4), channel_id=1, source_target_pairs={{0,4},{4,0},{8,12},{12,8},{16,20},{20,16},{24,28},{28,24},{1,5},{5... | collective-permute-start | bytes 1179656 | tf_op jit(solution)/shard_map/ppermute | solution.py:543
  130.7 8.4 %copy-start.6 = (bf16[8,96,2048]{2,1,0:T(8,128)(2,1)}, bf16[8,96,2048]{2,1,0:T(8,128)(2,1)S(1)}, u32[]{:S(2)}) copy-start(bf16[8,96,2048]{2,1,0:T(8,128)(2,1)S(1)} %bitcast_dynamic-update-slice_fusion) | copy-start | bytes 9437188
  130.8 5.1 %collective-permute-start.12 = (bf16[384,2048]{1,0:T(8,128)(2,1)}, bf16[384,2048]{1,0:T(8,128)(2,1)S(1)}, u32[]{:S(2)}, u32[]{:S(2)}) collective-permute-start(bf16[384,2048]{1,0:T(8,128)(2,1)} %bitcast.149), channel_id=1, source_target_pairs={{0,1},{1,0},{2,3},{3,2},{4,5},{5,4},{6,7},{7,6},{8,9},{9,8},{10,11... | collective-permute-start | bytes 4718600 | tf_op jit(solution)/shard_map/ppermute | solution.py:47
  130.9 6.0 %collective-permute-start.13 = (bf16[384,2048]{1,0:T(8,128)(2,1)}, bf16[384,2048]{1,0:T(8,128)(2,1)}, u32[]{:S(2)}, u32[]{:S(2)}) collective-permute-start(bf16[384,2048]{1,0:T(8,128)(2,1)} %bitcast.12.rest_3_.rest_5_), channel_id=1, source_target_pairs={{0,1},{1,0},{2,3},{3,2},{4,5},{5,4},{6,7},{7,6},{8,9},{9,8},{10,11... | collective-permute-start | bytes 4718600 | tf_op jit(solution)/shard_map/ppermute | solution.py:47
  131.4 7.7 %collective-permute-start.14 = (bf16[384,2048]{1,0:T(8,128)(2,1)}, bf16[384,2048]{1,0:T(8,128)(2,1)}, u32[]{:S(2)}, u32[]{:S(2)}) collective-permute-start(bf16[384,2048]{1,0:T(8,128)(2,1)} %bitcast.19.rest_6_.rest_12_), channel_id=1, source_target_pairs={{0,1},{1,0},{2,3},{3,2},{4,5},{5,4},{6,7},{7,6},{8,9},{9,8},{10,11... | collective-permute-start | bytes 4718600 | tf_op jit(solution)/shard_map/ppermute | solution.py:47
  131.4 25.4 %collective-permute-start.15 = (bf16[384,2048]{1,0:T(8,128)(2,1)}, bf16[384,2048]{1,0:T(8,128)(2,1)}, u32[]{:S(2)}, u32[]{:S(2)}) collective-permute-start(bf16[384,2048]{1,0:T(8,128)(2,1)} %collective-permute-done.1.rest_8_), channel_id=1, source_target_pairs={{0,1},{1,0},{2,3},{3,2},{4,5},{5,4},{6,7},{7,6},{8,9},{9,8},{10,11... | collective-permute-start | bytes 4718600 | tf_op jit(solution)/shard_map/ppermute | solution.py:47
  131.9 25.0 %collective-permute-start.16 = (bf16[384,2048]{1,0:T(8,128)(2,1)}, bf16[384,2048]{1,0:T(8,128)(2,1)}, u32[]{:S(2)}, u32[]{:S(2)}) collective-permute-start(bf16[384,2048]{1,0:T(8,128)(2,1)} %collective-permute-done.5.rest_9_), channel_id=1, source_target_pairs={{0,1},{1,0},{2,3},{3,2},{4,5},{5,4},{6,7},{7,6},{8,9},{9,8},{10,11... | collective-permute-start | bytes 4718600 | tf_op jit(solution)/shard_map/ppermute | solution.py:47
  135.9 21.0 %collective-permute-start.17 = (bf16[384,2048]{1,0:T(8,128)(2,1)}, bf16[384,2048]{1,0:T(8,128)(2,1)}, u32[]{:S(2)}, u32[]{:S(2)}) collective-permute-start(bf16[384,2048]{1,0:T(8,128)(2,1)} %collective-permute-done.11.rest_14_), channel_id=1, source_target_pairs={{0,1},{1,0},{2,3},{3,2},{4,5},{5,4},{6,7},{7,6},{8,9},{9,8},{10,11... | collective-permute-start | bytes 4718600 | tf_op jit(solution)/shard_map/ppermute | solution.py:47
  199.8 10.6 %collective-permute-start.23 = (bf16[768,2048]{1,0:T(8,128)(2,1)S(1)}, bf16[768,2048]{1,0:T(8,128)(2,1)S(1)}, u32[]{:S(2)}, u32[]{:S(2)}) collective-permute-start(bf16[768,2048]{1,0:T(8,128)(2,1)S(1)} %convolution_convert_fusion.1), channel_id=1, source_target_pairs={{0,1},{1,0},{2,3},{3,2},{4,5},{5,4},{6,7},{7,6},{8,9},{9,8},{10,11... | collective-permute-start | bytes 9437192 | tf_op jit(solution)/shard_map/ppermute | solution.py:47
  201.5 6.3 %collective-permute-start.24 = (bf16[384,2048]{1,0:T(8,128)(2,1)S(1)}, bf16[384,2048]{1,0:T(8,128)(2,1)S(1)}, u32[]{:S(2)}, u32[]{:S(2)}) collective-permute-start(bf16[384,2048]{1,0:T(8,128)(2,1)S(1)} %convolution_convert_fusion.3), channel_id=1, source_target_pairs={{0,1},{1,0},{2,3},{3,2},{4,5},{5,4},{6,7},{7,6},{8,9},{9,8},{10,11... | collective-permute-start | bytes 4718600 | tf_op jit(solution)/shard_map/ppermute | solution.py:47
  202.9 14.6 %collective-permute-start.22 = (bf16[96,2176]{1,0:T(8,128)(2,1)S(1)}, bf16[96,2176]{1,0:T(8,128)(2,1)S(1)}, u32[]{:S(2)}, u32[]{:S(2)}) collective-permute-start(bf16[96,2176]{1,0:T(8,128)(2,1)S(1)} %get-tuple-element.179), channel_id=1, source_target_pairs={{0,4},{4,0},{8,12},{12,8},{16,20},{20,16},{24,28},{28,24},{1,5},{5... | collective-permute-start | bytes 1253384 | tf_op jit(solution)/shard_map/ppermute | solution.py:543
  204.2 22.3 %collective-permute-start.21 = (bf16[96,2176]{1,0:T(8,128)(2,1)S(1)}, bf16[96,2176]{1,0:T(8,128)(2,1)S(1)}, u32[]{:S(2)}, u32[]{:S(2)}) collective-permute-start(bf16[96,2176]{1,0:T(8,128)(2,1)S(1)} %get-tuple-element.180), channel_id=1, source_target_pairs={{0,4},{4,0},{8,12},{12,8},{16,20},{20,16},{24,28},{28,24},{1,5},{5... | collective-permute-start | bytes 1253384 | tf_op jit(solution)/shard_map/ppermute | solution.py:543
  217.6 33.6 %copy-start.24 = (bf16[2048,16]{0,1:T(8,128)(2,1)S(1)}, bf16[2048,16]{0,1:T(8,128)(2,1)}, u32[]{:S(2)}) copy-start(bf16[2048,16]{0,1:T(8,128)(2,1)} %param.30) | copy-start | bytes 196612
  217.7 22.8 %collective-permute-start.25 = (bf16[96,2176]{1,0:T(8,128)(2,1)S(1)}, bf16[96,2176]{1,0:T(8,128)(2,1)S(1)}, u32[]{:S(2)}, u32[]{:S(2)}) collective-permute-start(bf16[96,2176]{1,0:T(8,128)(2,1)S(1)} %fusion.13), channel_id=1, source_target_pairs={{0,24},{4,28},{8,16},{12,20},{16,8},{20,12},{24,0},{28,4},{1,25},{... | collective-permute-start | bytes 1253384 | tf_op jit(solution)/shard_map/ppermute | solution.py:546
  221.1 19.4 %collective-permute-start.19 = (bf16[96,2176]{1,0:T(8,128)(2,1)S(1)}, bf16[96,2176]{1,0:T(8,128)(2,1)S(1)}, u32[]{:S(2)}, u32[]{:S(2)}) collective-permute-start(bf16[96,2176]{1,0:T(8,128)(2,1)S(1)} %get-tuple-element.178), channel_id=1, source_target_pairs={{0,4},{4,0},{8,12},{12,8},{16,20},{20,16},{24,28},{28,24},{1,5},{5... | collective-permute-start | bytes 1253384 | tf_op jit(solution)/shard_map/ppermute | solution.py:543
  221.6 47.3 %collective-permute-start.27 = (bf16[384,2048]{1,0:T(8,128)(2,1)}, bf16[384,2048]{1,0:T(8,128)(2,1)}, u32[]{:S(2)}, u32[]{:S(2)}) collective-permute-start(bf16[384,2048]{1,0:T(8,128)(2,1)} %get-tuple-element.183), channel_id=1, source_target_pairs={{0,2},{1,3},{2,0},{3,1},{4,6},{5,7},{6,4},{7,5},{8,10},{9,11},{10,... | collective-permute-start | bytes 4718600 | tf_op jit(solution)/shard_map/ppermute | solution.py:47
  223.0 45.8 %collective-permute-start.18 = (bf16[96,2176]{1,0:T(8,128)(2,1)}, bf16[96,2176]{1,0:T(8,128)(2,1)}, u32[]{:S(2)}, u32[]{:S(2)}) collective-permute-start(bf16[96,2176]{1,0:T(8,128)(2,1)} %get-tuple-element.181), channel_id=1, source_target_pairs={{0,4},{4,0},{8,12},{12,8},{16,20},{20,16},{24,28},{28,24},{1,5},{5... | collective-permute-start | bytes 1253384 | tf_op jit(solution)/shard_map/ppermute | solution.py:543
  241.6 28.0 %collective-permute-start.20 = (bf16[96,2176]{1,0:T(8,128)(2,1)}, bf16[96,2176]{1,0:T(8,128)(2,1)}, u32[]{:S(2)}, u32[]{:S(2)}) collective-permute-start(bf16[96,2176]{1,0:T(8,128)(2,1)} %get-tuple-element.176), channel_id=1, source_target_pairs={{0,16},{4,20},{8,24},{12,28},{16,0},{20,4},{24,8},{28,12},{1,17},{... | collective-permute-start | bytes 1253384 | tf_op jit(solution)/shard_map/ppermute | solution.py:546
  250.4 18.4 %collective-permute-start.26 = (bf16[96,2176]{1,0:T(8,128)(2,1)}, bf16[96,2176]{1,0:T(8,128)(2,1)}, u32[]{:S(2)}, u32[]{:S(2)}) collective-permute-start(bf16[96,2176]{1,0:T(8,128)(2,1)} %get-tuple-element.177), channel_id=1, source_target_pairs={{0,8},{4,12},{8,0},{12,4},{16,24},{20,28},{24,16},{28,20},{1,9},{5... | collective-permute-start | bytes 1253384 | tf_op jit(solution)/shard_map/ppermute | solution.py:546
  252.9 18.9 %copy-start.30 = (f32[96]{0:T(128)S(1)}, f32[96]{0:T(128)}, u32[]{:S(2)}) copy-start(f32[96]{0:T(128)} %copy-done.29) | copy-start | bytes 1156
  275.5 10.5 %collective-permute-start.28 = (bf16[96,2048]{1,0:T(8,128)(2,1)S(1)}, bf16[96,2048]{1,0:T(8,128)(2,1)S(1)}, u32[]{:S(2)}, u32[]{:S(2)}) collective-permute-start(bf16[96,2048]{1,0:T(8,128)(2,1)S(1)} %get-tuple-element.163), channel_id=1, source_target_pairs={{0,2},{1,3},{2,0},{3,1},{4,6},{5,7},{6,4},{7,5},{8,10},{9,11},{10,... | collective-permute-start | bytes 1179656 | tf_op jit(solution)/shard_map/ppermute | solution.py:47
  280.9 25.1 %collective-permute-start.45 = (bf16[768,2048]{1,0:T(8,128)(2,1)}, bf16[768,2048]{1,0:T(8,128)(2,1)}, u32[]{:S(2)}, u32[]{:S(2)}) collective-permute-start(bf16[768,2048]{1,0:T(8,128)(2,1)} %convolution_convert_fusion), channel_id=1, source_target_pairs={{0,1},{1,0},{2,3},{3,2},{4,5},{5,4},{6,7},{7,6},{8,9},{9,8},{10,11... | collective-permute-start | bytes 9437192 | tf_op jit(solution)/shard_map/ppermute | solution.py:47
  287.0 2.6 collective-permute-start.29
  295.9 60.3 %all-to-all-start = ((bf16[8,384,256]{2,1,0:T(8,128)(2,1)}), bf16[8,384,256]{2,1,0:T(8,128)(2,1)}, u32[]{:S(2)}, u32[]{:S(2)}) async-start(bf16[8,384,256]{2,1,0:T(8,128)(2,1)} %bitcast.146), calls=%async_computation | async-start | bytes 3145728 | tf_op jit(solution)/shard_map/all_to_all | solution.py:732
  300.4 130.7 %reduce-scatter.2.cloned.1.call-start = ((), (), s32[]{:S(2)}) async-start(), calls=%async_computation.4 | async-start | bytes 3538944 | tf_op jit(solution)/shard_map/reduce_scatter | solution.py:740
  300.5 37.7 %collective-permute-start.46 = (bf16[384,2048]{1,0:T(8,128)(2,1)}, bf16[384,2048]{1,0:T(8,128)(2,1)}, u32[]{:S(2)}, u32[]{:S(2)}) collective-permute-start(bf16[384,2048]{1,0:T(8,128)(2,1)} %get-tuple-element.124), channel_id=1, source_target_pairs={{0,2},{1,3},{2,0},{3,1},{4,6},{5,7},{6,4},{7,5},{8,10},{9,11},{10,... | collective-permute-start | bytes 4718600 | tf_op jit(solution)/shard_map/ppermute | solution.py:47
  306.0 6.3 %copy-start.17 = (bf16[96,2048]{1,0:T(8,128)(2,1)S(1)}, bf16[96,2048]{1,0:T(8,128)(2,1)}, u32[]{:S(2)}) copy-start(bf16[96,2048]{1,0:T(8,128)(2,1)} %copy-done.16) | copy-start | bytes 1179652
  306.0 79.4 %collective-permute-start.47 = (bf16[384,2048]{1,0:T(8,128)(2,1)}, bf16[384,2048]{1,0:T(8,128)(2,1)}, u32[]{:S(2)}, u32[]{:S(2)}) collective-permute-start(bf16[384,2048]{1,0:T(8,128)(2,1)} %convolution_convert_fusion.2), channel_id=1, source_target_pairs={{0,1},{1,0},{2,3},{3,2},{4,5},{5,4},{6,7},{7,6},{8,9},{9,8},{10,11... | collective-permute-start | bytes 4718600 | tf_op jit(solution)/shard_map/ppermute | solution.py:47
  315.3 70.1 %collective-permute-start.48 = (bf16[384,2048]{1,0:T(8,128)(2,1)}, bf16[384,2048]{1,0:T(8,128)(2,1)}, u32[]{:S(2)}, u32[]{:S(2)}) collective-permute-start(bf16[384,2048]{1,0:T(8,128)(2,1)} %add_convert_fusion.1), channel_id=1, source_target_pairs={{0,2},{1,3},{2,0},{3,1},{4,6},{5,7},{6,4},{7,5},{8,10},{9,11},{10,... | collective-permute-start | bytes 4718600 | tf_op jit(solution)/shard_map/ppermute | solution.py:47
  356.2 29.2 %copy-start.19 = (bf16[768,768]{1,0:T(8,128)(2,1)S(1)}, bf16[768,768]{1,0:T(8,128)(2,1)}, u32[]{:S(2)}) copy-start(bf16[768,768]{1,0:T(8,128)(2,1)} %get-tuple-element.83.rest_3_) | copy-start | bytes 3538948
  385.3 6.0 %collective-permute-start.33 = (bf16[2,96,2048]{2,1,0:T(8,128)(2,1)}, bf16[2,96,2048]{2,1,0:T(8,128)(2,1)}, u32[]{:S(2)}, u32[]{:S(2)}) collective-permute-start(bf16[2,96,2048]{2,1,0:T(8,128)(2,1)} %get-tuple-element.115), channel_id=1, source_target_pairs={{0,1},{1,0},{2,3},{3,2},{4,5},{5,4},{6,7},{7,6},{8,9},{9,8},{10,11... | collective-permute-start | bytes 2359304 | tf_op jit(solution)/shard_map/ppermute | solution.py:47
  391.3 13.6 %copy-start.15 = (bf16[384,2048]{1,0:T(8,128)(2,1)S(1)}, bf16[384,2048]{1,0:T(8,128)(2,1)}, u32[]{:S(2)}) copy-start(bf16[384,2048]{1,0:T(8,128)(2,1)} %x.5) | copy-start | bytes 4718596
  391.3 13.5 %copy-start.28 = (f32[2048]{0:T(1024)S(1)}, f32[2048]{0:T(1024)}, u32[]{:S(2)}) copy-start(f32[2048]{0:T(1024)} %param.22) | copy-start | bytes 24580
  393.3 11.6 %collective-permute-start.34 = (bf16[96,2048]{1,0:T(8,128)(2,1)S(1)}, bf16[96,2048]{1,0:T(8,128)(2,1)S(1)}, u32[]{:S(2)}, u32[]{:S(2)}) collective-permute-start(bf16[96,2048]{1,0:T(8,128)(2,1)S(1)} %fusion.32), channel_id=1, source_target_pairs={{0,2},{1,3},{2,0},{3,1},{4,6},{5,7},{6,4},{7,5},{8,10},{9,11},{10,... | collective-permute-start | bytes 1179656 | tf_op jit(solution)/shard_map/ppermute | solution.py:47
  395.1 10.3 %copy-start.5 = (f32[96,2048]{1,0:T(8,128)S(1)}, f32[96,2048]{1,0:T(8,128)}, u32[]{:S(2)}) copy-start(f32[96,2048]{1,0:T(8,128)} %copy-done.3) | copy-start | bytes 2359300
  395.1 10.3 %copy-start.11 = (f32[96,2048]{1,0:T(8,128)S(1)}, f32[96,2048]{1,0:T(8,128)}, u32[]{:S(2)}) copy-start(f32[96,2048]{1,0:T(8,128)} %copy-done.10) | copy-start | bytes 2359300
  407.0 10.8 %collective-permute-start.35 = (bf16[96,2048]{1,0:T(8,128)(2,1)S(1)}, bf16[96,2048]{1,0:T(8,128)(2,1)S(1)}, u32[]{:S(2)}, u32[]{:S(2)}) collective-permute-start(bf16[96,2048]{1,0:T(8,128)(2,1)S(1)} %get-tuple-element.159), channel_id=1, source_target_pairs={{0,2},{1,3},{2,0},{3,1},{4,6},{5,7},{6,4},{7,5},{8,10},{9,11},{10,... | collective-permute-start | bytes 1179656 | tf_op jit(solution)/shard_map/ppermute | solution.py:47
  412.5 18.7 %collective-permute-start.30 = (bf16[272,1280]{1,0:T(8,128)(2,1)S(1)}, bf16[272,1280]{1,0:T(8,128)(2,1)}, u32[]{:S(2)}, u32[]{:S(2)}) collective-permute-start(bf16[272,1280]{1,0:T(8,128)(2,1)S(1)} %get-tuple-element.175), channel_id=1, source_target_pairs={{0,4},{4,0},{8,12},{12,8},{16,20},{20,16},{24,28},{28,24},{1,5},{5... | collective-permute-start | bytes 2088968 | tf_op jit(solution)/shard_map/ppermute | solution.py:543
  413.5 32.6 %collective-permute-start.40 = (bf16[272,1280]{1,0:T(8,128)(2,1)}, bf16[272,1280]{1,0:T(8,128)(2,1)}, u32[]{:S(2)}, u32[]{:S(2)}) collective-permute-start(bf16[272,1280]{1,0:T(8,128)(2,1)} %get-tuple-element.173), channel_id=1, source_target_pairs={{0,4},{4,0},{8,12},{12,8},{16,20},{20,16},{24,28},{28,24},{1,5},{5... | collective-permute-start | bytes 2088968 | tf_op jit(solution)/shard_map/ppermute | solution.py:543
  414.6 46.5 %collective-permute-start.38 = (bf16[272,1280]{1,0:T(8,128)(2,1)}, bf16[272,1280]{1,0:T(8,128)(2,1)}, u32[]{:S(2)}, u32[]{:S(2)}) collective-permute-start(bf16[272,1280]{1,0:T(8,128)(2,1)} %get-tuple-element.172), channel_id=1, source_target_pairs={{0,4},{4,0},{8,12},{12,8},{16,20},{20,16},{24,28},{28,24},{1,5},{5... | collective-permute-start | bytes 2088968 | tf_op jit(solution)/shard_map/ppermute | solution.py:543
  415.5 58.8 %collective-permute-start.37 = (bf16[272,1280]{1,0:T(8,128)(2,1)S(1)}, bf16[272,1280]{1,0:T(8,128)(2,1)}, u32[]{:S(2)}, u32[]{:S(2)}) collective-permute-start(bf16[272,1280]{1,0:T(8,128)(2,1)S(1)} %get-tuple-element.174), channel_id=1, source_target_pairs={{0,4},{4,0},{8,12},{12,8},{16,20},{20,16},{24,28},{28,24},{1,5},{5... | collective-permute-start | bytes 2088968 | tf_op jit(solution)/shard_map/ppermute | solution.py:543
  417.8 6.1 %collective-permute-start.36 = (bf16[2,96,2048]{2,1,0:T(8,128)(2,1)S(1)}, bf16[2,96,2048]{2,1,0:T(8,128)(2,1)S(1)}, u32[]{:S(2)}, u32[]{:S(2)}) collective-permute-start(bf16[2,96,2048]{2,1,0:T(8,128)(2,1)S(1)} %pad_maximum_fusion.2), channel_id=1, source_target_pairs={{0,1},{1,0},{2,3},{3,2},{4,5},{5,4},{6,7},{7,6},{8,9},{9,8},{10,11... | collective-permute-start | bytes 2359304 | tf_op jit(solution)/shard_map/ppermute | solution.py:47
  432.7 16.3 %collective-permute-start.41 = (bf16[272,1280]{1,0:T(8,128)(2,1)S(1)}, bf16[272,1280]{1,0:T(8,128)(2,1)S(1)}, u32[]{:S(2)}, u32[]{:S(2)}) collective-permute-start(bf16[272,1280]{1,0:T(8,128)(2,1)S(1)} %fusion.5), channel_id=1, source_target_pairs={{0,24},{4,28},{8,16},{12,20},{16,8},{20,12},{24,0},{28,4},{1,25},{... | collective-permute-start | bytes 2088968 | tf_op jit(solution)/shard_map/ppermute | solution.py:546
  435.0 7.8 %collective-permute-start.31 = (bf16[96,2048]{1,0:T(8,128)(2,1)S(1)}, bf16[96,2048]{1,0:T(8,128)(2,1)S(1)}, u32[]{:S(2)}, u32[]{:S(2)}) collective-permute-start(bf16[96,2048]{1,0:T(8,128)(2,1)S(1)} %get-tuple-element.161), channel_id=1, source_target_pairs={{0,2},{1,3},{2,0},{3,1},{4,6},{5,7},{6,4},{7,5},{8,10},{9,11},{10,... | collective-permute-start | bytes 1179656 | tf_op jit(solution)/shard_map/ppermute | solution.py:47
  442.9 21.7 %collective-permute-start.32 = (bf16[2,96,2048]{2,1,0:T(8,128)(2,1)S(1)}, bf16[2,96,2048]{2,1,0:T(8,128)(2,1)S(1)}, u32[]{:S(2)}, u32[]{:S(2)}) collective-permute-start(bf16[2,96,2048]{2,1,0:T(8,128)(2,1)S(1)} %pad_maximum_fusion.1), channel_id=1, source_target_pairs={{0,1},{1,0},{2,3},{3,2},{4,5},{5,4},{6,7},{7,6},{8,9},{9,8},{10,11... | collective-permute-start | bytes 2359304 | tf_op jit(solution)/shard_map/ppermute | solution.py:47
  463.1 28.7 %collective-permute-start.39 = (bf16[272,1280]{1,0:T(8,128)(2,1)S(1)}, bf16[272,1280]{1,0:T(8,128)(2,1)S(1)}, u32[]{:S(2)}, u32[]{:S(2)}) collective-permute-start(bf16[272,1280]{1,0:T(8,128)(2,1)S(1)} %get-tuple-element.170), channel_id=1, source_target_pairs={{0,16},{4,20},{8,24},{12,28},{16,0},{20,4},{24,8},{28,12},{1,17},{... | collective-permute-start | bytes 2088968 | tf_op jit(solution)/shard_map/ppermute | solution.py:546
  463.2 29.9 %collective-permute-start.42 = (bf16[272,1280]{1,0:T(8,128)(2,1)S(1)}, bf16[272,1280]{1,0:T(8,128)(2,1)S(1)}, u32[]{:S(2)}, u32[]{:S(2)}) collective-permute-start(bf16[272,1280]{1,0:T(8,128)(2,1)S(1)} %get-tuple-element.171), channel_id=1, source_target_pairs={{0,8},{4,12},{8,0},{12,4},{16,24},{20,28},{24,16},{28,20},{1,9},{5... | collective-permute-start | bytes 2088968 | tf_op jit(solution)/shard_map/ppermute | solution.py:546
  494.9 1.3 collective-permute-start.43
  496.2 4.1 collective-permute-start.44
  (25 other events, 80.4 us)
Sparse Core Ops, SparseCore 0:
  10.8 85.9 all-gather.2
  130.9 116.1 all-gather.4
  316.0 86.2 reduce-scatter.1

commit v5 on v4

--- a/solution.py
+++ b/solution.py
@@ -725,23 +725,22 @@
     grad_normed_ffn = back_sum + mm(grad_logits, router, (1, 1))
     ffn_gain_part = jnp.sum(grad_normed_ffn * residual * inv_second, 0)
     grad_residual = grad_out + norm_back(grad_normed_ffn * ffn_gain, residual, inv_second)
-    grad_attn = gather_rows(bf(grad_residual))
-    grad_attn, *left = tie(grad_attn, *far_part[1:])
-    arrived += [swap(piece, 2) for piece in left]
     slice_rows = model_width // group
-    attn_cols = lax.all_to_all(
-        grad_attn.reshape(tok_count, group, slice_rows).transpose(1, 0, 2),
+    own_cols = lax.all_to_all(
+        bf(grad_residual).reshape(shard_rows, group, slice_rows).transpose(1, 0, 2),
         "expert",
         split_axis=0,
         concat_axis=0,
         tiled=True,
-    ).reshape(group * tok_count, slice_rows)
+    )
+    grad_attn = gather_rows(bf(grad_residual))
+    grad_attn, far_cols, *left = tie(grad_attn, swap(own_cols, 2), *far_part[1:])
+    arrived += [swap(piece, 2) for piece in left]
     grad_attn, out_part = tie(grad_attn, out_part)
     out_sum = lax.psum_scatter(
         out_part.reshape(group, shard_rows, model_width), "expert", scatter_dimension=0, tiled=False
     )
     spare = 16
-    grad_attn, attn_cols = tie(grad_attn, attn_cols)
     packed, gain_parts, attn_gain_part, keep, give_part = attend_back(
         ranks, hidden_in, normalized_input, grad_attn, w_query, w_key, value_weight, q_gain, k_gain, cosine,
         sine_table, w_out, qp, kp, q, k, v, prob, shard_rows, group, spare,
@@ -766,7 +765,12 @@
     packed = lax.dynamic_update_slice(
         packed, bf(small).reshape(group, spare, packed.shape[2]), (0, slice_rows, 0)
     )
-    packed, out_sum, _, _, _ = order.scatter(packed, out_sum, (), ())
+    packed, _, _, _, out_sum = order.scatter(packed, (), (), (), out_sum)
+    near_cols = swap(jnp.stack([own_cols, far_cols]), 1)
+    attn_cols = jnp.zeros((tensor_size, *own_cols.shape), own_cols.dtype)
+    for value, step in ((own_cols, 0), (far_cols, 2), (near_cols[0], 1), (near_cols[1], 3)):
+        attn_cols = lax.dynamic_update_index_in_dim(attn_cols, value, tensor_rank ^ step, 0)
+    attn_cols = attn_cols.transpose(1, 0, 2, 3).reshape(group * tok_count, slice_rows)
     w_out_grad = mm(attended_all, attn_cols, (0, 0))
     layer_out = gather_rows(bf(residual + out_sum.astype(jnp.float32)))
     query_width, key_width = w_query.shape[1], w_key.shape[1]

time: 520 us -> 557 us (1.071)
  starting transfers between devices: 55.6 us -> 74.4 us
  matrix products: 39.8 us -> 54.5 us
    ppermute x28 -> x30, waiting for transfers between devices: 72.4 us -> 109 us  [swap(): return lax.ppermute(value, 'tensor', [(i, i ^ step) for i in range(size)])]
    ppermute x12, waiting for transfers between devices: 58.8 us -> 27.4 us  [across(): return lax.ppermute(value, 'expert', [(i, i ^ 1) for i in range(8)])]
    ppermute x9, starting transfers between devices: 19.3 us -> 34.3 us  [along(): return lax.ppermute(value, 'expert', [(i, i ^ 2 * step) for i in range(8)])]
    dot_general x12, matrix products: 39.8 us -> 54.5 us  [mm(): lax.dot_general(left, right, (((contract[0],), (contract[1],)), ((), ()))...]
    ppermute x28 -> x30, starting transfers between devices: 18.6 us -> 22 us  [swap(): return lax.ppermute(value, 'tensor', [(i, i ^ step) for i in range(size)])]
  transfers between devices with their start and end apart: 53 -> 55, of which waited for: 31 -> 22; matrix products, arithmetic and copies ran while one was open for 19% -> 22% of each run, Pallas kernels for 21% -> 19%
where the time goes in v5:
time: 557 us; the launch traced here: 547 us
  waiting for transfers between devices  222 us (40%)
  Pallas kernels  106 us (19%)
  starting transfers between devices  74.4 us (13%)
  matrix products  54.5 us (10%)
  local copies, waits for them, and re-layouts  39 us (7%)
  other arithmetic  36.3 us (7%)
  between operations  15.1 us (3%)
    ppermute x30, waiting for transfers between devices, swap(): return lax.ppermute(value, 'tensor', [(i, i ^ step) for i in range(size)])  109 us
    ppermute x9, waiting for transfers between devices, along(): return lax.ppermute(value, 'expert', [(i, i ^ 2 * step) for i in range(8)])  74.1 us
    pallas_call x2, Pallas kernels, run_experts(): pl.pallas_call(functools.partial(experts_kernel, shards=shards, before=ea...  55.8 us
    dot_general x12, matrix products, mm(): lax.dot_general(left, right, (((contract[0],), (contract[1],)), ((), ()))...  54.5 us
    ppermute x9, starting transfers between devices, along(): return lax.ppermute(value, 'expert', [(i, i ^ 2 * step) for i in range(8)])  34.3 us
    pallas_call x1, Pallas kernels, attend_back(): pl.pallas_call(attend_back_kernel, grid_spec=pltpu.PrefetchScalarGridSpec...  28.6 us
    ppermute x12, waiting for transfers between devices, across(): return lax.ppermute(value, 'expert', [(i, i ^ 1) for i in range(8)])  27.4 us
    ppermute x30, starting transfers between devices, swap(): return lax.ppermute(value, 'tensor', [(i, i ^ step) for i in range(size)])  22 us
  transfers between devices with their start and end apart: 55, of which 22 were waited for; matrix products, arithmetic and copies ran while one was open for 22% of the time, Pallas kernels for 19%

profile of v5, /device:TPU:0, one launch (start us, length us, event | category | flops | bytes accessed | tf_op | source)
XLA Modules:
  0.0 547.0 jit_solution(5347784939833099642)
XLA Ops:
  10.0 3.0 collective-permute-start.1
  16.7 21.6 %attend.1 = (bf16[384,2048]{1,0:T(8,128)(2,1)}, f32[384,1024]{1,0:T(8,128)}, f32[384,128]{1,0:T(8,128)}, bf16[384,1024]{1,0:T(8,128)(2,1)}, bf16[384,128]{1,0:T(...) custom-call(s32[2]{0:T(128)} %pad_add_fusion.rank_ref, ...), custom_call_target="tpu_custom_call" | custom-call | flops 1048576 | bytes 65536 | tf_op jit(solution)/shard_map/attend/pallas_call | solution.py:136
  38.4 2.5 collective-permute-done
  41.8 1.8 convert_add_fusion.3
  43.6 3.9 collective-permute-done.1.rest_8_
  47.5 1.7 collective-permute-start.2
  49.5 10.0 %collective-permute-done.2 = bf16[96,2048]{1,0:T(8,128)(2,1)S(1)} collective-permute-done((bf16[96,2048]{1,0:T(8,128)(2,1)S(1)}, bf16[96,2048]{1,0:T(8,128)(2,1)S(1)}, u32[]{:S(2)}, u32[]{:S(2)}) %collective-permute-start.2) | collective-permute-done | bytes 393248 | tf_op jit(solution)/shard_map/ppermute | solution.py:47
  61.9 1.8 collective-permute-start.3
  63.7 2.6 collective-permute-start.7
  67.7 1.5 collective-permute-start.11
  69.2 3.0 collective-permute-done.3
  72.2 1.5 collective-permute-start.4
  73.7 26.6 %collective-permute-done.7 = bf16[96,2048]{1,0:T(8,128)(2,1)} collective-permute-done((bf16[96,2048]{1,0:T(8,128)(2,1)S(1)}, bf16[96,2048]{1,0:T(8,128)(2,1)}, u32[]{:S(2)}, u32[]{:S(2)}) %collective-permute-start.7) | collective-permute-done | bytes 393248 | tf_op jit(solution)/shard_map/ppermute | solution.py:546
  105.6 20.9 %collective-permute-done.6 = bf16[96,2048]{1,0:T(8,128)(2,1)S(1)} collective-permute-done((bf16[96,2048]{1,0:T(8,128)(2,1)}, bf16[96,2048]{1,0:T(8,128)(2,1)S(1)}, u32[]{:S(2)}, u32[]{:S(2)}) %collective-permute-start.6) | collective-permute-done | bytes 393248 | tf_op jit(solution)/shard_map/ppermute | solution.py:543
  132.0 4.0 collective-permute-done.12.rest_4_.rest_6_
  136.9 2.2 collective-permute-done.14.rest_7_.rest_13_
  139.1 17.9 %experts_near.1 = (bf16[768,1536]{1,0:T(8,128)(2,1)}, bf16[768,768]{1,0:T(8,128)(2,1)}, f32[768,128]{1,0:T(8,128)}, f32[768,128]{1,0:T(8,128)}) custom-call(s32[2]{0:T(128)} %pad_add_fusion.rank_ref, bf16[768,2048]{1,0:T(8,128)(2,1)} %bitcast.149, bf16[768,2176]{1,0:T(8,128)(2,1)} %all-gather.3.cloned.1.call-done.g.rest_0_, ...), custom_call_target="tpu_custom_call" | custom-call | flops 1048576 | bytes 65536 | tf_op jit(solution)/shard_map/experts_near/pallas_call | solution.py:517
  157.0 37.9 %experts_far.1 = (bf16[768,2048]{1,0:T(8,128)(2,1)}, bf16[768,2176]{1,0:T(8,128)(2,1)}, bf16[768,1536]{1,0:T(8,128)(2,1)}, bf16[768,768]{1,0:T(8,128)(2,1)}) custom-call(s32[2]{0:T(128)} %pad_add_fusion.rank_ref, bf16[768,2048]{1,0:T(8,128)(2,1)} %bitcast.150, bf16[768,2176]{1,0:T(8,128)(2,1)} %all-gather.3.cloned.1.call-done.g.rest_0_, ...), custom_call_target="tpu_custom_call" | custom-call | flops 1048576 | bytes 65536 | tf_op jit(solution)/shard_map/experts_far/pallas_call | solution.py:517
  195.0 6.7 %convolution_convert_fusion.1 = bf16[768,2048]{1,0:T(8,128)(2,1)} fusion(bf16[768,2048]{1,0:T(8,128)(2,1)} %bitcast.151, bf16[768,1536]{1,0:T(8,128)(2,1)} %get-tuple-element.88), kind=kOutput, calls=%fused_computation.3 | convolution fusion | flops 2417491968 | bytes 7471104 | tf_op jit(solution)/shard_map/dot_general | solution.py:36
  201.9 2.7 convolution_convert_fusion.3
  204.9 2.6 dynamic-slice_bitcast_fusion.6
  210.8 4.5 add_convert_fusion.1
  215.3 14.6 %add_convert_fusion = bf16[768,2048]{1,0:T(8,128)(2,1)S(1)} fusion(bf16[768,2048]{1,0:T(8,128)(2,1)} %collective-permute-done.23, bf16[768,2048]{1,0:T(8,128)(2,1)S(1)} %bitcast.153, bf16[768,1536]{1,0:T(8,128)(2,1)S(1)} %copy-done.35), kind=kOutput, calls=%fused_computation.1 | convolution fusion | flops 2420637696 | bytes 10616832 | tf_op jit(solution)/shard_map/dot_general | solution.py:36
  229.9 2.1 fusion.42
  232.0 1.9 fusion.14
  233.9 2.6 collective-permute-start.25
  236.6 1.5 collective-permute-start.27
  240.8 6.4 %collective-permute-done.25 = bf16[96,2176]{1,0:T(8,128)(2,1)} collective-permute-done((bf16[96,2176]{1,0:T(8,128)(2,1)}, bf16[96,2176]{1,0:T(8,128)(2,1)}, u32[]{:S(2)}, u32[]{:S(2)}) %collective-permute-start.25) | collective-permute-done | bytes 417824 | tf_op jit(solution)/shard_map/ppermute | solution.py:546
  247.2 1.6 fusion.15
  248.8 8.9 %collective-permute-start.20 = (bf16[96,2176]{1,0:T(8,128)(2,1)S(1)}, bf16[96,2176]{1,0:T(8,128)(2,1)}, u32[]{:S(2)}, u32[]{:S(2)}) collective-permute-start(bf16[96,2176]{1,0:T(8,128)(2,1)S(1)} %get-tuple-element.172), channel_id=1, source_target_pairs={{0,16},{4,20},{8,24},{12,28},{16,0},{20,4},{24,8},{28,12},{1,17},{... | collective-permute-start | bytes 1253384 | tf_op jit(solution)/shard_map/ppermute | solution.py:546
  257.7 5.9 %convolution_convert_fusion = bf16[768,2048]{1,0:T(8,128)(2,1)} fusion(bf16[768,2048]{1,0:T(8,128)(2,1)} %bitcast.152, bf16[768,1536]{1,0:T(8,128)(2,1)S(1)} %copy-done.18), kind=kOutput, calls=%fused_computation.2 | convolution fusion | flops 2417491968 | bytes 7471104 | tf_op jit(solution)/shard_map/dot_general | solution.py:36
  263.6 12.2 %collective-permute-done.26 = bf16[96,2176]{1,0:T(8,128)(2,1)} collective-permute-done((bf16[96,2176]{1,0:T(8,128)(2,1)S(1)}, bf16[96,2176]{1,0:T(8,128)(2,1)}, u32[]{:S(2)}, u32[]{:S(2)}) %collective-permute-start.26) | collective-permute-done | bytes 417824 | tf_op jit(solution)/shard_map/ppermute | solution.py:546
  275.9 1.8 fusion.16
  281.4 1.5 collective-permute-start.28
  282.9 2.6 convolution_convert_fusion.2
  285.5 5.5 %collective-permute-done.28 = bf16[96,2048]{1,0:T(8,128)(2,1)S(1)} collective-permute-done((bf16[96,2048]{1,0:T(8,128)(2,1)S(1)}, bf16[96,2048]{1,0:T(8,128)(2,1)S(1)}, u32[]{:S(2)}, u32[]{:S(2)}) %collective-permute-start.28) | collective-permute-done | bytes 393248 | tf_op jit(solution)/shard_map/ppermute | solution.py:47
  292.0 3.1 fusion.1
  296.5 3.5 all-to-all-start
  301.3 11.1 %all-to-all-done = bf16[8,96,256]{2,1,0:T(8,128)(2,1)S(1)} async-done(((bf16[8,96,256]{2,1,0:T(8,128)(2,1)}), bf16[8,96,256]{2,1,0:T(8,128)(2,1)S(1)}, u32[]{:S(2)}, u32[]{:S(2)}) %all-to-all-start) | async-done | bytes 393248 | tf_op jit(solution)/shard_map/all_to_all | solution.py:729
  312.4 1.5 collective-permute-start.30
  316.0 7.1 %collective-permute-done.30 = bf16[8,96,256]{2,1,0:T(8,128)(2,1)S(1)} collective-permute-done((bf16[8,96,256]{2,1,0:T(8,128)(2,1)S(1)}, bf16[8,96,256]{2,1,0:T(8,128)(2,1)S(1)}, u32[]{:S(2)}, u32[]{:S(2)}) %collective-permute-start.30) | collective-permute-done | bytes 393248 | tf_op jit(solution)/shard_map/ppermute | solution.py:47
  323.1 28.6 %attend_back.1 = (bf16[8,272,1280]{2,1,0:T(8,128)(2,1)}, f32[8,128]{1,0:T(8,128)}, f32[1,2048]{1,0:T(1,128)}, f32[2,96,2048]{2,1,0:T(8,128)}, bf16[2,96,2048]{2,1,0:T(8,128)(2,1)}) custom-call(s32[2]{0:T(128)} %pad_add_fusion.rank_ref, bf16[384,2048]{1,0:T(8,128)(2,1)} %x.5, bf16[384,2048]{1,0:T(8,128)(2,1)} %get-tuple-element.72.xn, ...), custom_call_target="tpu_custom_call" | custom-call | flops 30000001024 | bytes 1048576 | tf_op jit(solution)/shard_map/attend_back/pallas_call | solution.py:290
  354.0 3.1 dynamic-slice_bitcast_fusion
  358.6 6.3 %convert_add_fusion = f32[768,2048]{1,0:T(8,128)} fusion(bf16[768,2048]{1,0:T(8,128)(2,1)} %collective-permute-done.47, bf16[768,2048]{1,0:T(8,128)(2,1)S(1)} %bitcast.154, bf16[768,1536]{1,0:T(8,128)(2,1)S(1)} %copy-done.19), kind=kOutput, calls=%fused_computation | convolution fusion | flops 2419064832 | bytes 13762560 | tf_op jit(solution)/shard_map/dot_general | solution.py:36
  367.0 1.5 collective-permute-start.50
  370.0 3.4 collective-permute-done.32
  374.7 1.5 collective-permute-start.31
  376.5 1.6 collective-permute-start.37
  379.7 64.5 %collective-permute-done.37 = bf16[96,2048]{1,0:T(8,128)(2,1)S(1)} collective-permute-done((bf16[96,2048]{1,0:T(8,128)(2,1)S(1)}, bf16[96,2048]{1,0:T(8,128)(2,1)S(1)}, u32[]{:S(2)}, u32[]{:S(2)}) %collective-permute-start.37) | collective-permute-done | bytes 393248 | tf_op jit(solution)/shard_map/ppermute | solution.py:47
  444.6 1.6 constant_dynamic-update-slice_fusion.3
  446.2 1.6 collective-permute-start.38
  447.8 6.2 %fusion.47 = f32[1024,256]{1,0:T(8,128)} fusion(bf16[3072,1024]{1,0:T(8,128)(2,1)} %all-gather.5.cloned.1.call-done, bf16[3072,256]{1,0:T(8,128)(2,1)} %bitcast.61), kind=kOutput, calls=%fused_computation.146 | convolution fusion | flops 1610612736 | bytes 8912896 | tf_op jit(solution)/shard_map/dot_general | solution.py:36
  457.2 4.8 convert_add_fusion.1
  462.0 2.8 collective-permute-start.33
  464.9 5.6 %slice_add_fusion = (f32[384,2048]{1,0:T(8,128)}, f32[384,2048]{1,0:T(8,128)}) fusion(f32[768,2048]{1,0:T(8,128)S(1)} %bitcast.156, bf16[384,2048]{1,0:T(8,128)(2,1)} %collective-permute-done.48, bf16[384,2048]{1,0:T(8,128)(2,1)} %collective-permute-done.27), kind=kLoop, calls=%fused_computation.4 | loop fusion | flops 3145728 | bytes 15728640 | tf_op jit(solution)/shard_map/add | solution.py:789
  470.6 11.1 %collective-permute-done.33 = bf16[272,1280]{1,0:T(8,128)(2,1)} collective-permute-done((bf16[272,1280]{1,0:T(8,128)(2,1)S(1)}, bf16[272,1280]{1,0:T(8,128)(2,1)}, u32[]{:S(2)}, u32[]{:S(2)}) %collective-permute-start.33) | collective-permute-done | bytes 696352 | tf_op jit(solution)/shard_map/ppermute | solution.py:546
  481.7 2.1 fusion.6
  483.8 14.6 %collective-permute-start.42 = (bf16[272,1280]{1,0:T(8,128)(2,1)S(1)}, bf16[272,1280]{1,0:T(8,128)(2,1)S(1)}, u32[]{:S(2)}, u32[]{:S(2)}) collective-permute-start(bf16[272,1280]{1,0:T(8,128)(2,1)S(1)} %get-tuple-element.166), channel_id=1, source_target_pairs={{0,16},{4,20},{8,24},{12,28},{16,0},{20,4},{24,8},{28,12},{1,17},{... | collective-permute-start | bytes 2088968 | tf_op jit(solution)/shard_map/ppermute | solution.py:546
  500.5 1.5 collective-permute-start.34
  502.0 2.1 bitcast_convert_fusion
  504.2 6.4 %collective-permute-done.34 = bf16[96,2048]{1,0:T(8,128)(2,1)S(1)} collective-permute-done((bf16[96,2048]{1,0:T(8,128)(2,1)S(1)}, bf16[96,2048]{1,0:T(8,128)(2,1)S(1)}, u32[]{:S(2)}, u32[]{:S(2)}) %collective-permute-start.34) | collective-permute-done | bytes 393248 | tf_op jit(solution)/shard_map/ppermute | solution.py:47
  510.7 17.7 %collective-permute-done.42 = bf16[272,1280]{1,0:T(8,128)(2,1)S(1)} collective-permute-done((bf16[272,1280]{1,0:T(8,128)(2,1)S(1)}, bf16[272,1280]{1,0:T(8,128)(2,1)S(1)}, u32[]{:S(2)}, u32[]{:S(2)}) %collective-permute-start.42) | collective-permute-done | bytes 696352 | tf_op jit(solution)/shard_map/ppermute | solution.py:546
  528.5 1.9 fusion.7
  531.7 1.5 collective-permute-start.45
  (243 shorter events, 63.5 us)
Async XLA Ops:
  7.2 96.2 %all-gather.3.cloned.1.call-start = ((), (), s32[]{:S(2)}) async-start(), calls=%async_computation.2 | async-start | bytes 3760128 | tf_op jit(solution)/shard_map/all_gather | solution.py:625
  9.9 265.9 %all-gather.5.cloned.1.call-start = ((), (), s32[]{:S(2)}) async-start(), calls=%async_computation.3 | async-start | bytes 7077888 | tf_op jit(solution)/shard_map/all_gather | solution.py:675
  10.0 37.5 %collective-permute-start.1 = (bf16[384,2048]{1,0:T(8,128)(2,1)S(1)}, bf16[384,2048]{1,0:T(8,128)(2,1)}, u32[]{:S(2)}, u32[]{:S(2)}) collective-permute-start(bf16[384,2048]{1,0:T(8,128)(2,1)S(1)} %bitcast.160), channel_id=1, source_target_pairs={{0,2},{1,3},{2,0},{3,1},{4,6},{5,7},{6,4},{7,5},{8,10},{9,11},{10,... | collective-permute-start | bytes 4718600 | tf_op jit(solution)/shard_map/ppermute | solution.py:47
  38.3 2.6 collective-permute-start
  47.5 12.1 %collective-permute-start.2 = (bf16[96,2048]{1,0:T(8,128)(2,1)S(1)}, bf16[96,2048]{1,0:T(8,128)(2,1)S(1)}, u32[]{:S(2)}, u32[]{:S(2)}) collective-permute-start(bf16[96,2048]{1,0:T(8,128)(2,1)S(1)} %fusion.32), channel_id=1, source_target_pairs={{0,2},{1,3},{2,0},{3,1},{4,6},{5,7},{6,4},{7,5},{8,10},{9,11},{10,... | collective-permute-start | bytes 1179656 | tf_op jit(solution)/shard_map/ppermute | solution.py:47
  49.2 54.1 %collective-permute-start.5 = (bf16[384,2048]{1,0:T(8,128)(2,1)}, bf16[384,2048]{1,0:T(8,128)(2,1)}, u32[]{:S(2)}, u32[]{:S(2)}) collective-permute-start(bf16[384,2048]{1,0:T(8,128)(2,1)} %bitcast.12.rest_3_.rest_5_), channel_id=1, source_target_pairs={{0,2},{1,3},{2,0},{3,1},{4,6},{5,7},{6,4},{7,5},{8,10},{9,11},{10,... | collective-permute-start | bytes 4718600 | tf_op jit(solution)/shard_map/ppermute | solution.py:47
  61.9 65.7 %copy-start.15 = (bf16[96,2048]{1,0:T(8,128)(2,1)}, bf16[96,2048]{1,0:T(8,128)(2,1)S(1)}, u32[]{:S(2)}) copy-start(bf16[96,2048]{1,0:T(8,128)(2,1)S(1)} %get-tuple-element.161) | copy-start | bytes 1179652
  61.9 10.3 %collective-permute-start.3 = (bf16[96,2048]{1,0:T(8,128)(2,1)S(1)}, bf16[96,2048]{1,0:T(8,128)(2,1)}, u32[]{:S(2)}, u32[]{:S(2)}) collective-permute-start(bf16[96,2048]{1,0:T(8,128)(2,1)S(1)} %get-tuple-element.161), channel_id=1, source_target_pairs={{0,4},{4,0},{8,12},{12,8},{16,20},{20,16},{24,28},{28,24},{1,5},{5... | collective-permute-start | bytes 1179656 | tf_op jit(solution)/shard_map/ppermute | solution.py:543
  63.7 36.6 %collective-permute-start.7 = (bf16[96,2048]{1,0:T(8,128)(2,1)S(1)}, bf16[96,2048]{1,0:T(8,128)(2,1)}, u32[]{:S(2)}, u32[]{:S(2)}) collective-permute-start(bf16[96,2048]{1,0:T(8,128)(2,1)S(1)} %get-tuple-element.161), channel_id=1, source_target_pairs={{0,16},{4,20},{8,24},{12,28},{16,0},{20,4},{24,8},{28,12},{1,17},{... | collective-permute-start | bytes 1179656 | tf_op jit(solution)/shard_map/ppermute | solution.py:546
  66.3 35.1 %collective-permute-start.9 = (bf16[96,2048]{1,0:T(8,128)(2,1)S(1)}, bf16[96,2048]{1,0:T(8,128)(2,1)}, u32[]{:S(2)}, u32[]{:S(2)}) collective-permute-start(bf16[96,2048]{1,0:T(8,128)(2,1)S(1)} %get-tuple-element.161), channel_id=1, source_target_pairs={{0,24},{4,28},{8,16},{12,20},{16,8},{20,12},{24,0},{28,4},{1,25},{... | collective-permute-start | bytes 1179656 | tf_op jit(solution)/shard_map/ppermute | solution.py:546
  67.7 63.1 %collective-permute-start.11 = (bf16[384,2048]{1,0:T(8,128)(2,1)}, bf16[384,2048]{1,0:T(8,128)(2,1)}, u32[]{:S(2)}, u32[]{:S(2)}) collective-permute-start(bf16[384,2048]{1,0:T(8,128)(2,1)} %bitcast.19.rest_6_.rest_12_), channel_id=1, source_target_pairs={{0,2},{1,3},{2,0},{3,1},{4,6},{5,7},{6,4},{7,5},{8,10},{9,11},{10,... | collective-permute-start | bytes 4718600 | tf_op jit(solution)/shard_map/ppermute | solution.py:47
  72.2 31.2 %collective-permute-start.4 = (bf16[96,2048]{1,0:T(8,128)(2,1)S(1)}, bf16[96,2048]{1,0:T(8,128)(2,1)}, u32[]{:S(2)}, u32[]{:S(2)}) collective-permute-start(bf16[96,2048]{1,0:T(8,128)(2,1)S(1)} %get-tuple-element.161), channel_id=1, source_target_pairs={{0,8},{4,12},{8,0},{12,4},{16,24},{20,28},{24,16},{28,20},{1,9},{5... | collective-permute-start | bytes 1179656 | tf_op jit(solution)/shard_map/ppermute | solution.py:546
  100.3 27.3 %collective-permute-start.8 = (bf16[96,2048]{1,0:T(8,128)(2,1)}, bf16[96,2048]{1,0:T(8,128)(2,1)}, u32[]{:S(2)}, u32[]{:S(2)}) collective-permute-start(bf16[96,2048]{1,0:T(8,128)(2,1)} %collective-permute-done.7), channel_id=1, source_target_pairs={{0,4},{4,0},{8,12},{12,8},{16,20},{20,16},{24,28},{28,24},{1,5},{5... | collective-permute-start | bytes 1179656 | tf_op jit(solution)/shard_map/ppermute | solution.py:543
  101.4 28.3 %collective-permute-start.10 = (bf16[96,2048]{1,0:T(8,128)(2,1)}, bf16[96,2048]{1,0:T(8,128)(2,1)}, u32[]{:S(2)}, u32[]{:S(2)}) collective-permute-start(bf16[96,2048]{1,0:T(8,128)(2,1)} %collective-permute-done.9), channel_id=1, source_target_pairs={{0,4},{4,0},{8,12},{12,8},{16,20},{20,16},{24,28},{28,24},{1,5},{5... | collective-permute-start | bytes 1179656 | tf_op jit(solution)/shard_map/ppermute | solution.py:543
  103.4 23.1 %collective-permute-start.6 = (bf16[96,2048]{1,0:T(8,128)(2,1)}, bf16[96,2048]{1,0:T(8,128)(2,1)S(1)}, u32[]{:S(2)}, u32[]{:S(2)}) collective-permute-start(bf16[96,2048]{1,0:T(8,128)(2,1)} %collective-permute-done.4), channel_id=1, source_target_pairs={{0,4},{4,0},{8,12},{12,8},{16,20},{20,16},{24,28},{28,24},{1,5},{5... | collective-permute-start | bytes 1179656 | tf_op jit(solution)/shard_map/ppermute | solution.py:543
  130.8 5.1 collective-permute-start.12
  130.9 6.0 %collective-permute-start.13 = (bf16[384,2048]{1,0:T(8,128)(2,1)}, bf16[384,2048]{1,0:T(8,128)(2,1)}, u32[]{:S(2)}, u32[]{:S(2)}) collective-permute-start(bf16[384,2048]{1,0:T(8,128)(2,1)} %bitcast.12.rest_3_.rest_5_), channel_id=1, source_target_pairs={{0,1},{1,0},{2,3},{3,2},{4,5},{5,4},{6,7},{7,6},{8,9},{9,8},{10,11... | collective-permute-start | bytes 4718600 | tf_op jit(solution)/shard_map/ppermute | solution.py:47
  131.4 7.7 %collective-permute-start.14 = (bf16[384,2048]{1,0:T(8,128)(2,1)}, bf16[384,2048]{1,0:T(8,128)(2,1)}, u32[]{:S(2)}, u32[]{:S(2)}) collective-permute-start(bf16[384,2048]{1,0:T(8,128)(2,1)} %bitcast.19.rest_6_.rest_12_), channel_id=1, source_target_pairs={{0,1},{1,0},{2,3},{3,2},{4,5},{5,4},{6,7},{7,6},{8,9},{9,8},{10,11... | collective-permute-start | bytes 4718600 | tf_op jit(solution)/shard_map/ppermute | solution.py:47
  131.5 25.6 %collective-permute-start.15 = (bf16[384,2048]{1,0:T(8,128)(2,1)}, bf16[384,2048]{1,0:T(8,128)(2,1)}, u32[]{:S(2)}, u32[]{:S(2)}) collective-permute-start(bf16[384,2048]{1,0:T(8,128)(2,1)} %collective-permute-done.1.rest_8_), channel_id=1, source_target_pairs={{0,1},{1,0},{2,3},{3,2},{4,5},{5,4},{6,7},{7,6},{8,9},{9,8},{10,11... | collective-permute-start | bytes 4718600 | tf_op jit(solution)/shard_map/ppermute | solution.py:47
  131.9 25.1 %collective-permute-start.16 = (bf16[384,2048]{1,0:T(8,128)(2,1)}, bf16[384,2048]{1,0:T(8,128)(2,1)}, u32[]{:S(2)}, u32[]{:S(2)}) collective-permute-start(bf16[384,2048]{1,0:T(8,128)(2,1)} %collective-permute-done.5.rest_9_), channel_id=1, source_target_pairs={{0,1},{1,0},{2,3},{3,2},{4,5},{5,4},{6,7},{7,6},{8,9},{9,8},{10,11... | collective-permute-start | bytes 4718600 | tf_op jit(solution)/shard_map/ppermute | solution.py:47
  135.9 21.1 %collective-permute-start.17 = (bf16[384,2048]{1,0:T(8,128)(2,1)}, bf16[384,2048]{1,0:T(8,128)(2,1)}, u32[]{:S(2)}, u32[]{:S(2)}) collective-permute-start(bf16[384,2048]{1,0:T(8,128)(2,1)} %collective-permute-done.11.rest_14_), channel_id=1, source_target_pairs={{0,1},{1,0},{2,3},{3,2},{4,5},{5,4},{6,7},{7,6},{8,9},{9,8},{10,11... | collective-permute-start | bytes 4718600 | tf_op jit(solution)/shard_map/ppermute | solution.py:47
  201.7 13.6 %collective-permute-start.23 = (bf16[768,2048]{1,0:T(8,128)(2,1)}, bf16[768,2048]{1,0:T(8,128)(2,1)}, u32[]{:S(2)}, u32[]{:S(2)}) collective-permute-start(bf16[768,2048]{1,0:T(8,128)(2,1)} %convolution_convert_fusion.1), channel_id=1, source_target_pairs={{0,1},{1,0},{2,3},{3,2},{4,5},{5,4},{6,7},{7,6},{8,9},{9,8},{10,11... | collective-permute-start | bytes 9437192 | tf_op jit(solution)/shard_map/ppermute | solution.py:47
  204.5 6.2 %collective-permute-start.24 = (bf16[384,2048]{1,0:T(8,128)(2,1)}, bf16[384,2048]{1,0:T(8,128)(2,1)}, u32[]{:S(2)}, u32[]{:S(2)}) collective-permute-start(bf16[384,2048]{1,0:T(8,128)(2,1)} %convolution_convert_fusion.3), channel_id=1, source_target_pairs={{0,1},{1,0},{2,3},{3,2},{4,5},{5,4},{6,7},{7,6},{8,9},{9,8},{10,11... | collective-permute-start | bytes 4718600 | tf_op jit(solution)/shard_map/ppermute | solution.py:47
  207.4 24.5 %collective-permute-start.22 = (bf16[96,2176]{1,0:T(8,128)(2,1)S(1)}, bf16[96,2176]{1,0:T(8,128)(2,1)S(1)}, u32[]{:S(2)}, u32[]{:S(2)}) collective-permute-start(bf16[96,2176]{1,0:T(8,128)(2,1)S(1)} %get-tuple-element.175), channel_id=1, source_target_pairs={{0,4},{4,0},{8,12},{12,8},{16,20},{20,16},{24,28},{28,24},{1,5},{5... | collective-permute-start | bytes 1253384 | tf_op jit(solution)/shard_map/ppermute | solution.py:543
  208.7 32.1 %collective-permute-start.21 = (bf16[96,2176]{1,0:T(8,128)(2,1)}, bf16[96,2176]{1,0:T(8,128)(2,1)}, u32[]{:S(2)}, u32[]{:S(2)}) collective-permute-start(bf16[96,2176]{1,0:T(8,128)(2,1)} %get-tuple-element.176), channel_id=1, source_target_pairs={{0,4},{4,0},{8,12},{12,8},{16,20},{20,16},{24,28},{28,24},{1,5},{5... | collective-permute-start | bytes 1253384 | tf_op jit(solution)/shard_map/ppermute | solution.py:543
  209.5 37.7 %collective-permute-start.19 = (bf16[96,2176]{1,0:T(8,128)(2,1)}, bf16[96,2176]{1,0:T(8,128)(2,1)}, u32[]{:S(2)}, u32[]{:S(2)}) collective-permute-start(bf16[96,2176]{1,0:T(8,128)(2,1)} %get-tuple-element.174), channel_id=1, source_target_pairs={{0,4},{4,0},{8,12},{12,8},{16,20},{20,16},{24,28},{28,24},{1,5},{5... | collective-permute-start | bytes 1253384 | tf_op jit(solution)/shard_map/ppermute | solution.py:543
  233.9 13.3 %collective-permute-start.25 = (bf16[96,2176]{1,0:T(8,128)(2,1)}, bf16[96,2176]{1,0:T(8,128)(2,1)}, u32[]{:S(2)}, u32[]{:S(2)}) collective-permute-start(bf16[96,2176]{1,0:T(8,128)(2,1)} %fusion.14), channel_id=1, source_target_pairs={{0,24},{4,28},{8,16},{12,20},{16,8},{20,12},{24,0},{28,4},{1,25},{... | collective-permute-start | bytes 1253384 | tf_op jit(solution)/shard_map/ppermute | solution.py:546
  236.6 21.1 %copy-start.18 = (bf16[768,1536]{1,0:T(8,128)(2,1)S(1)}, bf16[768,1536]{1,0:T(8,128)(2,1)}, u32[]{:S(2)}) copy-start(bf16[768,1536]{1,0:T(8,128)(2,1)} %get-tuple-element.80.rest_2_) | copy-start | bytes 7077892
  236.6 39.2 %collective-permute-start.27 = (bf16[384,2048]{1,0:T(8,128)(2,1)}, bf16[384,2048]{1,0:T(8,128)(2,1)}, u32[]{:S(2)}, u32[]{:S(2)}) collective-permute-start(bf16[384,2048]{1,0:T(8,128)(2,1)} %get-tuple-element.179), channel_id=1, source_target_pairs={{0,2},{1,3},{2,0},{3,1},{4,6},{5,7},{6,4},{7,5},{8,10},{9,11},{10,... | collective-permute-start | bytes 4718600 | tf_op jit(solution)/shard_map/ppermute | solution.py:47
  239.7 36.1 %collective-permute-start.18 = (bf16[96,2176]{1,0:T(8,128)(2,1)}, bf16[96,2176]{1,0:T(8,128)(2,1)}, u32[]{:S(2)}, u32[]{:S(2)}) collective-permute-start(bf16[96,2176]{1,0:T(8,128)(2,1)} %get-tuple-element.177), channel_id=1, source_target_pairs={{0,4},{4,0},{8,12},{12,8},{16,20},{20,16},{24,28},{28,24},{1,5},{5... | collective-permute-start | bytes 1253384 | tf_op jit(solution)/shard_map/ppermute | solution.py:543
  248.8 27.0 %collective-permute-start.20 = (bf16[96,2176]{1,0:T(8,128)(2,1)S(1)}, bf16[96,2176]{1,0:T(8,128)(2,1)}, u32[]{:S(2)}, u32[]{:S(2)}) collective-permute-start(bf16[96,2176]{1,0:T(8,128)(2,1)S(1)} %get-tuple-element.172), channel_id=1, source_target_pairs={{0,16},{4,20},{8,24},{12,28},{16,0},{20,4},{24,8},{28,12},{1,17},{... | collective-permute-start | bytes 1253384 | tf_op jit(solution)/shard_map/ppermute | solution.py:546
  257.7 18.1 %collective-permute-start.26 = (bf16[96,2176]{1,0:T(8,128)(2,1)S(1)}, bf16[96,2176]{1,0:T(8,128)(2,1)}, u32[]{:S(2)}, u32[]{:S(2)}) collective-permute-start(bf16[96,2176]{1,0:T(8,128)(2,1)S(1)} %get-tuple-element.173), channel_id=1, source_target_pairs={{0,8},{4,12},{8,0},{12,4},{16,24},{20,28},{24,16},{28,20},{1,9},{5... | collective-permute-start | bytes 1253384 | tf_op jit(solution)/shard_map/ppermute | solution.py:546
  263.6 14.4 %copy-start.32 = (f32[96]{0:T(128)S(1)}, f32[96]{0:T(128)}, u32[]{:S(2)}) copy-start(f32[96]{0:T(128)} %copy-done.31) | copy-start | bytes 1156
  281.4 9.6 %collective-permute-start.28 = (bf16[96,2048]{1,0:T(8,128)(2,1)S(1)}, bf16[96,2048]{1,0:T(8,128)(2,1)S(1)}, u32[]{:S(2)}, u32[]{:S(2)}) collective-permute-start(bf16[96,2048]{1,0:T(8,128)(2,1)S(1)} %get-tuple-element.159), channel_id=1, source_target_pairs={{0,2},{1,3},{2,0},{3,1},{4,6},{5,7},{6,4},{7,5},{8,10},{9,11},{10,... | collective-permute-start | bytes 1179656 | tf_op jit(solution)/shard_map/ppermute | solution.py:47
  292.0 21.9 %collective-permute-start.29 = (bf16[2,96,2048]{2,1,0:T(8,128)(2,1)}, bf16[2,96,2048]{2,1,0:T(8,128)(2,1)}, u32[]{:S(2)}, u32[]{:S(2)}) collective-permute-start(bf16[2,96,2048]{2,1,0:T(8,128)(2,1)} %pad_maximum_fusion), channel_id=1, source_target_pairs={{0,1},{1,0},{2,3},{3,2},{4,5},{5,4},{6,7},{7,6},{8,9},{9,8},{10,11... | collective-permute-start | bytes 2359304 | tf_op jit(solution)/shard_map/ppermute | solution.py:47
  295.1 161.3 %collective-permute-start.49 = (bf16[384,2048]{1,0:T(8,128)(2,1)}, bf16[384,2048]{1,0:T(8,128)(2,1)}, u32[]{:S(2)}, u32[]{:S(2)}) collective-permute-start(bf16[384,2048]{1,0:T(8,128)(2,1)} %convolution_convert_fusion.2), channel_id=1, source_target_pairs={{0,1},{1,0},{2,3},{3,2},{4,5},{5,4},{6,7},{7,6},{8,9},{9,8},{10,11... | collective-permute-start | bytes 4718600 | tf_op jit(solution)/shard_map/ppermute | solution.py:47
  295.6 63.0 %collective-permute-start.47 = (bf16[768,2048]{1,0:T(8,128)(2,1)}, bf16[768,2048]{1,0:T(8,128)(2,1)}, u32[]{:S(2)}, u32[]{:S(2)}) collective-permute-start(bf16[768,2048]{1,0:T(8,128)(2,1)} %convolution_convert_fusion), channel_id=1, source_target_pairs={{0,1},{1,0},{2,3},{3,2},{4,5},{5,4},{6,7},{7,6},{8,9},{9,8},{10,11... | collective-permute-start | bytes 9437192 | tf_op jit(solution)/shard_map/ppermute | solution.py:47
  296.5 15.9 %all-to-all-start = ((bf16[8,96,256]{2,1,0:T(8,128)(2,1)}), bf16[8,96,256]{2,1,0:T(8,128)(2,1)S(1)}, u32[]{:S(2)}, u32[]{:S(2)}) async-start(bf16[8,96,256]{2,1,0:T(8,128)(2,1)} %bitcast.148), calls=%async_computation | async-start | bytes 786432 | tf_op jit(solution)/shard_map/all_to_all | solution.py:729
  299.9 181.8 %reduce-scatter.2.cloned.1.call-start = ((), (), s32[]{:S(2)}) async-start(), calls=%async_computation.4 | async-start | bytes 3538944 | tf_op jit(solution)/shard_map/reduce_scatter | solution.py:740
  312.4 10.7 %collective-permute-start.30 = (bf16[8,96,256]{2,1,0:T(8,128)(2,1)S(1)}, bf16[8,96,256]{2,1,0:T(8,128)(2,1)S(1)}, u32[]{:S(2)}, u32[]{:S(2)}) collective-permute-start(bf16[8,96,256]{2,1,0:T(8,128)(2,1)S(1)} %all-to-all-done), channel_id=1, source_target_pairs={{0,2},{1,3},{2,0},{3,1},{4,6},{5,7},{6,4},{7,5},{8,10},{9,11},{10,... | collective-permute-start | bytes 1179656 | tf_op jit(solution)/shard_map/ppermute | solution.py:47
  357.1 16.3 %collective-permute-start.32 = (bf16[272,1280]{1,0:T(8,128)(2,1)S(1)}, bf16[272,1280]{1,0:T(8,128)(2,1)S(1)}, u32[]{:S(2)}, u32[]{:S(2)}) collective-permute-start(bf16[272,1280]{1,0:T(8,128)(2,1)S(1)} %get-tuple-element.170), channel_id=1, source_target_pairs={{0,4},{4,0},{8,12},{12,8},{16,20},{20,16},{24,28},{28,24},{1,5},{5... | collective-permute-start | bytes 2088968 | tf_op jit(solution)/shard_map/ppermute | solution.py:543
  367.0 90.2 %collective-permute-start.50 = (bf16[384,2048]{1,0:T(8,128)(2,1)}, bf16[384,2048]{1,0:T(8,128)(2,1)}, u32[]{:S(2)}, u32[]{:S(2)}) collective-permute-start(bf16[384,2048]{1,0:T(8,128)(2,1)} %add_convert_fusion.1), channel_id=1, source_target_pairs={{0,2},{1,3},{2,0},{3,1},{4,6},{5,7},{6,4},{7,5},{8,10},{9,11},{10,... | collective-permute-start | bytes 4718600 | tf_op jit(solution)/shard_map/ppermute | solution.py:47
  368.5 93.5 %collective-permute-start.48 = (bf16[384,2048]{1,0:T(8,128)(2,1)}, bf16[384,2048]{1,0:T(8,128)(2,1)}, u32[]{:S(2)}, u32[]{:S(2)}) collective-permute-start(bf16[384,2048]{1,0:T(8,128)(2,1)} %get-tuple-element.120), channel_id=1, source_target_pairs={{0,2},{1,3},{2,0},{3,1},{4,6},{5,7},{6,4},{7,5},{8,10},{9,11},{10,... | collective-permute-start | bytes 4718600 | tf_op jit(solution)/shard_map/ppermute | solution.py:47
  369.0 5.7 %collective-permute-start.36 = (bf16[2,96,2048]{2,1,0:T(8,128)(2,1)}, bf16[2,96,2048]{2,1,0:T(8,128)(2,1)S(1)}, u32[]{:S(2)}, u32[]{:S(2)}) collective-permute-start(bf16[2,96,2048]{2,1,0:T(8,128)(2,1)} %get-tuple-element.112), channel_id=1, source_target_pairs={{0,1},{1,0},{2,3},{3,2},{4,5},{5,4},{6,7},{7,6},{8,9},{9,8},{10,11... | collective-permute-start | bytes 2359304 | tf_op jit(solution)/shard_map/ppermute | solution.py:47
  373.4 3.1 collective-permute-start.46
  374.7 95.9 %collective-permute-start.31 = (bf16[272,1280]{1,0:T(8,128)(2,1)}, bf16[272,1280]{1,0:T(8,128)(2,1)}, u32[]{:S(2)}, u32[]{:S(2)}) collective-permute-start(bf16[272,1280]{1,0:T(8,128)(2,1)} %get-tuple-element.171), channel_id=1, source_target_pairs={{0,4},{4,0},{8,12},{12,8},{16,20},{20,16},{24,28},{28,24},{1,5},{5... | collective-permute-start | bytes 2088968 | tf_op jit(solution)/shard_map/ppermute | solution.py:543
  376.4 67.7 %copy-start.14 = (bf16[384,2048]{1,0:T(8,128)(2,1)S(1)}, bf16[384,2048]{1,0:T(8,128)(2,1)}, u32[]{:S(2)}) copy-start(bf16[384,2048]{1,0:T(8,128)(2,1)} %x.5) | copy-start | bytes 4718596
  376.4 67.7 %copy-start.30 = (f32[2048]{0:T(1024)S(1)}, f32[2048]{0:T(1024)}, u32[]{:S(2)}) copy-start(f32[2048]{0:T(1024)} %param.22) | copy-start | bytes 24580
  376.5 67.6 %collective-permute-start.37 = (bf16[96,2048]{1,0:T(8,128)(2,1)S(1)}, bf16[96,2048]{1,0:T(8,128)(2,1)S(1)}, u32[]{:S(2)}, u32[]{:S(2)}) collective-permute-start(bf16[96,2048]{1,0:T(8,128)(2,1)S(1)} %fusion.33), channel_id=1, source_target_pairs={{0,2},{1,3},{2,0},{3,1},{4,6},{5,7},{6,4},{7,5},{8,10},{9,11},{10,... | collective-permute-start | bytes 1179656 | tf_op jit(solution)/shard_map/ppermute | solution.py:47
  379.7 65.0 %copy-start.5 = (f32[96,2048]{1,0:T(8,128)S(1)}, f32[96,2048]{1,0:T(8,128)}, u32[]{:S(2)}) copy-start(f32[96,2048]{1,0:T(8,128)} %copy-done.3) | copy-start | bytes 2359300
  379.7 65.0 %copy-start.11 = (f32[96,2048]{1,0:T(8,128)S(1)}, f32[96,2048]{1,0:T(8,128)}, u32[]{:S(2)}) copy-start(f32[96,2048]{1,0:T(8,128)} %copy-done.10) | copy-start | bytes 2359300
  446.2 8.7 %collective-permute-start.38 = (bf16[96,2048]{1,0:T(8,128)(2,1)S(1)}, bf16[96,2048]{1,0:T(8,128)(2,1)S(1)}, u32[]{:S(2)}, u32[]{:S(2)}) collective-permute-start(bf16[96,2048]{1,0:T(8,128)(2,1)S(1)} %get-tuple-element.155), channel_id=1, source_target_pairs={{0,2},{1,3},{2,0},{3,1},{4,6},{5,7},{6,4},{7,5},{8,10},{9,11},{10,... | collective-permute-start | bytes 1179656 | tf_op jit(solution)/shard_map/ppermute | solution.py:47
  447.8 9.4 %copy-start.9 = (f32[384,2048]{1,0:T(8,128)S(1)}, f32[384,2048]{1,0:T(8,128)}, u32[]{:S(2)}) copy-start(f32[384,2048]{1,0:T(8,128)} %fusion.1) | copy-start | bytes 9437188
  455.0 26.7 %collective-permute-start.41 = (bf16[272,1280]{1,0:T(8,128)(2,1)}, bf16[272,1280]{1,0:T(8,128)(2,1)}, u32[]{:S(2)}, u32[]{:S(2)}) collective-permute-start(bf16[272,1280]{1,0:T(8,128)(2,1)} %get-tuple-element.168), channel_id=1, source_target_pairs={{0,4},{4,0},{8,12},{12,8},{16,20},{20,16},{24,28},{28,24},{1,5},{5... | collective-permute-start | bytes 2088968 | tf_op jit(solution)/shard_map/ppermute | solution.py:543
  456.4 54.3 %collective-permute-start.40 = (bf16[272,1280]{1,0:T(8,128)(2,1)S(1)}, bf16[272,1280]{1,0:T(8,128)(2,1)}, u32[]{:S(2)}, u32[]{:S(2)}) collective-permute-start(bf16[272,1280]{1,0:T(8,128)(2,1)S(1)} %get-tuple-element.169), channel_id=1, source_target_pairs={{0,4},{4,0},{8,12},{12,8},{16,20},{20,16},{24,28},{28,24},{1,5},{5... | collective-permute-start | bytes 2088968 | tf_op jit(solution)/shard_map/ppermute | solution.py:543
  457.2 13.3 %collective-permute-start.39 = (bf16[2,96,2048]{2,1,0:T(8,128)(2,1)S(1)}, bf16[2,96,2048]{2,1,0:T(8,128)(2,1)S(1)}, u32[]{:S(2)}, u32[]{:S(2)}) collective-permute-start(bf16[2,96,2048]{2,1,0:T(8,128)(2,1)S(1)} %pad_maximum_fusion.2), channel_id=1, source_target_pairs={{0,1},{1,0},{2,3},{3,2},{4,5},{5,4},{6,7},{7,6},{8,9},{9,8},{10,11... | collective-permute-start | bytes 2359304 | tf_op jit(solution)/shard_map/ppermute | solution.py:47
  462.0 19.7 %collective-permute-start.33 = (bf16[272,1280]{1,0:T(8,128)(2,1)S(1)}, bf16[272,1280]{1,0:T(8,128)(2,1)}, u32[]{:S(2)}, u32[]{:S(2)}) collective-permute-start(bf16[272,1280]{1,0:T(8,128)(2,1)S(1)} %fusion.8), channel_id=1, source_target_pairs={{0,24},{4,28},{8,16},{12,20},{16,8},{20,12},{24,0},{28,4},{1,25},{... | collective-permute-start | bytes 2088968 | tf_op jit(solution)/shard_map/ppermute | solution.py:546
  483.8 15.9 %copy-start.28 = (bf16[1,96,2048]{2,1,0:T(8,128)(2,1)S(1)}, bf16[1,96,2048]{2,1,0:T(8,128)(2,1)}, u32[]{:S(2)}) copy-start(bf16[1,96,2048]{2,1,0:T(8,128)(2,1)} %reduce-scatter.2.cloned.1.call-done) | copy-start | bytes 1179652
  483.8 44.6 %collective-permute-start.42 = (bf16[272,1280]{1,0:T(8,128)(2,1)S(1)}, bf16[272,1280]{1,0:T(8,128)(2,1)S(1)}, u32[]{:S(2)}, u32[]{:S(2)}) collective-permute-start(bf16[272,1280]{1,0:T(8,128)(2,1)S(1)} %get-tuple-element.166), channel_id=1, source_target_pairs={{0,16},{4,20},{8,24},{12,28},{16,0},{20,4},{24,8},{28,12},{1,17},{... | collective-permute-start | bytes 2088968 | tf_op jit(solution)/shard_map/ppermute | solution.py:546
  498.3 30.1 %collective-permute-start.43 = (bf16[272,1280]{1,0:T(8,128)(2,1)S(1)}, bf16[272,1280]{1,0:T(8,128)(2,1)S(1)}, u32[]{:S(2)}, u32[]{:S(2)}) collective-permute-start(bf16[272,1280]{1,0:T(8,128)(2,1)S(1)} %get-tuple-element.167), channel_id=1, source_target_pairs={{0,8},{4,12},{8,0},{12,4},{16,24},{20,28},{24,16},{28,20},{1,9},{5... | collective-permute-start | bytes 2088968 | tf_op jit(solution)/shard_map/ppermute | solution.py:546
  500.5 10.0 %collective-permute-start.34 = (bf16[96,2048]{1,0:T(8,128)(2,1)S(1)}, bf16[96,2048]{1,0:T(8,128)(2,1)S(1)}, u32[]{:S(2)}, u32[]{:S(2)}) collective-permute-start(bf16[96,2048]{1,0:T(8,128)(2,1)S(1)} %get-tuple-element.157), channel_id=1, source_target_pairs={{0,2},{1,3},{2,0},{3,1},{4,6},{5,7},{6,4},{7,5},{8,10},{9,11},{10,... | collective-permute-start | bytes 1179656 | tf_op jit(solution)/shard_map/ppermute | solution.py:47
  510.6 27.9 %collective-permute-start.35 = (bf16[2,96,2048]{2,1,0:T(8,128)(2,1)S(1)}, bf16[2,96,2048]{2,1,0:T(8,128)(2,1)S(1)}, u32[]{:S(2)}, u32[]{:S(2)}) collective-permute-start(bf16[2,96,2048]{2,1,0:T(8,128)(2,1)S(1)} %pad_maximum_fusion.1), channel_id=1, source_target_pairs={{0,1},{1,0},{2,3},{3,2},{4,5},{5,4},{6,7},{7,6},{8,9},{9,8},{10,11... | collective-permute-start | bytes 2359304 | tf_op jit(solution)/shard_map/ppermute | solution.py:47
  530.4 1.3 collective-permute-start.44
  531.7 4.1 collective-permute-start.45
  (31 other events, 147.0 us)
Sparse Core Ops, SparseCore 0:
  10.8 85.9 all-gather.2
  130.9 98.3 all-gather.4
  369.2 78.2 reduce-scatter.1

commit v6 on v5

--- a/solution.py
+++ b/solution.py
@@ -765,7 +765,7 @@
     packed = lax.dynamic_update_slice(
         packed, bf(small).reshape(group, spare, packed.shape[2]), (0, slice_rows, 0)
     )
-    packed, _, _, _, out_sum = order.scatter(packed, (), (), (), out_sum)
+    packed, out_sum, _, _, _ = order.scatter(packed, out_sum, (), ())
     near_cols = swap(jnp.stack([own_cols, far_cols]), 1)
     attn_cols = jnp.zeros((tensor_size, *own_cols.shape), own_cols.dtype)
     for value, step in ((own_cols, 0), (far_cols, 2), (near_cols[0], 1), (near_cols[1], 3)):

time: 557 us -> 520 us (0.934)
  waiting for transfers between devices: 222 us -> 197 us
  matrix products: 54.5 us -> 39.2 us
    ppermute x30, waiting for transfers between devices: 109 us -> 84.5 us  [swap(): return lax.ppermute(value, 'tensor', [(i, i ^ step) for i in range(size)])]
    dot_general x12, matrix products: 54.5 us -> 39.2 us  [mm(): lax.dot_general(left, right, (((contract[0],), (contract[1],)), ((), ()))...]
    reduce_scatter x1, waiting for transfers between devices: 0.01 us -> 13.6 us  [body(): lax.psum_scatter(out_part.reshape(group, shard_rows, model_width), 'exper...]
    ppermute x9, waiting for transfers between devices: 74.1 us -> 67.7 us  [along(): return lax.ppermute(value, 'expert', [(i, i ^ 2 * step) for i in range(8)])]
  transfers between devices with their start and end apart: 55 -> 55, of which waited for: 22 -> 23; matrix products, arithmetic and copies ran while one was open for 22% -> 21% of each run, Pallas kernels for 19% -> 21%
where the time goes in v6:
time: 520 us; the launch traced here: 510 us
  waiting for transfers between devices  197 us (38%)
  Pallas kernels  106 us (20%)
  starting transfers between devices  75.4 us (15%)
  local copies, waits for them, and re-layouts  41.8 us (8%)
  matrix products  39.2 us (8%)
  other arithmetic  35.8 us (7%)
  between operations  14.9 us (3%)
    ppermute x30, waiting for transfers between devices, swap(): return lax.ppermute(value, 'tensor', [(i, i ^ step) for i in range(size)])  84.5 us
    ppermute x9, waiting for transfers between devices, along(): return lax.ppermute(value, 'expert', [(i, i ^ 2 * step) for i in range(8)])  67.7 us
    pallas_call x2, Pallas kernels, run_experts(): pl.pallas_call(functools.partial(experts_kernel, shards=shards, before=ea...  55.7 us
    dot_general x12, matrix products, mm(): lax.dot_general(left, right, (((contract[0],), (contract[1],)), ((), ()))...  39.2 us
    ppermute x9, starting transfers between devices, along(): return lax.ppermute(value, 'expert', [(i, i ^ 2 * step) for i in range(8)])  34 us
    pallas_call x1, Pallas kernels, attend_back(): pl.pallas_call(attend_back_kernel, grid_spec=pltpu.PrefetchScalarGridSpec...  28.8 us
    ppermute x12, waiting for transfers between devices, across(): return lax.ppermute(value, 'expert', [(i, i ^ 1) for i in range(8)])  22.5 us
    pallas_call x1, Pallas kernels, attend(): pl.pallas_call(attend_kernel, grid_spec=pltpu.PrefetchScalarGridSpec(num_...  21.6 us
  transfers between devices with their start and end apart: 55, of which 23 were waited for; matrix products, arithmetic and copies ran while one was open for 21% of the time, Pallas kernels for 21%

profile of v6, /device:TPU:0, one launch (start us, length us, event | category | flops | bytes accessed | tf_op | source)
XLA Modules:
  0.0 509.9 jit_solution(10373991439488257210)
XLA Ops:
  10.0 3.0 collective-permute-start.1
  16.6 21.6 %attend.1 = (bf16[384,2048]{1,0:T(8,128)(2,1)}, f32[384,1024]{1,0:T(8,128)}, f32[384,128]{1,0:T(8,128)}, bf16[384,1024]{1,0:T(8,128)(2,1)}, bf16[384,128]{1,0:T(...) custom-call(s32[2]{0:T(128)} %pad_add_fusion.rank_ref, ...), custom_call_target="tpu_custom_call" | custom-call | flops 1048576 | bytes 65536 | tf_op jit(solution)/shard_map/attend/pallas_call | solution.py:136
  38.4 2.5 collective-permute-done
  41.7 1.8 convert_add_fusion.3
  44.3 3.3 collective-permute-done.1.rest_8_
  47.6 1.7 collective-permute-start.2
  49.6 10.2 %collective-permute-done.2 = bf16[96,2048]{1,0:T(8,128)(2,1)S(1)} collective-permute-done((bf16[96,2048]{1,0:T(8,128)(2,1)}, bf16[96,2048]{1,0:T(8,128)(2,1)S(1)}, u32[]{:S(2)}, u32[]{:S(2)}) %collective-permute-start.2) | collective-permute-done | bytes 393248 | tf_op jit(solution)/shard_map/ppermute | solution.py:47
  62.2 1.8 collective-permute-start.3
  64.0 1.6 collective-permute-start.4
  65.6 2.6 collective-permute-start.7
  68.2 4.0 collective-permute-done.3
  72.2 3.3 collective-permute-start.9
  76.5 15.5 %collective-permute-done.5.rest_9_ = bf16[384,2048]{1,0:T(8,128)(2,1)} collective-permute-done((bf16[384,2048]{1,0:T(8,128)(2,1)}, bf16[384,2048]{1,0:T(8,128)(2,1)}, u32[]{:S(2)}, u32[]{:S(2)}) %collective-permute-start.5) | collective-permute-done | bytes 1572896 | tf_op jit(solution)/shard_map/ppermute | solution.py:47
  93.4 1.5 collective-permute-start.8
  95.0 8.4 %collective-permute-done.9 = bf16[96,2048]{1,0:T(8,128)(2,1)} collective-permute-done((bf16[96,2048]{1,0:T(8,128)(2,1)S(1)}, bf16[96,2048]{1,0:T(8,128)(2,1)}, u32[]{:S(2)}, u32[]{:S(2)}) %collective-permute-start.9) | collective-permute-done | bytes 393248 | tf_op jit(solution)/shard_map/ppermute | solution.py:546
  103.5 2.0 collective-permute-start.6
  106.5 16.5 %collective-permute-done.6 = bf16[96,2048]{1,0:T(8,128)(2,1)S(1)} collective-permute-done((bf16[96,2048]{1,0:T(8,128)(2,1)}, bf16[96,2048]{1,0:T(8,128)(2,1)S(1)}, u32[]{:S(2)}, u32[]{:S(2)}) %collective-permute-start.6) | collective-permute-done | bytes 393248 | tf_op jit(solution)/shard_map/ppermute | solution.py:543
  128.4 4.0 collective-permute-done.13.rest_5_.rest_7_
  133.5 17.8 %experts_near.1 = (bf16[768,1536]{1,0:T(8,128)(2,1)}, bf16[768,768]{1,0:T(8,128)(2,1)}, f32[768,128]{1,0:T(8,128)}, f32[768,128]{1,0:T(8,128)}) custom-call(s32[2]{0:T(128)} %pad_add_fusion.rank_ref, bf16[768,2048]{1,0:T(8,128)(2,1)} %bitcast.149, bf16[768,2176]{1,0:T(8,128)(2,1)} %all-gather.3.cloned.1.call-done.g.rest_0_, ...), custom_call_target="tpu_custom_call" | custom-call | flops 1048576 | bytes 65536 | tf_op jit(solution)/shard_map/experts_near/pallas_call | solution.py:517
  151.3 37.9 %experts_far.1 = (bf16[768,2048]{1,0:T(8,128)(2,1)}, bf16[768,2176]{1,0:T(8,128)(2,1)}, bf16[768,1536]{1,0:T(8,128)(2,1)}, bf16[768,768]{1,0:T(8,128)(2,1)}) custom-call(s32[2]{0:T(128)} %pad_add_fusion.rank_ref, bf16[768,2048]{1,0:T(8,128)(2,1)} %bitcast.150, bf16[768,2176]{1,0:T(8,128)(2,1)} %all-gather.3.cloned.1.call-done.g.rest_0_, ...), custom_call_target="tpu_custom_call" | custom-call | flops 1048576 | bytes 65536 | tf_op jit(solution)/shard_map/experts_far/pallas_call | solution.py:517
  189.2 6.7 %convolution_convert_fusion.1 = bf16[768,2048]{1,0:T(8,128)(2,1)} fusion(bf16[768,2048]{1,0:T(8,128)(2,1)} %bitcast.151, bf16[768,1536]{1,0:T(8,128)(2,1)} %get-tuple-element.89), kind=kOutput, calls=%fused_computation.3 | convolution fusion | flops 2417491968 | bytes 7471104 | tf_op jit(solution)/shard_map/dot_general | solution.py:36
  196.1 2.6 convolution_convert_fusion.3
  200.8 1.6 dynamic-slice_bitcast_fusion.6
  205.5 4.5 add_convert_fusion.1
  210.0 4.8 add_convert_fusion
  214.8 1.6 fusion.42
  217.9 1.7 collective-permute-done.22
  220.7 3.4 collective-permute-start.25
  224.1 4.0 convolution_convert_fusion
  228.9 14.3 %collective-permute-done.25 = bf16[96,2176]{1,0:T(8,128)(2,1)S(1)} collective-permute-done((bf16[96,2176]{1,0:T(8,128)(2,1)S(1)}, bf16[96,2176]{1,0:T(8,128)(2,1)S(1)}, u32[]{:S(2)}, u32[]{:S(2)}) %collective-permute-start.25) | collective-permute-done | bytes 417824 | tf_op jit(solution)/shard_map/ppermute | solution.py:546
  244.7 6.3 %collective-permute-start.20 = (bf16[96,2176]{1,0:T(8,128)(2,1)S(1)}, bf16[96,2176]{1,0:T(8,128)(2,1)}, u32[]{:S(2)}, u32[]{:S(2)}) collective-permute-start(bf16[96,2176]{1,0:T(8,128)(2,1)S(1)} %get-tuple-element.174), channel_id=1, source_target_pairs={{0,16},{4,20},{8,24},{12,28},{16,0},{20,4},{24,8},{28,12},{1,17},{... | collective-permute-start | bytes 1253384 | tf_op jit(solution)/shard_map/ppermute | solution.py:546
  251.0 3.1 fusion.1
  254.1 2.6 convolution_convert_fusion.2
  256.7 11.9 %collective-permute-done.26 = bf16[96,2176]{1,0:T(8,128)(2,1)S(1)} collective-permute-done((bf16[96,2176]{1,0:T(8,128)(2,1)S(1)}, bf16[96,2176]{1,0:T(8,128)(2,1)S(1)}, u32[]{:S(2)}, u32[]{:S(2)}) %collective-permute-start.26) | collective-permute-done | bytes 417824 | tf_op jit(solution)/shard_map/ppermute | solution.py:546
  270.7 1.8 fusion.16
  273.5 1.6 constant_dynamic-update-slice_fusion.7
  277.8 6.1 %convert_add_fusion = f32[768,2048]{1,0:T(8,128)} fusion(bf16[768,2048]{1,0:T(8,128)(2,1)} %collective-permute-done.47, bf16[768,2048]{1,0:T(8,128)(2,1)S(1)} %bitcast.154, bf16[768,1536]{1,0:T(8,128)(2,1)S(1)} %copy-done.17), kind=kOutput, calls=%fused_computation | convolution fusion | flops 2419064832 | bytes 13762560 | tf_op jit(solution)/shard_map/dot_general | solution.py:36
  284.6 5.1 all-to-all-start
  293.4 8.2 %all-to-all-done = bf16[8,96,256]{2,1,0:T(8,128)(2,1)S(1)} async-done(((bf16[8,96,256]{2,1,0:T(8,128)(2,1)}), bf16[8,96,256]{2,1,0:T(8,128)(2,1)S(1)}, u32[]{:S(2)}, u32[]{:S(2)}) %all-to-all-start) | async-done | bytes 393248 | tf_op jit(solution)/shard_map/all_to_all | solution.py:729
  302.2 1.8 slice_dynamic-update-slice_fusion.7
  304.0 1.8 slice_dynamic-update-slice_fusion.6
  305.7 4.9 collective-permute-done.30
  311.0 1.7 collective-permute-start.48
  313.6 28.8 %attend_back.1 = (bf16[8,272,1280]{2,1,0:T(8,128)(2,1)}, f32[8,128]{1,0:T(8,128)}, f32[1,2048]{1,0:T(1,128)}, f32[2,96,2048]{2,1,0:T(8,128)}, bf16[2,96,2048]{2,1,0:T(8,128)(2,1)}) custom-call(s32[2]{0:T(128)} %pad_add_fusion.rank_ref, bf16[384,2048]{1,0:T(8,128)(2,1)} %x.5, bf16[384,2048]{1,0:T(8,128)(2,1)} %get-tuple-element.73.xn, ...), custom_call_target="tpu_custom_call" | custom-call | flops 30000001024 | bytes 1048576 | tf_op jit(solution)/shard_map/attend_back/pallas_call | solution.py:290
  345.5 3.3 dynamic-slice_bitcast_fusion.1
  348.9 2.6 collective-permute-start.31
  354.5 31.3 %collective-permute-done.35 = bf16[96,2048]{1,0:T(8,128)(2,1)S(1)} collective-permute-done((bf16[96,2048]{1,0:T(8,128)(2,1)S(1)}, bf16[96,2048]{1,0:T(8,128)(2,1)S(1)}, u32[]{:S(2)}, u32[]{:S(2)}) %collective-permute-start.35) | collective-permute-done | bytes 393248 | tf_op jit(solution)/shard_map/ppermute | solution.py:47
  386.4 1.7 constant_dynamic-update-slice_fusion.3
  388.5 2.8 fusion.47
  391.3 4.6 collective-permute-done.36
  395.9 4.8 collective-permute-start.41
  400.9 4.5 convert_add_fusion.1
  405.5 2.0 collective-permute-start.38
  407.5 5.1 %slice_add_fusion = (f32[384,2048]{1,0:T(8,128)}, f32[384,2048]{1,0:T(8,128)}) fusion(f32[768,2048]{1,0:T(8,128)S(1)} %bitcast.158, bf16[384,2048]{1,0:T(8,128)(2,1)} %collective-permute-done.48, bf16[384,2048]{1,0:T(8,128)(2,1)S(1)} %copy-done.24), kind=kLoop, calls=%fused_computation.4 | loop fusion | flops 3145728 | bytes 15728640 | tf_op jit(solution)/shard_map/add | solution.py:789
  412.7 13.6 %reduce-scatter.2.cloned.1.call-done = bf16[1,96,2048]{2,1,0:T(8,128)(2,1)} async-done(((bf16[8,96,2048]{2,1,0:T(8,128)(2,1)}), bf16[1,96,2048]{2,1,0:T(8,128)(2,1)}) %reduce-scatter.2.cloned.1.call-update) | async-done | bytes 393232 | tf_op jit(solution)/shard_map/reduce_scatter | solution.py:740
  426.3 1.5 fusion.6
  427.8 1.9 collective-permute-start.42
  433.4 2.1 bitcast_convert_fusion
  435.5 6.1 %collective-permute-done.32 = bf16[96,2048]{1,0:T(8,128)(2,1)S(1)} collective-permute-done((bf16[96,2048]{1,0:T(8,128)(2,1)S(1)}, bf16[96,2048]{1,0:T(8,128)(2,1)S(1)}, u32[]{:S(2)}, u32[]{:S(2)}) %collective-permute-start.32) | collective-permute-done | bytes 393248 | tf_op jit(solution)/shard_map/ppermute | solution.py:47
  441.8 4.6 collective-permute-done.42
  446.4 2.1 fusion.7
  448.5 14.9 %collective-permute-start.40 = (bf16[272,1280]{1,0:T(8,128)(2,1)S(1)}, bf16[272,1280]{1,0:T(8,128)(2,1)S(1)}, u32[]{:S(2)}, u32[]{:S(2)}) collective-permute-start(bf16[272,1280]{1,0:T(8,128)(2,1)S(1)} %get-tuple-element.168), channel_id=1, source_target_pairs={{0,16},{4,20},{8,24},{12,28},{16,0},{20,4},{24,8},{28,12},{1,17},{... | collective-permute-start | bytes 2088968 | tf_op jit(solution)/shard_map/ppermute | solution.py:546
  464.9 28.4 %collective-permute-done.40 = bf16[272,1280]{1,0:T(8,128)(2,1)S(1)} collective-permute-done((bf16[272,1280]{1,0:T(8,128)(2,1)S(1)}, bf16[272,1280]{1,0:T(8,128)(2,1)S(1)}, u32[]{:S(2)}, u32[]{:S(2)}) %collective-permute-start.40) | collective-permute-done | bytes 696352 | tf_op jit(solution)/shard_map/ppermute | solution.py:546
  493.3 1.8 fusion.8
  (260 shorter events, 63.6 us)
Async XLA Ops:
  7.2 96.3 %all-gather.3.cloned.1.call-start = ((), (), s32[]{:S(2)}) async-start(), calls=%async_computation.2 | async-start | bytes 3760128 | tf_op jit(solution)/shard_map/all_gather | solution.py:625
  9.9 260.8 %all-gather.5.cloned.1.call-start = ((), (), s32[]{:S(2)}) async-start(), calls=%async_computation.3 | async-start | bytes 7077888 | tf_op jit(solution)/shard_map/all_gather | solution.py:675
  10.0 37.6 %collective-permute-start.1 = (bf16[384,2048]{1,0:T(8,128)(2,1)}, bf16[384,2048]{1,0:T(8,128)(2,1)S(1)}, u32[]{:S(2)}, u32[]{:S(2)}) collective-permute-start(bf16[384,2048]{1,0:T(8,128)(2,1)} %bitcast.8.rest_2_.rest_4_), channel_id=1, source_target_pairs={{0,2},{1,3},{2,0},{3,1},{4,6},{5,7},{6,4},{7,5},{8,10},{9,11},{10,... | collective-permute-start | bytes 4718600 | tf_op jit(solution)/shard_map/ppermute | solution.py:47
  38.3 2.6 collective-permute-start
  47.6 12.3 %collective-permute-start.2 = (bf16[96,2048]{1,0:T(8,128)(2,1)}, bf16[96,2048]{1,0:T(8,128)(2,1)S(1)}, u32[]{:S(2)}, u32[]{:S(2)}) collective-permute-start(bf16[96,2048]{1,0:T(8,128)(2,1)} %fusion.32), channel_id=1, source_target_pairs={{0,2},{1,3},{2,0},{3,1},{4,6},{5,7},{6,4},{7,5},{8,10},{9,11},{10,... | collective-permute-start | bytes 1179656 | tf_op jit(solution)/shard_map/ppermute | solution.py:47
  49.3 42.7 %collective-permute-start.5 = (bf16[384,2048]{1,0:T(8,128)(2,1)}, bf16[384,2048]{1,0:T(8,128)(2,1)}, u32[]{:S(2)}, u32[]{:S(2)}) collective-permute-start(bf16[384,2048]{1,0:T(8,128)(2,1)} %bitcast.12.rest_3_.rest_5_), channel_id=1, source_target_pairs={{0,2},{1,3},{2,0},{3,1},{4,6},{5,7},{6,4},{7,5},{8,10},{9,11},{10,... | collective-permute-start | bytes 4718600 | tf_op jit(solution)/shard_map/ppermute | solution.py:47
  62.2 61.9 %copy-start.13 = (bf16[96,2048]{1,0:T(8,128)(2,1)}, bf16[96,2048]{1,0:T(8,128)(2,1)S(1)}, u32[]{:S(2)}) copy-start(bf16[96,2048]{1,0:T(8,128)(2,1)S(1)} %get-tuple-element.163) | copy-start | bytes 1179652
  62.2 10.0 %collective-permute-start.3 = (bf16[96,2048]{1,0:T(8,128)(2,1)S(1)}, bf16[96,2048]{1,0:T(8,128)(2,1)}, u32[]{:S(2)}, u32[]{:S(2)}) collective-permute-start(bf16[96,2048]{1,0:T(8,128)(2,1)S(1)} %get-tuple-element.163), channel_id=1, source_target_pairs={{0,4},{4,0},{8,12},{12,8},{16,20},{20,16},{24,28},{28,24},{1,5},{5... | collective-permute-start | bytes 1179656 | tf_op jit(solution)/shard_map/ppermute | solution.py:543
  64.0 64.3 %collective-permute-start.12 = (bf16[384,2048]{1,0:T(8,128)(2,1)}, bf16[384,2048]{1,0:T(8,128)(2,1)}, u32[]{:S(2)}, u32[]{:S(2)}) collective-permute-start(bf16[384,2048]{1,0:T(8,128)(2,1)} %bitcast.8.rest_2_.rest_4_), channel_id=1, source_target_pairs={{0,1},{1,0},{2,3},{3,2},{4,5},{5,4},{6,7},{7,6},{8,9},{9,8},{10,11... | collective-permute-start | bytes 4718600 | tf_op jit(solution)/shard_map/ppermute | solution.py:47
  64.0 39.5 %collective-permute-start.4 = (bf16[96,2048]{1,0:T(8,128)(2,1)S(1)}, bf16[96,2048]{1,0:T(8,128)(2,1)}, u32[]{:S(2)}, u32[]{:S(2)}) collective-permute-start(bf16[96,2048]{1,0:T(8,128)(2,1)S(1)} %get-tuple-element.163), channel_id=1, source_target_pairs={{0,8},{4,12},{8,0},{12,4},{16,24},{20,28},{24,16},{28,20},{1,9},{5... | collective-permute-start | bytes 1179656 | tf_op jit(solution)/shard_map/ppermute | solution.py:546
  65.6 27.9 %collective-permute-start.7 = (bf16[96,2048]{1,0:T(8,128)(2,1)S(1)}, bf16[96,2048]{1,0:T(8,128)(2,1)}, u32[]{:S(2)}, u32[]{:S(2)}) collective-permute-start(bf16[96,2048]{1,0:T(8,128)(2,1)S(1)} %get-tuple-element.163), channel_id=1, source_target_pairs={{0,16},{4,20},{8,24},{12,28},{16,0},{20,4},{24,8},{28,12},{1,17},{... | collective-permute-start | bytes 1179656 | tf_op jit(solution)/shard_map/ppermute | solution.py:546
  72.2 31.2 %collective-permute-start.9 = (bf16[96,2048]{1,0:T(8,128)(2,1)S(1)}, bf16[96,2048]{1,0:T(8,128)(2,1)}, u32[]{:S(2)}, u32[]{:S(2)}) collective-permute-start(bf16[96,2048]{1,0:T(8,128)(2,1)S(1)} %get-tuple-element.163), channel_id=1, source_target_pairs={{0,24},{4,28},{8,16},{12,20},{16,8},{20,12},{24,0},{28,4},{1,25},{... | collective-permute-start | bytes 1179656 | tf_op jit(solution)/shard_map/ppermute | solution.py:546
  92.0 35.2 %collective-permute-start.11 = (bf16[384,2048]{1,0:T(8,128)(2,1)}, bf16[384,2048]{1,0:T(8,128)(2,1)}, u32[]{:S(2)}, u32[]{:S(2)}) collective-permute-start(bf16[384,2048]{1,0:T(8,128)(2,1)} %bitcast.160), channel_id=1, source_target_pairs={{0,2},{1,3},{2,0},{3,1},{4,6},{5,7},{6,4},{7,5},{8,10},{9,11},{10,... | collective-permute-start | bytes 4718600 | tf_op jit(solution)/shard_map/ppermute | solution.py:47
  93.4 30.6 %collective-permute-start.8 = (bf16[96,2048]{1,0:T(8,128)(2,1)}, bf16[96,2048]{1,0:T(8,128)(2,1)}, u32[]{:S(2)}, u32[]{:S(2)}) collective-permute-start(bf16[96,2048]{1,0:T(8,128)(2,1)} %collective-permute-done.7), channel_id=1, source_target_pairs={{0,4},{4,0},{8,12},{12,8},{16,20},{20,16},{24,28},{28,24},{1,5},{5... | collective-permute-start | bytes 1179656 | tf_op jit(solution)/shard_map/ppermute | solution.py:543
  103.4 22.7 %collective-permute-start.10 = (bf16[96,2048]{1,0:T(8,128)(2,1)}, bf16[96,2048]{1,0:T(8,128)(2,1)}, u32[]{:S(2)}, u32[]{:S(2)}) collective-permute-start(bf16[96,2048]{1,0:T(8,128)(2,1)} %collective-permute-done.9), channel_id=1, source_target_pairs={{0,4},{4,0},{8,12},{12,8},{16,20},{20,16},{24,28},{28,24},{1,5},{5... | collective-permute-start | bytes 1179656 | tf_op jit(solution)/shard_map/ppermute | solution.py:543
  103.5 19.5 %collective-permute-start.6 = (bf16[96,2048]{1,0:T(8,128)(2,1)}, bf16[96,2048]{1,0:T(8,128)(2,1)S(1)}, u32[]{:S(2)}, u32[]{:S(2)}) collective-permute-start(bf16[96,2048]{1,0:T(8,128)(2,1)} %collective-permute-done.4), channel_id=1, source_target_pairs={{0,4},{4,0},{8,12},{12,8},{16,20},{20,16},{24,28},{28,24},{1,5},{5... | collective-permute-start | bytes 1179656 | tf_op jit(solution)/shard_map/ppermute | solution.py:543
  127.2 5.1 %collective-permute-start.13 = (bf16[384,2048]{1,0:T(8,128)(2,1)}, bf16[384,2048]{1,0:T(8,128)(2,1)S(1)}, u32[]{:S(2)}, u32[]{:S(2)}) collective-permute-start(bf16[384,2048]{1,0:T(8,128)(2,1)} %bitcast.12.rest_3_.rest_5_), channel_id=1, source_target_pairs={{0,1},{1,0},{2,3},{3,2},{4,5},{5,4},{6,7},{7,6},{8,9},{9,8},{10,11... | collective-permute-start | bytes 4718600 | tf_op jit(solution)/shard_map/ppermute | solution.py:47
  127.3 6.0 %collective-permute-start.14 = (bf16[384,2048]{1,0:T(8,128)(2,1)}, bf16[384,2048]{1,0:T(8,128)(2,1)}, u32[]{:S(2)}, u32[]{:S(2)}) collective-permute-start(bf16[384,2048]{1,0:T(8,128)(2,1)} %bitcast.161), channel_id=1, source_target_pairs={{0,1},{1,0},{2,3},{3,2},{4,5},{5,4},{6,7},{7,6},{8,9},{9,8},{10,11... | collective-permute-start | bytes 4718600 | tf_op jit(solution)/shard_map/ppermute | solution.py:47
  127.8 23.5 %collective-permute-start.15 = (bf16[384,2048]{1,0:T(8,128)(2,1)}, bf16[384,2048]{1,0:T(8,128)(2,1)}, u32[]{:S(2)}, u32[]{:S(2)}) collective-permute-start(bf16[384,2048]{1,0:T(8,128)(2,1)} %copy-done.22), channel_id=1, source_target_pairs={{0,1},{1,0},{2,3},{3,2},{4,5},{5,4},{6,7},{7,6},{8,9},{9,8},{10,11... | collective-permute-start | bytes 4718600 | tf_op jit(solution)/shard_map/ppermute | solution.py:47
  127.9 23.4 %collective-permute-start.16 = (bf16[384,2048]{1,0:T(8,128)(2,1)}, bf16[384,2048]{1,0:T(8,128)(2,1)}, u32[]{:S(2)}, u32[]{:S(2)}) collective-permute-start(bf16[384,2048]{1,0:T(8,128)(2,1)} %collective-permute-done.5.rest_9_), channel_id=1, source_target_pairs={{0,1},{1,0},{2,3},{3,2},{4,5},{5,4},{6,7},{7,6},{8,9},{9,8},{10,11... | collective-permute-start | bytes 4718600 | tf_op jit(solution)/shard_map/ppermute | solution.py:47
  128.3 23.0 %collective-permute-start.17 = (bf16[384,2048]{1,0:T(8,128)(2,1)}, bf16[384,2048]{1,0:T(8,128)(2,1)}, u32[]{:S(2)}, u32[]{:S(2)}) collective-permute-start(bf16[384,2048]{1,0:T(8,128)(2,1)} %collective-permute-done.11.rest_14_), channel_id=1, source_target_pairs={{0,1},{1,0},{2,3},{3,2},{4,5},{5,4},{6,7},{7,6},{8,9},{9,8},{10,11... | collective-permute-start | bytes 4718600 | tf_op jit(solution)/shard_map/ppermute | solution.py:47
  195.9 14.1 %collective-permute-start.23 = (bf16[768,2048]{1,0:T(8,128)(2,1)}, bf16[768,2048]{1,0:T(8,128)(2,1)}, u32[]{:S(2)}, u32[]{:S(2)}) collective-permute-start(bf16[768,2048]{1,0:T(8,128)(2,1)} %convolution_convert_fusion.1), channel_id=1, source_target_pairs={{0,1},{1,0},{2,3},{3,2},{4,5},{5,4},{6,7},{7,6},{8,9},{9,8},{10,11... | collective-permute-start | bytes 9437192 | tf_op jit(solution)/shard_map/ppermute | solution.py:47
  198.7 6.8 %collective-permute-start.24 = (bf16[384,2048]{1,0:T(8,128)(2,1)}, bf16[384,2048]{1,0:T(8,128)(2,1)}, u32[]{:S(2)}, u32[]{:S(2)}) collective-permute-start(bf16[384,2048]{1,0:T(8,128)(2,1)} %convolution_convert_fusion.3), channel_id=1, source_target_pairs={{0,1},{1,0},{2,3},{3,2},{4,5},{5,4},{6,7},{7,6},{8,9},{9,8},{10,11... | collective-permute-start | bytes 4718600 | tf_op jit(solution)/shard_map/ppermute | solution.py:47
  202.4 17.2 %collective-permute-start.22 = (bf16[96,2176]{1,0:T(8,128)(2,1)S(1)}, bf16[96,2176]{1,0:T(8,128)(2,1)S(1)}, u32[]{:S(2)}, u32[]{:S(2)}) collective-permute-start(bf16[96,2176]{1,0:T(8,128)(2,1)S(1)} %get-tuple-element.177), channel_id=1, source_target_pairs={{0,4},{4,0},{8,12},{12,8},{16,20},{20,16},{24,28},{28,24},{1,5},{5... | collective-permute-start | bytes 1253384 | tf_op jit(solution)/shard_map/ppermute | solution.py:543
  203.5 25.0 %collective-permute-start.21 = (bf16[96,2176]{1,0:T(8,128)(2,1)S(1)}, bf16[96,2176]{1,0:T(8,128)(2,1)S(1)}, u32[]{:S(2)}, u32[]{:S(2)}) collective-permute-start(bf16[96,2176]{1,0:T(8,128)(2,1)S(1)} %get-tuple-element.178), channel_id=1, source_target_pairs={{0,4},{4,0},{8,12},{12,8},{16,20},{20,16},{24,28},{28,24},{1,5},{5... | collective-permute-start | bytes 1253384 | tf_op jit(solution)/shard_map/ppermute | solution.py:543
  204.5 38.7 %collective-permute-start.19 = (bf16[96,2176]{1,0:T(8,128)(2,1)S(1)}, bf16[96,2176]{1,0:T(8,128)(2,1)S(1)}, u32[]{:S(2)}, u32[]{:S(2)}) collective-permute-start(bf16[96,2176]{1,0:T(8,128)(2,1)S(1)} %get-tuple-element.176), channel_id=1, source_target_pairs={{0,4},{4,0},{8,12},{12,8},{16,20},{20,16},{24,28},{28,24},{1,5},{5... | collective-permute-start | bytes 1253384 | tf_op jit(solution)/shard_map/ppermute | solution.py:543
  216.4 52.2 %collective-permute-start.27 = (bf16[384,2048]{1,0:T(8,128)(2,1)S(1)}, bf16[384,2048]{1,0:T(8,128)(2,1)S(1)}, u32[]{:S(2)}, u32[]{:S(2)}) collective-permute-start(bf16[384,2048]{1,0:T(8,128)(2,1)S(1)} %get-tuple-element.181), channel_id=1, source_target_pairs={{0,2},{1,3},{2,0},{3,1},{4,6},{5,7},{6,4},{7,5},{8,10},{9,11},{10,... | collective-permute-start | bytes 4718600 | tf_op jit(solution)/shard_map/ppermute | solution.py:47
  220.7 22.5 %collective-permute-start.25 = (bf16[96,2176]{1,0:T(8,128)(2,1)S(1)}, bf16[96,2176]{1,0:T(8,128)(2,1)S(1)}, u32[]{:S(2)}, u32[]{:S(2)}) collective-permute-start(bf16[96,2176]{1,0:T(8,128)(2,1)S(1)} %fusion.14), channel_id=1, source_target_pairs={{0,24},{4,28},{8,16},{12,20},{16,8},{20,12},{24,0},{28,4},{1,25},{... | collective-permute-start | bytes 1253384 | tf_op jit(solution)/shard_map/ppermute | solution.py:546
  228.1 22.8 %copy-start.15 = (bf16[768,768]{1,0:T(8,128)(2,1)S(1)}, bf16[768,768]{1,0:T(8,128)(2,1)}, u32[]{:S(2)}) copy-start(bf16[768,768]{1,0:T(8,128)(2,1)} %get-tuple-element.82.rest_3_) | copy-start | bytes 3538948
  228.1 49.6 %collective-permute-start.47 = (bf16[768,2048]{1,0:T(8,128)(2,1)}, bf16[768,2048]{1,0:T(8,128)(2,1)}, u32[]{:S(2)}, u32[]{:S(2)}) collective-permute-start(bf16[768,2048]{1,0:T(8,128)(2,1)} %convolution_convert_fusion), channel_id=1, source_target_pairs={{0,1},{1,0},{2,3},{3,2},{4,5},{5,4},{6,7},{7,6},{8,9},{9,8},{10,11... | collective-permute-start | bytes 9437192 | tf_op jit(solution)/shard_map/ppermute | solution.py:47
  228.5 41.3 %collective-permute-start.18 = (bf16[96,2176]{1,0:T(8,128)(2,1)S(1)}, bf16[96,2176]{1,0:T(8,128)(2,1)S(1)}, u32[]{:S(2)}, u32[]{:S(2)}) collective-permute-start(bf16[96,2176]{1,0:T(8,128)(2,1)S(1)} %get-tuple-element.179), channel_id=1, source_target_pairs={{0,4},{4,0},{8,12},{12,8},{16,20},{20,16},{24,28},{28,24},{1,5},{5... | collective-permute-start | bytes 1253384 | tf_op jit(solution)/shard_map/ppermute | solution.py:543
  244.7 26.1 %collective-permute-start.20 = (bf16[96,2176]{1,0:T(8,128)(2,1)S(1)}, bf16[96,2176]{1,0:T(8,128)(2,1)}, u32[]{:S(2)}, u32[]{:S(2)}) collective-permute-start(bf16[96,2176]{1,0:T(8,128)(2,1)S(1)} %get-tuple-element.174), channel_id=1, source_target_pairs={{0,16},{4,20},{8,24},{12,28},{16,0},{20,4},{24,8},{28,12},{1,17},{... | collective-permute-start | bytes 1253384 | tf_op jit(solution)/shard_map/ppermute | solution.py:546
  251.0 17.6 %collective-permute-start.26 = (bf16[96,2176]{1,0:T(8,128)(2,1)S(1)}, bf16[96,2176]{1,0:T(8,128)(2,1)S(1)}, u32[]{:S(2)}, u32[]{:S(2)}) collective-permute-start(bf16[96,2176]{1,0:T(8,128)(2,1)S(1)} %get-tuple-element.175), channel_id=1, source_target_pairs={{0,8},{4,12},{8,0},{12,4},{16,24},{20,28},{24,16},{28,20},{1,9},{5... | collective-permute-start | bytes 1253384 | tf_op jit(solution)/shard_map/ppermute | solution.py:546
  268.6 132.1 %collective-permute-start.49 = (bf16[384,2048]{1,0:T(8,128)(2,1)}, bf16[384,2048]{1,0:T(8,128)(2,1)}, u32[]{:S(2)}, u32[]{:S(2)}) collective-permute-start(bf16[384,2048]{1,0:T(8,128)(2,1)} %convolution_convert_fusion.2), channel_id=1, source_target_pairs={{0,1},{1,0},{2,3},{3,2},{4,5},{5,4},{6,7},{7,6},{8,9},{9,8},{10,11... | collective-permute-start | bytes 4718600 | tf_op jit(solution)/shard_map/ppermute | solution.py:47
  276.3 13.4 %collective-permute-start.28 = (bf16[96,2048]{1,0:T(8,128)(2,1)S(1)}, bf16[96,2048]{1,0:T(8,128)(2,1)S(1)}, u32[]{:S(2)}, u32[]{:S(2)}) collective-permute-start(bf16[96,2048]{1,0:T(8,128)(2,1)S(1)} %get-tuple-element.161), channel_id=1, source_target_pairs={{0,2},{1,3},{2,0},{3,1},{4,6},{5,7},{6,4},{7,5},{8,10},{9,11},{10,... | collective-permute-start | bytes 1179656 | tf_op jit(solution)/shard_map/ppermute | solution.py:47
  284.6 17.0 %all-to-all-start = ((bf16[8,96,256]{2,1,0:T(8,128)(2,1)}), bf16[8,96,256]{2,1,0:T(8,128)(2,1)S(1)}, u32[]{:S(2)}, u32[]{:S(2)}) async-start(bf16[8,96,256]{2,1,0:T(8,128)(2,1)} %bitcast.148), calls=%async_computation | async-start | bytes 786432 | tf_op jit(solution)/shard_map/all_to_all | solution.py:729
  289.7 136.6 %reduce-scatter.2.cloned.1.call-start = ((), (), s32[]{:S(2)}) async-start(), calls=%async_computation.4 | async-start | bytes 3538944 | tf_op jit(solution)/shard_map/reduce_scatter | solution.py:740
  290.7 11.5 %collective-permute-start.29 = (bf16[2,96,2048]{2,1,0:T(8,128)(2,1)}, bf16[2,96,2048]{2,1,0:T(8,128)(2,1)}, u32[]{:S(2)}, u32[]{:S(2)}) collective-permute-start(bf16[2,96,2048]{2,1,0:T(8,128)(2,1)} %pad_maximum_fusion), channel_id=1, source_target_pairs={{0,1},{1,0},{2,3},{3,2},{4,5},{5,4},{6,7},{7,6},{8,9},{9,8},{10,11... | collective-permute-start | bytes 2359304 | tf_op jit(solution)/shard_map/ppermute | solution.py:47
  301.6 9.1 %collective-permute-start.30 = (bf16[8,96,256]{2,1,0:T(8,128)(2,1)S(1)}, bf16[8,96,256]{2,1,0:T(8,128)(2,1)S(1)}, u32[]{:S(2)}, u32[]{:S(2)}) collective-permute-start(bf16[8,96,256]{2,1,0:T(8,128)(2,1)S(1)} %all-to-all-done), channel_id=1, source_target_pairs={{0,2},{1,3},{2,0},{3,1},{4,6},{5,7},{6,4},{7,5},{8,10},{9,11},{10,... | collective-permute-start | bytes 1179656 | tf_op jit(solution)/shard_map/ppermute | solution.py:47
  310.7 90.2 %collective-permute-start.50 = (bf16[384,2048]{1,0:T(8,128)(2,1)}, bf16[384,2048]{1,0:T(8,128)(2,1)}, u32[]{:S(2)}, u32[]{:S(2)}) collective-permute-start(bf16[384,2048]{1,0:T(8,128)(2,1)} %add_convert_fusion.1), channel_id=1, source_target_pairs={{0,2},{1,3},{2,0},{3,1},{4,6},{5,7},{6,4},{7,5},{8,10},{9,11},{10,... | collective-permute-start | bytes 4718600 | tf_op jit(solution)/shard_map/ppermute | solution.py:47
  311.0 94.5 %collective-permute-start.48 = (bf16[384,2048]{1,0:T(8,128)(2,1)}, bf16[384,2048]{1,0:T(8,128)(2,1)}, u32[]{:S(2)}, u32[]{:S(2)}) collective-permute-start(bf16[384,2048]{1,0:T(8,128)(2,1)} %get-tuple-element.122), channel_id=1, source_target_pairs={{0,2},{1,3},{2,0},{3,1},{4,6},{5,7},{6,4},{7,5},{8,10},{9,11},{10,... | collective-permute-start | bytes 4718600 | tf_op jit(solution)/shard_map/ppermute | solution.py:47
  313.6 38.1 %collective-permute-start.46 = (bf16[2,8,96,256]{3,2,0,1:T(8,128)(2,1)}, bf16[2,8,96,256]{3,2,0,1:T(8,128)(2,1)}, u32[]{:S(2)}, u32[]{:S(2)}) collective-permute-start(bf16[2,8,96,256]{3,2,0,1:T(8,128)(2,1)} %pad_maximum_fusion.3), channel_id=1, source_target_pairs={{0,1},{1,0},{2,3},{3,2},{4,5},{5,4},{6,7},{7,6},{8,9},{9,8},{10,11... | collective-permute-start | bytes 2359304 | tf_op jit(solution)/shard_map/ppermute | solution.py:47
  343.9 5.0 collective-permute-start.34
  345.5 42.9 %slice-start = ((s8[6291456]{0:T(1024)(128)(4,1)}), s8[2097152]{0:T(1024)(128)(4,1)S(1)}, s32[]{:S(2)}) async-start(s8[6291456]{0:T(1024)(128)(4,1)} %bitcast.155), calls=%async_computation.5 | async-start | bytes 4194304
  348.9 63.8 %collective-permute-start.31 = (bf16[272,1280]{1,0:T(8,128)(2,1)S(1)}, bf16[272,1280]{1,0:T(8,128)(2,1)}, u32[]{:S(2)}, u32[]{:S(2)}) collective-permute-start(bf16[272,1280]{1,0:T(8,128)(2,1)S(1)} %get-tuple-element.173), channel_id=1, source_target_pairs={{0,4},{4,0},{8,12},{12,8},{16,20},{20,16},{24,28},{28,24},{1,5},{5... | collective-permute-start | bytes 2088968 | tf_op jit(solution)/shard_map/ppermute | solution.py:543
  351.5 37.0 %slice-start.1 = ((s8[6291456]{0:T(1024)(128)(4,1)}), s8[4194304]{0:T(1024)(128)(4,1)S(1)}, s32[]{:S(2)}) async-start(s8[6291456]{0:T(1024)(128)(4,1)} %bitcast.155), calls=%async_computation.6 | async-start | bytes 8388608
  351.7 34.1 %copy-start.12 = (bf16[384,2048]{1,0:T(8,128)(2,1)S(1)}, bf16[384,2048]{1,0:T(8,128)(2,1)}, u32[]{:S(2)}) copy-start(bf16[384,2048]{1,0:T(8,128)(2,1)} %x.5) | copy-start | bytes 4718596
  351.7 34.1 %copy-start.33 = (f32[2048]{0:T(1024)S(1)}, f32[2048]{0:T(1024)}, u32[]{:S(2)}) copy-start(f32[2048]{0:T(1024)} %param.22) | copy-start | bytes 24580
  351.8 34.0 %collective-permute-start.35 = (bf16[96,2048]{1,0:T(8,128)(2,1)S(1)}, bf16[96,2048]{1,0:T(8,128)(2,1)S(1)}, u32[]{:S(2)}, u32[]{:S(2)}) collective-permute-start(bf16[96,2048]{1,0:T(8,128)(2,1)S(1)} %fusion.33), channel_id=1, source_target_pairs={{0,2},{1,3},{2,0},{3,1},{4,6},{5,7},{6,4},{7,5},{8,10},{9,11},{10,... | collective-permute-start | bytes 1179656 | tf_op jit(solution)/shard_map/ppermute | solution.py:47
  354.4 31.7 %copy-start.9 = (bf16[4,8,96,256]{3,2,0,1:T(8,128)(2,1)}, bf16[4,8,96,256]{3,2,0,1:T(8,128)(2,1)S(1)}, u32[]{:S(2)}) copy-start(bf16[4,8,96,256]{3,2,0,1:T(8,128)(2,1)S(1)} %slice_dynamic-update-slice_fusion) | copy-start | bytes 4718596
  354.4 31.9 %copy-start.36 = (f32[96]{0:T(128)S(1)}, f32[96]{0:T(128)}, u32[]{:S(2)}) copy-start(f32[96]{0:T(128)} %copy-done.34) | copy-start | bytes 1156
  354.5 31.9 %copy-start.39 = (f32[96]{0:T(128)S(1)}, f32[96]{0:T(128)}, u32[]{:S(2)}) copy-start(f32[96]{0:T(128)} %copy-done.38) | copy-start | bytes 1156
  388.0 7.8 %collective-permute-start.36 = (bf16[96,2048]{1,0:T(8,128)(2,1)S(1)}, bf16[96,2048]{1,0:T(8,128)(2,1)S(1)}, u32[]{:S(2)}, u32[]{:S(2)}) collective-permute-start(bf16[96,2048]{1,0:T(8,128)(2,1)S(1)} %get-tuple-element.157), channel_id=1, source_target_pairs={{0,2},{1,3},{2,0},{3,1},{4,6},{5,7},{6,4},{7,5},{8,10},{9,11},{10,... | collective-permute-start | bytes 1179656 | tf_op jit(solution)/shard_map/ppermute | solution.py:47
  395.9 45.9 %collective-permute-start.41 = (bf16[272,1280]{1,0:T(8,128)(2,1)}, bf16[272,1280]{1,0:T(8,128)(2,1)}, u32[]{:S(2)}, u32[]{:S(2)}) collective-permute-start(bf16[272,1280]{1,0:T(8,128)(2,1)} %get-tuple-element.171), channel_id=1, source_target_pairs={{0,4},{4,0},{8,12},{12,8},{16,20},{20,16},{24,28},{28,24},{1,5},{5... | collective-permute-start | bytes 2088968 | tf_op jit(solution)/shard_map/ppermute | solution.py:543
  400.7 45.7 %collective-permute-start.39 = (bf16[272,1280]{1,0:T(8,128)(2,1)}, bf16[272,1280]{1,0:T(8,128)(2,1)}, u32[]{:S(2)}, u32[]{:S(2)}) collective-permute-start(bf16[272,1280]{1,0:T(8,128)(2,1)} %get-tuple-element.170), channel_id=1, source_target_pairs={{0,4},{4,0},{8,12},{12,8},{16,20},{20,16},{24,28},{28,24},{1,5},{5... | collective-permute-start | bytes 2088968 | tf_op jit(solution)/shard_map/ppermute | solution.py:543
  400.8 11.8 %collective-permute-start.37 = (bf16[2,96,2048]{2,1,0:T(8,128)(2,1)S(1)}, bf16[2,96,2048]{2,1,0:T(8,128)(2,1)S(1)}, u32[]{:S(2)}, u32[]{:S(2)}) collective-permute-start(bf16[2,96,2048]{2,1,0:T(8,128)(2,1)S(1)} %pad_maximum_fusion.2), channel_id=1, source_target_pairs={{0,1},{1,0},{2,3},{3,2},{4,5},{5,4},{6,7},{7,6},{8,9},{9,8},{10,11... | collective-permute-start | bytes 2359304 | tf_op jit(solution)/shard_map/ppermute | solution.py:47
  405.5 59.4 %collective-permute-start.38 = (bf16[272,1280]{1,0:T(8,128)(2,1)}, bf16[272,1280]{1,0:T(8,128)(2,1)}, u32[]{:S(2)}, u32[]{:S(2)}) collective-permute-start(bf16[272,1280]{1,0:T(8,128)(2,1)} %get-tuple-element.172), channel_id=1, source_target_pairs={{0,4},{4,0},{8,12},{12,8},{16,20},{20,16},{24,28},{28,24},{1,5},{5... | collective-permute-start | bytes 2088968 | tf_op jit(solution)/shard_map/ppermute | solution.py:543
  427.8 18.6 %collective-permute-start.42 = (bf16[272,1280]{1,0:T(8,128)(2,1)S(1)}, bf16[272,1280]{1,0:T(8,128)(2,1)S(1)}, u32[]{:S(2)}, u32[]{:S(2)}) collective-permute-start(bf16[272,1280]{1,0:T(8,128)(2,1)S(1)} %fusion.6), channel_id=1, source_target_pairs={{0,24},{4,28},{8,16},{12,20},{16,8},{20,12},{24,0},{28,4},{1,25},{... | collective-permute-start | bytes 2088968 | tf_op jit(solution)/shard_map/ppermute | solution.py:546
  431.9 9.7 %collective-permute-start.32 = (bf16[96,2048]{1,0:T(8,128)(2,1)S(1)}, bf16[96,2048]{1,0:T(8,128)(2,1)S(1)}, u32[]{:S(2)}, u32[]{:S(2)}) collective-permute-start(bf16[96,2048]{1,0:T(8,128)(2,1)S(1)} %get-tuple-element.159), channel_id=1, source_target_pairs={{0,2},{1,3},{2,0},{3,1},{4,6},{5,7},{6,4},{7,5},{8,10},{9,11},{10,... | collective-permute-start | bytes 1179656 | tf_op jit(solution)/shard_map/ppermute | solution.py:47
  441.7 22.4 %collective-permute-start.33 = (bf16[2,96,2048]{2,1,0:T(8,128)(2,1)S(1)}, bf16[2,96,2048]{2,1,0:T(8,128)(2,1)S(1)}, u32[]{:S(2)}, u32[]{:S(2)}) collective-permute-start(bf16[2,96,2048]{2,1,0:T(8,128)(2,1)S(1)} %pad_maximum_fusion.1), channel_id=1, source_target_pairs={{0,1},{1,0},{2,3},{3,2},{4,5},{5,4},{6,7},{7,6},{8,9},{9,8},{10,11... | collective-permute-start | bytes 2359304 | tf_op jit(solution)/shard_map/ppermute | solution.py:47
  448.5 44.8 %collective-permute-start.40 = (bf16[272,1280]{1,0:T(8,128)(2,1)S(1)}, bf16[272,1280]{1,0:T(8,128)(2,1)S(1)}, u32[]{:S(2)}, u32[]{:S(2)}) collective-permute-start(bf16[272,1280]{1,0:T(8,128)(2,1)S(1)} %get-tuple-element.168), channel_id=1, source_target_pairs={{0,16},{4,20},{8,24},{12,28},{16,0},{20,4},{24,8},{28,12},{1,17},{... | collective-permute-start | bytes 2088968 | tf_op jit(solution)/shard_map/ppermute | solution.py:546
  463.4 29.9 %collective-permute-start.43 = (bf16[272,1280]{1,0:T(8,128)(2,1)S(1)}, bf16[272,1280]{1,0:T(8,128)(2,1)S(1)}, u32[]{:S(2)}, u32[]{:S(2)}) collective-permute-start(bf16[272,1280]{1,0:T(8,128)(2,1)S(1)} %get-tuple-element.169), channel_id=1, source_target_pairs={{0,8},{4,12},{8,0},{12,4},{16,24},{20,28},{24,16},{28,20},{1,9},{5... | collective-permute-start | bytes 2088968 | tf_op jit(solution)/shard_map/ppermute | solution.py:546
  495.1 1.3 collective-permute-start.44
  496.4 4.1 collective-permute-start.45
  (39 other events, 215.8 us)
Sparse Core Ops, SparseCore 0:
  10.8 79.2 all-gather.2
  127.4 114.2 all-gather.4
  344.0 82.2 reduce-scatter.1
